TPU v7x, 256 devices: a whole 4x4x8 slice. The times are simulated.
256 devices in a mesh: ctx: 16 (over z, y_lo), grp: 16 (over y_hi, x, core).
Axes of the slice: x: 4, y: 4 (y_hi: 2, y_lo: 2; y = y_hi * 2 + y_lo), z: 8, core: 2. Of those that a mesh axis runs over, the one named last changes fastest.
Arguments:
- tokens: bfloat16 [32768, 3072], P(('ctx', 'grp')), may hold values from -48 to 48
- w_qkv: bfloat16 [3072, 6144], P(None, 'grp')
- w_out: bfloat16 [2048, 3072], P('grp'), may hold values from -0.125 to 0.125
- source_row: int32 [16, 2048], P('ctx'), may hold values from 0 to 2047, each once within a row
- key_tiles: int32 [256, 30], P('ctx'), may hold values from 0 to 255, as said below
- key_count: int32 [256], P('ctx'), may hold values from 6 to 30
Outputs:
- mixed: bfloat16 [32768, 3072], P(('ctx', 'grp'))
Inputs may be any that keep to these rules, and one draw needn't show every extreme that they name: Each row of source_row names every loader row of its tile-frame once. Tile q lies in tile-frame q // 16. key_tiles[q, j] for j < key_count[q] are distinct tiles in tile-frames at most 2 away from q's; entries from key_count[q] on equal q.
All inputs are finite; a program needn't handle non-finite values.
Results may differ from a plain program's by a relative error of at most 0.019.
Values may be sent and summed in bfloat16 or wider, within the bound.
No kernel may reach another device: no remote copies, remote signals or barrier semaphores. Data moves between devices by JAX's collectives and lax.ppermute only.
A program may use at most 64 MiB of HBM per device.

v0:
```python
import math

import jax
import jax.numpy as jnp
from jax import lax
from jax.sharding import PartitionSpec as P


def from_behind(array, axis, by):
    length = lax.axis_size(axis)
    pairs = [(i, i + by) for i in range(length) if 0 <= i + by < length]
    return lax.ppermute(array, axis, pairs)


def body(tokens, w_qkv, w_out, source_row, key_tiles, key_count):
    head_size = w_out.shape[0]
    local_tiles = key_tiles.shape[0]
    listed_slots = key_tiles.shape[1]
    loader_qkv = jnp.dot(
        lax.all_gather(tokens, "grp", axis=0, tiled=True), w_qkv, preferred_element_type=jnp.float32
    ).astype(jnp.bfloat16)
    qkv = loader_qkv[source_row[0]]
    group_rows = qkv.shape[0]
    tile_rows = group_rows // local_tiles
    queries = qkv[:, :head_size].reshape(local_tiles, tile_rows, head_size)
    kv_local = qkv[:, head_size:]
    span_frames = max(lax.axis_size("ctx") // 8, 1)
    before_list = []
    after_list = []
    for distance in range(1, span_frames + 1):
        before_list.append(from_behind(kv_local, "ctx", distance))
        after_list.append(from_behind(kv_local, "ctx", -distance))
    window = jnp.concatenate(before_list[::-1] + [kv_local] + after_list, axis=0)
    window_tiles = window.reshape(-1, tile_rows, 2 * head_size)
    first_tile = (lax.axis_index("ctx") - span_frames) * local_tiles
    local_index = key_tiles - first_tile
    tiles_per_step = 1
    while tiles_per_step * 2 <= local_tiles and tiles_per_step * tile_rows < 512:
        tiles_per_step = tiles_per_step * 2
    score_scale = 1.0 / math.sqrt(head_size)
    slot_number = jnp.arange(listed_slots * tile_rows, dtype=jnp.int32) // tile_rows

    def attend(bundle):
        query_group, index_group, count_group = bundle
        gathered = window_tiles[index_group].reshape(
            tiles_per_step, listed_slots * tile_rows, 2 * head_size
        )
        scores = (
            jnp.einsum(
                "gqd,gkd->gqk",
                query_group,
                gathered[:, :, :head_size],
                preferred_element_type=jnp.float32,
            )
            * score_scale
        )
        allowed = slot_number[None, None, :] < count_group[:, None, None]
        scores = jnp.where(allowed, scores, -1e30)
        row_max = jnp.max(scores, axis=2, keepdims=True)
        exponent = jnp.exp(scores - row_max)
        totals = jnp.sum(exponent, axis=2, keepdims=True)
        weights = exponent.astype(jnp.bfloat16)
        weighted = jnp.einsum(
            "gqk,gkd->gqd", weights, gathered[:, :, head_size:], preferred_element_type=jnp.float32
        )
        return (weighted / totals).astype(jnp.bfloat16)

    steps_count = local_tiles // tiles_per_step
    attended = lax.map(
        attend,
        (
            queries.reshape(steps_count, tiles_per_step, tile_rows, head_size),
            local_index.reshape(steps_count, tiles_per_step, listed_slots),
            key_count.reshape(steps_count, tiles_per_step),
        ),
    )
    attended = attended.reshape(group_rows, head_size)
    return lax.psum_scatter(
        jnp.dot(attended, w_out, preferred_element_type=jnp.float32).astype(jnp.bfloat16),
        "grp",
        scatter_dimension=0,
        tiled=True,
    )


def solution(mesh):
    in_specs = (
        P(("ctx", "grp"), None),
        P(None, "grp"),
        P("grp", None),
        P("ctx", None),
        P("ctx", None),
        P("ctx"),
    )
    out_specs = P(("ctx", "grp"), None)
    return jax.shard_map(body, mesh=mesh, in_specs=in_specs, out_specs=out_specs, check_vma=False)
```

profile of v0, /device:TPU:1, one launch (start us, length us, event | category | flops | bytes accessed | tf_op | source)
XLA Modules:
  0.0 401.6 jit_solution(2454501354178696943)
XLA Ops:
  8.0 102.3 %all-gather.2.cloned.1.call-done = bf16[2048,3072]{1,0:T(8,128)(2,1)} async-done(((bf16[128,3072]{1,0:T(8,128)(2,1)}), bf16[2048,3072]{1,0:T(8,128)(2,1)}) %all-gather.2.cloned.1.call-update) | async-done | bytes 12582928 | tf_op jit(solution)/shard_map/all_gather | solution.py:20
  110.4 10.5 %convolution_convert_fusion.1 = bf16[2048,384]{1,0:T(8,128)(2,1)} fusion(bf16[2048,3072]{1,0:T(8,128)(2,1)} %all-gather.2.cloned.1.call-done, bf16[3072,384]{1,0:T(8,128)(2,1)S(1)} %copy-done), kind=kOutput, calls=%fused_computation.38 | convolution fusion | flops 4832624640 | bytes 16515072 | tf_op jit(solution)/shard_map/dot_general | solution.py:19
  120.9 10.5 %gather_fusion.1 = bf16[2048,384]{1,0:T(8,128)(2,1)} fusion(bf16[2048,384]{1,0:T(8,128)(2,1)} %convolution_convert_fusion.1, s32[2048]{0:T(1024)S(1)} %broadcast_clamp_fusion), kind=kCustom, calls=%fused_computation.1 | custom fusion | bytes 3153920 | tf_op jit(solution)/shard_map/gather | solution.py:22
  131.4 2.3 slice.23
  133.7 4.2 %collective-permute-start = (bf16[2048,256]{1,0:T(8,128)(2,1)}, bf16[2048,256]{1,0:T(8,128)(2,1)}, u32[]{:S(2)}, u32[]{:S(2)}) collective-permute-start(bf16[2048,256]{1,0:T(8,128)(2,1)} %slice.23), channel_id=1, source_target_pairs={{0,32},{16,48},{32,64},{48,80},{64,96},{80,112},{96,128},{112,144}... | collective-permute-start | bytes 3145736 | tf_op jit(solution)/shard_map/ppermute | solution.py:12
  137.8 3.2 collective-permute-start.1
  143.7 15.7 %collective-permute-done = bf16[2048,256]{1,0:T(8,128)(2,1)} collective-permute-done((bf16[2048,256]{1,0:T(8,128)(2,1)}, bf16[2048,256]{1,0:T(8,128)(2,1)}, u32[]{:S(2)}, u32[]{:S(2)}) %collective-permute-start) | collective-permute-done | bytes 1048608 | tf_op jit(solution)/shard_map/ppermute | solution.py:12
  159.5 1.3 constant_dynamic-update-slice_fusion.4
  160.8 24.0 %collective-permute-done.1 = bf16[2048,256]{1,0:T(8,128)(2,1)} collective-permute-done((bf16[2048,256]{1,0:T(8,128)(2,1)}, bf16[2048,256]{1,0:T(8,128)(2,1)}, u32[]{:S(2)}, u32[]{:S(2)}) %collective-permute-start.1) | collective-permute-done | bytes 1048608 | tf_op jit(solution)/shard_map/ppermute | solution.py:12
  184.8 1.3 constant_dynamic-update-slice_fusion.3
  186.1 1.3 constant_dynamic-update-slice_fusion.2
  187.4 1.3 constant_dynamic-update-slice_fusion.1
  189.6 2.3 copy-done.1
  191.9 67.7 %while.11 = (s32[]{:T(128)}, bf16[4,4,128,128]{3,2,1,0:T(8,128)(2,1)S(1)}, s32[4,4]{1,0:T(4,128)S(1)}, bf16[4,4,128,128]{3,2,1,0:T(8,128)(2,1)S(1)}, s32[4,4,30]...) while((s32[]{:T(128)}, bf16[4,4,128,128]{3,2,1,0:T(8,128)(2,1)S(1)}, ...), condition=%wide.region_3.4_spmd.clone, body=%wide.region_0.3_spmd.clone.sunk | while | flops 1028437376 | bytes 71151096 | solution.py:69
  192.0 8.9 %gather_fusion = bf16[120,128,256]{2,1,0:T(8,128)(2,1)} fusion(bf16[80,128,256]{2,1,0:T(8,128)(2,1)} %get-tuple-element.131, s32[1024]{0:T(1024)S(1)} %pad_clamp_fusion.2), kind=kCustom, calls=%fused_computation.clone.clone.1 | custom fusion | bytes 15729120 | tf_op jit(solution)/shard_map/while/body/eval_jaxpr/gather | solution.py:45
  201.0 3.7 fusion.56
  204.7 1.9 fusion.57
  206.6 2.2 fusion.58
  208.9 8.9 %gather_fusion = bf16[120,128,256]{2,1,0:T(8,128)(2,1)} fusion(bf16[80,128,256]{2,1,0:T(8,128)(2,1)} %get-tuple-element.131, s32[1024]{0:T(1024)S(1)} %pad_clamp_fusion.2), kind=kCustom, calls=%fused_computation.clone.clone.1 | custom fusion | bytes 15729120 | tf_op jit(solution)/shard_map/while/body/eval_jaxpr/gather | solution.py:45
  217.9 3.7 fusion.56
  221.6 1.9 fusion.57
  223.5 2.2 fusion.58
  225.9 8.9 %gather_fusion = bf16[120,128,256]{2,1,0:T(8,128)(2,1)} fusion(bf16[80,128,256]{2,1,0:T(8,128)(2,1)} %get-tuple-element.131, s32[1024]{0:T(1024)S(1)} %pad_clamp_fusion.2), kind=kCustom, calls=%fused_computation.clone.clone.1 | custom fusion | bytes 15729120 | tf_op jit(solution)/shard_map/while/body/eval_jaxpr/gather | solution.py:45
  234.9 3.7 fusion.56
  238.5 1.9 fusion.57
  240.4 2.2 fusion.58
  242.8 8.9 %gather_fusion = bf16[120,128,256]{2,1,0:T(8,128)(2,1)} fusion(bf16[80,128,256]{2,1,0:T(8,128)(2,1)} %get-tuple-element.131, s32[1024]{0:T(1024)S(1)} %pad_clamp_fusion.2), kind=kCustom, calls=%fused_computation.clone.clone.1 | custom fusion | bytes 15729120 | tf_op jit(solution)/shard_map/while/body/eval_jaxpr/gather | solution.py:45
  251.8 3.7 fusion.56
  255.5 1.9 fusion.57
  257.4 2.2 fusion.58
  259.6 7.5 %convolution_convert_fusion = bf16[2048,3072]{1,0:T(8,128)(2,1)} fusion(bf16[2048,128]{1,0:T(8,128)(2,1)S(1)} %bitcast.43, bf16[128,3072]{1,0:T(8,128)(2,1)} %param.10), kind=kOutput, calls=%fused_computation.37 | convolution fusion | flops 1616904192 | bytes 13893632 | tf_op jit(solution)/shard_map/dot_general | solution.py:79
  267.1 127.7 %reduce-scatter.2.cloned.1.call-done = bf16[128,3072]{1,0:T(8,128)(2,1)} async-done(((bf16[2048,3072]{1,0:T(8,128)(2,1)}), bf16[128,3072]{1,0:T(8,128)(2,1)}) %reduce-scatter.2.cloned.1.call-update) | async-done | bytes 786448 | tf_op jit(solution)/shard_map/reduce_scatter | solution.py:78
  (67 shorter events, 5.8 us)
Async XLA Ops:
  6.5 103.8 %copy-start = (bf16[3072,384]{1,0:T(8,128)(2,1)S(1)}, bf16[3072,384]{1,0:T(8,128)(2,1)}, u32[]{:S(2)}) copy-start(bf16[3072,384]{1,0:T(8,128)(2,1)} %param.9) | copy-start | bytes 7077892
  6.5 103.8 %all-gather.2.cloned.1.call-start = ((), (), s32[]{:S(2)}) async-start(), calls=%async_computation.1 | async-start | bytes 13369344 | tf_op jit(solution)/shard_map/all_gather | solution.py:20
  7.3 387.5 %reduce-scatter.2.cloned.1.call-start = ((), (), s32[]{:S(2)}) async-start(), calls=%async_computation.2 | async-start | bytes 13369344 | tf_op jit(solution)/shard_map/reduce_scatter | solution.py:78
  120.9 21.5 %copy-start.2 = (s32[16,30]{1,0:T(8,128)S(1)}, s32[16,30]{1,0:T(8,128)}, u32[]{:S(2)}) copy-start(s32[16,30]{1,0:T(8,128)} %param.12) | copy-start | bytes 5764
  120.9 21.5 %copy-start.3 = (s32[16]{0:T(128)S(1)}, s32[16]{0:T(128)}, u32[]{:S(2)}) copy-start(s32[16]{0:T(128)} %param.13) | copy-start | bytes 196
  131.3 60.6 %slice-start.2 = ((bf16[2048,384]{1,0:T(8,128)(2,1)}), bf16[2048,128]{1,0:T(8,128)(2,1)S(1)}, s32[]{:S(2)}) async-start(bf16[2048,384]{1,0:T(8,128)(2,1)} %gather_fusion.1), calls=%async_computation.5 | async-start | bytes 1048576 | tf_op jit(solution)/shard_map/slice | solution.py:25
  133.7 25.8 %collective-permute-start = (bf16[2048,256]{1,0:T(8,128)(2,1)}, bf16[2048,256]{1,0:T(8,128)(2,1)}, u32[]{:S(2)}, u32[]{:S(2)}) collective-permute-start(bf16[2048,256]{1,0:T(8,128)(2,1)} %slice.23), channel_id=1, source_target_pairs={{0,32},{16,48},{32,64},{48,80},{64,96},{80,112},{96,128},{112,144}... | collective-permute-start | bytes 3145736 | tf_op jit(solution)/shard_map/ppermute | solution.py:12
  137.8 47.0 %collective-permute-start.1 = (bf16[2048,256]{1,0:T(8,128)(2,1)}, bf16[2048,256]{1,0:T(8,128)(2,1)}, u32[]{:S(2)}, u32[]{:S(2)}) collective-permute-start(bf16[2048,256]{1,0:T(8,128)(2,1)} %slice.23), channel_id=1, source_target_pairs={{0,16},{16,32},{32,48},{48,64},{64,80},{80,96},{96,112},{112,128},... | collective-permute-start | bytes 3145736 | tf_op jit(solution)/shard_map/ppermute | solution.py:12
  141.0 46.4 %collective-permute-start.2 = (bf16[2048,256]{1,0:T(8,128)(2,1)}, bf16[2048,256]{1,0:T(8,128)(2,1)}, u32[]{:S(2)}, u32[]{:S(2)}) collective-permute-start(bf16[2048,256]{1,0:T(8,128)(2,1)} %slice.23), channel_id=1, source_target_pairs={{16,0},{32,16},{48,32},{64,48},{80,64},{96,80},{112,96},{128,112},... | collective-permute-start | bytes 3145736 | tf_op jit(solution)/shard_map/ppermute | solution.py:12
  142.4 47.0 %collective-permute-start.3 = (bf16[2048,256]{1,0:T(8,128)(2,1)}, bf16[2048,256]{1,0:T(8,128)(2,1)S(1)}, u32[]{:S(2)}, u32[]{:S(2)}) collective-permute-start(bf16[2048,256]{1,0:T(8,128)(2,1)} %slice.23), channel_id=1, source_target_pairs={{32,0},{48,16},{64,32},{80,48},{96,64},{112,80},{128,96},{144,112}... | collective-permute-start | bytes 3145736 | tf_op jit(solution)/shard_map/ppermute | solution.py:12
  189.6 2.3 copy-start.1
  201.0 5.6 %slice-start = ((s8[7864320]{0:T(1024)(128)(4,1)}), s8[4194304]{0:T(1024)(128)(4,1)S(1)}, s32[]{:S(2)}) async-start(s8[7864320]{0:T(1024)(128)(4,1)} %bitcast.38), calls=%async_computation.3 | async-start | bytes 8388608 | tf_op jit(solution)/shard_map/while
  201.0 5.6 %slice-start.1 = ((s8[7864320]{0:T(1024)(128)(4,1)}), s8[3670016]{0:T(1024)(128)(4,1)S(1)}, s32[]{:S(2)}) async-start(s8[7864320]{0:T(1024)(128)(4,1)} %bitcast.38), calls=%async_computation.4 | async-start | bytes 7340032 | tf_op jit(solution)/shard_map/while
  217.9 5.6 %slice-start = ((s8[7864320]{0:T(1024)(128)(4,1)}), s8[4194304]{0:T(1024)(128)(4,1)S(1)}, s32[]{:S(2)}) async-start(s8[7864320]{0:T(1024)(128)(4,1)} %bitcast.38), calls=%async_computation.3 | async-start | bytes 8388608 | tf_op jit(solution)/shard_map/while
  217.9 5.6 %slice-start.1 = ((s8[7864320]{0:T(1024)(128)(4,1)}), s8[3670016]{0:T(1024)(128)(4,1)S(1)}, s32[]{:S(2)}) async-start(s8[7864320]{0:T(1024)(128)(4,1)} %bitcast.38), calls=%async_computation.4 | async-start | bytes 7340032 | tf_op jit(solution)/shard_map/while
  234.8 5.6 %slice-start = ((s8[7864320]{0:T(1024)(128)(4,1)}), s8[4194304]{0:T(1024)(128)(4,1)S(1)}, s32[]{:S(2)}) async-start(s8[7864320]{0:T(1024)(128)(4,1)} %bitcast.38), calls=%async_computation.3 | async-start | bytes 8388608 | tf_op jit(solution)/shard_map/while
  234.8 5.6 %slice-start.1 = ((s8[7864320]{0:T(1024)(128)(4,1)}), s8[3670016]{0:T(1024)(128)(4,1)S(1)}, s32[]{:S(2)}) async-start(s8[7864320]{0:T(1024)(128)(4,1)} %bitcast.38), calls=%async_computation.4 | async-start | bytes 7340032 | tf_op jit(solution)/shard_map/while
  251.8 5.6 %slice-start = ((s8[7864320]{0:T(1024)(128)(4,1)}), s8[4194304]{0:T(1024)(128)(4,1)S(1)}, s32[]{:S(2)}) async-start(s8[7864320]{0:T(1024)(128)(4,1)} %bitcast.38), calls=%async_computation.3 | async-start | bytes 8388608 | tf_op jit(solution)/shard_map/while
  251.8 5.6 %slice-start.1 = ((s8[7864320]{0:T(1024)(128)(4,1)}), s8[3670016]{0:T(1024)(128)(4,1)S(1)}, s32[]{:S(2)}) async-start(s8[7864320]{0:T(1024)(128)(4,1)} %bitcast.38), calls=%async_computation.4 | async-start | bytes 7340032 | tf_op jit(solution)/shard_map/while
Sparse Core Ops, SparseCore 0:
  10.1 100.2 all-gather.1
  267.2 127.5 reduce-scatter.1
where the time goes:
time: 402 us
  waiting for transfers between devices  271 us (67%)
  local copies, waits for them, and re-layouts  56.4 us (14%)
  matrix products  41.4 us (10%)
  between operations  13.5 us (3%)
  starting transfers between devices  9.95 us (2%)
  other arithmetic  8.73 us (2%)
    reduce_scatter x1, waiting for transfers between devices, body(): lax.psum_scatter(jnp.dot(attended, w_out, preferred_element_type=jnp.floa...  128 us
    all_gather x1, waiting for transfers between devices, body(): lax.all_gather(tokens, 'grp', axis=0, tiled=True)  102 us
    ppermute x4, waiting for transfers between devices, from_behind(): return lax.ppermute(array, axis, pairs)  40.6 us
    gather x4, local copies, waits for them, and re-layouts, attend(): window_tiles[index_group]  35.5 us
    dot_general x4, matrix products, attend(): jnp.einsum('gqd,gkd->gqk', query_group, gathered[:, :, :head_size], prefe...  14.7 us
    dot_general x1, matrix products, body(): jnp.dot(lax.all_gather(tokens, 'grp', axis=0, tiled=True), w_qkv, preferr...  10.5 us
    gather x1, local copies, waits for them, and re-layouts, body(): qkv = loader_qkv[source_row[0]]  10.5 us
    ppermute x4, starting transfers between devices, from_behind(): return lax.ppermute(array, axis, pairs)  9.9 us
  transfers between devices with their start and end apart: 6, of which 5 were waited for; matrix products, arithmetic and copies ran while one was open for 1% of the time, Pallas kernels for 0%

commit v1 on v0

v1 whole, which is shorter than its diff:
```python
import functools
import math

import jax
import jax.numpy as jnp
from jax import lax
from jax.experimental import pallas as pl
from jax.experimental.pallas import tpu as pltpu
from jax.sharding import Mesh
from jax.sharding import PartitionSpec as P

BF = jnp.bfloat16
F32 = jnp.float32
TILE = 128
LOG2E = 1.4426950408889634
VM = pltpu.VMEM
SM = pltpu.SMEM
CTX = ("z", "yl")
CHIPS = ("yh", "x")
ALL = ("z", "yl", "yh", "x", "core")
WHOLE_VM = pl.BlockSpec(memory_space=VM)
WHOLE_SM = pl.BlockSpec(memory_space=SM)
WHOLE_ANY = pl.BlockSpec(memory_space=pl.ANY)


def round_x(array, by):
    return lax.ppermute(array, "x", [(i, (i + by) % 4) for i in range(4)])


def swap(array, axis):
    return lax.ppermute(array, axis, [(0, 1), (1, 0)])


def cut(array, dim, start, stop):
    return lax.slice_in_dim(array, start, stop, axis=dim)


def gather_chips(array, dim, first, half_own, half_rest):
    size = array.shape[dim]
    rest = cut(array, dim, first, size)
    far = swap(rest, "yh")

    def along_x(block, half):
        one, three = round_x(block, 1), round_x(block, -1)
        low = round_x(cut(one, dim, 0, half), 1)
        high = round_x(cut(three, dim, half, block.shape[dim]), -1)
        return one, three, low, high

    one, three, low, high = along_x(array, half_own)
    f_one, f_three, f_low, f_high = along_x(far, half_rest)
    out = [(0, 0, 0, size, array), (0, 1, 0, size, one), (0, 3, 0, size, three), (0, 2, 0, half_own, low), (0, 2, half_own, size, high)]
    turn = first + half_rest
    out += [(1, 0, first, size, far), (1, 1, first, size, f_one), (1, 3, first, size, f_three)]
    out += [(1, 2, first, turn, f_low), (1, 2, turn, size, f_high)]
    for dx, block in ((0, array), (1, one), (3, three), (2, low)):
        out.append((1, dx, 0, first, swap(cut(block, dim, 0, first), "yh")))
    return out


def permute_kernel(parts, want_ref, *refs):
    ids, data = refs[:parts], refs[parts : 2 * parts]
    q_ref, kv_ref = refs[2 * parts :]
    rows = 512

    def step(i, carry):
        start = pl.multiple_of(i * rows, rows)
        want = want_ref[pl.ds(start, rows), :]
        picked = None
        for id_ref, data_ref in zip(ids, data):
            hot = jnp.where(want == id_ref[...], 1.0, 0.0).astype(BF)
            part = jnp.dot(hot, data_ref[...], preferred_element_type=F32)
            picked = part if picked is None else picked + part
        picked = picked.astype(BF)
        q_ref[pl.ds(start, rows), :] = picked[:, :TILE]
        kv_ref[pl.ds(start, rows), :] = picked[:, TILE:]
        return carry

    lax.fori_loop(0, q_ref.shape[0] // rows, step, 0)


def permute(want, ids, data):
    n, width = want.shape[0], data[0].shape[1]
    return pl.pallas_call(
        functools.partial(permute_kernel, len(ids)),
        out_shape=(jax.ShapeDtypeStruct((n, TILE), BF), jax.ShapeDtypeStruct((n, width - TILE), BF)),
        in_specs=[WHOLE_VM] * (1 + 2 * len(ids)),
        out_specs=(WHOLE_VM,) * 2,
        compiler_params=pltpu.CompilerParams(vmem_limit_bytes=40 << 20),
        cost_estimate=pl.CostEstimate(flops=2 * n * n * width, bytes_accessed=4 << 20, transcendentals=0),
    )(want, *ids, *data)


def attend_kernel(slots, together, index_ref, count_ref, q_ref, *refs):
    frames = refs[:-4]
    out_ref, win_ref, score_ref, sems = refs[-4:]
    copies = []
    start = 0
    for i, frame in enumerate(frames):
        n = frame.shape[0]
        copies.append(pltpu.make_async_copy(frame, win_ref.at[pl.ds(start, n)], sems.at[i]))
        start += n
    for copy in copies:
        copy.start()
    for copy in copies:
        copy.wait()
    scale = LOG2E / math.sqrt(TILE)

    def tile(t, u):
        base = pl.multiple_of(t * TILE, TILE)
        q = q_ref[pl.ds(base, TILE), :]
        count = count_ref[t]
        top = None
        offs = [pl.multiple_of(index_ref[t, j] * TILE, TILE) for j in range(slots)]
        for j in range(0, slots, 2):
            k = jnp.concatenate([win_ref[pl.ds(offs[j], TILE), :TILE], win_ref[pl.ds(offs[j + 1], TILE), :TILE]], axis=0)
            s = lax.dot_general(q, k, (((1,), (1,)), ((), ())), preferred_element_type=F32)
            for h in range(2):
                part = jnp.where(j + h < count, s[:, h * TILE : (h + 1) * TILE], -1e30)
                score_ref[u, j + h] = part
                top = part if top is None else jnp.maximum(top, part)
        row_max = jnp.max(top, axis=1, keepdims=True) * scale
        total = jnp.zeros((TILE, TILE), F32)
        acc = jnp.zeros((TILE, TILE), F32)
        for j in range(0, slots, 2):
            weights = []
            for h in range(2):
                e = jnp.exp2(score_ref[u, j + h] * scale - row_max)
                total = total + e
                weights.append(e.astype(BF))
            v = jnp.concatenate([win_ref[pl.ds(offs[j], TILE), TILE:], win_ref[pl.ds(offs[j + 1], TILE), TILE:]], axis=0)
            acc = acc + jnp.dot(jnp.concatenate(weights, axis=1), v, preferred_element_type=F32)
        out_ref[pl.ds(base, TILE), :] = (acc / jnp.sum(total, axis=1, keepdims=True)).astype(BF)

    def step(i, carry):
        for u in range(together):
            tile(i * together + u, u)
        return carry

    lax.fori_loop(0, q_ref.shape[0] // TILE // together, step, 0)


def attend(index, count, q, frames):
    n, slots, together = q.shape[0], index.shape[1], 2
    rows = sum(f.shape[0] for f in frames)
    return pl.pallas_call(
        functools.partial(attend_kernel, slots, together),
        out_shape=jax.ShapeDtypeStruct((n, TILE), BF),
        in_specs=[WHOLE_SM] * 2 + [WHOLE_VM] + [WHOLE_ANY] * len(frames),
        out_specs=WHOLE_VM,
        scratch_shapes=[
            VM((rows, 2 * TILE), BF),
            VM((together, slots, TILE, TILE), F32),
            pltpu.SemaphoreType.DMA((len(frames),)),
        ],
        compiler_params=pltpu.CompilerParams(vmem_limit_bytes=40 << 20),
        cost_estimate=pl.CostEstimate(
            flops=4 * n * slots * TILE * TILE, bytes_accessed=6 << 20, transcendentals=n * slots * TILE
        ),
    )(index, count, q, *frames)


def project_kernel(layout, order_ref, att_ref, *refs):
    pieces = refs[: sum(len(p) for p in layout)]
    mine_ref, other_ref = refs[-2:]
    own = pl.multiple_of(order_ref[len(layout)] * TILE, TILE)
    away = pl.multiple_of(TILE - own, TILE)
    mine = jnp.concatenate([att_ref[order_ref[b], pl.ds(own, TILE), :] for b in range(len(layout))], axis=1)
    other = jnp.concatenate([att_ref[order_ref[b], pl.ds(away, TILE), :] for b in range(len(layout))], axis=1)
    left = jnp.concatenate([mine, other], axis=0)
    step = 256
    for column in range(0, mine_ref.shape[1], step):
        blocks, k = [], 0
        for spans in layout:
            for start, stop in spans:
                if start <= column and column + step <= stop:
                    blocks.append(pieces[k][:, column - start : column - start + step])
                k += 1
        assert len(blocks) == len(layout)
        done = jnp.dot(left, jnp.concatenate(blocks, axis=0), preferred_element_type=F32)
        mine_ref[:, column : column + step] = done[:TILE]
        other_ref[:, column : column + step] = done[TILE:].astype(BF)


def project(order, attended, layout, pieces):
    width = max(stop for spans in layout for _, stop in spans)
    return pl.pallas_call(
        functools.partial(project_kernel, layout),
        out_shape=(jax.ShapeDtypeStruct((TILE, width), F32), jax.ShapeDtypeStruct((TILE, width), BF)),
        in_specs=[WHOLE_SM] + [WHOLE_VM] * (1 + len(pieces)),
        out_specs=(WHOLE_VM,) * 2,
        compiler_params=pltpu.CompilerParams(vmem_limit_bytes=40 << 20),
        cost_estimate=pl.CostEstimate(flops=4 * TILE * 8 * TILE * width, bytes_accessed=10 << 20, transcendentals=0),
    )(order, attended, *pieces)


def body(tokens, w_qkv, w_out, source_row, key_tiles, key_count):
    rows = tokens.shape[0]
    z, yl = lax.axis_index("z"), lax.axis_index("yl")
    yh, x, core = lax.axis_index("yh"), lax.axis_index("x"), lax.axis_index("core")

    gathered = gather_chips(tokens, 0, 48, 64, 32)
    near, far = gathered[:5], gathered[5:]

    def ids(part, of_core):
        spans = []
        for dy, dx, start, stop, _ in part:
            chip = ((yh + dy) % 2) * 4 + (x + 4 - dx) % 4
            spans.append((chip * 2 + of_core) * rows + jnp.arange(start, stop, dtype=jnp.int32))
        return jnp.concatenate(spans)[None, :]

    w_both = jnp.concatenate([w_qkv, swap(w_qkv, "core")], axis=1)
    width = w_qkv.shape[1]
    all_ids, all_data = [], []
    for part in (near, far):
        block = jnp.concatenate([p[4] for p in part], axis=0)
        made = jnp.dot(block, w_both, preferred_element_type=F32).astype(BF)
        all_ids += [ids(part, core), ids(part, 1 - core)]
        all_data += [made[:, :width], swap(made[:, width:], "core")]
    want = source_row[0][:, None]
    q, kv = permute(want, all_ids, all_data)

    w_late, kv = lax.optimization_barrier((w_out, kv))
    w_blocks = gather_chips(w_late, 1, 1280, 1536, 768)

    group = kv.shape[0]
    half = group // 2
    behind = lax.ppermute(kv, "z", [(i, (i + 1) % 8) for i in range(8)])
    ahead = lax.ppermute(kv, "z", [(i, (i + 7) % 8) for i in range(8)])
    beside = swap(kv, "yl")
    cross_low = swap(jnp.where(yl == 0, ahead, behind)[:half], "yl")
    onward = [(2 * i, 2 * ((i + 1) % 8)) for i in range(8)] + [(2 * i + 1, 2 * ((i + 7) % 8) + 1) for i in range(8)]
    cross_high = lax.ppermute(beside[half:], CTX, onward)
    frames = [behind, beside, kv, ahead, cross_low, cross_high]

    tiles = key_tiles.shape[0]
    relative = key_tiles - ((z * 2 + yl) - 2) * tiles
    frame, inside = relative // tiles, relative % tiles
    place = jnp.where(frame == 0, 0, jnp.where(frame == 2, 2, jnp.where(frame == 4, 3, jnp.where((frame == 1) == (yl == 0), 4, 1))))
    attended = attend(place * tiles + inside, key_count, q, frames)

    pieces = lax.all_to_all(attended.reshape(8, 2 * TILE, TILE), CHIPS, split_axis=0, concat_axis=0, tiled=True)
    blocks = sorted({(dy, dx) for dy, dx, *_ in w_blocks})
    layout = tuple(tuple((s, e) for dy, dx, s, e, _ in w_blocks if (dy, dx) == b) for b in blocks)
    flat = [p for b in blocks for dy, dx, _, _, p in w_blocks if (dy, dx) == b]
    order = jnp.stack([((yh + dy) % 2) * 4 + (x + 4 - dx) % 4 for dy, dx in blocks] + [core]).astype(jnp.int32)
    mine, other = project(order, pieces, layout, flat)
    return (mine + swap(other, "core").astype(F32)).astype(BF)


def solution(mesh):
    fine = Mesh(mesh.devices.reshape(8, 2, 2, 4, 2), ALL)
    in_specs = (
        P(ALL, None),
        P(None, ("yh", "x", "core")),
        P(("yh", "x", "core"), None),
        P(CTX, None),
        P(CTX, None),
        P(CTX),
    )
    return jax.shard_map(body, mesh=fine, in_specs=in_specs, out_specs=P(ALL, None), check_vma=False)
```

time: 402 us -> 211 us (0.52)
  waiting for transfers between devices: 271 us -> 81.5 us
  starting transfers between devices: 9.95 us -> 61.2 us
  matrix products: 41.4 us -> 5.21 us
  Pallas kernels: 0 us -> 28.6 us
  local copies, waits for them, and re-layouts: 56.4 us -> 29.6 us
  between operations: 13.5 us -> 0.54 us
  other arithmetic: 8.73 us -> 3.48 us
    reduce_scatter x1 -> x0, waiting for transfers between devices: 128 us -> none  [body(): lax.psum_scatter(jnp.dot(attended, w_out, preferred_element_type=jnp.floa...]
    all_gather x1 -> x0, waiting for transfers between devices: 102 us -> none  [body(): lax.all_gather(tokens, 'grp', axis=0, tiled=True)]
    ppermute x4 -> x35, starting transfers between devices: 9.9 us -> 56.2 us  [the longest x16 34.1 us: swap(): return lax.ppermute(array, axis, [(0, 1), (1, 0)])]
    gather x5 -> x0, local copies, waits for them, and re-layouts: 46 us -> none  [the longest x4 35.5 us: attend(): window_tiles[index_group]]
    ppermute x4 -> x35, waiting for transfers between devices: 40.6 us -> 81.5 us  [the longest x16 32.5 us: swap(): return lax.ppermute(array, axis, [(0, 1), (1, 0)])]
    dot_general x10 -> x2, matrix products: 41.4 us -> 5.21 us  [body(): made = jnp.dot(block, w_both, preferred_element_type=F32).astype(BF)]
    pallas_call x0 -> x3, Pallas kernels: none -> 28.6 us  [the longest x1 19 us: attend(): pl.pallas_call(functools.partial(attend_kernel, slots, together), out_sha...]
    slice x3 -> x21, local copies, waits for them, and re-layouts: 2.33 us -> 14.3 us  [the longest x18 10.7 us: cut(): return lax.slice_in_dim(array, start, stop, axis=dim)]
  transfers between devices with their start and end apart: 6 -> 36, of which waited for: 5 -> 14; matrix products, arithmetic and copies ran while one was open for 1% -> 12% of each run, Pallas kernels for 0% -> 9%
where the time goes in v1:
time: 211 us; the launch traced here: 210 us
  waiting for transfers between devices  81.5 us (39%)
  starting transfers between devices  61.2 us (29%)
  local copies, waits for them, and re-layouts  29.6 us (14%)
  Pallas kernels  28.6 us (14%)
  matrix products  5.21 us (2%)
  other arithmetic  3.48 us (2%)
    ppermute x16, starting transfers between devices, swap(): return lax.ppermute(array, axis, [(0, 1), (1, 0)])  34.1 us
    ppermute x16, waiting for transfers between devices, swap(): return lax.ppermute(array, axis, [(0, 1), (1, 0)])  32.5 us
    ppermute x16, waiting for transfers between devices, round_x(): return lax.ppermute(array, 'x', [(i, (i + by) % 4) for i in range(4)])  27.2 us
    ppermute x1, waiting for transfers between devices, body(): behind = lax.ppermute(kv, 'z', [(i, (i + 1) % 8) for i in range(8)])  21.8 us
    pallas_call x1, Pallas kernels, attend(): pl.pallas_call(functools.partial(attend_kernel, slots, together), out_sha...  19 us
    ppermute x16, starting transfers between devices, round_x(): return lax.ppermute(array, 'x', [(i, (i + by) % 4) for i in range(4)])  17.2 us
    unnamed x45, local copies, waits for them, and re-layouts  12.4 us
    slice x18, local copies, waits for them, and re-layouts, cut(): return lax.slice_in_dim(array, start, stop, axis=dim)  10.7 us
  transfers between devices with their start and end apart: 36, of which 14 were waited for; matrix products, arithmetic and copies ran while one was open for 12% of the time, Pallas kernels for 9%

profile of v1, /device:TPU:1, one launch (start us, length us, event | category | flops | bytes accessed | tf_op | source)
XLA Modules:
  0.0 210.1 jit_solution(6676913064594980371)
XLA Ops:
  5.3 3.0 %collective-permute-start.6 = (bf16[80,3072]{1,0:T(8,128)(2,1)}, bf16[80,3072]{1,0:T(8,128)(2,1)}, u32[]{:S(2)}, u32[]{:S(2)}) collective-permute-start(bf16[80,3072]{1,0:T(8,128)(2,1)} %slice.76), channel_id=1, source_target_pairs={{0,8},{8,0},{1,9},{9,1},{2,10},{10,2},{3,11},{11,3},{4,12},{12,4},... | collective-permute-start | bytes 1474568 | tf_op jit(solution)/shard_map/ppermute | solution.py:31
  10.0 3.6 %collective-permute-start.4 = (bf16[3072,384]{1,0:T(8,128)(2,1)}, bf16[3072,384]{1,0:T(8,128)(2,1)}, u32[]{:S(2)}, u32[]{:S(2)}) collective-permute-start(bf16[3072,384]{1,0:T(8,128)(2,1)} %param.7), channel_id=1, source_target_pairs={{0,1},{1,0},{2,3},{3,2},{4,5},{5,4},{6,7},{7,6},{8,9},{9,8},{10,11... | collective-permute-start | bytes 7077896 | tf_op jit(solution)/shard_map/ppermute | solution.py:31
  13.7 3.4 %constant_dynamic-update-slice_fusion.6 = bf16[3072,768]{1,0:T(8,128)(2,1)} fusion(bf16[3072,384]{1,0:T(8,128)(2,1)} %param.7), kind=kLoop, calls=%fused_computation.10 | loop fusion | bytes 4718592
  19.7 2.4 %collective-permute-start.8 = (bf16[80,3072]{1,0:T(8,128)(2,1)}, bf16[80,3072]{1,0:T(8,128)(2,1)S(1)}, u32[]{:S(2)}, u32[]{:S(2)}) collective-permute-start(bf16[80,3072]{1,0:T(8,128)(2,1)} %collective-permute-done.6), channel_id=1, source_target_pairs={{0,6},{2,0},{4,2},{6,4},{1,7},{3,1},{5,3},{7,5},{8,14},{10,8},{12,... | collective-permute-start | bytes 1474568 | tf_op jit(solution)/shard_map/ppermute | solution.py:27
  22.1 3.6 %collective-permute-start.12 = (bf16[48,3072]{1,0:T(8,128)(2,1)S(1)}, bf16[48,3072]{1,0:T(8,128)(2,1)S(1)}, u32[]{:S(2)}, u32[]{:S(2)}) collective-permute-start(bf16[48,3072]{1,0:T(8,128)(2,1)S(1)} %slice.102), channel_id=1, source_target_pairs={{0,8},{8,0},{1,9},{9,1},{2,10},{10,2},{3,11},{11,3},{4,12},{12,4},... | collective-permute-start | bytes 884744 | tf_op jit(solution)/shard_map/ppermute | solution.py:31
  28.1 3.0 %collective-permute-start.3 = (bf16[64,3072]{1,0:T(8,128)(2,1)S(1)}, bf16[64,3072]{1,0:T(8,128)(2,1)S(1)}, u32[]{:S(2)}, u32[]{:S(2)}) collective-permute-start(bf16[64,3072]{1,0:T(8,128)(2,1)S(1)} %slice.97), channel_id=1, source_target_pairs={{0,6},{2,0},{4,2},{6,4},{1,7},{3,1},{5,3},{7,5},{8,14},{10,8},{12,... | collective-permute-start | bytes 1179656 | tf_op jit(solution)/shard_map/ppermute | solution.py:27
  31.2 6.5 %collective-permute-done.2 = bf16[64,3072]{1,0:T(8,128)(2,1)S(1)} collective-permute-done((bf16[64,3072]{1,0:T(8,128)(2,1)S(1)}, bf16[64,3072]{1,0:T(8,128)(2,1)S(1)}, u32[]{:S(2)}, u32[]{:S(2)}) %collective-permute-start.2) | collective-permute-done | bytes 393248 | tf_op jit(solution)/shard_map/ppermute | solution.py:27
  37.7 2.5 %collective-permute-start.13 = (bf16[48,3072]{1,0:T(8,128)(2,1)S(1)}, bf16[48,3072]{1,0:T(8,128)(2,1)S(1)}, u32[]{:S(2)}, u32[]{:S(2)}) collective-permute-start(bf16[48,3072]{1,0:T(8,128)(2,1)S(1)} %slice.103), channel_id=1, source_target_pairs={{0,8},{8,0},{1,9},{9,1},{2,10},{10,2},{3,11},{11,3},{4,12},{12,4},... | collective-permute-start | bytes 884744 | tf_op jit(solution)/shard_map/ppermute | solution.py:31
  40.4 6.9 %collective-permute-done.9 = bf16[32,3072]{1,0:T(8,128)(2,1)S(1)} collective-permute-done((bf16[32,3072]{1,0:T(8,128)(2,1)S(1)}, bf16[32,3072]{1,0:T(8,128)(2,1)S(1)}, u32[]{:S(2)}, u32[]{:S(2)}) %collective-permute-start.9) | collective-permute-done | bytes 196640 | tf_op jit(solution)/shard_map/ppermute | solution.py:27
  47.3 5.8 %collective-permute-done.10 = bf16[48,3072]{1,0:T(8,128)(2,1)S(1)} collective-permute-done((bf16[48,3072]{1,0:T(8,128)(2,1)S(1)}, bf16[48,3072]{1,0:T(8,128)(2,1)S(1)}, u32[]{:S(2)}, u32[]{:S(2)}) %collective-permute-start.10) | collective-permute-done | bytes 294944 | tf_op jit(solution)/shard_map/ppermute | solution.py:27
  54.5 5.8 %collective-permute-done.14 = bf16[48,3072]{1,0:T(8,128)(2,1)S(1)} collective-permute-done((bf16[48,3072]{1,0:T(8,128)(2,1)S(1)}, bf16[48,3072]{1,0:T(8,128)(2,1)S(1)}, u32[]{:S(2)}, u32[]{:S(2)}) %collective-permute-start.14) | collective-permute-done | bytes 294944 | tf_op jit(solution)/shard_map/ppermute | solution.py:31
  60.3 2.1 %constant_dynamic-update-slice_fusion.5 = bf16[3072,768]{1,0:T(8,128)(2,1)S(1)} fusion(bf16[3072,768]{1,0:T(8,128)(2,1)S(1)} %bitcast.25, bf16[3072,384]{1,0:T(8,128)(2,1)} %collective-permute-done.4), kind=kLoop, calls=%fused_computation.9 | loop fusion | bytes 4718592 | tf_op jit(solution)/shard_map/concatenate | solution.py:211
  62.5 2.6 %convolution_convert_fusion = bf16[512,768]{1,0:T(8,128)(2,1)S(1)} fusion(bf16[512,3072]{1,0:T(8,128)(2,1)S(1)} %constant_dynamic-update-slice_fusion.7, bf16[3072,768]{1,0:T(8,128)(2,1)S(1)} %constant_dynamic-update-slice_fusion.5), kind=kOutput, calls=%fused_computation.1 | convolution fusion | flops 2416312320 | bytes 8650752 | tf_op jit(solution)/shard_map/dot_general | solution.py:216
  65.9 9.0 %collective-permute-start.15 = (bf16[512,384]{1,0:T(8,128)(2,1)}, bf16[512,384]{1,0:T(8,128)(2,1)S(1)}, u32[]{:S(2)}, u32[]{:S(2)}) collective-permute-start(bf16[512,384]{1,0:T(8,128)(2,1)} %get-tuple-element.17), channel_id=1, source_target_pairs={{0,1},{1,0},{2,3},{3,2},{4,5},{5,4},{6,7},{7,6},{8,9},{9,8},{10,11... | collective-permute-start | bytes 1179656 | tf_op jit(solution)/shard_map/ppermute | solution.py:31
  74.9 2.6 %convolution_convert_fusion.1 = bf16[512,768]{1,0:T(8,128)(2,1)S(1)} fusion(bf16[512,3072]{1,0:T(8,128)(2,1)S(1)} %constant_dynamic-update-slice_fusion, bf16[3072,768]{1,0:T(8,128)(2,1)S(1)} %constant_dynamic-update-slice_fusion.5), kind=kOutput, calls=%fused_computation.2 | convolution fusion | flops 2416312320 | bytes 8650752 | tf_op jit(solution)/shard_map/dot_general | solution.py:216
  80.3 6.2 %shard_map.64 = (bf16[2048,128]{1,0:T(8,128)(2,1)S(1)}, bf16[2048,256]{1,0:T(8,128)(2,1)}) custom-call(s32[2048,1]{1,0:T(8,128)S(1)} %copy.7.want_ref, s32[1,512]{1,0:T(1,128)S(1)} %bitcast.21, s32[1,512]{1,0:T(1,128)S(1)} %bitcast.20, s32[1,512]{1,0:T(1,128)S(1)} %bitcast.23, s32[1,512]{1,0:T(1,128)S(1)} %bitcast.22, ...), custom_call_target="tpu_custom_call" | custom-call | flops 3221225472 | bytes 4194304 | tf_op jit(solution)/shard_map/pallas_call | solution.py:83
  88.3 3.9 %collective-permute-start.18 = (bf16[2048,256]{1,0:T(8,128)(2,1)}, bf16[2048,256]{1,0:T(8,128)(2,1)}, u32[]{:S(2)}, u32[]{:S(2)}) collective-permute-start(bf16[2048,256]{1,0:T(8,128)(2,1)} %get-tuple-element.13.refs_2_), channel_id=1, source_target_pairs={{0,224},{32,0},{64,32},{96,64},{128,96},{160,128},{192,160},{224,1... | collective-permute-start | bytes 3145736 | tf_op jit(solution)/shard_map/ppermute | solution.py:228
  94.1 21.8 %collective-permute-done.16.refs_0_ = bf16[2048,256]{1,0:T(8,128)(2,1)S(1)} collective-permute-done((bf16[2048,256]{1,0:T(8,128)(2,1)}, bf16[2048,256]{1,0:T(8,128)(2,1)S(1)}, u32[]{:S(2)}, u32[]{:S(2)}) %collective-permute-start.16) | collective-permute-done | bytes 1048608 | tf_op jit(solution)/shard_map/ppermute | solution.py:227
  115.8 2.3 %slice_select_fusion = bf16[1024,256]{1,0:T(8,128)(2,1)} fusion(bf16[2048,256]{1,0:T(8,128)(2,1)S(1)} %collective-permute-done.16.refs_0_, bf16[2048,256]{1,0:T(8,128)(2,1)} %collective-permute-done.18.refs_3_, pred[]{:T(512)S(6)} %eq.108), kind=kLoop, calls=%fused_computation.3 | loop fusion | flops 262144 | bytes 1572865 | tf_op jit(solution)/shard_map/jit(_where)/select_n | solution.py:230
  120.4 6.5 %collective-permute-done.25.refs_5_ = bf16[128,1792]{1,0:T(8,128)(2,1)} collective-permute-done((bf16[128,1792]{1,0:T(8,128)(2,1)S(1)}, bf16[128,1792]{1,0:T(8,128)(2,1)}, u32[]{:S(2)}, u32[]{:S(2)}) %collective-permute-start.25) | collective-permute-done | bytes 458784 | tf_op jit(solution)/shard_map/ppermute | solution.py:31
  126.9 2.9 %collective-permute-start.23 = (bf16[128,3072]{1,0:T(8,128)(2,1)S(1)}, bf16[128,3072]{1,0:T(8,128)(2,1)S(1)}, u32[]{:S(2)}, u32[]{:S(2)}) collective-permute-start(bf16[128,3072]{1,0:T(8,128)(2,1)S(1)} %copy-done), channel_id=1, source_target_pairs={{0,6},{2,0},{4,2},{6,4},{1,7},{3,1},{5,3},{7,5},{8,14},{10,8},{12,... | collective-permute-start | bytes 2359304 | tf_op jit(solution)/shard_map/ppermute | solution.py:27
  132.8 5.8 %collective-permute-done.27.refs_7_ = bf16[128,1792]{1,0:T(8,128)(2,1)S(1)} collective-permute-done((bf16[128,1792]{1,0:T(8,128)(2,1)}, bf16[128,1792]{1,0:T(8,128)(2,1)S(1)}, u32[]{:S(2)}, u32[]{:S(2)}) %collective-permute-start.27) | collective-permute-done | bytes 458784 | tf_op jit(solution)/shard_map/ppermute | solution.py:27
  143.1 19.0 %shard_map.65 = bf16[2048,128]{1,0:T(8,128)(2,1)S(1)} custom-call(s32[16,30]{1,0:T(8,128)S(1)} %fusion.index_ref, s32[16]{0:T(128)S(1)} %copy-done.8, bf16[2048,128]{1,0:T(8,128)(2,1)S(1)} %copy-done.10, bf16[2048,256]{1,0:T(8,128)(2,1)S(1)} %copy-done.5, bf16[2048,256]{1,0:T(8,128)(2,1)} %collective-permute-done.17.refs_1_, ...), custom_call_target="tpu_custom_call" | custom-call | flops 4026531840 | bytes 6291456 | tf_op jit(solution)/shard_map/pallas_call | solution.py:145
  162.9 5.0 %all-to-all-start = ((bf16[8,256,128]{2,1,0:T(8,128)(2,1)}), bf16[8,256,128]{2,1,0:T(8,128)(2,1)S(1)}, u32[]{:S(2)}, u32[]{:S(2)}) async-start(bf16[8,256,128]{2,1,0:T(8,128)(2,1)} %bitcast.19), calls=%async_computation | async-start | bytes 1048576 | tf_op jit(solution)/shard_map/all_to_all | solution.py:241
  168.7 2.7 %collective-permute-start.24 = (bf16[128,1536]{1,0:T(8,128)(2,1)}, bf16[128,1536]{1,0:T(8,128)(2,1)}, u32[]{:S(2)}, u32[]{:S(2)}) collective-permute-start(bf16[128,1536]{1,0:T(8,128)(2,1)} %slice.111), channel_id=1, source_target_pairs={{0,6},{2,0},{4,2},{6,4},{1,7},{3,1},{5,3},{7,5},{8,14},{10,8},{12,... | collective-permute-start | bytes 1179656 | tf_op jit(solution)/shard_map/ppermute | solution.py:27
  172.9 2.7 %collective-permute-start.28 = (bf16[128,1280]{1,0:T(8,128)(2,1)}, bf16[128,1280]{1,0:T(8,128)(2,1)}, u32[]{:S(2)}, u32[]{:S(2)}) collective-permute-start(bf16[128,1280]{1,0:T(8,128)(2,1)} %slice.112), channel_id=1, source_target_pairs={{0,8},{8,0},{1,9},{9,1},{2,10},{10,2},{3,11},{11,3},{4,12},{12,4},... | collective-permute-start | bytes 983048 | tf_op jit(solution)/shard_map/ppermute | solution.py:31
  176.6 2.7 %collective-permute-start.32 = (bf16[128,1280]{1,0:T(8,128)(2,1)}, bf16[128,1280]{1,0:T(8,128)(2,1)}, u32[]{:S(2)}, u32[]{:S(2)}) collective-permute-start(bf16[128,1280]{1,0:T(8,128)(2,1)} %slice.115), channel_id=1, source_target_pairs={{0,8},{8,0},{1,9},{9,1},{2,10},{10,2},{3,11},{11,3},{4,12},{12,4},... | collective-permute-start | bytes 983048 | tf_op jit(solution)/shard_map/ppermute | solution.py:31
  182.3 2.4 %collective-permute-done.28.refs_8_ = bf16[128,1280]{1,0:T(8,128)(2,1)} collective-permute-done((bf16[128,1280]{1,0:T(8,128)(2,1)}, bf16[128,1280]{1,0:T(8,128)(2,1)}, u32[]{:S(2)}, u32[]{:S(2)}) %collective-permute-start.28) | collective-permute-done | bytes 327712 | tf_op jit(solution)/shard_map/ppermute | solution.py:31
  184.8 7.0 %collective-permute-done.33.refs_13_ = bf16[128,1280]{1,0:T(8,128)(2,1)} collective-permute-done((bf16[128,1280]{1,0:T(8,128)(2,1)}, bf16[128,1280]{1,0:T(8,128)(2,1)}, u32[]{:S(2)}, u32[]{:S(2)}) %collective-permute-start.33) | collective-permute-done | bytes 327712 | tf_op jit(solution)/shard_map/ppermute | solution.py:31
  191.8 7.0 %collective-permute-done.32.refs_11_ = bf16[128,1280]{1,0:T(8,128)(2,1)} collective-permute-done((bf16[128,1280]{1,0:T(8,128)(2,1)}, bf16[128,1280]{1,0:T(8,128)(2,1)}, u32[]{:S(2)}, u32[]{:S(2)}) %collective-permute-start.32) | collective-permute-done | bytes 327712 | tf_op jit(solution)/shard_map/ppermute | solution.py:31
  200.8 3.5 %shard_map.66 = (f32[128,3072]{1,0:T(8,128)S(1)}, bf16[128,3072]{1,0:T(8,128)(2,1)S(1)}) custom-call(s32[9]{0:T(128)S(1)} %stack.39.order_ref, bf16[8,256,128]{2,1,0:T(8,128)(2,1)S(1)} %all-to-all-done.att_ref, bf16[128,3072]{1,0:T(8,128)(2,1)S(1)} %copy-done, bf16[128,3072]{1,0:T(8,128)(2,1)S(1)} %collective-permute-done.21.refs_1_, ...), custom_call_target="tpu_custom_call" | custom-call | flops 1610612736 | bytes 10485760 | tf_op jit(solution)/shard_map/pallas_call | solution.py:186
  204.2 2.9 %collective-permute-start.34 = (bf16[128,3072]{1,0:T(8,128)(2,1)S(1)}, bf16[128,3072]{1,0:T(8,128)(2,1)S(1)}, u32[]{:S(2)}, u32[]{:S(2)}) collective-permute-start(bf16[128,3072]{1,0:T(8,128)(2,1)S(1)} %get-tuple-element.16), channel_id=1, source_target_pairs={{0,1},{1,0},{2,3},{3,2},{4,5},{5,4},{6,7},{7,6},{8,9},{9,8},{10,11... | collective-permute-start | bytes 2359304 | tf_op jit(solution)/shard_map/ppermute | solution.py:31
  (142 shorter events, 42.4 us)
Async XLA Ops:
  0.0 19.6 %collective-permute-start = (bf16[128,3072]{1,0:T(8,128)(2,1)}, bf16[128,3072]{1,0:T(8,128)(2,1)S(1)}, u32[]{:S(2)}, u32[]{:S(2)}) collective-permute-start(bf16[128,3072]{1,0:T(8,128)(2,1)} %param.6), channel_id=1, source_target_pairs={{0,2},{2,4},{4,6},{6,0},{1,3},{3,5},{5,7},{7,1},{8,10},{10,12},{12... | collective-permute-start | bytes 2359304 | tf_op jit(solution)/shard_map/ppermute | solution.py:27
  2.0 20.1 %collective-permute-start.1 = (bf16[128,3072]{1,0:T(8,128)(2,1)}, bf16[128,3072]{1,0:T(8,128)(2,1)S(1)}, u32[]{:S(2)}, u32[]{:S(2)}) collective-permute-start(bf16[128,3072]{1,0:T(8,128)(2,1)} %param.6), channel_id=1, source_target_pairs={{0,6},{2,0},{4,2},{6,4},{1,7},{3,1},{5,3},{7,5},{8,14},{10,8},{12,... | collective-permute-start | bytes 2359304 | tf_op jit(solution)/shard_map/ppermute | solution.py:27
  5.3 12.6 %collective-permute-start.6 = (bf16[80,3072]{1,0:T(8,128)(2,1)}, bf16[80,3072]{1,0:T(8,128)(2,1)}, u32[]{:S(2)}, u32[]{:S(2)}) collective-permute-start(bf16[80,3072]{1,0:T(8,128)(2,1)} %slice.76), channel_id=1, source_target_pairs={{0,8},{8,0},{1,9},{9,1},{2,10},{10,2},{3,11},{11,3},{4,12},{12,4},... | collective-permute-start | bytes 1474568 | tf_op jit(solution)/shard_map/ppermute | solution.py:31
  10.0 43.4 %collective-permute-start.11 = (bf16[48,3072]{1,0:T(8,128)(2,1)}, bf16[48,3072]{1,0:T(8,128)(2,1)}, u32[]{:S(2)}, u32[]{:S(2)}) collective-permute-start(bf16[48,3072]{1,0:T(8,128)(2,1)} %slice.79), channel_id=1, source_target_pairs={{0,8},{8,0},{1,9},{9,1},{2,10},{10,2},{3,11},{11,3},{4,12},{12,4},... | collective-permute-start | bytes 884744 | tf_op jit(solution)/shard_map/ppermute | solution.py:31
  10.0 50.3 %collective-permute-start.4 = (bf16[3072,384]{1,0:T(8,128)(2,1)}, bf16[3072,384]{1,0:T(8,128)(2,1)}, u32[]{:S(2)}, u32[]{:S(2)}) collective-permute-start(bf16[3072,384]{1,0:T(8,128)(2,1)} %param.7), channel_id=1, source_target_pairs={{0,1},{1,0},{2,3},{3,2},{4,5},{5,4},{6,7},{7,6},{8,9},{9,8},{10,11... | collective-permute-start | bytes 7077896 | tf_op jit(solution)/shard_map/ppermute | solution.py:31
  17.9 9.2 %collective-permute-start.7 = (bf16[80,3072]{1,0:T(8,128)(2,1)}, bf16[80,3072]{1,0:T(8,128)(2,1)S(1)}, u32[]{:S(2)}, u32[]{:S(2)}) collective-permute-start(bf16[80,3072]{1,0:T(8,128)(2,1)} %collective-permute-done.6), channel_id=1, source_target_pairs={{0,2},{2,4},{4,6},{6,0},{1,3},{3,5},{5,7},{7,1},{8,10},{10,12},{12... | collective-permute-start | bytes 1474568 | tf_op jit(solution)/shard_map/ppermute | solution.py:27
  19.7 8.5 %collective-permute-start.8 = (bf16[80,3072]{1,0:T(8,128)(2,1)}, bf16[80,3072]{1,0:T(8,128)(2,1)S(1)}, u32[]{:S(2)}, u32[]{:S(2)}) collective-permute-start(bf16[80,3072]{1,0:T(8,128)(2,1)} %collective-permute-done.6), channel_id=1, source_target_pairs={{0,6},{2,0},{4,2},{6,4},{1,7},{3,1},{5,3},{7,5},{8,14},{10,8},{12,... | collective-permute-start | bytes 1474568 | tf_op jit(solution)/shard_map/ppermute | solution.py:27
  22.1 32.3 %collective-permute-start.12 = (bf16[48,3072]{1,0:T(8,128)(2,1)S(1)}, bf16[48,3072]{1,0:T(8,128)(2,1)S(1)}, u32[]{:S(2)}, u32[]{:S(2)}) collective-permute-start(bf16[48,3072]{1,0:T(8,128)(2,1)S(1)} %slice.102), channel_id=1, source_target_pairs={{0,8},{8,0},{1,9},{9,1},{2,10},{10,2},{3,11},{11,3},{4,12},{12,4},... | collective-permute-start | bytes 884744 | tf_op jit(solution)/shard_map/ppermute | solution.py:31
  27.1 10.6 %collective-permute-start.2 = (bf16[64,3072]{1,0:T(8,128)(2,1)S(1)}, bf16[64,3072]{1,0:T(8,128)(2,1)S(1)}, u32[]{:S(2)}, u32[]{:S(2)}) collective-permute-start(bf16[64,3072]{1,0:T(8,128)(2,1)S(1)} %slice.96), channel_id=1, source_target_pairs={{0,2},{2,4},{4,6},{6,0},{1,3},{3,5},{5,7},{7,1},{8,10},{10,12},{12... | collective-permute-start | bytes 1179656 | tf_op jit(solution)/shard_map/ppermute | solution.py:27
  28.1 12.1 %collective-permute-start.3 = (bf16[64,3072]{1,0:T(8,128)(2,1)S(1)}, bf16[64,3072]{1,0:T(8,128)(2,1)S(1)}, u32[]{:S(2)}, u32[]{:S(2)}) collective-permute-start(bf16[64,3072]{1,0:T(8,128)(2,1)S(1)} %slice.97), channel_id=1, source_target_pairs={{0,6},{2,0},{4,2},{6,4},{1,7},{3,1},{5,3},{7,5},{8,14},{10,8},{12,... | collective-permute-start | bytes 1179656 | tf_op jit(solution)/shard_map/ppermute | solution.py:27
  37.7 16.7 %collective-permute-start.13 = (bf16[48,3072]{1,0:T(8,128)(2,1)S(1)}, bf16[48,3072]{1,0:T(8,128)(2,1)S(1)}, u32[]{:S(2)}, u32[]{:S(2)}) collective-permute-start(bf16[48,3072]{1,0:T(8,128)(2,1)S(1)} %slice.103), channel_id=1, source_target_pairs={{0,8},{8,0},{1,9},{9,1},{2,10},{10,2},{3,11},{11,3},{4,12},{12,4},... | collective-permute-start | bytes 884744 | tf_op jit(solution)/shard_map/ppermute | solution.py:31
  53.2 7.1 %collective-permute-start.14 = (bf16[48,3072]{1,0:T(8,128)(2,1)S(1)}, bf16[48,3072]{1,0:T(8,128)(2,1)S(1)}, u32[]{:S(2)}, u32[]{:S(2)}) collective-permute-start(bf16[48,3072]{1,0:T(8,128)(2,1)S(1)} %slice.104), channel_id=1, source_target_pairs={{0,8},{8,0},{1,9},{9,1},{2,10},{10,2},{3,11},{11,3},{4,12},{12,4},... | collective-permute-start | bytes 884744 | tf_op jit(solution)/shard_map/ppermute | solution.py:31
  65.9 12.6 %collective-permute-start.15 = (bf16[512,384]{1,0:T(8,128)(2,1)}, bf16[512,384]{1,0:T(8,128)(2,1)S(1)}, u32[]{:S(2)}, u32[]{:S(2)}) collective-permute-start(bf16[512,384]{1,0:T(8,128)(2,1)} %get-tuple-element.17), channel_id=1, source_target_pairs={{0,1},{1,0},{2,3},{3,2},{4,5},{5,4},{6,7},{7,6},{8,9},{9,8},{10,11... | collective-permute-start | bytes 1179656 | tf_op jit(solution)/shard_map/ppermute | solution.py:31
  87.3 28.5 %collective-permute-start.16 = (bf16[2048,256]{1,0:T(8,128)(2,1)}, bf16[2048,256]{1,0:T(8,128)(2,1)S(1)}, u32[]{:S(2)}, u32[]{:S(2)}) collective-permute-start(bf16[2048,256]{1,0:T(8,128)(2,1)} %get-tuple-element.13.refs_2_), channel_id=1, source_target_pairs={{0,32},{32,64},{64,96},{96,128},{128,160},{160,192},{192,224},{224... | collective-permute-start | bytes 3145736 | tf_op jit(solution)/shard_map/ppermute | solution.py:227
  88.3 27.6 %collective-permute-start.18 = (bf16[2048,256]{1,0:T(8,128)(2,1)}, bf16[2048,256]{1,0:T(8,128)(2,1)}, u32[]{:S(2)}, u32[]{:S(2)}) collective-permute-start(bf16[2048,256]{1,0:T(8,128)(2,1)} %get-tuple-element.13.refs_2_), channel_id=1, source_target_pairs={{0,224},{32,0},{64,32},{96,64},{128,96},{160,128},{192,160},{224,1... | collective-permute-start | bytes 3145736 | tf_op jit(solution)/shard_map/ppermute | solution.py:228
  92.2 26.3 %collective-permute-start.17 = (bf16[2048,256]{1,0:T(8,128)(2,1)}, bf16[2048,256]{1,0:T(8,128)(2,1)}, u32[]{:S(2)}, u32[]{:S(2)}) collective-permute-start(bf16[2048,256]{1,0:T(8,128)(2,1)} %get-tuple-element.13.refs_2_), channel_id=1, source_target_pairs={{0,16},{16,0},{1,17},{17,1},{2,18},{18,2},{3,19},{19,3},{4,20},{20... | collective-permute-start | bytes 3145736 | tf_op jit(solution)/shard_map/ppermute | solution.py:31
  92.6 34.3 %collective-permute-start.25 = (bf16[128,1792]{1,0:T(8,128)(2,1)S(1)}, bf16[128,1792]{1,0:T(8,128)(2,1)}, u32[]{:S(2)}, u32[]{:S(2)}) collective-permute-start(bf16[128,1792]{1,0:T(8,128)(2,1)S(1)} %slice.89), channel_id=1, source_target_pairs={{0,8},{8,0},{1,9},{9,1},{2,10},{10,2},{3,11},{11,3},{4,12},{12,4},... | collective-permute-start | bytes 1376264 | tf_op jit(solution)/shard_map/ppermute | solution.py:31
  94.1 36.5 %collective-permute-start.21 = (bf16[128,3072]{1,0:T(8,128)(2,1)S(1)}, bf16[128,3072]{1,0:T(8,128)(2,1)S(1)}, u32[]{:S(2)}, u32[]{:S(2)}) collective-permute-start(bf16[128,3072]{1,0:T(8,128)(2,1)S(1)} %copy-done), channel_id=1, source_target_pairs={{0,2},{2,4},{4,6},{6,0},{1,3},{3,5},{5,7},{7,1},{8,10},{10,12},{12... | collective-permute-start | bytes 2359304 | tf_op jit(solution)/shard_map/ppermute | solution.py:27
  118.1 22.6 %collective-permute-start.19 = (bf16[1024,256]{1,0:T(8,128)(2,1)}, bf16[1024,256]{1,0:T(8,128)(2,1)}, u32[]{:S(2)}, u32[]{:S(2)}) collective-permute-start(bf16[1024,256]{1,0:T(8,128)(2,1)} %slice_select_fusion), channel_id=1, source_target_pairs={{0,16},{16,0},{1,17},{17,1},{2,18},{18,2},{3,19},{19,3},{4,20},{20... | collective-permute-start | bytes 1572872 | tf_op jit(solution)/shard_map/ppermute | solution.py:31
  120.4 20.4 %collective-permute-start.20 = (bf16[1024,256]{1,0:T(8,128)(2,1)}, bf16[1024,256]{1,0:T(8,128)(2,1)}, u32[]{:S(2)}, u32[]{:S(2)}) collective-permute-start(bf16[1024,256]{1,0:T(8,128)(2,1)} %slice.109), channel_id=1, source_target_pairs={{0,32},{32,64},{64,96},{96,128},{128,160},{160,192},{192,224},{224... | collective-permute-start | bytes 1572872 | tf_op jit(solution)/shard_map/ppermute | solution.py:232
  126.9 11.7 %collective-permute-start.27 = (bf16[128,1792]{1,0:T(8,128)(2,1)}, bf16[128,1792]{1,0:T(8,128)(2,1)S(1)}, u32[]{:S(2)}, u32[]{:S(2)}) collective-permute-start(bf16[128,1792]{1,0:T(8,128)(2,1)} %collective-permute-done.25.refs_5_), channel_id=1, source_target_pairs={{0,2},{2,4},{4,6},{6,0},{1,3},{3,5},{5,7},{7,1},{8,10},{10,12},{12... | collective-permute-start | bytes 1376264 | tf_op jit(solution)/shard_map/ppermute | solution.py:27
  126.9 41.0 %collective-permute-start.23 = (bf16[128,3072]{1,0:T(8,128)(2,1)S(1)}, bf16[128,3072]{1,0:T(8,128)(2,1)S(1)}, u32[]{:S(2)}, u32[]{:S(2)}) collective-permute-start(bf16[128,3072]{1,0:T(8,128)(2,1)S(1)} %copy-done), channel_id=1, source_target_pairs={{0,6},{2,0},{4,2},{6,4},{1,7},{3,1},{5,3},{7,5},{8,14},{10,8},{12,... | collective-permute-start | bytes 2359304 | tf_op jit(solution)/shard_map/ppermute | solution.py:27
  130.6 42.3 %collective-permute-start.26 = (bf16[128,1280]{1,0:T(8,128)(2,1)}, bf16[128,1280]{1,0:T(8,128)(2,1)}, u32[]{:S(2)}, u32[]{:S(2)}) collective-permute-start(bf16[128,1280]{1,0:T(8,128)(2,1)} %slice.90), channel_id=1, source_target_pairs={{0,8},{8,0},{1,9},{9,1},{2,10},{10,2},{3,11},{11,3},{4,12},{12,4},... | collective-permute-start | bytes 983048 | tf_op jit(solution)/shard_map/ppermute | solution.py:31
  138.6 38.0 %collective-permute-start.30 = (bf16[128,1792]{1,0:T(8,128)(2,1)}, bf16[128,1792]{1,0:T(8,128)(2,1)}, u32[]{:S(2)}, u32[]{:S(2)}) collective-permute-start(bf16[128,1792]{1,0:T(8,128)(2,1)} %collective-permute-done.25.refs_5_), channel_id=1, source_target_pairs={{0,6},{2,0},{4,2},{6,4},{1,7},{3,1},{5,3},{7,5},{8,14},{10,8},{12,... | collective-permute-start | bytes 1376264 | tf_op jit(solution)/shard_map/ppermute | solution.py:27
  140.7 34.9 %collective-permute-start.22 = (bf16[128,1536]{1,0:T(8,128)(2,1)}, bf16[128,1536]{1,0:T(8,128)(2,1)S(1)}, u32[]{:S(2)}, u32[]{:S(2)}) collective-permute-start(bf16[128,1536]{1,0:T(8,128)(2,1)} %slice.110), channel_id=1, source_target_pairs={{0,2},{2,4},{4,6},{6,0},{1,3},{3,5},{5,7},{7,1},{8,10},{10,12},{12... | collective-permute-start | bytes 1179656 | tf_op jit(solution)/shard_map/ppermute | solution.py:27
  140.8 40.2 %collective-permute-start.29 = (bf16[128,768]{1,0:T(8,128)(2,1)}, bf16[128,768]{1,0:T(8,128)(2,1)S(1)}, u32[]{:S(2)}, u32[]{:S(2)}) collective-permute-start(bf16[128,768]{1,0:T(8,128)(2,1)} %slice.113), channel_id=1, source_target_pairs={{0,2},{2,4},{4,6},{6,0},{1,3},{3,5},{5,7},{7,1},{8,10},{10,12},{12... | collective-permute-start | bytes 589832 | tf_op jit(solution)/shard_map/ppermute | solution.py:27
  162.9 35.9 %all-to-all-start = ((bf16[8,256,128]{2,1,0:T(8,128)(2,1)}), bf16[8,256,128]{2,1,0:T(8,128)(2,1)S(1)}, u32[]{:S(2)}, u32[]{:S(2)}) async-start(bf16[8,256,128]{2,1,0:T(8,128)(2,1)} %bitcast.19), calls=%async_computation | async-start | bytes 1048576 | tf_op jit(solution)/shard_map/all_to_all | solution.py:241
  168.7 23.1 %collective-permute-start.24 = (bf16[128,1536]{1,0:T(8,128)(2,1)}, bf16[128,1536]{1,0:T(8,128)(2,1)}, u32[]{:S(2)}, u32[]{:S(2)}) collective-permute-start(bf16[128,1536]{1,0:T(8,128)(2,1)} %slice.111), channel_id=1, source_target_pairs={{0,6},{2,0},{4,2},{6,4},{1,7},{3,1},{5,3},{7,5},{8,14},{10,8},{12,... | collective-permute-start | bytes 1179656 | tf_op jit(solution)/shard_map/ppermute | solution.py:27
  172.9 11.9 %collective-permute-start.28 = (bf16[128,1280]{1,0:T(8,128)(2,1)}, bf16[128,1280]{1,0:T(8,128)(2,1)}, u32[]{:S(2)}, u32[]{:S(2)}) collective-permute-start(bf16[128,1280]{1,0:T(8,128)(2,1)} %slice.112), channel_id=1, source_target_pairs={{0,8},{8,0},{1,9},{9,1},{2,10},{10,2},{3,11},{11,3},{4,12},{12,4},... | collective-permute-start | bytes 983048 | tf_op jit(solution)/shard_map/ppermute | solution.py:31
  175.6 16.2 %collective-permute-start.33 = (bf16[128,1280]{1,0:T(8,128)(2,1)}, bf16[128,1280]{1,0:T(8,128)(2,1)}, u32[]{:S(2)}, u32[]{:S(2)}) collective-permute-start(bf16[128,1280]{1,0:T(8,128)(2,1)} %slice.116), channel_id=1, source_target_pairs={{0,8},{8,0},{1,9},{9,1},{2,10},{10,2},{3,11},{11,3},{4,12},{12,4},... | collective-permute-start | bytes 983048 | tf_op jit(solution)/shard_map/ppermute | solution.py:31
  176.6 22.2 %collective-permute-start.32 = (bf16[128,1280]{1,0:T(8,128)(2,1)}, bf16[128,1280]{1,0:T(8,128)(2,1)}, u32[]{:S(2)}, u32[]{:S(2)}) collective-permute-start(bf16[128,1280]{1,0:T(8,128)(2,1)} %slice.115), channel_id=1, source_target_pairs={{0,8},{8,0},{1,9},{9,1},{2,10},{10,2},{3,11},{11,3},{4,12},{12,4},... | collective-permute-start | bytes 983048 | tf_op jit(solution)/shard_map/ppermute | solution.py:31
  181.7 10.1 %collective-permute-start.31 = (bf16[128,1024]{1,0:T(8,128)(2,1)}, bf16[128,1024]{1,0:T(8,128)(2,1)S(1)}, u32[]{:S(2)}, u32[]{:S(2)}) collective-permute-start(bf16[128,1024]{1,0:T(8,128)(2,1)} %slice.114), channel_id=1, source_target_pairs={{0,6},{2,0},{4,2},{6,4},{1,7},{3,1},{5,3},{7,5},{8,14},{10,8},{12,... | collective-permute-start | bytes 786440 | tf_op jit(solution)/shard_map/ppermute | solution.py:27
  (20 other events, 270.5 us)

commit v2 on v1

v2 whole, which is shorter than its diff:
```python
import functools
import math

import jax
import jax.numpy as jnp
from jax import lax
from jax.experimental import pallas as pl
from jax.experimental.pallas import tpu as pltpu
from jax.sharding import Mesh
from jax.sharding import PartitionSpec as P

BF = jnp.bfloat16
F32 = jnp.float32
TILE = 128
LOG2E = 1.4426950408889634
VM = pltpu.VMEM
SM = pltpu.SMEM
CTX = ("z", "yl")
CHIPS = ("yh", "x")
ALL = ("z", "yl", "yh", "x", "core")
TURNS = (0, 1, 3, 2)
WHOLE_VM = pl.BlockSpec(memory_space=VM)
WHOLE_SM = pl.BlockSpec(memory_space=SM)
WHOLE_ANY = pl.BlockSpec(memory_space=pl.ANY)


def round_x(array, by):
    return lax.ppermute(array, "x", [(i, (i + by) % 4) for i in range(4)])


def swap(array, axis):
    return lax.ppermute(array, axis, [(0, 1), (1, 0)])


def gather_small(array):
    pair = jnp.concatenate([array, swap(array, "yh")], axis=0)
    turned = [pair if dx == 0 else lax.ppermute(pair, "x", [(i, (i + dx) % 4) for i in range(4)]) for dx in TURNS]
    n = array.shape[0]
    return jnp.concatenate([p[dy * n : (dy + 1) * n] for dy in range(2) for p in turned], axis=0)


def qkv_kernel(heights, own_ref, other_ref, *refs):
    pieces = refs[: len(heights)]
    mine_ref, theirs_ref, rows_ref, sems = refs[len(heights) :]
    copies, start = [], 0
    for i, height in enumerate(heights):
        copies.append(pltpu.make_async_copy(pieces[i], rows_ref.at[pl.ds(start, height)], sems.at[i]))
        start += height
    for copy in copies:
        copy.start()
    for copy in copies:
        copy.wait()
    theirs_ref[...] = jnp.dot(rows_ref[...], other_ref[...], preferred_element_type=F32).astype(BF)
    mine_ref[...] = jnp.dot(rows_ref[...], own_ref[...], preferred_element_type=F32).astype(BF)


def qkv(own, other, pieces):
    heights = tuple(p.shape[0] for p in pieces)
    n, depth, width = sum(heights), own.shape[0], own.shape[1]
    return pl.pallas_call(
        functools.partial(qkv_kernel, heights),
        out_shape=(jax.ShapeDtypeStruct((n, width), BF),) * 2,
        in_specs=[WHOLE_VM] * 2 + [WHOLE_ANY] * len(pieces),
        out_specs=(WHOLE_VM,) * 2,
        scratch_shapes=[VM((n, depth), BF), pltpu.SemaphoreType.DMA((len(pieces),))],
        compiler_params=pltpu.CompilerParams(vmem_limit_bytes=40 << 20),
        cost_estimate=pl.CostEstimate(flops=4 * n * depth * width, bytes_accessed=8 << 20, transcendentals=0),
    )(own, other, *pieces)


def hot_rows(want, frame, block_ref, blocks):
    n = want.shape[0]
    high = jnp.broadcast_to(want[:, 2 * frame : 2 * frame + 1], (n, TILE)).astype(BF)
    low = jnp.broadcast_to(want[:, 2 * frame + 1 : 2 * frame + 2], (n, TILE))
    lane = lax.broadcasted_iota(jnp.int32, (n, TILE), 1).astype(F32)
    inside = jnp.where(low == lane, 1.0, 0.0).astype(BF)
    zero = jnp.zeros((n, TILE), BF)
    return jnp.concatenate(
        [jnp.where(high == block_ref[b].astype(BF), inside, zero) for b in range(blocks)], axis=1
    )


def place_kernel(frames, block_ref, want_ref, *refs):
    data, outs = refs[: 2 * frames], refs[2 * frames :]
    rows = 512
    half = 512

    def step(i, carry):
        start = pl.multiple_of(i * rows, rows)
        want = want_ref[pl.ds(start, rows), :]
        for f in range(frames):
            hot = hot_rows(want, f, block_ref, 8)
            first, second = data[2 * f], data[2 * f + 1]
            done = jnp.dot(hot[:, :half], first[:half, :], preferred_element_type=F32)
            done = done + jnp.dot(hot[:, half:], second[:half, :], preferred_element_type=F32)
            outs[f][pl.ds(start, rows), :] = done.astype(BF)
        return carry

    lax.fori_loop(0, want_ref.shape[0] // rows, step, 0)


def place(blocks, want, data):
    n, frames = want.shape[0], len(data) // 2
    widths = [d.shape[1] for d in data[::2]]
    return pl.pallas_call(
        functools.partial(place_kernel, frames),
        out_shape=tuple(jax.ShapeDtypeStruct((n, w), BF) for w in widths),
        in_specs=[WHOLE_SM] + [WHOLE_VM] * (1 + len(data)),
        out_specs=(WHOLE_VM,) * frames,
        compiler_params=pltpu.CompilerParams(vmem_limit_bytes=48 << 20),
        cost_estimate=pl.CostEstimate(flops=2 * n * n // 2 * sum(widths), bytes_accessed=8 << 20, transcendentals=0),
    )(blocks, want, *data)


def attend_kernel(slots, together, frames, index_ref, count_ref, block_ref, want_ref, *refs):
    data, before = refs[: 2 * frames], refs[2 * frames : 3 * frames]
    out_ref, q_ref, win_ref, score_ref = refs[3 * frames :]
    n = q_ref.shape[0]
    rows = 512
    half = 512

    def fill(i, carry):
        start = pl.multiple_of(i * rows, rows)
        want = want_ref[pl.ds(start, rows), :]
        for f in range(frames):
            hot = hot_rows(want, f, block_ref, 8)
            first, second = data[2 * f], data[2 * f + 1]
            done = jnp.dot(hot[:, :half], first[:half, :], preferred_element_type=F32)
            done = done + jnp.dot(hot[:, half:], second[:half, :], preferred_element_type=F32)
            done = done.astype(BF) + before[f][pl.ds(start, rows), :]
            if f == 0:
                q_ref[pl.ds(start, rows), :] = done[:, :TILE]
                done = done[:, TILE:]
            win_ref[pl.ds(pl.multiple_of(f * n + start, rows), rows), :] = done
        return carry

    lax.fori_loop(0, n // rows, fill, 0)
    scale = LOG2E / math.sqrt(TILE)

    def tile(t, u):
        base = pl.multiple_of(t * TILE, TILE)
        q = q_ref[pl.ds(base, TILE), :]
        count = count_ref[t]
        top = None
        offs = [pl.multiple_of(index_ref[t, j] * TILE, TILE) for j in range(slots)]
        for j in range(0, slots, 2):
            k = jnp.concatenate([win_ref[pl.ds(offs[j], TILE), :TILE], win_ref[pl.ds(offs[j + 1], TILE), :TILE]], axis=0)
            s = lax.dot_general(q, k, (((1,), (1,)), ((), ())), preferred_element_type=F32)
            for h in range(2):
                part = jnp.where(j + h < count, s[:, h * TILE : (h + 1) * TILE], -1e30)
                score_ref[u, j + h] = part
                top = part if top is None else jnp.maximum(top, part)
        row_max = jnp.max(top, axis=1, keepdims=True) * scale
        total = jnp.zeros((TILE, TILE), F32)
        acc = jnp.zeros((TILE, TILE), F32)
        for j in range(0, slots, 2):
            weights = []
            for h in range(2):
                e = jnp.exp2(score_ref[u, j + h] * scale - row_max)
                total = total + e
                weights.append(e.astype(BF))
            v = jnp.concatenate([win_ref[pl.ds(offs[j], TILE), TILE:], win_ref[pl.ds(offs[j + 1], TILE), TILE:]], axis=0)
            acc = acc + jnp.dot(jnp.concatenate(weights, axis=1), v, preferred_element_type=F32)
        out_ref[pl.ds(base, TILE), :] = (acc / jnp.sum(total, axis=1, keepdims=True)).astype(BF)

    def step(i, carry):
        for u in range(together):
            tile(i * together + u, u)
        return carry

    lax.fori_loop(0, n // TILE // together, step, 0)


def attend(index, count, blocks, want, data, before):
    n, slots, together, frames = want.shape[0], index.shape[1], 2, len(before)
    return pl.pallas_call(
        functools.partial(attend_kernel, slots, together, frames),
        out_shape=jax.ShapeDtypeStruct((n, TILE), BF),
        in_specs=[WHOLE_SM] * 3 + [WHOLE_VM] * (1 + len(data) + frames),
        out_specs=WHOLE_VM,
        scratch_shapes=[
            VM((n, TILE), BF),
            VM((frames * n, 2 * TILE), BF),
            VM((together, slots, TILE, TILE), F32),
        ],
        compiler_params=pltpu.CompilerParams(vmem_limit_bytes=48 << 20),
        cost_estimate=pl.CostEstimate(
            flops=4 * n * slots * TILE * TILE + n * n * 1408, bytes_accessed=9 << 20, transcendentals=n * slots * TILE
        ),
    )(index, count, blocks, want, *data, *before)


def project_kernel(order_ref, att_ref, w_ref, mine_ref, other_ref):
    blocks = w_ref.shape[1]
    own = pl.multiple_of(order_ref[blocks] * TILE, TILE)
    away = pl.multiple_of(TILE - own, TILE)
    mine = jnp.concatenate([att_ref[order_ref[b], pl.ds(own, TILE), :] for b in range(blocks)], axis=1)
    other = jnp.concatenate([att_ref[order_ref[b], pl.ds(away, TILE), :] for b in range(blocks)], axis=1)
    left = jnp.concatenate([mine, other], axis=0)
    step = 256
    for column in range(0, mine_ref.shape[1], step):
        right = jnp.concatenate([w_ref[:, b, :, column : column + step].reshape(TILE, step) for b in range(blocks)], axis=0)
        done = jnp.dot(left, right, preferred_element_type=F32)
        mine_ref[:, column : column + step] = done[:TILE]
        other_ref[:, column : column + step] = done[TILE:].astype(BF)


def project(order, attended, w):
    width = w.shape[-1]
    return pl.pallas_call(
        project_kernel,
        out_shape=(jax.ShapeDtypeStruct((TILE, width), F32), jax.ShapeDtypeStruct((TILE, width), BF)),
        in_specs=[WHOLE_SM] + [WHOLE_VM] * 2,
        out_specs=(WHOLE_VM,) * 2,
        compiler_params=pltpu.CompilerParams(vmem_limit_bytes=40 << 20),
        cost_estimate=pl.CostEstimate(flops=4 * TILE * 8 * TILE * width, bytes_accessed=10 << 20, transcendentals=0),
    )(order, attended, w)


def exchange(payload, yl):
    half = payload.shape[0] // 2 // TILE * TILE
    behind = lax.ppermute(payload, "z", [(i, (i + 1) % 8) for i in range(8)])
    ahead = lax.ppermute(payload, "z", [(i, (i + 7) % 8) for i in range(8)])
    beside = swap(payload, "yl")
    cross_low = swap(jnp.where(yl == 0, ahead[:half], behind[:half]), "yl")
    onward = [(2 * i, 2 * ((i + 1) % 8)) for i in range(8)] + [(2 * i + 1, 2 * ((i + 7) % 8) + 1) for i in range(8)]
    cross_high = lax.ppermute(beside[half:], CTX, onward)
    return behind, beside, ahead, cross_low, cross_high


def body(tokens, w_qkv, w_out, source_row, key_tiles, key_count):
    z, yl = lax.axis_index("z"), lax.axis_index("yl")
    yh, x, core = lax.axis_index("yh"), lax.axis_index("x"), lax.axis_index("core")
    chip_of = [((yh + dy) % 2) * 4 + (x + 4 - dx) % 4 for dy in range(2) for dx in TURNS]

    first, half_rest = 48, 32
    far_own = swap(tokens[first:], "yh")
    one, three = round_x(tokens, 1), round_x(tokens, -1)
    w_other = swap(w_qkv, "core")
    slice_rows = w_out.shape[0] // 8
    w_few = gather_small(lax.dynamic_slice_in_dim(w_out, z * slice_rows, slice_rows, 0))
    w_all = lax.all_gather(w_few, "z", axis=0, tiled=True).reshape(8, 8, slice_rows, w_out.shape[1])

    half = tokens.shape[0] // 2
    low, high = round_x(one[:half], 1), round_x(three[half:], -1)
    f_one, f_three = round_x(far_own, 1), round_x(far_own, -1)
    f_low, f_high = round_x(f_one[:half_rest], 1), round_x(f_three[half_rest:], -1)
    near_mine, near_theirs = qkv(w_qkv, w_other, [tokens, one, three, low, high])
    near_other = swap(near_theirs, "core")
    low_top, _ = lax.optimization_barrier((low[:first], near_theirs))
    tops = [swap(b[:first], "yh") for b in (tokens, one, three)] + [swap(low_top, "yh")]

    source = source_row[0]
    tail = jnp.stack([source // TILE, source % TILE]).astype(BF).reshape(-1, 2 * TILE)
    near_kv = jnp.concatenate([near_mine[:, TILE:], near_other[:, TILE:], tail], axis=0)
    near_in = exchange(near_kv, yl)

    far_pieces = [tops[0], far_own, tops[1], f_one, tops[2], f_three, tops[3], f_low, f_high]
    far_pieces, _ = lax.optimization_barrier((far_pieces, near_in[:3]))
    far_mine, far_theirs = qkv(w_qkv, w_other, far_pieces)
    far_other = swap(far_theirs, "core")
    far_kv = jnp.concatenate([far_mine[:, TILE:], far_other[:, TILE:]], axis=0)
    far_kv, _ = lax.optimization_barrier((far_kv, near_in[3:]))
    far_in = exchange(far_kv, yl)

    n = near_mine.shape[0]
    def halves(got):
        behind, beside, ahead, low_part, high_part = got
        return [behind[:n], behind[n : 2 * n], beside[:n], beside[n : 2 * n], ahead[:n], ahead[n : 2 * n], low_part, high_part[:n]]

    tails = [tail] + [g[-tail.shape[0] :] for g in (near_in[0], near_in[1], near_in[2], near_in[4])]
    want = jnp.concatenate([t.reshape(2, -1) for t in tails], axis=0).astype(F32).T
    near_blocks = jnp.stack([2 * c + side for side in (core, 1 - core) for c in chip_of[:4]]).astype(F32)
    far_blocks = jnp.stack([2 * c + side for side in (core, 1 - core) for c in chip_of[4:]]).astype(F32)
    before = place(near_blocks, want, [near_mine, near_other] + halves(near_in))

    tiles = key_tiles.shape[0]
    relative = key_tiles - ((z * 2 + yl) - 2) * tiles
    frame, inside = relative // tiles, relative % tiles
    slot = jnp.where(frame == 0, 1, jnp.where(frame == 2, 0, jnp.where(frame == 4, 3, jnp.where((frame == 1) == (yl == 0), 4, 2))))
    attended = attend(slot * tiles + inside, key_count, far_blocks, want, [far_mine, far_other] + halves(far_in), before)

    pieces = lax.all_to_all(attended.reshape(8, 2 * TILE, TILE), CHIPS, split_axis=0, concat_axis=0, tiled=True)
    order = jnp.stack(chip_of + [core]).astype(jnp.int32)
    mine, other = project(order, pieces, w_all)
    return (mine + swap(other, "core").astype(F32)).astype(BF)


def solution(mesh):
    fine = Mesh(mesh.devices.reshape(8, 2, 2, 4, 2), ALL)
    in_specs = (
        P(ALL, None),
        P(None, ("yh", "x", "core")),
        P(("yh", "x", "core"), None),
        P(CTX, None),
        P(CTX, None),
        P(CTX),
    )
    return jax.shard_map(body, mesh=fine, in_specs=in_specs, out_specs=P(ALL, None), check_vma=False)
```

time: 211 us -> 223 us (1.057)
  Pallas kernels: 28.6 us -> 47.8 us
  between operations: 0.54 us -> 13.9 us
  local copies, waits for them, and re-layouts: 29.6 us -> 21.3 us
  starting transfers between devices: 61.2 us -> 55.3 us
  matrix products: 5.21 us -> 0 us
  waiting for transfers between devices: 81.5 us -> 79.1 us
    pallas_call x3 -> x5, Pallas kernels: 28.6 us -> 47.8 us  [the longest x1 27 us: attend(): pl.pallas_call(functools.partial(attend_kernel, slots, together, frames),...]
    ppermute x16 -> x14, waiting for transfers between devices: 32.5 us -> 20.1 us  [swap(): return lax.ppermute(array, axis, [(0, 1), (1, 0)])]
    all_to_all x1, waiting for transfers between devices: 0.01 us -> 9.26 us  [body(): lax.all_to_all(attended.reshape(8, 2 * TILE, TILE), CHIPS, split_axis=0,...]
    ppermute x16 -> x14, starting transfers between devices: 34.1 us -> 26.3 us  [swap(): return lax.ppermute(array, axis, [(0, 1), (1, 0)])]
    ppermute x3 -> x9, starting transfers between devices: 4.91 us -> 12.7 us  [the longest x2 5.75 us: exchange(): ahead = lax.ppermute(payload, 'z', [(i, (i + 7) % 8) for i in range(8)])]
    ppermute x16 -> x8, starting transfers between devices: 17.2 us -> 9.65 us  [round_x(): return lax.ppermute(array, 'x', [(i, (i + by) % 4) for i in range(4)])]
    ppermute x16 -> x8, waiting for transfers between devices: 27.2 us -> 34.2 us  [round_x(): return lax.ppermute(array, 'x', [(i, (i + by) % 4) for i in range(4)])]
    ppermute x3 -> x9, waiting for transfers between devices: 21.8 us -> 15.5 us  [the longest x3 6.45 us: gather_small(): lax.ppermute(pair, 'x', [(i, (i + dx) % 4) for i in range(4)])]
  transfers between devices with their start and end apart: 36 -> 33, of which waited for: 14 -> 15; matrix products, arithmetic and copies ran while one was open for 12% -> 7% of each run, Pallas kernels for 9% -> 20%
where the time goes in v2:
time: 223 us
  waiting for transfers between devices  79.1 us (35%)
  starting transfers between devices  55.3 us (25%)
  Pallas kernels  47.8 us (21%)
  local copies, waits for them, and re-layouts  21.3 us (10%)
  between operations  13.9 us (6%)
  other arithmetic  5.42 us (2%)
    ppermute x8, waiting for transfers between devices, round_x(): return lax.ppermute(array, 'x', [(i, (i + by) % 4) for i in range(4)])  34.2 us
    pallas_call x1, Pallas kernels, attend(): pl.pallas_call(functools.partial(attend_kernel, slots, together, frames),...  27 us
    ppermute x14, starting transfers between devices, swap(): return lax.ppermute(array, axis, [(0, 1), (1, 0)])  26.3 us
    ppermute x14, waiting for transfers between devices, swap(): return lax.ppermute(array, axis, [(0, 1), (1, 0)])  20.1 us
    unnamed x37, local copies, waits for them, and re-layouts  10 us
    pallas_call x1, Pallas kernels, place(): pl.pallas_call(functools.partial(place_kernel, frames), out_shape=tuple((...  9.73 us
    ppermute x8, starting transfers between devices, round_x(): return lax.ppermute(array, 'x', [(i, (i + by) % 4) for i in range(4)])  9.65 us
    all_to_all x1, waiting for transfers between devices, body(): lax.all_to_all(attended.reshape(8, 2 * TILE, TILE), CHIPS, split_axis=0,...  9.26 us
  transfers between devices with their start and end apart: 33, of which 15 were waited for; matrix products, arithmetic and copies ran while one was open for 7% of the time, Pallas kernels for 20%

profile of v2, /device:TPU:1, one launch (start us, length us, event | category | flops | bytes accessed | tf_op | source)
XLA Modules:
  0.0 222.8 jit_solution(16525450175641062524)
XLA Ops:
  7.5 3.8 %collective-permute-start.26 = (bf16[16,3072]{1,0:T(8,128)(2,1)S(1)}, bf16[16,3072]{1,0:T(8,128)(2,1)S(1)}, u32[]{:S(2)}, u32[]{:S(2)}) collective-permute-start(bf16[16,3072]{1,0:T(8,128)(2,1)S(1)} %get-tuple-element.50), channel_id=1, source_target_pairs={{0,8},{8,0},{1,9},{9,1},{2,10},{10,2},{3,11},{11,3},{4,12},{12,4},... | collective-permute-start | bytes 294920 | tf_op jit(solution)/shard_map/ppermute | solution.py:32
  11.4 2.0 collective-permute-done.26
  19.2 4.9 %collective-permute-done.29 = bf16[32,3072]{1,0:T(8,128)(2,1)S(1)} collective-permute-done((bf16[32,3072]{1,0:T(8,128)(2,1)S(1)}, bf16[32,3072]{1,0:T(8,128)(2,1)S(1)}, u32[]{:S(2)}, u32[]{:S(2)}) %collective-permute-start.29) | collective-permute-done | bytes 196640 | tf_op jit(solution)/shard_map/ppermute | solution.py:37
  25.2 3.5 %collective-permute-start = (bf16[3072,384]{1,0:T(8,128)(2,1)}, bf16[3072,384]{1,0:T(8,128)(2,1)S(1)}, u32[]{:S(2)}, u32[]{:S(2)}) collective-permute-start(bf16[3072,384]{1,0:T(8,128)(2,1)} %own_ref.3), channel_id=1, source_target_pairs={{0,1},{1,0},{2,3},{3,2},{4,5},{5,4},{6,7},{7,6},{8,9},{9,8},{10,11... | collective-permute-start | bytes 7077896 | tf_op jit(solution)/shard_map/ppermute | solution.py:32
  29.2 2.2 collective-permute-start.2
  32.1 2.6 %collective-permute-start.10 = (bf16[48,3072]{1,0:T(8,128)(2,1)}, bf16[48,3072]{1,0:T(8,128)(2,1)}, u32[]{:S(2)}, u32[]{:S(2)}) collective-permute-start(bf16[48,3072]{1,0:T(8,128)(2,1)} %slice.125), channel_id=1, source_target_pairs={{0,8},{8,0},{1,9},{9,1},{2,10},{10,2},{3,11},{11,3},{4,12},{12,4},... | collective-permute-start | bytes 884744 | tf_op jit(solution)/shard_map/ppermute | solution.py:32
  35.2 13.9 %collective-permute-done.1.refs_1_ = bf16[128,3072]{1,0:T(8,128)(2,1)S(1)} collective-permute-done((bf16[128,3072]{1,0:T(8,128)(2,1)S(1)}, bf16[128,3072]{1,0:T(8,128)(2,1)S(1)}, u32[]{:S(2)}, u32[]{:S(2)}) %collective-permute-start.1) | collective-permute-done | bytes 786464 | tf_op jit(solution)/shard_map/ppermute | solution.py:28
  49.3 2.7 %collective-permute-start.4 = (bf16[64,3072]{1,0:T(8,128)(2,1)S(1)}, bf16[64,3072]{1,0:T(8,128)(2,1)S(1)}, u32[]{:S(2)}, u32[]{:S(2)}) collective-permute-start(bf16[64,3072]{1,0:T(8,128)(2,1)S(1)} %slice.154), channel_id=1, source_target_pairs={{0,6},{2,0},{4,2},{6,4},{1,7},{3,1},{5,3},{7,5},{8,14},{10,8},{12,... | collective-permute-start | bytes 1179656 | tf_op jit(solution)/shard_map/ppermute | solution.py:28
  52.0 8.4 %collective-permute-done.3.refs_3_ = bf16[64,3072]{1,0:T(8,128)(2,1)S(1)} collective-permute-done((bf16[64,3072]{1,0:T(8,128)(2,1)S(1)}, bf16[64,3072]{1,0:T(8,128)(2,1)S(1)}, u32[]{:S(2)}, u32[]{:S(2)}) %collective-permute-start.3) | collective-permute-done | bytes 393248 | tf_op jit(solution)/shard_map/ppermute | solution.py:28
  60.4 4.0 %shard_map.64 = (bf16[512,384]{1,0:T(8,128)(2,1)S(1)}, bf16[512,384]{1,0:T(8,128)(2,1)}) custom-call(bf16[3072,384]{1,0:T(8,128)(2,1)S(1)} %copy-done.3, bf16[3072,384]{1,0:T(8,128)(2,1)S(1)} %collective-permute-done.other_ref, bf16[128,3072]{1,0:T(8,128)(2,1)S(1)} %copy-done.2, bf16[128,3072]{1,0:T(8,128)(2,1)S(1)} %collective-permute-done.1.refs_1_, ...), custom_call_target="tpu_custom_call" | custom-call | flops 2415919104 | bytes 8388608 | tf_op jit(solution)/shard_map/pallas_call | solution.py:60
  66.2 2.9 %collective-permute-start.15 = (bf16[80,3072]{1,0:T(8,128)(2,1)}, bf16[80,3072]{1,0:T(8,128)(2,1)S(1)}, u32[]{:S(2)}, u32[]{:S(2)}) collective-permute-start(bf16[80,3072]{1,0:T(8,128)(2,1)} %collective-permute-done.11.refs_1_), channel_id=1, source_target_pairs={{0,6},{2,0},{4,2},{6,4},{1,7},{3,1},{5,3},{7,5},{8,14},{10,8},{12,... | collective-permute-start | bytes 1474568 | tf_op jit(solution)/shard_map/ppermute | solution.py:28
  71.0 2.7 %collective-permute-start.12 = (bf16[48,3072]{1,0:T(8,128)(2,1)S(1)}, bf16[48,3072]{1,0:T(8,128)(2,1)S(1)}, u32[]{:S(2)}, u32[]{:S(2)}) collective-permute-start(bf16[48,3072]{1,0:T(8,128)(2,1)S(1)} %slice.161), channel_id=1, source_target_pairs={{0,8},{8,0},{1,9},{9,1},{2,10},{10,2},{3,11},{11,3},{4,12},{12,4},... | collective-permute-start | bytes 884744 | tf_op jit(solution)/shard_map/ppermute | solution.py:32
  74.2 6.6 %collective-permute-done.13.refs_3_ = bf16[80,3072]{1,0:T(8,128)(2,1)} collective-permute-done((bf16[80,3072]{1,0:T(8,128)(2,1)}, bf16[80,3072]{1,0:T(8,128)(2,1)}, u32[]{:S(2)}, u32[]{:S(2)}) %collective-permute-start.13) | collective-permute-done | bytes 491552 | tf_op jit(solution)/shard_map/ppermute | solution.py:28
  82.1 3.9 %collective-permute-start.8 = (bf16[1040,256]{1,0:T(8,128)(2,1)}, bf16[1040,256]{1,0:T(8,128)(2,1)}, u32[]{:S(2)}, u32[]{:S(2)}) collective-permute-start(bf16[1040,256]{1,0:T(8,128)(2,1)} %pad_maximum_fusion), channel_id=1, source_target_pairs={{0,224},{32,0},{64,32},{96,64},{128,96},{160,128},{192,160},{224,1... | collective-permute-start | bytes 1597448 | tf_op jit(solution)/shard_map/ppermute | solution.py:223
  86.8 5.2 %collective-permute-done.12.refs_2_ = bf16[48,3072]{1,0:T(8,128)(2,1)S(1)} collective-permute-done((bf16[48,3072]{1,0:T(8,128)(2,1)S(1)}, bf16[48,3072]{1,0:T(8,128)(2,1)S(1)}, u32[]{:S(2)}, u32[]{:S(2)}) %collective-permute-start.12) | collective-permute-done | bytes 294944 | tf_op jit(solution)/shard_map/ppermute | solution.py:32
  93.1 5.2 %collective-permute-done.14.refs_4_ = bf16[48,3072]{1,0:T(8,128)(2,1)S(1)} collective-permute-done((bf16[48,3072]{1,0:T(8,128)(2,1)S(1)}, bf16[48,3072]{1,0:T(8,128)(2,1)S(1)}, u32[]{:S(2)}, u32[]{:S(2)}) %collective-permute-start.14) | collective-permute-done | bytes 294944 | tf_op jit(solution)/shard_map/ppermute | solution.py:32
  100.8 5.3 %collective-permute-done.17.refs_7_ = bf16[32,3072]{1,0:T(8,128)(2,1)S(1)} collective-permute-done((bf16[32,3072]{1,0:T(8,128)(2,1)S(1)}, bf16[32,3072]{1,0:T(8,128)(2,1)S(1)}, u32[]{:S(2)}, u32[]{:S(2)}) %collective-permute-start.17) | collective-permute-done | bytes 196640 | tf_op jit(solution)/shard_map/ppermute | solution.py:28
  107.3 2.7 %collective-permute-done.6 = bf16[1040,256]{1,0:T(8,128)(2,1)} collective-permute-done((bf16[1040,256]{1,0:T(8,128)(2,1)}, bf16[1040,256]{1,0:T(8,128)(2,1)}, u32[]{:S(2)}, u32[]{:S(2)}) %collective-permute-start.6) | collective-permute-done | bytes 532512 | tf_op jit(solution)/shard_map/ppermute | solution.py:222
  113.4 4.8 %shard_map.65 = (bf16[512,384]{1,0:T(8,128)(2,1)S(1)}, bf16[512,384]{1,0:T(8,128)(2,1)S(1)}) custom-call(bf16[3072,384]{1,0:T(8,128)(2,1)S(1)} %copy-done.4, bf16[3072,384]{1,0:T(8,128)(2,1)S(1)} %copy-done.6, bf16[48,3072]{1,0:T(8,128)(2,1)} %collective-permute-done.10.refs_0_, bf16[80,3072]{1,0:T(8,128)(2,1)} %collective-permute-done.11.refs_1_, ...), custom_call_target="tpu_custom_call" | custom-call | flops 2415919104 | bytes 8388608 | tf_op jit(solution)/shard_map/pallas_call | solution.py:60
  120.8 3.0 %collective-permute-start.20 = (bf16[512,256]{1,0:T(8,128)(2,1)S(1)}, bf16[512,256]{1,0:T(8,128)(2,1)S(1)}, u32[]{:S(2)}, u32[]{:S(2)}) collective-permute-start(bf16[512,256]{1,0:T(8,128)(2,1)S(1)} %get-tuple-element.54), channel_id=1, source_target_pairs={{0,16},{16,0},{1,17},{17,1},{2,18},{18,2},{3,19},{19,3},{4,20},{20... | collective-permute-start | bytes 786440 | tf_op jit(solution)/shard_map/ppermute | solution.py:32
  124.7 5.8 %collective-permute-done.20.refs_8_ = bf16[512,256]{1,0:T(8,128)(2,1)S(1)} collective-permute-done((bf16[512,256]{1,0:T(8,128)(2,1)S(1)}, bf16[512,256]{1,0:T(8,128)(2,1)S(1)}, u32[]{:S(2)}, u32[]{:S(2)}) %collective-permute-start.20) | collective-permute-done | bytes 262176 | tf_op jit(solution)/shard_map/ppermute | solution.py:32
  130.5 1.8 collective-permute-start.23
  139.8 3.9 %collective-permute-done.23 = bf16[1024,256]{1,0:T(8,128)(2,1)} collective-permute-done((bf16[1024,256]{1,0:T(8,128)(2,1)}, bf16[1024,256]{1,0:T(8,128)(2,1)}, u32[]{:S(2)}, u32[]{:S(2)}) %collective-permute-start.23) | collective-permute-done | bytes 524320 | tf_op jit(solution)/shard_map/ppermute | solution.py:223
  143.7 2.5 %collective-permute-done.21 = bf16[1024,256]{1,0:T(8,128)(2,1)} collective-permute-done((bf16[1024,256]{1,0:T(8,128)(2,1)}, bf16[1024,256]{1,0:T(8,128)(2,1)}, u32[]{:S(2)}, u32[]{:S(2)}) %collective-permute-start.21) | collective-permute-done | bytes 524320 | tf_op jit(solution)/shard_map/ppermute | solution.py:222
  149.6 9.7 %shard_map.66 = (bf16[2048,384]{1,0:T(8,128)(2,1)}, bf16[2048,256]{1,0:T(8,128)(2,1)S(1)}, bf16[2048,256]{1,0:T(8,128)(2,1)S(1)}, bf16[2048,256]{1,0:T(8,128)(2,1)S(1)}, bf16[2048,256]{1,0:T(8,128)(2,1)}) custom-call(f32[8]{0:T(128)S(1)} %convert_element_type.23.block_ref, f32[2048,10]{1,0:T(8,128)} %bitcast.29, ...), custom_call_target="tpu_custom_call" | custom-call | flops 5905580032 | bytes 8388608 | tf_op jit(solution)/shard_map/pallas_call | solution.py:105
  161.3 27.0 %shard_map.67 = bf16[2048,128]{1,0:T(8,128)(2,1)} custom-call(s32[16,30]{1,0:T(8,128)S(1)} %fusion.index_ref, s32[16]{0:T(128)S(1)} %copy-done.9, f32[8]{0:T(128)S(1)} %convert_element_type.20.block_ref, f32[2048,10]{1,0:T(8,128)S(1)} %bitcast.30, bf16[512,384]{1,0:T(8,128)(2,1)S(1)} %get-tuple-element.39.refs_0_, ...), custom_call_target="tpu_custom_call" | custom-call | flops 9932111872 | bytes 9437184 | tf_op jit(solution)/shard_map/pallas_call | solution.py:176
  188.3 6.6 %all-to-all-start = ((bf16[8,256,128]{2,1,0:T(8,128)(2,1)}), bf16[8,256,128]{2,1,0:T(8,128)(2,1)S(1)}, u32[]{:S(2)}, u32[]{:S(2)}) async-start(bf16[8,256,128]{2,1,0:T(8,128)(2,1)} %bitcast.26), calls=%async_computation | async-start | bytes 1048576 | tf_op jit(solution)/shard_map/all_to_all | solution.py:283
  195.0 9.3 %all-to-all-done.att_ref = bf16[8,256,128]{2,1,0:T(8,128)(2,1)S(1)} async-done(((bf16[8,256,128]{2,1,0:T(8,128)(2,1)}), bf16[8,256,128]{2,1,0:T(8,128)(2,1)S(1)}, u32[]{:S(2)}, u32[]{:S(2)}) %all-to-all-start) | async-done | bytes 524320 | tf_op jit(solution)/shard_map/all_to_all | solution.py:283
  204.3 2.8 %copy-done = bf16[1024,3072]{1,0:T(8,128)(2,1)S(1)} copy-done((bf16[1024,3072]{1,0:T(8,128)(2,1)S(1)}, bf16[1024,3072]{1,0:T(8,128)(2,1)}, u32[]{:S(2)}) %copy-start) | copy-done | bytes 6291480
  207.1 2.4 %shard_map.68 = (f32[128,3072]{1,0:T(8,128)S(1)}, bf16[128,3072]{1,0:T(8,128)(2,1)S(1)}) custom-call(s32[9]{0:T(128)S(1)} %stack.98.order_ref, bf16[8,256,128]{2,1,0:T(8,128)(2,1)S(1)} %all-to-all-done.att_ref, bf16[8,8,16,3072]{3,2,1,0:T(8,128)(2,1)S(1)} %bitcast.28), custom_call_target="tpu_custom_call" | custom-call | flops 1610612736 | bytes 10485760 | tf_op jit(solution)/shard_map/pallas_call | solution.py:210
  209.5 3.5 %collective-permute-start.30 = (bf16[128,3072]{1,0:T(8,128)(2,1)S(1)}, bf16[128,3072]{1,0:T(8,128)(2,1)S(1)}, u32[]{:S(2)}, u32[]{:S(2)}) collective-permute-start(bf16[128,3072]{1,0:T(8,128)(2,1)S(1)} %get-tuple-element.48), channel_id=1, source_target_pairs={{0,1},{1,0},{2,3},{3,2},{4,5},{5,4},{6,7},{7,6},{8,9},{9,8},{10,11... | collective-permute-start | bytes 2359304 | tf_op jit(solution)/shard_map/ppermute | solution.py:32
  213.0 1.9 collective-permute-done.30
  (121 shorter events, 41.5 us)
Async XLA Ops:
  6.5 197.8 %all-gather.2.cloned.1.call-start = ((), (), s32[]{:S(2)}) async-start(), calls=%async_computation.1 | async-start | bytes 7077888 | tf_op jit(solution)/shard_map/all_gather | solution.py:242
  7.5 5.8 %collective-permute-start.26 = (bf16[16,3072]{1,0:T(8,128)(2,1)S(1)}, bf16[16,3072]{1,0:T(8,128)(2,1)S(1)}, u32[]{:S(2)}, u32[]{:S(2)}) collective-permute-start(bf16[16,3072]{1,0:T(8,128)(2,1)S(1)} %get-tuple-element.50), channel_id=1, source_target_pairs={{0,8},{8,0},{1,9},{9,1},{2,10},{10,2},{3,11},{11,3},{4,12},{12,4},... | collective-permute-start | bytes 294920 | tf_op jit(solution)/shard_map/ppermute | solution.py:32
  13.4 5.8 %collective-permute-start.27 = (bf16[32,3072]{1,0:T(8,128)(2,1)S(1)}, bf16[32,3072]{1,0:T(8,128)(2,1)S(1)}, u32[]{:S(2)}, u32[]{:S(2)}) collective-permute-start(bf16[32,3072]{1,0:T(8,128)(2,1)S(1)} %pad_maximum_fusion.2), channel_id=1, source_target_pairs={{0,2},{2,4},{4,6},{6,0},{1,3},{3,5},{5,7},{7,1},{8,10},{10,12},{12... | collective-permute-start | bytes 589832 | tf_op jit(solution)/shard_map/ppermute | solution.py:37
  16.1 8.1 %collective-permute-start.29 = (bf16[32,3072]{1,0:T(8,128)(2,1)S(1)}, bf16[32,3072]{1,0:T(8,128)(2,1)S(1)}, u32[]{:S(2)}, u32[]{:S(2)}) collective-permute-start(bf16[32,3072]{1,0:T(8,128)(2,1)S(1)} %pad_maximum_fusion.2), channel_id=1, source_target_pairs={{0,4},{2,6},{4,0},{6,2},{1,5},{3,7},{5,1},{7,3},{8,12},{10,14},{12... | collective-permute-start | bytes 589832 | tf_op jit(solution)/shard_map/ppermute | solution.py:37
  25.2 35.2 %collective-permute-start = (bf16[3072,384]{1,0:T(8,128)(2,1)}, bf16[3072,384]{1,0:T(8,128)(2,1)S(1)}, u32[]{:S(2)}, u32[]{:S(2)}) collective-permute-start(bf16[3072,384]{1,0:T(8,128)(2,1)} %own_ref.3), channel_id=1, source_target_pairs={{0,1},{1,0},{2,3},{3,2},{4,5},{5,4},{6,7},{7,6},{8,9},{9,8},{10,11... | collective-permute-start | bytes 7077896 | tf_op jit(solution)/shard_map/ppermute | solution.py:32
  28.7 20.4 %collective-permute-start.1 = (bf16[128,3072]{1,0:T(8,128)(2,1)S(1)}, bf16[128,3072]{1,0:T(8,128)(2,1)S(1)}, u32[]{:S(2)}, u32[]{:S(2)}) collective-permute-start(bf16[128,3072]{1,0:T(8,128)(2,1)S(1)} %copy-done.2), channel_id=1, source_target_pairs={{0,2},{2,4},{4,6},{6,0},{1,3},{3,5},{5,7},{7,1},{8,10},{10,12},{12... | collective-permute-start | bytes 2359304 | tf_op jit(solution)/shard_map/ppermute | solution.py:28
  29.2 20.0 %collective-permute-start.2 = (bf16[128,3072]{1,0:T(8,128)(2,1)S(1)}, bf16[128,3072]{1,0:T(8,128)(2,1)S(1)}, u32[]{:S(2)}, u32[]{:S(2)}) collective-permute-start(bf16[128,3072]{1,0:T(8,128)(2,1)S(1)} %copy-done.2), channel_id=1, source_target_pairs={{0,6},{2,0},{4,2},{6,4},{1,7},{3,1},{5,3},{7,5},{8,14},{10,8},{12,... | collective-permute-start | bytes 2359304 | tf_op jit(solution)/shard_map/ppermute | solution.py:28
  32.1 41.6 %collective-permute-start.10 = (bf16[48,3072]{1,0:T(8,128)(2,1)}, bf16[48,3072]{1,0:T(8,128)(2,1)}, u32[]{:S(2)}, u32[]{:S(2)}) collective-permute-start(bf16[48,3072]{1,0:T(8,128)(2,1)} %slice.125), channel_id=1, source_target_pairs={{0,8},{8,0},{1,9},{9,1},{2,10},{10,2},{3,11},{11,3},{4,12},{12,4},... | collective-permute-start | bytes 884744 | tf_op jit(solution)/shard_map/ppermute | solution.py:32
  34.7 31.4 %collective-permute-start.11 = (bf16[80,3072]{1,0:T(8,128)(2,1)S(1)}, bf16[80,3072]{1,0:T(8,128)(2,1)}, u32[]{:S(2)}, u32[]{:S(2)}) collective-permute-start(bf16[80,3072]{1,0:T(8,128)(2,1)S(1)} %slice.126), channel_id=1, source_target_pairs={{0,8},{8,0},{1,9},{9,1},{2,10},{10,2},{3,11},{11,3},{4,12},{12,4},... | collective-permute-start | bytes 1474568 | tf_op jit(solution)/shard_map/ppermute | solution.py:32
  49.1 11.3 %collective-permute-start.3 = (bf16[64,3072]{1,0:T(8,128)(2,1)S(1)}, bf16[64,3072]{1,0:T(8,128)(2,1)S(1)}, u32[]{:S(2)}, u32[]{:S(2)}) collective-permute-start(bf16[64,3072]{1,0:T(8,128)(2,1)S(1)} %slice.153), channel_id=1, source_target_pairs={{0,2},{2,4},{4,6},{6,0},{1,3},{3,5},{5,7},{7,1},{8,10},{10,12},{12... | collective-permute-start | bytes 1179656 | tf_op jit(solution)/shard_map/ppermute | solution.py:28
  49.3 11.1 %collective-permute-start.4 = (bf16[64,3072]{1,0:T(8,128)(2,1)S(1)}, bf16[64,3072]{1,0:T(8,128)(2,1)S(1)}, u32[]{:S(2)}, u32[]{:S(2)}) collective-permute-start(bf16[64,3072]{1,0:T(8,128)(2,1)S(1)} %slice.154), channel_id=1, source_target_pairs={{0,6},{2,0},{4,2},{6,4},{1,7},{3,1},{5,3},{7,5},{8,14},{10,8},{12,... | collective-permute-start | bytes 1179656 | tf_op jit(solution)/shard_map/ppermute | solution.py:28
  64.4 4.7 %collective-permute-start.5 = (bf16[512,384]{1,0:T(8,128)(2,1)}, bf16[512,384]{1,0:T(8,128)(2,1)S(1)}, u32[]{:S(2)}, u32[]{:S(2)}) collective-permute-start(bf16[512,384]{1,0:T(8,128)(2,1)} %get-tuple-element.28), channel_id=1, source_target_pairs={{0,1},{1,0},{2,3},{3,2},{4,5},{5,4},{6,7},{7,6},{8,9},{9,8},{10,11... | collective-permute-start | bytes 1179656 | tf_op jit(solution)/shard_map/ppermute | solution.py:32
  66.1 14.7 %collective-permute-start.13 = (bf16[80,3072]{1,0:T(8,128)(2,1)}, bf16[80,3072]{1,0:T(8,128)(2,1)}, u32[]{:S(2)}, u32[]{:S(2)}) collective-permute-start(bf16[80,3072]{1,0:T(8,128)(2,1)} %collective-permute-done.11.refs_1_), channel_id=1, source_target_pairs={{0,2},{2,4},{4,6},{6,0},{1,3},{3,5},{5,7},{7,1},{8,10},{10,12},{12... | collective-permute-start | bytes 1474568 | tf_op jit(solution)/shard_map/ppermute | solution.py:28
  66.2 15.9 %collective-permute-start.15 = (bf16[80,3072]{1,0:T(8,128)(2,1)}, bf16[80,3072]{1,0:T(8,128)(2,1)S(1)}, u32[]{:S(2)}, u32[]{:S(2)}) collective-permute-start(bf16[80,3072]{1,0:T(8,128)(2,1)} %collective-permute-done.11.refs_1_), channel_id=1, source_target_pairs={{0,6},{2,0},{4,2},{6,4},{1,7},{3,1},{5,3},{7,5},{8,14},{10,8},{12,... | collective-permute-start | bytes 1474568 | tf_op jit(solution)/shard_map/ppermute | solution.py:28
  70.0 29.7 %collective-permute-start.7 = (bf16[1040,256]{1,0:T(8,128)(2,1)}, bf16[1040,256]{1,0:T(8,128)(2,1)}, u32[]{:S(2)}, u32[]{:S(2)}) collective-permute-start(bf16[1040,256]{1,0:T(8,128)(2,1)} %pad_maximum_fusion), channel_id=1, source_target_pairs={{0,16},{16,0},{1,17},{17,1},{2,18},{18,2},{3,19},{19,3},{4,20},{20... | collective-permute-start | bytes 1597448 | tf_op jit(solution)/shard_map/ppermute | solution.py:32
  71.0 21.0 %collective-permute-start.12 = (bf16[48,3072]{1,0:T(8,128)(2,1)S(1)}, bf16[48,3072]{1,0:T(8,128)(2,1)S(1)}, u32[]{:S(2)}, u32[]{:S(2)}) collective-permute-start(bf16[48,3072]{1,0:T(8,128)(2,1)S(1)} %slice.161), channel_id=1, source_target_pairs={{0,8},{8,0},{1,9},{9,1},{2,10},{10,2},{3,11},{11,3},{4,12},{12,4},... | collective-permute-start | bytes 884744 | tf_op jit(solution)/shard_map/ppermute | solution.py:32
  73.7 24.6 %collective-permute-start.14 = (bf16[48,3072]{1,0:T(8,128)(2,1)S(1)}, bf16[48,3072]{1,0:T(8,128)(2,1)S(1)}, u32[]{:S(2)}, u32[]{:S(2)}) collective-permute-start(bf16[48,3072]{1,0:T(8,128)(2,1)S(1)} %slice.162), channel_id=1, source_target_pairs={{0,8},{8,0},{1,9},{9,1},{2,10},{10,2},{3,11},{11,3},{4,12},{12,4},... | collective-permute-start | bytes 884744 | tf_op jit(solution)/shard_map/ppermute | solution.py:32
  80.8 29.3 %collective-permute-start.6 = (bf16[1040,256]{1,0:T(8,128)(2,1)}, bf16[1040,256]{1,0:T(8,128)(2,1)}, u32[]{:S(2)}, u32[]{:S(2)}) collective-permute-start(bf16[1040,256]{1,0:T(8,128)(2,1)} %pad_maximum_fusion), channel_id=1, source_target_pairs={{0,32},{32,64},{64,96},{96,128},{128,160},{160,192},{192,224},{224... | collective-permute-start | bytes 1597448 | tf_op jit(solution)/shard_map/ppermute | solution.py:222
  82.1 28.0 %collective-permute-start.8 = (bf16[1040,256]{1,0:T(8,128)(2,1)}, bf16[1040,256]{1,0:T(8,128)(2,1)}, u32[]{:S(2)}, u32[]{:S(2)}) collective-permute-start(bf16[1040,256]{1,0:T(8,128)(2,1)} %pad_maximum_fusion), channel_id=1, source_target_pairs={{0,224},{32,0},{64,32},{96,64},{128,96},{160,128},{192,160},{224,1... | collective-permute-start | bytes 1597448 | tf_op jit(solution)/shard_map/ppermute | solution.py:223
  92.0 15.4 %collective-permute-start.18 = (bf16[48,3072]{1,0:T(8,128)(2,1)}, bf16[48,3072]{1,0:T(8,128)(2,1)S(1)}, u32[]{:S(2)}, u32[]{:S(2)}) collective-permute-start(bf16[48,3072]{1,0:T(8,128)(2,1)} %slice.165), channel_id=1, source_target_pairs={{0,6},{2,0},{4,2},{6,4},{1,7},{3,1},{5,3},{7,5},{8,14},{10,8},{12,... | collective-permute-start | bytes 884744 | tf_op jit(solution)/shard_map/ppermute | solution.py:28
  98.3 9.1 %collective-permute-start.16 = (bf16[48,3072]{1,0:T(8,128)(2,1)S(1)}, bf16[48,3072]{1,0:T(8,128)(2,1)S(1)}, u32[]{:S(2)}, u32[]{:S(2)}) collective-permute-start(bf16[48,3072]{1,0:T(8,128)(2,1)S(1)} %slice.163), channel_id=1, source_target_pairs={{0,8},{8,0},{1,9},{9,1},{2,10},{10,2},{3,11},{11,3},{4,12},{12,4},... | collective-permute-start | bytes 884744 | tf_op jit(solution)/shard_map/ppermute | solution.py:32
  99.7 6.4 %collective-permute-start.17 = (bf16[32,3072]{1,0:T(8,128)(2,1)S(1)}, bf16[32,3072]{1,0:T(8,128)(2,1)S(1)}, u32[]{:S(2)}, u32[]{:S(2)}) collective-permute-start(bf16[32,3072]{1,0:T(8,128)(2,1)S(1)} %slice.164), channel_id=1, source_target_pairs={{0,2},{2,4},{4,6},{6,0},{1,3},{3,5},{5,7},{7,1},{8,10},{10,12},{12... | collective-permute-start | bytes 589832 | tf_op jit(solution)/shard_map/ppermute | solution.py:28
  106.1 24.4 %collective-permute-start.9 = (bf16[528,256]{1,0:T(8,128)(2,1)S(1)}, bf16[528,256]{1,0:T(8,128)(2,1)}, u32[]{:S(2)}, u32[]{:S(2)}) collective-permute-start(bf16[528,256]{1,0:T(8,128)(2,1)S(1)} %slice.159), channel_id=1, source_target_pairs={{0,32},{32,64},{64,96},{96,128},{128,160},{160,192},{192,224},{224... | collective-permute-start | bytes 811016 | tf_op jit(solution)/shard_map/ppermute | solution.py:227
  118.2 5.7 %collective-permute-start.19 = (bf16[512,384]{1,0:T(8,128)(2,1)S(1)}, bf16[512,384]{1,0:T(8,128)(2,1)S(1)}, u32[]{:S(2)}, u32[]{:S(2)}) collective-permute-start(bf16[512,384]{1,0:T(8,128)(2,1)S(1)} %get-tuple-element.40), channel_id=1, source_target_pairs={{0,1},{1,0},{2,3},{3,2},{4,5},{5,4},{6,7},{7,6},{8,9},{9,8},{10,11... | collective-permute-start | bytes 1179656 | tf_op jit(solution)/shard_map/ppermute | solution.py:32
  120.8 9.7 %collective-permute-start.20 = (bf16[512,256]{1,0:T(8,128)(2,1)S(1)}, bf16[512,256]{1,0:T(8,128)(2,1)S(1)}, u32[]{:S(2)}, u32[]{:S(2)}) collective-permute-start(bf16[512,256]{1,0:T(8,128)(2,1)S(1)} %get-tuple-element.54), channel_id=1, source_target_pairs={{0,16},{16,0},{1,17},{17,1},{2,18},{18,2},{3,19},{19,3},{4,20},{20... | collective-permute-start | bytes 786440 | tf_op jit(solution)/shard_map/ppermute | solution.py:32
  130.5 13.2 %collective-permute-start.23 = (bf16[1024,256]{1,0:T(8,128)(2,1)}, bf16[1024,256]{1,0:T(8,128)(2,1)}, u32[]{:S(2)}, u32[]{:S(2)}) collective-permute-start(bf16[1024,256]{1,0:T(8,128)(2,1)} %pad_maximum_fusion.1), channel_id=1, source_target_pairs={{0,224},{32,0},{64,32},{96,64},{128,96},{160,128},{192,160},{224,1... | collective-permute-start | bytes 1572872 | tf_op jit(solution)/shard_map/ppermute | solution.py:223
  132.3 13.9 %collective-permute-start.21 = (bf16[1024,256]{1,0:T(8,128)(2,1)}, bf16[1024,256]{1,0:T(8,128)(2,1)}, u32[]{:S(2)}, u32[]{:S(2)}) collective-permute-start(bf16[1024,256]{1,0:T(8,128)(2,1)} %pad_maximum_fusion.1), channel_id=1, source_target_pairs={{0,32},{32,64},{64,96},{96,128},{128,160},{160,192},{192,224},{224... | collective-permute-start | bytes 1572872 | tf_op jit(solution)/shard_map/ppermute | solution.py:222
  132.3 16.1 %collective-permute-start.22 = (bf16[1024,256]{1,0:T(8,128)(2,1)}, bf16[1024,256]{1,0:T(8,128)(2,1)}, u32[]{:S(2)}, u32[]{:S(2)}) collective-permute-start(bf16[1024,256]{1,0:T(8,128)(2,1)} %pad_maximum_fusion.1), channel_id=1, source_target_pairs={{0,16},{16,0},{1,17},{17,1},{2,18},{18,2},{3,19},{19,3},{4,20},{20... | collective-permute-start | bytes 1572872 | tf_op jit(solution)/shard_map/ppermute | solution.py:32
  147.4 13.9 %collective-permute-start.24 = (bf16[512,256]{1,0:T(8,128)(2,1)S(1)}, bf16[512,256]{1,0:T(8,128)(2,1)S(1)}, u32[]{:S(2)}, u32[]{:S(2)}) collective-permute-start(bf16[512,256]{1,0:T(8,128)(2,1)S(1)} %get-tuple-element.60), channel_id=1, source_target_pairs={{0,16},{16,0},{1,17},{17,1},{2,18},{18,2},{3,19},{19,3},{4,20},{20... | collective-permute-start | bytes 786440 | tf_op jit(solution)/shard_map/ppermute | solution.py:32
  149.5 11.8 %collective-permute-start.25 = (bf16[512,256]{1,0:T(8,128)(2,1)S(1)}, bf16[512,256]{1,0:T(8,128)(2,1)S(1)}, u32[]{:S(2)}, u32[]{:S(2)}) collective-permute-start(bf16[512,256]{1,0:T(8,128)(2,1)S(1)} %get-tuple-element.65.refs_5_), channel_id=1, source_target_pairs={{0,32},{32,64},{64,96},{96,128},{128,160},{160,192},{192,224},{224... | collective-permute-start | bytes 786440 | tf_op jit(solution)/shard_map/ppermute | solution.py:227
  188.3 16.0 %all-to-all-start = ((bf16[8,256,128]{2,1,0:T(8,128)(2,1)}), bf16[8,256,128]{2,1,0:T(8,128)(2,1)S(1)}, u32[]{:S(2)}, u32[]{:S(2)}) async-start(bf16[8,256,128]{2,1,0:T(8,128)(2,1)} %bitcast.26), calls=%async_computation | async-start | bytes 1048576 | tf_op jit(solution)/shard_map/all_to_all | solution.py:283
  209.5 5.4 %collective-permute-start.30 = (bf16[128,3072]{1,0:T(8,128)(2,1)S(1)}, bf16[128,3072]{1,0:T(8,128)(2,1)S(1)}, u32[]{:S(2)}, u32[]{:S(2)}) collective-permute-start(bf16[128,3072]{1,0:T(8,128)(2,1)S(1)} %get-tuple-element.48), channel_id=1, source_target_pairs={{0,1},{1,0},{2,3},{3,2},{4,5},{5,4},{6,7},{7,6},{8,9},{9,8},{10,11... | collective-permute-start | bytes 2359304 | tf_op jit(solution)/shard_map/ppermute | solution.py:32
  (16 other events, 152.5 us)
Sparse Core Ops, SparseCore 0:
  25.3 91.4 all-gather.1

commit v3 on v2

v3 whole, which is shorter than its diff:
```python
import functools
import math

import jax
import jax.numpy as jnp
from jax import lax
from jax.experimental import pallas as pl
from jax.experimental.pallas import tpu as pltpu
from jax.sharding import Mesh
from jax.sharding import PartitionSpec as P

BF = jnp.bfloat16
F32 = jnp.float32
TILE = 128
LOG2E = 1.4426950408889634
VM = pltpu.VMEM
SM = pltpu.SMEM
CTX = ("z", "yl")
CHIPS = ("yh", "x")
ALL = ("z", "yl", "yh", "x", "core")
NEAR = ((0, 0), (0, 1), (0, 3), (1, 0))
FAR = ((0, 2), (1, 1), (1, 3), (1, 2))
WHOLE_VM = pl.BlockSpec(memory_space=VM)
WHOLE_SM = pl.BlockSpec(memory_space=SM)
WHOLE_ANY = pl.BlockSpec(memory_space=pl.ANY)


def round_x(array, by):
    return lax.ppermute(array, "x", [(i, (i + by) % 4) for i in range(4)])


def swap(array, axis):
    return lax.ppermute(array, axis, [(0, 1), (1, 0)])


def qkv_kernel(heights, own_ref, other_ref, *refs):
    pieces = refs[: len(heights)]
    mine_ref, theirs_ref, rows_ref, sems = refs[len(heights) :]
    copies, start = [], 0
    for i, height in enumerate(heights):
        copies.append(pltpu.make_async_copy(pieces[i], rows_ref.at[pl.ds(start, height)], sems.at[i]))
        start += height
    for copy in copies:
        copy.start()
    for copy in copies:
        copy.wait()
    theirs_ref[...] = jnp.dot(rows_ref[...], other_ref[...], preferred_element_type=F32).astype(BF)
    mine_ref[...] = jnp.dot(rows_ref[...], own_ref[...], preferred_element_type=F32).astype(BF)


def qkv(own, other, pieces):
    heights = tuple(p.shape[0] for p in pieces)
    n, depth, width = sum(heights), own.shape[0], own.shape[1]
    return pl.pallas_call(
        functools.partial(qkv_kernel, heights),
        out_shape=(jax.ShapeDtypeStruct((n, width), BF),) * 2,
        in_specs=[WHOLE_VM] * 2 + [WHOLE_ANY] * len(pieces),
        out_specs=(WHOLE_VM,) * 2,
        scratch_shapes=[VM((n, depth), BF), pltpu.SemaphoreType.DMA((len(pieces),))],
        compiler_params=pltpu.CompilerParams(vmem_limit_bytes=40 << 20),
        cost_estimate=pl.CostEstimate(flops=4 * n * depth * width, bytes_accessed=8 << 20, transcendentals=0),
    )(own, other, *pieces)


def hot_rows(want, block_ref):
    n = want.shape[0]
    high = jnp.broadcast_to(want[:, 0:1], (n, TILE)).astype(BF)
    low = jnp.broadcast_to(want[:, 1:2], (n, TILE))
    lane = lax.broadcasted_iota(jnp.int32, (n, TILE), 1).astype(F32)
    inside = jnp.where(low == lane, 1.0, 0.0).astype(BF)
    zero = jnp.zeros((n, TILE), BF)
    picks = [jnp.where(high == block_ref[b].astype(BF), inside, zero) for b in range(block_ref.shape[0])]
    return jnp.concatenate(picks, axis=1)


def pick(want, block_ref, first_ref, second_ref):
    hot, half = hot_rows(want, block_ref), first_ref.shape[0]
    done = jnp.dot(hot[:, :half], first_ref[...], preferred_element_type=F32)
    return done + jnp.dot(hot[:, half:], second_ref[...], preferred_element_type=F32)


def place_near_kernel(block_ref, want_ref, first_ref, second_ref, out_ref):
    rows = 512

    def step(i, carry):
        spot = pl.ds(pl.multiple_of(i * rows, rows), rows)
        out_ref[spot, :] = pick(want_ref[spot, :], block_ref, first_ref, second_ref).astype(BF)
        return carry

    lax.fori_loop(0, want_ref.shape[0] // rows, step, 0)


def place_far_kernel(block_ref, want_ref, first_ref, second_ref, near_ref, q_ref, kv_ref):
    rows = 512

    def step(i, carry):
        start = pl.multiple_of(i * rows, rows)
        spot = pl.ds(start, rows)
        done = pick(want_ref[spot, :], block_ref, first_ref, second_ref) + near_ref[spot, :].astype(F32)
        q_ref[spot, :] = done[:, :TILE].astype(BF)
        kv_ref[spot, TILE:] = done[:, 2 * TILE :].astype(BF)
        for t in range(0, rows, TILE):
            keys = done[t : t + TILE, TILE : 2 * TILE]
            kv_ref[pl.ds(pl.multiple_of(start + t, TILE), TILE), :TILE] = keys.T.astype(BF)
        return carry

    lax.fori_loop(0, want_ref.shape[0] // rows, step, 0)


def place(blocks, want, first, second, near=None):
    n, width = want.shape[0], first.shape[1]
    if near is None:
        kernel, out = place_near_kernel, jax.ShapeDtypeStruct((n, width), BF)
    else:
        kernel = place_far_kernel
        out = (jax.ShapeDtypeStruct((n, TILE), BF), jax.ShapeDtypeStruct((n, width - TILE), BF))
    operands = (want, first, second) + (() if near is None else (near,))
    return pl.pallas_call(
        kernel,
        out_shape=out,
        in_specs=[WHOLE_SM] + [WHOLE_VM] * len(operands),
        out_specs=WHOLE_VM if near is None else (WHOLE_VM,) * 2,
        compiler_params=pltpu.CompilerParams(vmem_limit_bytes=40 << 20),
        cost_estimate=pl.CostEstimate(flops=n * n * width, bytes_accessed=4 << 20, transcendentals=0),
    )(blocks, *operands)


def attend_kernel(sizes, together, parts, last, index_ref, count_ref, q_ref, *refs):
    frames = refs[:parts]
    refs = refs[parts:]
    if last:
        old_ref, stat_ref, out_ref = refs[:3]
    else:
        out_ref, stat_ref = refs[:2]
    win_ref, score_ref, sems = refs[-3:]
    copies, start = [], 0
    for i, frame in enumerate(frames):
        copies.append(pltpu.make_async_copy(frame, win_ref.at[pl.ds(start, frame.shape[0])], sems.at[i]))
        start += frame.shape[0]
    for copy in copies:
        copy.start()
    for copy in copies:
        copy.wait()
    scale = LOG2E / math.sqrt(TILE)

    ones = jnp.ones((2 * TILE, TILE), BF)
    none = jnp.zeros((TILE, TILE), BF)

    def look(t, u, slots):
        q = q_ref[pl.ds(pl.multiple_of(t * TILE, TILE), TILE), :]
        top = None
        for j in range(0, slots, 2):
            spots = [pl.multiple_of(index_ref[t, j + h] * TILE, TILE) for h in range(2)]
            k = jnp.concatenate([win_ref[pl.ds(s, TILE), :TILE] for s in spots], axis=1)
            s = jnp.dot(q, k, preferred_element_type=F32)
            score_ref[u, j // 2] = s
            s = jnp.maximum(s[:, :TILE], s[:, TILE:])
            top = s if top is None else jnp.maximum(top, s)
        return jnp.max(top, axis=1, keepdims=True) * scale

    def weigh(t, u, slots, peak):
        base = pl.multiple_of(t * TILE, TILE)
        count = count_ref[t]
        if last:
            old = stat_ref[pl.ds(base, TILE), :]
            before = old[:, 0:1]
            peak = jnp.where(count > 0, jnp.maximum(peak, before), before)
        done = None
        for j in range(0, slots, 2):
            spots = [pl.multiple_of(index_ref[t, j + h] * TILE, TILE) for h in range(2)]
            e = jnp.exp2(score_ref[u, j // 2] * scale - peak).astype(BF)
            e = jnp.concatenate([jnp.where(j + h < count, e[:, h * TILE : (h + 1) * TILE], none) for h in range(2)], axis=1)
            v = jnp.concatenate([win_ref[pl.ds(s, TILE), TILE:] for s in spots], axis=0)
            part = jnp.dot(e, jnp.concatenate([v, ones], axis=1), preferred_element_type=F32)
            done = part if done is None else done + part
        value, total = done[:, :TILE], done[:, TILE:]
        if last:
            shrink = jnp.exp2(before - peak)
            total = total + shrink * old[:, 1:2]
            value = value + shrink * old_ref[pl.ds(base, TILE), :]
            out_ref[pl.ds(base, TILE), :] = (value / total).astype(BF)
        else:
            peak = jnp.where(count > 0, peak, -1e30)
            out_ref[pl.ds(base, TILE), :] = value
            lane = lax.broadcasted_iota(jnp.int32, (TILE, TILE), 1)
            stat_ref[pl.ds(base, TILE), :] = jnp.where(lane == 0, peak, total)

    def step(i, carry):
        tiles = [i * together + u for u in range(together)]
        most = functools.reduce(jnp.maximum, [count_ref[t] for t in tiles])
        for k, slots in enumerate(sizes):
            fits = most <= slots
            if k > 0:
                fits = jnp.logical_and(fits, most > sizes[k - 1])

            @pl.when(fits)
            def _(slots=slots):
                peaks = [look(t, u, slots) for u, t in enumerate(tiles)]
                for u, t in enumerate(tiles):
                    weigh(t, u, slots, peaks[u])

        return carry

    lax.fori_loop(0, q_ref.shape[0] // TILE // together, step, 0)


def attend(index, count, q, frames, sizes, old=None, together=2):
    n, slots = q.shape[0], index.shape[1]
    rows = sum(f.shape[0] for f in frames)
    wide = jax.ShapeDtypeStruct((n, TILE), F32)
    return pl.pallas_call(
        functools.partial(attend_kernel, sizes, together, len(frames), old is not None),
        out_shape=(wide, wide) if old is None else jax.ShapeDtypeStruct((n, TILE), BF),
        in_specs=[WHOLE_SM] * 2 + [WHOLE_VM] + [WHOLE_ANY] * len(frames) + [WHOLE_VM] * (0 if old is None else 2),
        out_specs=(WHOLE_VM,) * 2 if old is None else WHOLE_VM,
        scratch_shapes=[
            VM((rows, 2 * TILE), BF),
            VM((together, sizes[-1] // 2, TILE, 2 * TILE), F32),
            pltpu.SemaphoreType.DMA((len(frames),)),
        ],
        compiler_params=pltpu.CompilerParams(vmem_limit_bytes=40 << 20),
        cost_estimate=pl.CostEstimate(
            flops=12 * 4 * n * slots * TILE * TILE, bytes_accessed=6 << 20, transcendentals=n * slots * TILE
        ),
    )(index, count, q, *frames, *(old or ()))


def project_kernel(att_ref, w_ref, core_ref, mine_ref, other_ref):
    chips = w_ref.shape[1]
    own = pl.multiple_of(core_ref[0] * TILE, TILE)
    away = pl.multiple_of(TILE - own, TILE)
    mine = jnp.concatenate([att_ref[b, pl.ds(own, TILE), :] for b in range(chips)], axis=1)
    other = jnp.concatenate([att_ref[b, pl.ds(away, TILE), :] for b in range(chips)], axis=1)
    left = jnp.concatenate([mine, other], axis=0)
    step = 256
    for column in range(0, mine_ref.shape[1], step):
        right = jnp.concatenate([w_ref[:, b, :, column : column + step].reshape(TILE, step) for b in range(chips)], axis=0)
        done = jnp.dot(left, right, preferred_element_type=F32)
        mine_ref[:, column : column + step] = done[:TILE]
        other_ref[:, column : column + step] = done[TILE:].astype(BF)


def project(attended, w, core):
    width = w.shape[-1]
    return pl.pallas_call(
        project_kernel,
        out_shape=(jax.ShapeDtypeStruct((TILE, width), F32), jax.ShapeDtypeStruct((TILE, width), BF)),
        in_specs=[WHOLE_VM] * 2 + [WHOLE_SM],
        out_specs=(WHOLE_VM,) * 2,
        compiler_params=pltpu.CompilerParams(vmem_limit_bytes=40 << 20),
        cost_estimate=pl.CostEstimate(flops=4 * TILE * 8 * TILE * width, bytes_accessed=10 << 20, transcendentals=0),
    )(attended, w, core.astype(jnp.int32).reshape(1))


def listed(place, chosen, slots):
    before = jnp.arange(place.shape[1])[None, :] < jnp.arange(place.shape[1])[:, None]
    rank = jnp.sum(jnp.where(before[None] & chosen[:, None, :], 1, 0), axis=2)
    count = jnp.sum(chosen.astype(jnp.int32), axis=1)
    lead = jnp.minimum(jnp.arange(slots)[None, :], jnp.maximum(count - 1, 0)[:, None])
    lead = jnp.where(jnp.arange(slots)[None, :] < count[:, None], lead, 0)
    hit = (rank[:, None, :] == lead[:, :, None]) & chosen[:, None, :]
    return jnp.sum(jnp.where(hit, place[:, None, :], 0), axis=2).astype(jnp.int32), count


def body(tokens, w_qkv, w_out, source_row, key_tiles, key_count):
    z, yl = lax.axis_index("z"), lax.axis_index("yl")
    yh, x, core = lax.axis_index("yh"), lax.axis_index("x"), lax.axis_index("core")

    one, three = round_x(tokens, 1), round_x(tokens, -1)
    far_own = swap(tokens, "yh")
    w_other = swap(w_qkv, "core")
    half = tokens.shape[0] // 2
    low, high = round_x(one[:half], 1), round_x(three[half:], -1)
    f_one, f_three = round_x(far_own, 1), round_x(far_own, -1)
    near_mine, near_theirs = qkv(w_qkv, w_other, [tokens, one, three, far_own])
    near_other = swap(near_theirs, "core")
    two = jnp.concatenate([low, high], axis=0)
    far_two = swap(two, "yh")

    share = w_out.shape[0] // 8
    w_share = lax.dynamic_slice_in_dim(w_out, z * share, share, 0)
    w_share, _ = lax.optimization_barrier((w_share, w_other))
    w_share = jnp.broadcast_to(w_share[None], (8,) + w_share.shape)
    w_chips = lax.all_to_all(w_share, CHIPS, split_axis=0, concat_axis=0, tiled=True)
    w_all = lax.all_gather(w_chips.reshape(8 * share, -1), "z", axis=0, tiled=True)
    w_all = w_all.reshape(8, 8, share, w_out.shape[1])

    def blocks(part):
        chips = [((yh + dy) % 2) * 4 + (x + 4 - dx) % 4 for dy, dx in part]
        return jnp.stack([2 * c + side for side in (core, 1 - core) for c in chips]).astype(F32)

    source = source_row[0]
    want = jnp.stack([source // TILE, source % TILE], axis=1).astype(F32)
    near = place(blocks(NEAR), want, near_mine, near_other)
    far_mine, far_theirs = qkv(w_qkv, w_other, [low, high, f_one, f_three, far_two])
    far_other = swap(far_theirs, "core")
    q, kv = place(blocks(FAR), want, far_mine, far_other, near)

    behind = lax.ppermute(kv, "z", [(i, (i + 1) % 8) for i in range(8)])
    ahead = lax.ppermute(kv, "z", [(i, (i + 7) % 8) for i in range(8)])
    beside = swap(kv, "yl")
    mid = kv.shape[0] // 2
    cross_low = swap(jnp.where(yl == 0, ahead[:mid], behind[:mid]), "yl")
    onward = [(2 * i, 2 * ((i + 1) % 8)) for i in range(8)] + [(2 * i + 1, 2 * ((i + 7) % 8) + 1) for i in range(8)]
    cross_high = lax.ppermute(beside[mid:], CTX, onward)

    tiles, slots = key_tiles.shape
    relative = key_tiles - ((z * 2 + yl) - 2) * tiles
    frame, inside = relative // tiles, relative % tiles
    crossing = frame == jnp.where(yl == 0, 1, 3)
    window = jnp.where(frame == 2, 0, jnp.where(frame == 0, 1, jnp.where(frame == 4, 3, 2)))
    valid = jnp.arange(slots)[None, :] < key_count[:, None]
    index, count = listed(window * tiles + inside, valid & ~crossing, slots)
    cross_index, cross_count = listed(inside, valid & crossing, tiles)
    state = attend(index, count, q, [kv, behind, beside, ahead], (24, slots), together=4)
    attended = attend(cross_index, cross_count, q, [cross_low, cross_high], (6, tiles), state, together=4)

    pieces = lax.all_to_all(attended.reshape(8, 2 * TILE, TILE), CHIPS, split_axis=0, concat_axis=0, tiled=True)
    mine, other = project(pieces, w_all, core)
    return (mine + swap(other, "core").astype(F32)).astype(BF)


def solution(mesh):
    fine = Mesh(mesh.devices.reshape(8, 2, 2, 4, 2), ALL)
    in_specs = (
        P(ALL, None),
        P(None, ("yh", "x", "core")),
        P(("yh", "x", "core"), None),
        P(CTX, None),
        P(CTX, None),
        P(CTX),
    )
    return jax.shard_map(body, mesh=fine, in_specs=in_specs, out_specs=P(ALL, None), check_vma=False)
```

time: 223 us -> 195 us (0.87)
  starting transfers between devices: 55.3 us -> 36.2 us
  blocking collectives: 0 us -> 15.2 us
  waiting for transfers between devices: 79.1 us -> 66.4 us
  local copies, waits for them, and re-layouts: 21.3 us -> 13.6 us
  Pallas kernels: 47.8 us -> 40.5 us
  other arithmetic: 5.42 us -> 8.6 us
    ppermute x9 -> x3, waiting for transfers between devices: 15.5 us -> 42.9 us  [the longest x1 38.3 us: body(): ahead = lax.ppermute(kv, 'z', [(i, (i + 7) % 8) for i in range(8)])]
    ppermute x14 -> x8, waiting for transfers between devices: 20.1 us -> 4.12 us  [swap(): return lax.ppermute(array, axis, [(0, 1), (1, 0)])]
    all_to_all x0 -> x1, blocking collectives: none -> 15.2 us  [body(): lax.all_to_all(attended.reshape(8, 2 * TILE, TILE), CHIPS, split_axis=0,...]
    ppermute x8 -> x6, waiting for transfers between devices: 34.2 us -> 19.4 us  [round_x(): return lax.ppermute(array, 'x', [(i, (i + by) % 4) for i in range(4)])]
    pallas_call x2 -> x4, Pallas kernels: 36.7 us -> 25 us  [the longest x2 16.1 us: attend(): pl.pallas_call(functools.partial(attend_kernel, sizes, together, len(fram...]
    all_to_all x1, waiting for transfers between devices: 9.26 us -> 0.01 us  [body(): lax.all_to_all(w_share, CHIPS, split_axis=0, concat_axis=0, tiled=True)]
    slice x19 -> x1, local copies, waits for them, and re-layouts: 9.49 us -> 1.08 us  [body(): cross_high = lax.ppermute(beside[mid:], CTX, onward)]
    ppermute x14 -> x8, starting transfers between devices: 26.3 us -> 18.1 us  [swap(): return lax.ppermute(array, axis, [(0, 1), (1, 0)])]
  transfers between devices with their start and end apart: 33 -> 19, of which waited for: 15 -> 9; matrix products, arithmetic and copies ran while one was open for 7% -> 6% of each run, Pallas kernels for 20% -> 20%
where the time goes in v3:
time: 195 us; the launch traced here: 194 us
  waiting for transfers between devices  66.4 us (34%)
  Pallas kernels  40.5 us (21%)
  starting transfers between devices  36.2 us (19%)
  blocking collectives  15.2 us (8%)
  between operations  13.7 us (7%)
  local copies, waits for them, and re-layouts  13.6 us (7%)
  other arithmetic  8.6 us (4%)
    ppermute x1, waiting for transfers between devices, body(): ahead = lax.ppermute(kv, 'z', [(i, (i + 7) % 8) for i in range(8)])  38.3 us
    ppermute x6, waiting for transfers between devices, round_x(): return lax.ppermute(array, 'x', [(i, (i + by) % 4) for i in range(4)])  19.4 us
    ppermute x8, starting transfers between devices, swap(): return lax.ppermute(array, axis, [(0, 1), (1, 0)])  18.1 us
    pallas_call x2, Pallas kernels, attend(): pl.pallas_call(functools.partial(attend_kernel, sizes, together, len(fram...  16.1 us
    all_to_all x1, blocking collectives, body(): lax.all_to_all(attended.reshape(8, 2 * TILE, TILE), CHIPS, split_axis=0,...  15.2 us
    pallas_call x2, Pallas kernels, qkv(): pl.pallas_call(functools.partial(qkv_kernel, heights), out_shape=(jax.Sha...  13.7 us
    pallas_call x2, Pallas kernels, place(): pl.pallas_call(kernel, out_shape=out, in_specs=[WHOLE_SM] + [WHOLE_VM] *...  8.94 us
    unnamed x32, local copies, waits for them, and re-layouts  8.94 us
  transfers between devices with their start and end apart: 19, of which 9 were waited for; matrix products, arithmetic and copies ran while one was open for 6% of the time, Pallas kernels for 20%

profile of v3, /device:TPU:1, one launch (start us, length us, event | category | flops | bytes accessed | tf_op | source)
XLA Modules:
  0.0 194.2 jit_solution(7020941076606057199)
XLA Ops:
  6.5 3.2 %collective-permute-start = (bf16[3072,384]{1,0:T(8,128)(2,1)}, bf16[3072,384]{1,0:T(8,128)(2,1)}, u32[]{:S(2)}, u32[]{:S(2)}) collective-permute-start(bf16[3072,384]{1,0:T(8,128)(2,1)} %own_ref.3), channel_id=1, source_target_pairs={{0,1},{1,0},{2,3},{3,2},{4,5},{5,4},{6,7},{7,6},{8,9},{9,8},{10,11... | collective-permute-start | bytes 7077896 | tf_op jit(solution)/shard_map/ppermute | solution.py:33
  9.8 2.7 %collective-permute-start.3 = (bf16[128,3072]{1,0:T(8,128)(2,1)}, bf16[128,3072]{1,0:T(8,128)(2,1)S(1)}, u32[]{:S(2)}, u32[]{:S(2)}) collective-permute-start(bf16[128,3072]{1,0:T(8,128)(2,1)} %refs_0_.1), channel_id=1, source_target_pairs={{0,6},{2,0},{4,2},{6,4},{1,7},{3,1},{5,3},{7,5},{8,14},{10,8},{12,... | collective-permute-start | bytes 2359304 | tf_op jit(solution)/shard_map/ppermute | solution.py:29
  15.2 5.0 %all-to-all-start.1 = ((bf16[8,16,3072]{2,1,0:T(8,128)(2,1)}), bf16[8,16,3072]{2,1,0:T(8,128)(2,1)}, u32[]{:S(2)}, u32[]{:S(2)}) async-start(bf16[8,16,3072]{2,1,0:T(8,128)(2,1)} %broadcast_in_dim.52), calls=%async_computation.1 | async-start | bytes 1572864 | tf_op jit(solution)/shard_map/all_to_all | solution.py:284
  20.3 14.3 %collective-permute-done.1.refs_1_ = bf16[128,3072]{1,0:T(8,128)(2,1)S(1)} collective-permute-done((bf16[128,3072]{1,0:T(8,128)(2,1)}, bf16[128,3072]{1,0:T(8,128)(2,1)S(1)}, u32[]{:S(2)}, u32[]{:S(2)}) %collective-permute-start.1) | collective-permute-done | bytes 786464 | tf_op jit(solution)/shard_map/ppermute | solution.py:29
  35.5 2.7 %collective-permute-start.4 = (bf16[64,3072]{1,0:T(8,128)(2,1)}, bf16[64,3072]{1,0:T(8,128)(2,1)S(1)}, u32[]{:S(2)}, u32[]{:S(2)}) collective-permute-start(bf16[64,3072]{1,0:T(8,128)(2,1)} %slice.21), channel_id=1, source_target_pairs={{0,6},{2,0},{4,2},{6,4},{1,7},{3,1},{5,3},{7,5},{8,14},{10,8},{12,... | collective-permute-start | bytes 1179656 | tf_op jit(solution)/shard_map/ppermute | solution.py:29
  38.8 2.7 %collective-permute-start.7 = (bf16[128,3072]{1,0:T(8,128)(2,1)}, bf16[128,3072]{1,0:T(8,128)(2,1)}, u32[]{:S(2)}, u32[]{:S(2)}) collective-permute-start(bf16[128,3072]{1,0:T(8,128)(2,1)} %collective-permute-done.5.refs_3_), channel_id=1, source_target_pairs={{0,6},{2,0},{4,2},{6,4},{1,7},{3,1},{5,3},{7,5},{8,14},{10,8},{12,... | collective-permute-start | bytes 2359304 | tf_op jit(solution)/shard_map/ppermute | solution.py:29
  41.5 5.0 %collective-permute-done.2.refs_0_ = bf16[64,3072]{1,0:T(8,128)(2,1)S(1)} collective-permute-done((bf16[64,3072]{1,0:T(8,128)(2,1)S(1)}, bf16[64,3072]{1,0:T(8,128)(2,1)S(1)}, u32[]{:S(2)}, u32[]{:S(2)}) %collective-permute-start.2) | collective-permute-done | bytes 393248 | tf_op jit(solution)/shard_map/ppermute | solution.py:29
  47.4 1.9 collective-permute-start.8
  50.0 1.4 convert_reduce_fusion
  51.4 1.7 copy-done.2
  54.2 6.5 %shard_map.65 = (bf16[512,384]{1,0:T(8,128)(2,1)S(1)}, bf16[512,384]{1,0:T(8,128)(2,1)S(1)}) custom-call(bf16[3072,384]{1,0:T(8,128)(2,1)S(1)} %copy-done.2, bf16[3072,384]{1,0:T(8,128)(2,1)} %collective-permute-done.other_ref, bf16[128,3072]{1,0:T(8,128)(2,1)S(1)} %copy-done.3, bf16[128,3072]{1,0:T(8,128)(2,1)S(1)} %collective-permute-done.1.refs_1_, ...), custom_call_target="tpu_custom_call" | custom-call | flops 2415919104 | bytes 8388608 | tf_op jit(solution)/shard_map/pallas_call | solution.py:54
  61.6 1.7 collective-permute-start.10
  63.5 1.6 collective-permute-done.8.refs_4_
  65.0 7.2 %shard_map.64 = (bf16[512,384]{1,0:T(8,128)(2,1)S(1)}, bf16[512,384]{1,0:T(8,128)(2,1)S(1)}) custom-call(bf16[3072,384]{1,0:T(8,128)(2,1)S(1)} %copy-done.2, bf16[3072,384]{1,0:T(8,128)(2,1)} %collective-permute-done.other_ref, bf16[64,3072]{1,0:T(8,128)(2,1)S(1)} %collective-permute-done.2.refs_0_, bf16[64,3072]{1,0:T(8,128)(2,1)S(1)} %collective-permute-done.4.refs_1_, ...), custom_call_target="tpu_custom_call" | custom-call | flops 2415919104 | bytes 8388608 | tf_op jit(solution)/shard_map/pallas_call | solution.py:54
  73.0 4.1 %collective-permute-start.9 = (bf16[512,384]{1,0:T(8,128)(2,1)S(1)}, bf16[512,384]{1,0:T(8,128)(2,1)}, u32[]{:S(2)}, u32[]{:S(2)}) collective-permute-start(bf16[512,384]{1,0:T(8,128)(2,1)S(1)} %get-tuple-element.17), channel_id=1, source_target_pairs={{0,1},{1,0},{2,3},{3,2},{4,5},{5,4},{6,7},{7,6},{8,9},{9,8},{10,11... | collective-permute-start | bytes 1179656 | tf_op jit(solution)/shard_map/ppermute | solution.py:33
  77.2 1.3 copy.13
  78.5 1.3 convert_element_type.23.want_ref
  81.1 3.6 %shard_map.66.near_ref = bf16[2048,384]{1,0:T(8,128)(2,1)S(1)} custom-call(f32[8]{0:T(128)S(1)} %convert_element_type.24.block_ref, f32[2048,2]{1,0:T(8,128)S(1)} %convert_element_type.23.want_ref, bf16[512,384]{1,0:T(8,128)(2,1)S(1)} %copy-done.5, bf16[512,384]{1,0:T(8,128)(2,1)S(1)} %collective-permute-done.10.second_ref), custom_call_target="tpu_custom_call" | custom-call | flops 1610612736 | bytes 4194304 | tf_op jit(solution)/shard_map/pallas_call | solution.py:118
  84.8 5.3 %shard_map.67 = (bf16[2048,128]{1,0:T(8,128)(2,1)S(1)}, bf16[2048,256]{1,0:T(8,128)(2,1)}) custom-call(f32[8]{0:T(128)S(1)} %convert_element_type.22.block_ref, f32[2048,2]{1,0:T(8,128)S(1)} %convert_element_type.23.want_ref, bf16[512,384]{1,0:T(8,128)(2,1)S(1)} %copy-done.7, bf16[512,384]{1,0:T(8,128)(2,1)} %collective-permute-done.9.second_ref, ...), custom_call_target="tpu_custom_call" | custom-call | flops 1610612736 | bytes 4194304 | tf_op jit(solution)/shard_map/pallas_call | solution.py:118
  90.9 4.6 %collective-permute-start.11 = (bf16[2048,256]{1,0:T(8,128)(2,1)}, bf16[2048,256]{1,0:T(8,128)(2,1)S(1)}, u32[]{:S(2)}, u32[]{:S(2)}) collective-permute-start(bf16[2048,256]{1,0:T(8,128)(2,1)} %get-tuple-element.21.refs_0_), channel_id=1, source_target_pairs={{0,224},{32,0},{64,32},{96,64},{128,96},{160,128},{192,160},{224,1... | collective-permute-start | bytes 3145736 | tf_op jit(solution)/shard_map/ppermute | solution.py:300
  95.6 1.3 collective-permute-start.14
  99.6 38.3 %collective-permute-done.11.refs_3_ = bf16[2048,256]{1,0:T(8,128)(2,1)S(1)} collective-permute-done((bf16[2048,256]{1,0:T(8,128)(2,1)}, bf16[2048,256]{1,0:T(8,128)(2,1)S(1)}, u32[]{:S(2)}, u32[]{:S(2)}) %collective-permute-start.11) | collective-permute-done | bytes 1048608 | tf_op jit(solution)/shard_map/ppermute | solution.py:300
  137.8 1.7 collective-permute-done.12.refs_1_
  139.6 1.3 collective-permute-start.13
  142.3 10.7 %shard_map.68 = (f32[2048,128]{1,0:T(8,128)S(1)}, f32[2048,128]{1,0:T(8,128)S(1)}) custom-call(s32[16,30]{1,0:T(8,128)S(1)} %copy.16.index_ref, s32[16]{0:T(128)S(1)} %get-tuple-element.29.count_ref, bf16[2048,128]{1,0:T(8,128)(2,1)S(1)} %copy-done.9, bf16[2048,256]{1,0:T(8,128)(2,1)} %get-tuple-element.21.refs_0_, ...), custom_call_target="tpu_custom_call" | custom-call | flops 48318382080 | bytes 6291456 | tf_op jit(solution)/shard_map/pallas_call | solution.py:211
  153.0 3.0 %collective-permute-done.15.refs_1_ = bf16[1024,256]{1,0:T(8,128)(2,1)S(1)} collective-permute-done((bf16[1024,256]{1,0:T(8,128)(2,1)S(1)}, bf16[1024,256]{1,0:T(8,128)(2,1)S(1)}, u32[]{:S(2)}, u32[]{:S(2)}) %collective-permute-start.15) | collective-permute-done | bytes 524320 | tf_op jit(solution)/shard_map/ppermute | solution.py:305
  156.0 5.3 %shard_map.69 = bf16[2048,128]{1,0:T(8,128)(2,1)S(1)} custom-call(s32[16,16]{1,0:T(8,128)S(1)} %select_reduce_fusion.3.index_ref, s32[16]{0:T(128)S(1)} %get-tuple-element.36.count_ref, bf16[2048,128]{1,0:T(8,128)(2,1)S(1)} %copy-done.9, bf16[1024,256]{1,0:T(8,128)(2,1)S(1)} %collective-permute-done.13.refs_0_, ...), custom_call_target="tpu_custom_call" | custom-call | flops 25769803776 | bytes 6291456 | tf_op jit(solution)/shard_map/pallas_call | solution.py:211
  161.3 15.2 %all_to_all.10.att_ref = bf16[8,256,128]{2,1,0:T(8,128)(2,1)S(1)} all-to-all(bf16[8,256,128]{2,1,0:T(8,128)(2,1)S(1)} %bitcast.33), channel_id=1, replica_groups=mesh['z'=8,'yl'=2,'yh'=2,'x'=4,'core'=2] {'yh','x'}, dimensions={0} | all-to-all | bytes 1048576 | tf_op jit(solution)/shard_map/all_to_all | solution.py:318
  176.5 2.8 %copy-done.1 = bf16[1024,3072]{1,0:T(8,128)(2,1)S(1)} copy-done((bf16[1024,3072]{1,0:T(8,128)(2,1)S(1)}, bf16[1024,3072]{1,0:T(8,128)(2,1)}, u32[]{:S(2)}) %copy-start.1) | copy-done | bytes 6291480
  179.3 1.8 shard_map.70
  181.1 3.4 %collective-permute-start.16 = (bf16[128,3072]{1,0:T(8,128)(2,1)S(1)}, bf16[128,3072]{1,0:T(8,128)(2,1)S(1)}, u32[]{:S(2)}, u32[]{:S(2)}) collective-permute-start(bf16[128,3072]{1,0:T(8,128)(2,1)S(1)} %get-tuple-element.26), channel_id=1, source_target_pairs={{0,1},{1,0},{2,3},{3,2},{4,5},{5,4},{6,7},{7,6},{8,9},{9,8},{10,11... | collective-permute-start | bytes 2359304 | tf_op jit(solution)/shard_map/ppermute | solution.py:33
  184.5 1.9 collective-permute-done.16
  (78 shorter events, 16.1 us)
Async XLA Ops:
  6.5 7.1 %copy-start = (bf16[128,3072]{1,0:T(8,128)(2,1)S(1)}, bf16[128,3072]{1,0:T(8,128)(2,1)}, u32[]{:S(2)}) copy-start(bf16[128,3072]{1,0:T(8,128)(2,1)} %param.8) | copy-start | bytes 2359300
  6.5 7.7 %collective-permute-start = (bf16[3072,384]{1,0:T(8,128)(2,1)}, bf16[3072,384]{1,0:T(8,128)(2,1)}, u32[]{:S(2)}, u32[]{:S(2)}) collective-permute-start(bf16[3072,384]{1,0:T(8,128)(2,1)} %own_ref.3), channel_id=1, source_target_pairs={{0,1},{1,0},{2,3},{3,2},{4,5},{5,4},{6,7},{7,6},{8,9},{9,8},{10,11... | collective-permute-start | bytes 7077896 | tf_op jit(solution)/shard_map/ppermute | solution.py:33
  9.8 24.8 %collective-permute-start.1 = (bf16[128,3072]{1,0:T(8,128)(2,1)}, bf16[128,3072]{1,0:T(8,128)(2,1)S(1)}, u32[]{:S(2)}, u32[]{:S(2)}) collective-permute-start(bf16[128,3072]{1,0:T(8,128)(2,1)} %refs_0_.1), channel_id=1, source_target_pairs={{0,2},{2,4},{4,6},{6,0},{1,3},{3,5},{5,7},{7,1},{8,10},{10,12},{12... | collective-permute-start | bytes 2359304 | tf_op jit(solution)/shard_map/ppermute | solution.py:29
  9.8 25.0 %collective-permute-start.3 = (bf16[128,3072]{1,0:T(8,128)(2,1)}, bf16[128,3072]{1,0:T(8,128)(2,1)S(1)}, u32[]{:S(2)}, u32[]{:S(2)}) collective-permute-start(bf16[128,3072]{1,0:T(8,128)(2,1)} %refs_0_.1), channel_id=1, source_target_pairs={{0,6},{2,0},{4,2},{6,4},{1,7},{3,1},{5,3},{7,5},{8,14},{10,8},{12,... | collective-permute-start | bytes 2359304 | tf_op jit(solution)/shard_map/ppermute | solution.py:29
  12.5 26.4 %collective-permute-start.5 = (bf16[128,3072]{1,0:T(8,128)(2,1)}, bf16[128,3072]{1,0:T(8,128)(2,1)}, u32[]{:S(2)}, u32[]{:S(2)}) collective-permute-start(bf16[128,3072]{1,0:T(8,128)(2,1)} %refs_0_.1), channel_id=1, source_target_pairs={{0,8},{8,0},{1,9},{9,1},{2,10},{10,2},{3,11},{11,3},{4,12},{12,4},... | collective-permute-start | bytes 2359304 | tf_op jit(solution)/shard_map/ppermute | solution.py:33
  15.2 23.0 %copy-start.13 = (s32[1,2048]{1,0:T(1,128)S(1)}, s32[1,2048]{1,0:T(1,128)}, u32[]{:S(2)}) copy-start(s32[1,2048]{1,0:T(1,128)} %param.9) | copy-start | bytes 24580
  15.2 26.3 %all-to-all-start.1 = ((bf16[8,16,3072]{2,1,0:T(8,128)(2,1)}), bf16[8,16,3072]{2,1,0:T(8,128)(2,1)}, u32[]{:S(2)}, u32[]{:S(2)}) async-start(bf16[8,16,3072]{2,1,0:T(8,128)(2,1)} %broadcast_in_dim.52), calls=%async_computation.1 | async-start | bytes 1572864 | tf_op jit(solution)/shard_map/all_to_all | solution.py:284
  20.3 156.2 %all-gather.2.cloned.1.call-start = ((), (), s32[]{:S(2)}) async-start(), calls=%async_computation.2 | async-start | bytes 7077888 | tf_op jit(solution)/shard_map/all_gather | solution.py:285
  34.6 11.9 %collective-permute-start.2 = (bf16[64,3072]{1,0:T(8,128)(2,1)S(1)}, bf16[64,3072]{1,0:T(8,128)(2,1)S(1)}, u32[]{:S(2)}, u32[]{:S(2)}) collective-permute-start(bf16[64,3072]{1,0:T(8,128)(2,1)S(1)} %slice.20), channel_id=1, source_target_pairs={{0,2},{2,4},{4,6},{6,0},{1,3},{3,5},{5,7},{7,1},{8,10},{10,12},{12... | collective-permute-start | bytes 1179656 | tf_op jit(solution)/shard_map/ppermute | solution.py:29
  35.5 11.0 %collective-permute-start.4 = (bf16[64,3072]{1,0:T(8,128)(2,1)}, bf16[64,3072]{1,0:T(8,128)(2,1)S(1)}, u32[]{:S(2)}, u32[]{:S(2)}) collective-permute-start(bf16[64,3072]{1,0:T(8,128)(2,1)} %slice.21), channel_id=1, source_target_pairs={{0,6},{2,0},{4,2},{6,4},{1,7},{3,1},{5,3},{7,5},{8,14},{10,8},{12,... | collective-permute-start | bytes 1179656 | tf_op jit(solution)/shard_map/ppermute | solution.py:29
  38.8 24.6 %collective-permute-start.6 = (bf16[128,3072]{1,0:T(8,128)(2,1)}, bf16[128,3072]{1,0:T(8,128)(2,1)}, u32[]{:S(2)}, u32[]{:S(2)}) collective-permute-start(bf16[128,3072]{1,0:T(8,128)(2,1)} %collective-permute-done.5.refs_3_), channel_id=1, source_target_pairs={{0,2},{2,4},{4,6},{6,0},{1,3},{3,5},{5,7},{7,1},{8,10},{10,12},{12... | collective-permute-start | bytes 2359304 | tf_op jit(solution)/shard_map/ppermute | solution.py:29
  38.8 24.6 %collective-permute-start.7 = (bf16[128,3072]{1,0:T(8,128)(2,1)}, bf16[128,3072]{1,0:T(8,128)(2,1)}, u32[]{:S(2)}, u32[]{:S(2)}) collective-permute-start(bf16[128,3072]{1,0:T(8,128)(2,1)} %collective-permute-done.5.refs_3_), channel_id=1, source_target_pairs={{0,6},{2,0},{4,2},{6,4},{1,7},{3,1},{5,3},{7,5},{8,14},{10,8},{12,... | collective-permute-start | bytes 2359304 | tf_op jit(solution)/shard_map/ppermute | solution.py:29
  46.5 2.9 %copy-start.12 = (s32[2048,1]{0,1:T(1,128)S(1)}, s32[2048,1]{0,1:T(1,128)}, u32[]{:S(2)}) copy-start(s32[2048,1]{0,1:T(1,128)} %get-tuple-element.34) | copy-start | bytes 24580
  47.4 17.6 %collective-permute-start.8 = (bf16[128,3072]{1,0:T(8,128)(2,1)}, bf16[128,3072]{1,0:T(8,128)(2,1)}, u32[]{:S(2)}, u32[]{:S(2)}) collective-permute-start(bf16[128,3072]{1,0:T(8,128)(2,1)} %pad_maximum_fusion), channel_id=1, source_target_pairs={{0,8},{8,0},{1,9},{9,1},{2,10},{10,2},{3,11},{11,3},{4,12},{12,4},... | collective-permute-start | bytes 2359304 | tf_op jit(solution)/shard_map/ppermute | solution.py:33
  51.4 1.7 copy-start.2
  53.1 1.1 copy-start.3
  61.6 15.6 %copy-start.10 = (s32[2048,2]{0,1:T(2,128)S(1)}, s32[2048,2]{0,1:T(2,128)}, u32[]{:S(2)}) copy-start(s32[2048,2]{0,1:T(2,128)} %pad_add_fusion) | copy-start | bytes 49156
  61.6 18.5 %collective-permute-start.10 = (bf16[512,384]{1,0:T(8,128)(2,1)S(1)}, bf16[512,384]{1,0:T(8,128)(2,1)S(1)}, u32[]{:S(2)}, u32[]{:S(2)}) collective-permute-start(bf16[512,384]{1,0:T(8,128)(2,1)S(1)} %get-tuple-element.19), channel_id=1, source_target_pairs={{0,1},{1,0},{2,3},{3,2},{4,5},{5,4},{6,7},{7,6},{8,9},{9,8},{10,11... | collective-permute-start | bytes 1179656 | tf_op jit(solution)/shard_map/ppermute | solution.py:33
  73.0 11.8 %collective-permute-start.9 = (bf16[512,384]{1,0:T(8,128)(2,1)S(1)}, bf16[512,384]{1,0:T(8,128)(2,1)}, u32[]{:S(2)}, u32[]{:S(2)}) collective-permute-start(bf16[512,384]{1,0:T(8,128)(2,1)S(1)} %get-tuple-element.17), channel_id=1, source_target_pairs={{0,1},{1,0},{2,3},{3,2},{4,5},{5,4},{6,7},{7,6},{8,9},{9,8},{10,11... | collective-permute-start | bytes 1179656 | tf_op jit(solution)/shard_map/ppermute | solution.py:33
  77.2 2.8 %copy-start.14 = (pred[16,30]{1,0:T(8,128)(4,1)S(1)}, pred[16,30]{1,0:T(8,128)(4,1)}, u32[]{:S(2)}) copy-start(pred[16,30]{1,0:T(8,128)(4,1)} %get-tuple-element.31) | copy-start | bytes 1444
  77.2 2.8 %copy-start.15 = (s32[16]{0:T(128)S(1)}, s32[16]{0:T(128)}, u32[]{:S(2)}) copy-start(s32[16]{0:T(128)} %param.11) | copy-start | bytes 196
  80.1 1.0 copy-start.5
  81.1 3.6 %copy-start.7 = (bf16[512,384]{1,0:T(8,128)(2,1)S(1)}, bf16[512,384]{1,0:T(8,128)(2,1)}, u32[]{:S(2)}) copy-start(bf16[512,384]{1,0:T(8,128)(2,1)} %copy-done.6) | copy-start | bytes 1179652
  84.7 13.4 %copy-start.11 = (s32[16,30]{1,0:T(8,128)S(1)}, s32[16,30]{1,0:T(8,128)}, u32[]{:S(2)}) copy-start(s32[16,30]{1,0:T(8,128)} %get-tuple-element.38) | copy-start | bytes 5764
  90.9 46.9 %collective-permute-start.11 = (bf16[2048,256]{1,0:T(8,128)(2,1)}, bf16[2048,256]{1,0:T(8,128)(2,1)S(1)}, u32[]{:S(2)}, u32[]{:S(2)}) collective-permute-start(bf16[2048,256]{1,0:T(8,128)(2,1)} %get-tuple-element.21.refs_0_), channel_id=1, source_target_pairs={{0,224},{32,0},{64,32},{96,64},{128,96},{160,128},{192,160},{224,1... | collective-permute-start | bytes 3145736 | tf_op jit(solution)/shard_map/ppermute | solution.py:300
  95.5 44.0 %collective-permute-start.12 = (bf16[2048,256]{1,0:T(8,128)(2,1)}, bf16[2048,256]{1,0:T(8,128)(2,1)S(1)}, u32[]{:S(2)}, u32[]{:S(2)}) collective-permute-start(bf16[2048,256]{1,0:T(8,128)(2,1)} %get-tuple-element.21.refs_0_), channel_id=1, source_target_pairs={{0,32},{32,64},{64,96},{96,128},{128,160},{160,192},{192,224},{224... | collective-permute-start | bytes 3145736 | tf_op jit(solution)/shard_map/ppermute | solution.py:299
  95.6 45.3 %collective-permute-start.14 = (bf16[2048,256]{1,0:T(8,128)(2,1)}, bf16[2048,256]{1,0:T(8,128)(2,1)}, u32[]{:S(2)}, u32[]{:S(2)}) collective-permute-start(bf16[2048,256]{1,0:T(8,128)(2,1)} %get-tuple-element.21.refs_0_), channel_id=1, source_target_pairs={{0,16},{16,0},{1,17},{17,1},{2,18},{18,2},{3,19},{19,3},{4,20},{20... | collective-permute-start | bytes 3145736 | tf_op jit(solution)/shard_map/ppermute | solution.py:33
  99.0 43.2 %copy-start.9 = (bf16[2048,128]{1,0:T(8,128)(2,1)S(1)}, bf16[2048,128]{1,0:T(8,128)(2,1)}, u32[]{:S(2)}) copy-start(bf16[2048,128]{1,0:T(8,128)(2,1)} %copy-done.8) | copy-start | bytes 1572868
  139.6 13.4 %collective-permute-start.13 = (bf16[1024,256]{1,0:T(8,128)(2,1)S(1)}, bf16[1024,256]{1,0:T(8,128)(2,1)S(1)}, u32[]{:S(2)}, u32[]{:S(2)}) collective-permute-start(bf16[1024,256]{1,0:T(8,128)(2,1)S(1)} %slice_select_fusion), channel_id=1, source_target_pairs={{0,16},{16,0},{1,17},{17,1},{2,18},{18,2},{3,19},{19,3},{4,20},{20... | collective-permute-start | bytes 1572872 | tf_op jit(solution)/shard_map/ppermute | solution.py:33
  141.9 14.0 %collective-permute-start.15 = (bf16[1024,256]{1,0:T(8,128)(2,1)S(1)}, bf16[1024,256]{1,0:T(8,128)(2,1)S(1)}, u32[]{:S(2)}, u32[]{:S(2)}) collective-permute-start(bf16[1024,256]{1,0:T(8,128)(2,1)S(1)} %slice.24), channel_id=1, source_target_pairs={{0,32},{32,64},{64,96},{96,128},{128,160},{160,192},{192,224},{224... | collective-permute-start | bytes 1572872 | tf_op jit(solution)/shard_map/ppermute | solution.py:305
  176.5 2.8 %copy-start.1 = (bf16[1024,3072]{1,0:T(8,128)(2,1)S(1)}, bf16[1024,3072]{1,0:T(8,128)(2,1)}, u32[]{:S(2)}) copy-start(bf16[1024,3072]{1,0:T(8,128)(2,1)} %all-gather.2.cloned.1.call-done) | copy-start | bytes 18874372
  181.1 5.3 %collective-permute-start.16 = (bf16[128,3072]{1,0:T(8,128)(2,1)S(1)}, bf16[128,3072]{1,0:T(8,128)(2,1)S(1)}, u32[]{:S(2)}, u32[]{:S(2)}) collective-permute-start(bf16[128,3072]{1,0:T(8,128)(2,1)S(1)} %get-tuple-element.26), channel_id=1, source_target_pairs={{0,1},{1,0},{2,3},{3,2},{4,5},{5,4},{6,7},{7,6},{8,9},{9,8},{10,11... | collective-permute-start | bytes 2359304 | tf_op jit(solution)/shard_map/ppermute | solution.py:33
  (3 other events, 2.3 us)
Sparse Core Ops, SparseCore 0:
  41.7 95.4 all-gather.1

commit v4 on v3

--- a/solution.py
+++ b/solution.py
@@ -38,14 +38,22 @@
     mine_ref, theirs_ref, rows_ref, sems = refs[len(heights) :]
     copies, start = [], 0
     for i, height in enumerate(heights):
-        copies.append(pltpu.make_async_copy(pieces[i], rows_ref.at[pl.ds(start, height)], sems.at[i]))
+        copies.append((pltpu.make_async_copy(pieces[i], rows_ref.at[pl.ds(start, height)], sems.at[i]), start + height))
         start += height
-    for copy in copies:
+    for copy, _ in copies:
         copy.start()
-    for copy in copies:
-        copy.wait()
-    theirs_ref[...] = jnp.dot(rows_ref[...], other_ref[...], preferred_element_type=F32).astype(BF)
-    mine_ref[...] = jnp.dot(rows_ref[...], own_ref[...], preferred_element_type=F32).astype(BF)
+    part = start // 2
+    for low in range(0, start, part):
+        for copy, end in copies:
+            if low < end <= low + part:
+                copy.wait()
+        rows = rows_ref[low : low + part, :]
+        theirs_ref[low : low + part, TILE:] = jnp.dot(rows, other_ref[:, TILE:], preferred_element_type=F32).astype(BF)
+        both = jnp.concatenate([other_ref[:, :TILE], own_ref[:, :TILE]], axis=1)
+        both = jnp.dot(rows, both, preferred_element_type=F32).astype(BF)
+        theirs_ref[low : low + part, :TILE] = both[:, :TILE]
+        mine_ref[low : low + part, :TILE] = both[:, TILE:]
+        mine_ref[low : low + part, TILE:] = jnp.dot(rows, own_ref[:, TILE:], preferred_element_type=F32).astype(BF)
 
 
 def qkv(own, other, pieces):
@@ -57,17 +65,17 @@
         in_specs=[WHOLE_VM] * 2 + [WHOLE_ANY] * len(pieces),
         out_specs=(WHOLE_VM,) * 2,
         scratch_shapes=[VM((n, depth), BF), pltpu.SemaphoreType.DMA((len(pieces),))],
-        compiler_params=pltpu.CompilerParams(vmem_limit_bytes=40 << 20),
+        compiler_params=pltpu.CompilerParams(vmem_limit_bytes=24 << 20),
         cost_estimate=pl.CostEstimate(flops=4 * n * depth * width, bytes_accessed=8 << 20, transcendentals=0),
     )(own, other, *pieces)
 
 
 def hot_rows(want, block_ref):
     n = want.shape[0]
-    high = jnp.broadcast_to(want[:, 0:1], (n, TILE)).astype(BF)
-    low = jnp.broadcast_to(want[:, 1:2], (n, TILE))
-    lane = lax.broadcasted_iota(jnp.int32, (n, TILE), 1).astype(F32)
-    inside = jnp.where(low == lane, 1.0, 0.0).astype(BF)
+    want = jnp.broadcast_to(want, (n, TILE))
+    high = lax.shift_right_logical(want, 7).astype(F32).astype(BF)
+    low = want & (TILE - 1)
+    inside = jnp.where(low == lax.broadcasted_iota(jnp.int32, (n, TILE), 1), 1.0, 0.0).astype(BF)
     zero = jnp.zeros((n, TILE), BF)
     picks = [jnp.where(high == block_ref[b].astype(BF), inside, zero) for b in range(block_ref.shape[0])]
     return jnp.concatenate(picks, axis=1)
@@ -120,7 +128,7 @@
         out_shape=out,
         in_specs=[WHOLE_SM] + [WHOLE_VM] * len(operands),
         out_specs=WHOLE_VM if near is None else (WHOLE_VM,) * 2,
-        compiler_params=pltpu.CompilerParams(vmem_limit_bytes=40 << 20),
+        compiler_params=pltpu.CompilerParams(vmem_limit_bytes=24 << 20),
         cost_estimate=pl.CostEstimate(flops=n * n * width, bytes_accessed=4 << 20, transcendentals=0),
     )(blocks, *operands)
 
@@ -218,38 +226,39 @@
             VM((together, sizes[-1] // 2, TILE, 2 * TILE), F32),
             pltpu.SemaphoreType.DMA((len(frames),)),
         ],
-        compiler_params=pltpu.CompilerParams(vmem_limit_bytes=40 << 20),
+        compiler_params=pltpu.CompilerParams(vmem_limit_bytes=24 << 20),
         cost_estimate=pl.CostEstimate(
-            flops=12 * 4 * n * slots * TILE * TILE, bytes_accessed=6 << 20, transcendentals=n * slots * TILE
+            flops=4 * 4 * n * slots * TILE * TILE, bytes_accessed=6 << 20, transcendentals=n * slots * TILE
         ),
     )(index, count, q, *frames, *(old or ()))
 
 
-def project_kernel(att_ref, w_ref, core_ref, mine_ref, other_ref):
-    chips = w_ref.shape[1]
-    own = pl.multiple_of(core_ref[0] * TILE, TILE)
+def project_kernel(order_ref, att_ref, *refs):
+    weights, mine_ref, other_ref = refs[:-2], refs[-2], refs[-1]
+    chips = att_ref.shape[0]
+    own = pl.multiple_of(order_ref[chips] * TILE, TILE)
     away = pl.multiple_of(TILE - own, TILE)
-    mine = jnp.concatenate([att_ref[b, pl.ds(own, TILE), :] for b in range(chips)], axis=1)
-    other = jnp.concatenate([att_ref[b, pl.ds(away, TILE), :] for b in range(chips)], axis=1)
+    mine = jnp.concatenate([att_ref[order_ref[b], pl.ds(own, TILE), :] for b in range(chips)], axis=1)
+    other = jnp.concatenate([att_ref[order_ref[b], pl.ds(away, TILE), :] for b in range(chips)], axis=1)
     left = jnp.concatenate([mine, other], axis=0)
     step = 256
     for column in range(0, mine_ref.shape[1], step):
-        right = jnp.concatenate([w_ref[:, b, :, column : column + step].reshape(TILE, step) for b in range(chips)], axis=0)
+        right = jnp.concatenate([w[:, column : column + step] for w in weights], axis=0)
         done = jnp.dot(left, right, preferred_element_type=F32)
         mine_ref[:, column : column + step] = done[:TILE]
         other_ref[:, column : column + step] = done[TILE:].astype(BF)
 
 
-def project(attended, w, core):
-    width = w.shape[-1]
+def project(order, attended, weights):
+    width = weights[0].shape[1]
     return pl.pallas_call(
         project_kernel,
         out_shape=(jax.ShapeDtypeStruct((TILE, width), F32), jax.ShapeDtypeStruct((TILE, width), BF)),
-        in_specs=[WHOLE_VM] * 2 + [WHOLE_SM],
+        in_specs=[WHOLE_SM] + [WHOLE_VM] * (1 + len(weights)),
         out_specs=(WHOLE_VM,) * 2,
-        compiler_params=pltpu.CompilerParams(vmem_limit_bytes=40 << 20),
+        compiler_params=pltpu.CompilerParams(vmem_limit_bytes=24 << 20),
         cost_estimate=pl.CostEstimate(flops=4 * TILE * 8 * TILE * width, bytes_accessed=10 << 20, transcendentals=0),
-    )(attended, w, core.astype(jnp.int32).reshape(1))
+    )(order, attended, *weights)
 
 
 def listed(place, chosen, slots):
@@ -265,40 +274,43 @@
 def body(tokens, w_qkv, w_out, source_row, key_tiles, key_count):
     z, yl = lax.axis_index("z"), lax.axis_index("yl")
     yh, x, core = lax.axis_index("yh"), lax.axis_index("x"), lax.axis_index("core")
+    after = lax.optimization_barrier
+
+    def chips(part):
+        return [((yh + dy) % 2) * 4 + (x + 4 - dx) % 4 for dy, dx in part]
+
+    def blocks(part):
+        return jnp.stack([2 * c + side for side in (core, 1 - core) for c in chips(part)]).astype(F32)
 
     one, three = round_x(tokens, 1), round_x(tokens, -1)
     far_own = swap(tokens, "yh")
     w_other = swap(w_qkv, "core")
     half = tokens.shape[0] // 2
     low, high = round_x(one[:half], 1), round_x(three[half:], -1)
-    f_one, f_three = round_x(far_own, 1), round_x(far_own, -1)
+    far_next, _ = after((far_own, (one, three)))
+    f_one, f_three = round_x(far_next, 1), round_x(far_next, -1)
+    far_two = swap(jnp.concatenate([low, high], axis=0), "yh")
     near_mine, near_theirs = qkv(w_qkv, w_other, [tokens, one, three, far_own])
     near_other = swap(near_theirs, "core")
-    two = jnp.concatenate([low, high], axis=0)
-    far_two = swap(two, "yh")
-
-    share = w_out.shape[0] // 8
-    w_share = lax.dynamic_slice_in_dim(w_out, z * share, share, 0)
-    w_share, _ = lax.optimization_barrier((w_share, w_other))
-    w_share = jnp.broadcast_to(w_share[None], (8,) + w_share.shape)
-    w_chips = lax.all_to_all(w_share, CHIPS, split_axis=0, concat_axis=0, tiled=True)
-    w_all = lax.all_gather(w_chips.reshape(8 * share, -1), "z", axis=0, tiled=True)
-    w_all = w_all.reshape(8, 8, share, w_out.shape[1])
-
-    def blocks(part):
-        chips = [((yh + dy) % 2) * 4 + (x + 4 - dx) % 4 for dy, dx in part]
-        return jnp.stack([2 * c + side for side in (core, 1 - core) for c in chips]).astype(F32)
-
-    source = source_row[0]
-    want = jnp.stack([source // TILE, source % TILE], axis=1).astype(F32)
+    want = source_row[0][:, None]
     near = place(blocks(NEAR), want, near_mine, near_other)
+    far_two, near = after((far_two, near))
     far_mine, far_theirs = qkv(w_qkv, w_other, [low, high, f_one, f_three, far_two])
     far_other = swap(far_theirs, "core")
+
+    w_start, _ = after((w_out, near))
+    w_one, w_three = round_x(w_start, 1), round_x(w_start, -1)
+    w_turn, _ = after((w_out, far_two))
+    w_two, w_far = round_x(w_turn, 2), lax.ppermute(w_turn, ("yl", "yh"), [(i, 3 - i) for i in range(4)])
+
     q, kv = place(blocks(FAR), want, far_mine, far_other, near)
-
+    kv, _ = after((kv, (w_one, w_three)))
     behind = lax.ppermute(kv, "z", [(i, (i + 1) % 8) for i in range(8)])
     ahead = lax.ppermute(kv, "z", [(i, (i + 7) % 8) for i in range(8)])
     beside = swap(kv, "yl")
+
+    wf_one, wf_three, wf_two = (round_x(w_far, by) for by in (1, -1, 2))
+
     mid = kv.shape[0] // 2
     cross_low = swap(jnp.where(yl == 0, ahead[:mid], behind[:mid]), "yl")
     onward = [(2 * i, 2 * ((i + 1) % 8)) for i in range(8)] + [(2 * i + 1, 2 * ((i + 7) % 8) + 1) for i in range(8)]
@@ -316,7 +328,9 @@
     attended = attend(cross_index, cross_count, q, [cross_low, cross_high], (6, tiles), state, together=4)
 
     pieces = lax.all_to_all(attended.reshape(8, 2 * TILE, TILE), CHIPS, split_axis=0, concat_axis=0, tiled=True)
-    mine, other = project(pieces, w_all, core)
+    order = jnp.stack(chips(((0, 0), (0, 1), (0, 3), (0, 2), (1, 0), (1, 1), (1, 3), (1, 2))) + [core]).astype(jnp.int32)
+    weights = [w_out, w_one, w_three, w_two, w_far, wf_one, wf_three, wf_two]
+    mine, other = project(order, pieces, weights)
     return (mine + swap(other, "core").astype(F32)).astype(BF)
 
 

time: 195 us -> 159 us (0.82)
  blocking collectives: 15.2 us -> 0 us
  between operations: 13.7 us -> 0.26 us
  local copies, waits for them, and re-layouts: 13.6 us -> 8.53 us
  waiting for transfers between devices: 66.4 us -> 69.2 us
  other arithmetic: 8.6 us -> 5.84 us
  Pallas kernels: 40.5 us -> 38.5 us
    ppermute x1, waiting for transfers between devices: 38.3 us -> 2.5 us  [body(): ahead = lax.ppermute(kv, 'z', [(i, (i + 7) % 8) for i in range(8)])]
    all_to_all x1 -> x0, blocking collectives: 15.2 us -> none  [body(): lax.all_to_all(attended.reshape(8, 2 * TILE, TILE), CHIPS, split_axis=0,...]
    ppermute x0 -> x1, waiting for transfers between devices: none -> 13.7 us  [body(): lax.ppermute(w_turn, ('yl', 'yh'), [(i, 3 - i) for i in range(4)])]
    ppermute x6 -> x12, waiting for transfers between devices: 19.4 us -> 31.2 us  [round_x(): return lax.ppermute(array, 'x', [(i, (i + by) % 4) for i in range(4)])]
    all_to_all x1, waiting for transfers between devices: 0.01 us -> 10.2 us  [body(): lax.all_to_all(attended.reshape(8, 2 * TILE, TILE), CHIPS, split_axis=0,...]
    ppermute x8, starting transfers between devices: 18.1 us -> 12.8 us  [swap(): return lax.ppermute(array, axis, [(0, 1), (1, 0)])]
    pallas_call x2, Pallas kernels: 13.7 us -> 8.9 us  [qkv(): pl.pallas_call(functools.partial(qkv_kernel, heights), out_shape=(jax.Sha...]
    ppermute x6 -> x12, starting transfers between devices: 8.09 us -> 11.9 us  [round_x(): return lax.ppermute(array, 'x', [(i, (i + by) % 4) for i in range(4)])]
  transfers between devices with their start and end apart: 19 -> 25, of which waited for: 9 -> 12; matrix products, arithmetic and copies ran while one was open for 6% -> 4% of each run, Pallas kernels for 20% -> 22%
where the time goes in v4:
time: 159 us
  waiting for transfers between devices  69.2 us (44%)
  Pallas kernels  38.5 us (24%)
  starting transfers between devices  36.5 us (23%)
  local copies, waits for them, and re-layouts  8.53 us (5%)
  other arithmetic  5.84 us (4%)
    ppermute x12, waiting for transfers between devices, round_x(): return lax.ppermute(array, 'x', [(i, (i + by) % 4) for i in range(4)])  31.2 us
    pallas_call x2, Pallas kernels, attend(): pl.pallas_call(functools.partial(attend_kernel, sizes, together, len(fram...  17.2 us
    ppermute x1, waiting for transfers between devices, body(): lax.ppermute(w_turn, ('yl', 'yh'), [(i, 3 - i) for i in range(4)])  13.7 us
    ppermute x8, starting transfers between devices, swap(): return lax.ppermute(array, axis, [(0, 1), (1, 0)])  12.8 us
    ppermute x12, starting transfers between devices, round_x(): return lax.ppermute(array, 'x', [(i, (i + by) % 4) for i in range(4)])  11.9 us
    all_to_all x1, waiting for transfers between devices, body(): lax.all_to_all(attended.reshape(8, 2 * TILE, TILE), CHIPS, split_axis=0,...  10.2 us
    pallas_call x2, Pallas kernels, qkv(): pl.pallas_call(functools.partial(qkv_kernel, heights), out_shape=(jax.Sha...  8.9 us
    pallas_call x2, Pallas kernels, place(): pl.pallas_call(kernel, out_shape=out, in_specs=[WHOLE_SM] + [WHOLE_VM] *...  8.47 us
  transfers between devices with their start and end apart: 25, of which 12 were waited for; matrix products, arithmetic and copies ran while one was open for 4% of the time, Pallas kernels for 22%

profile of v4, /device:TPU:1, one launch (start us, length us, event | category | flops | bytes accessed | tf_op | source)
XLA Modules:
  0.0 158.7 jit_solution(14433584320268930703)
XLA Ops:
  0.0 3.2 %collective-permute-start = (bf16[3072,384]{1,0:T(8,128)(2,1)}, bf16[3072,384]{1,0:T(8,128)(2,1)S(1)}, u32[]{:S(2)}, u32[]{:S(2)}) collective-permute-start(bf16[3072,384]{1,0:T(8,128)(2,1)} %own_ref.3), channel_id=1, source_target_pairs={{0,1},{1,0},{2,3},{3,2},{4,5},{5,4},{6,7},{7,6},{8,9},{9,8},{10,11... | collective-permute-start | bytes 7077896 | tf_op jit(solution)/shard_map/ppermute | solution.py:33
  3.2 2.7 %collective-permute-start.3 = (bf16[128,3072]{1,0:T(8,128)(2,1)}, bf16[128,3072]{1,0:T(8,128)(2,1)S(1)}, u32[]{:S(2)}, u32[]{:S(2)}) collective-permute-start(bf16[128,3072]{1,0:T(8,128)(2,1)} %refs_0_.2), channel_id=1, source_target_pairs={{0,6},{2,0},{4,2},{6,4},{1,7},{3,1},{5,3},{7,5},{8,14},{10,8},{12,... | collective-permute-start | bytes 2359304 | tf_op jit(solution)/shard_map/ppermute | solution.py:29
  5.9 1.2 collective-permute-start.5
  7.1 16.8 %collective-permute-done.1.refs_1_ = bf16[128,3072]{1,0:T(8,128)(2,1)S(1)} collective-permute-done((bf16[128,3072]{1,0:T(8,128)(2,1)}, bf16[128,3072]{1,0:T(8,128)(2,1)S(1)}, u32[]{:S(2)}, u32[]{:S(2)}) %collective-permute-start.1) | collective-permute-done | bytes 786464 | tf_op jit(solution)/shard_map/ppermute | solution.py:29
  24.1 2.7 %collective-permute-start.4 = (bf16[64,3072]{1,0:T(8,128)(2,1)S(1)}, bf16[64,3072]{1,0:T(8,128)(2,1)S(1)}, u32[]{:S(2)}, u32[]{:S(2)}) collective-permute-start(bf16[64,3072]{1,0:T(8,128)(2,1)S(1)} %slice.21), channel_id=1, source_target_pairs={{0,6},{2,0},{4,2},{6,4},{1,7},{3,1},{5,3},{7,5},{8,14},{10,8},{12,... | collective-permute-start | bytes 1179656 | tf_op jit(solution)/shard_map/ppermute | solution.py:29
  26.8 8.4 %collective-permute-done.2.refs_0_ = bf16[64,3072]{1,0:T(8,128)(2,1)S(1)} collective-permute-done((bf16[64,3072]{1,0:T(8,128)(2,1)S(1)}, bf16[64,3072]{1,0:T(8,128)(2,1)S(1)}, u32[]{:S(2)}, u32[]{:S(2)}) %collective-permute-start.2) | collective-permute-done | bytes 393248 | tf_op jit(solution)/shard_map/ppermute | solution.py:29
  37.8 2.7 %collective-permute-start.7 = (bf16[128,3072]{1,0:T(8,128)(2,1)}, bf16[128,3072]{1,0:T(8,128)(2,1)}, u32[]{:S(2)}, u32[]{:S(2)}) collective-permute-start(bf16[128,3072]{1,0:T(8,128)(2,1)} %collective-permute-done.5.refs_3_), channel_id=1, source_target_pairs={{0,6},{2,0},{4,2},{6,4},{1,7},{3,1},{5,3},{7,5},{8,14},{10,8},{12,... | collective-permute-start | bytes 2359304 | tf_op jit(solution)/shard_map/ppermute | solution.py:29
  40.5 1.1 copy-done.9
  41.6 3.8 %shard_map.64 = (bf16[512,384]{1,0:T(8,128)(2,1)S(1)}, bf16[512,384]{1,0:T(8,128)(2,1)S(1)}) custom-call(bf16[3072,384]{1,0:T(8,128)(2,1)S(1)} %copy-done.5, bf16[3072,384]{1,0:T(8,128)(2,1)S(1)} %collective-permute-done.other_ref, bf16[128,3072]{1,0:T(8,128)(2,1)S(1)} %copy-done.9, bf16[128,3072]{1,0:T(8,128)(2,1)S(1)} %collective-permute-done.1.refs_1_, ...), custom_call_target="tpu_custom_call" | custom-call | flops 2415919104 | bytes 8388608 | tf_op jit(solution)/shard_map/pallas_call | solution.py:62
  45.4 2.7 %collective-permute-start.9 = (bf16[512,384]{1,0:T(8,128)(2,1)S(1)}, bf16[512,384]{1,0:T(8,128)(2,1)S(1)}, u32[]{:S(2)}, u32[]{:S(2)}) collective-permute-start(bf16[512,384]{1,0:T(8,128)(2,1)S(1)} %get-tuple-element.23), channel_id=1, source_target_pairs={{0,1},{1,0},{2,3},{3,2},{4,5},{5,4},{6,7},{7,6},{8,9},{9,8},{10,11... | collective-permute-start | bytes 1179656 | tf_op jit(solution)/shard_map/ppermute | solution.py:33
  49.5 3.6 %shard_map.65.near_ref = bf16[2048,384]{1,0:T(8,128)(2,1)S(1)} custom-call(f32[8]{0:T(128)S(1)} %convert_element_type.20.block_ref, s32[2048,1]{1,0:T(8,128)S(1)} %copy.11.want_ref, bf16[512,384]{1,0:T(8,128)(2,1)S(1)} %get-tuple-element.22.first_ref, bf16[512,384]{1,0:T(8,128)(2,1)S(1)} %collective-permute-done.9.second_ref), custom_call_target="tpu_custom_call" | custom-call | flops 1610612736 | bytes 4194304 | tf_op jit(solution)/shard_map/pallas_call | solution.py:126
  53.1 3.2 %collective-permute-done.8.refs_4_ = bf16[128,3072]{1,0:T(8,128)(2,1)S(1)} collective-permute-done((bf16[128,3072]{1,0:T(8,128)(2,1)}, bf16[128,3072]{1,0:T(8,128)(2,1)S(1)}, u32[]{:S(2)}, u32[]{:S(2)}) %collective-permute-start.8) | collective-permute-done | bytes 786464 | tf_op jit(solution)/shard_map/ppermute | solution.py:33
  57.1 2.7 %collective-permute-start.12 = (bf16[128,3072]{1,0:T(8,128)(2,1)S(1)}, bf16[128,3072]{1,0:T(8,128)(2,1)S(1)}, u32[]{:S(2)}, u32[]{:S(2)}) collective-permute-start(bf16[128,3072]{1,0:T(8,128)(2,1)S(1)} %copy-done), channel_id=1, source_target_pairs={{0,6},{2,0},{4,2},{6,4},{1,7},{3,1},{5,3},{7,5},{8,14},{10,8},{12,... | collective-permute-start | bytes 2359304 | tf_op jit(solution)/shard_map/ppermute | solution.py:29
  59.8 1.7 %copy-done.8 = bf16[3072,384]{1,0:T(8,128)(2,1)S(1)} copy-done((bf16[3072,384]{1,0:T(8,128)(2,1)S(1)}, bf16[3072,384]{1,0:T(8,128)(2,1)}, u32[]{:S(2)}) %copy-start.8) | copy-done | bytes 2359320
  62.6 5.1 %shard_map.66 = (bf16[512,384]{1,0:T(8,128)(2,1)S(1)}, bf16[512,384]{1,0:T(8,128)(2,1)S(1)}) custom-call(bf16[3072,384]{1,0:T(8,128)(2,1)S(1)} %copy-done.6, bf16[3072,384]{1,0:T(8,128)(2,1)S(1)} %copy-done.8, bf16[64,3072]{1,0:T(8,128)(2,1)S(1)} %copy-done.2, bf16[64,3072]{1,0:T(8,128)(2,1)S(1)} %copy-done.4, ...), custom_call_target="tpu_custom_call" | custom-call | flops 2415919104 | bytes 8388608 | tf_op jit(solution)/shard_map/pallas_call | solution.py:62
  67.7 3.1 %collective-permute-start.10 = (bf16[512,384]{1,0:T(8,128)(2,1)S(1)}, bf16[512,384]{1,0:T(8,128)(2,1)S(1)}, u32[]{:S(2)}, u32[]{:S(2)}) collective-permute-start(bf16[512,384]{1,0:T(8,128)(2,1)S(1)} %get-tuple-element.26), channel_id=1, source_target_pairs={{0,1},{1,0},{2,3},{3,2},{4,5},{5,4},{6,7},{7,6},{8,9},{9,8},{10,11... | collective-permute-start | bytes 1179656 | tf_op jit(solution)/shard_map/ppermute | solution.py:33
  71.1 1.2 collective-permute-done.10.second_ref
  72.2 4.9 %shard_map.67 = (bf16[2048,128]{1,0:T(8,128)(2,1)S(1)}, bf16[2048,256]{1,0:T(8,128)(2,1)}) custom-call(f32[8]{0:T(128)S(1)} %convert_element_type.19.block_ref, s32[2048,1]{1,0:T(8,128)S(1)} %copy.11.want_ref, bf16[512,384]{1,0:T(8,128)(2,1)S(1)} %get-tuple-element.25.first_ref, bf16[512,384]{1,0:T(8,128)(2,1)S(1)} %collective-permute-done.10.second_ref, ...), custom_call_target="tpu_custom_call" | custom-call | flops 1610612736 | bytes 4194304 | tf_op jit(solution)/shard_map/pallas_call | solution.py:126
  77.9 3.7 %collective-permute-start.13 = (bf16[2048,256]{1,0:T(8,128)(2,1)}, bf16[2048,256]{1,0:T(8,128)(2,1)S(1)}, u32[]{:S(2)}, u32[]{:S(2)}) collective-permute-start(bf16[2048,256]{1,0:T(8,128)(2,1)} %get-tuple-element.31.refs_0_), channel_id=1, source_target_pairs={{0,224},{32,0},{64,32},{96,64},{128,96},{160,128},{192,160},{224,1... | collective-permute-start | bytes 3145736 | tf_op jit(solution)/shard_map/ppermute | solution.py:309
  81.7 2.8 %collective-permute-start.19 = (bf16[128,3072]{1,0:T(8,128)(2,1)S(1)}, bf16[128,3072]{1,0:T(8,128)(2,1)}, u32[]{:S(2)}, u32[]{:S(2)}) collective-permute-start(bf16[128,3072]{1,0:T(8,128)(2,1)S(1)} %copy-done), channel_id=1, source_target_pairs={{0,24},{8,16},{16,8},{24,0},{1,25},{9,17},{17,9},{25,1},{2,26},{10... | collective-permute-start | bytes 2359304 | tf_op jit(solution)/shard_map/ppermute | solution.py:304
  87.8 13.7 %collective-permute-done.19.refs_4_ = bf16[128,3072]{1,0:T(8,128)(2,1)} collective-permute-done((bf16[128,3072]{1,0:T(8,128)(2,1)S(1)}, bf16[128,3072]{1,0:T(8,128)(2,1)}, u32[]{:S(2)}, u32[]{:S(2)}) %collective-permute-start.19) | collective-permute-done | bytes 786464 | tf_op jit(solution)/shard_map/ppermute | solution.py:304
  101.6 2.5 %collective-permute-done.13.refs_3_ = bf16[2048,256]{1,0:T(8,128)(2,1)S(1)} collective-permute-done((bf16[2048,256]{1,0:T(8,128)(2,1)}, bf16[2048,256]{1,0:T(8,128)(2,1)S(1)}, u32[]{:S(2)}, u32[]{:S(2)}) %collective-permute-start.13) | collective-permute-done | bytes 1048608 | tf_op jit(solution)/shard_map/ppermute | solution.py:309
  104.2 2.9 %collective-permute-done.14.refs_1_ = bf16[2048,256]{1,0:T(8,128)(2,1)} collective-permute-done((bf16[2048,256]{1,0:T(8,128)(2,1)}, bf16[2048,256]{1,0:T(8,128)(2,1)}, u32[]{:S(2)}, u32[]{:S(2)}) %collective-permute-start.14) | collective-permute-done | bytes 1048608 | tf_op jit(solution)/shard_map/ppermute | solution.py:308
  108.2 1.2 collective-permute-start.15
  110.8 11.1 %shard_map.68 = (f32[2048,128]{1,0:T(8,128)S(1)}, f32[2048,128]{1,0:T(8,128)S(1)}) custom-call(s32[16,30]{1,0:T(8,128)S(1)} %copy.14.index_ref, s32[16]{0:T(128)S(1)} %get-tuple-element.39.count_ref, bf16[2048,128]{1,0:T(8,128)(2,1)S(1)} %copy-done.13, bf16[2048,256]{1,0:T(8,128)(2,1)} %get-tuple-element.31.refs_0_, ...), custom_call_target="tpu_custom_call" | custom-call | flops 16106127360 | bytes 6291456 | tf_op jit(solution)/shard_map/pallas_call | solution.py:219
  122.0 1.7 %collective-permute-done.17.refs_1_ = bf16[1024,256]{1,0:T(8,128)(2,1)S(1)} collective-permute-done((bf16[1024,256]{1,0:T(8,128)(2,1)S(1)}, bf16[1024,256]{1,0:T(8,128)(2,1)S(1)}, u32[]{:S(2)}, u32[]{:S(2)}) %collective-permute-start.17) | collective-permute-done | bytes 524320 | tf_op jit(solution)/shard_map/ppermute | solution.py:317
  123.7 6.2 %shard_map.69 = bf16[2048,128]{1,0:T(8,128)(2,1)} custom-call(s32[16,16]{1,0:T(8,128)S(1)} %select_reduce_fusion.3.index_ref, s32[16]{0:T(128)S(1)} %get-tuple-element.44.count_ref, bf16[2048,128]{1,0:T(8,128)(2,1)S(1)} %copy-done.13, bf16[1024,256]{1,0:T(8,128)(2,1)S(1)} %collective-permute-done.15.refs_0_, ...), custom_call_target="tpu_custom_call" | custom-call | flops 8589934592 | bytes 6291456 | tf_op jit(solution)/shard_map/pallas_call | solution.py:219
  129.9 5.1 %all-to-all-start = ((bf16[8,256,128]{2,1,0:T(8,128)(2,1)}), bf16[8,256,128]{2,1,0:T(8,128)(2,1)S(1)}, u32[]{:S(2)}, u32[]{:S(2)}) async-start(bf16[8,256,128]{2,1,0:T(8,128)(2,1)} %bitcast.26), calls=%async_computation | async-start | bytes 1048576 | tf_op jit(solution)/shard_map/all_to_all | solution.py:330
  135.1 6.0 %collective-permute-done.22.refs_7_ = bf16[128,3072]{1,0:T(8,128)(2,1)} collective-permute-done((bf16[128,3072]{1,0:T(8,128)(2,1)}, bf16[128,3072]{1,0:T(8,128)(2,1)}, u32[]{:S(2)}, u32[]{:S(2)}) %collective-permute-start.22) | collective-permute-done | bytes 786464 | tf_op jit(solution)/shard_map/ppermute | solution.py:29
  141.1 10.2 %all-to-all-done.att_ref = bf16[8,256,128]{2,1,0:T(8,128)(2,1)S(1)} async-done(((bf16[8,256,128]{2,1,0:T(8,128)(2,1)}), bf16[8,256,128]{2,1,0:T(8,128)(2,1)S(1)}, u32[]{:S(2)}, u32[]{:S(2)}) %all-to-all-start) | async-done | bytes 524320 | tf_op jit(solution)/shard_map/all_to_all | solution.py:330
  151.3 3.9 %shard_map.70 = (f32[128,3072]{1,0:T(8,128)S(1)}, bf16[128,3072]{1,0:T(8,128)(2,1)S(1)}) custom-call(s32[9]{0:T(128)S(1)} %stack.93.order_ref, bf16[8,256,128]{2,1,0:T(8,128)(2,1)S(1)} %all-to-all-done.att_ref, bf16[128,3072]{1,0:T(8,128)(2,1)S(1)} %copy-done, bf16[128,3072]{1,0:T(8,128)(2,1)S(1)} %collective-permute-done.11.refs_1_, ...), custom_call_target="tpu_custom_call" | custom-call | flops 1610612736 | bytes 10485760 | tf_op jit(solution)/shard_map/pallas_call | solution.py:254
  155.8 1.9 %collective-permute-done.23 = bf16[128,3072]{1,0:T(8,128)(2,1)S(1)} collective-permute-done((bf16[128,3072]{1,0:T(8,128)(2,1)S(1)}, bf16[128,3072]{1,0:T(8,128)(2,1)S(1)}, u32[]{:S(2)}, u32[]{:S(2)}) %collective-permute-start.23) | collective-permute-done | bytes 786464 | tf_op jit(solution)/shard_map/ppermute | solution.py:33
  (85 shorter events, 15.0 us)
Async XLA Ops:
  0.0 40.5 %copy-start.5 = (bf16[3072,384]{1,0:T(8,128)(2,1)S(1)}, bf16[3072,384]{1,0:T(8,128)(2,1)}, u32[]{:S(2)}) copy-start(bf16[3072,384]{1,0:T(8,128)(2,1)} %own_ref.3) | copy-start | bytes 7077892
  0.0 40.5 %collective-permute-start = (bf16[3072,384]{1,0:T(8,128)(2,1)}, bf16[3072,384]{1,0:T(8,128)(2,1)S(1)}, u32[]{:S(2)}, u32[]{:S(2)}) collective-permute-start(bf16[3072,384]{1,0:T(8,128)(2,1)} %own_ref.3), channel_id=1, source_target_pairs={{0,1},{1,0},{2,3},{3,2},{4,5},{5,4},{6,7},{7,6},{8,9},{9,8},{10,11... | collective-permute-start | bytes 7077896 | tf_op jit(solution)/shard_map/ppermute | solution.py:33
  3.2 20.7 %collective-permute-start.1 = (bf16[128,3072]{1,0:T(8,128)(2,1)}, bf16[128,3072]{1,0:T(8,128)(2,1)S(1)}, u32[]{:S(2)}, u32[]{:S(2)}) collective-permute-start(bf16[128,3072]{1,0:T(8,128)(2,1)} %refs_0_.2), channel_id=1, source_target_pairs={{0,2},{2,4},{4,6},{6,0},{1,3},{3,5},{5,7},{7,1},{8,10},{10,12},{12... | collective-permute-start | bytes 2359304 | tf_op jit(solution)/shard_map/ppermute | solution.py:29
  3.2 20.8 %collective-permute-start.3 = (bf16[128,3072]{1,0:T(8,128)(2,1)}, bf16[128,3072]{1,0:T(8,128)(2,1)S(1)}, u32[]{:S(2)}, u32[]{:S(2)}) collective-permute-start(bf16[128,3072]{1,0:T(8,128)(2,1)} %refs_0_.2), channel_id=1, source_target_pairs={{0,6},{2,0},{4,2},{6,4},{1,7},{3,1},{5,3},{7,5},{8,14},{10,8},{12,... | collective-permute-start | bytes 2359304 | tf_op jit(solution)/shard_map/ppermute | solution.py:29
  5.9 31.9 %collective-permute-start.5 = (bf16[128,3072]{1,0:T(8,128)(2,1)}, bf16[128,3072]{1,0:T(8,128)(2,1)}, u32[]{:S(2)}, u32[]{:S(2)}) collective-permute-start(bf16[128,3072]{1,0:T(8,128)(2,1)} %refs_0_.2), channel_id=1, source_target_pairs={{0,8},{8,0},{1,9},{9,1},{2,10},{10,2},{3,11},{11,3},{4,12},{12,4},... | collective-permute-start | bytes 2359304 | tf_op jit(solution)/shard_map/ppermute | solution.py:33
  24.0 11.3 %collective-permute-start.2 = (bf16[64,3072]{1,0:T(8,128)(2,1)S(1)}, bf16[64,3072]{1,0:T(8,128)(2,1)S(1)}, u32[]{:S(2)}, u32[]{:S(2)}) collective-permute-start(bf16[64,3072]{1,0:T(8,128)(2,1)S(1)} %slice.20), channel_id=1, source_target_pairs={{0,2},{2,4},{4,6},{6,0},{1,3},{3,5},{5,7},{7,1},{8,10},{10,12},{12... | collective-permute-start | bytes 1179656 | tf_op jit(solution)/shard_map/ppermute | solution.py:29
  24.1 11.1 %collective-permute-start.4 = (bf16[64,3072]{1,0:T(8,128)(2,1)S(1)}, bf16[64,3072]{1,0:T(8,128)(2,1)S(1)}, u32[]{:S(2)}, u32[]{:S(2)}) collective-permute-start(bf16[64,3072]{1,0:T(8,128)(2,1)S(1)} %slice.21), channel_id=1, source_target_pairs={{0,6},{2,0},{4,2},{6,4},{1,7},{3,1},{5,3},{7,5},{8,14},{10,8},{12,... | collective-permute-start | bytes 1179656 | tf_op jit(solution)/shard_map/ppermute | solution.py:29
  35.2 13.0 %copy-start.14 = (s32[1,2048]{1,0:T(1,128)S(1)}, s32[1,2048]{1,0:T(1,128)}, u32[]{:S(2)}) copy-start(s32[1,2048]{1,0:T(1,128)} %param.9) | copy-start | bytes 24580
  35.2 13.4 %copy-start.15 = (s32[16,30]{1,0:T(8,128)S(1)}, s32[16,30]{1,0:T(8,128)}, u32[]{:S(2)}) copy-start(s32[16,30]{1,0:T(8,128)} %param.10) | copy-start | bytes 5764
  35.3 13.4 %copy-start.16 = (s32[16]{0:T(128)S(1)}, s32[16]{0:T(128)}, u32[]{:S(2)}) copy-start(s32[16]{0:T(128)} %param.11) | copy-start | bytes 196
  37.0 19.2 %collective-permute-start.8 = (bf16[128,3072]{1,0:T(8,128)(2,1)}, bf16[128,3072]{1,0:T(8,128)(2,1)S(1)}, u32[]{:S(2)}, u32[]{:S(2)}) collective-permute-start(bf16[128,3072]{1,0:T(8,128)(2,1)} %pad_maximum_fusion), channel_id=1, source_target_pairs={{0,8},{8,0},{1,9},{9,1},{2,10},{10,2},{3,11},{11,3},{4,12},{12,4},... | collective-permute-start | bytes 2359304 | tf_op jit(solution)/shard_map/ppermute | solution.py:33
  37.8 22.0 %collective-permute-start.6 = (bf16[128,3072]{1,0:T(8,128)(2,1)}, bf16[128,3072]{1,0:T(8,128)(2,1)}, u32[]{:S(2)}, u32[]{:S(2)}) collective-permute-start(bf16[128,3072]{1,0:T(8,128)(2,1)} %collective-permute-done.5.refs_3_), channel_id=1, source_target_pairs={{0,2},{2,4},{4,6},{6,0},{1,3},{3,5},{5,7},{7,1},{8,10},{10,12},{12... | collective-permute-start | bytes 2359304 | tf_op jit(solution)/shard_map/ppermute | solution.py:29
  37.8 22.0 %collective-permute-start.7 = (bf16[128,3072]{1,0:T(8,128)(2,1)}, bf16[128,3072]{1,0:T(8,128)(2,1)}, u32[]{:S(2)}, u32[]{:S(2)}) collective-permute-start(bf16[128,3072]{1,0:T(8,128)(2,1)} %collective-permute-done.5.refs_3_), channel_id=1, source_target_pairs={{0,6},{2,0},{4,2},{6,4},{1,7},{3,1},{5,3},{7,5},{8,14},{10,8},{12,... | collective-permute-start | bytes 2359304 | tf_op jit(solution)/shard_map/ppermute | solution.py:29
  45.4 4.0 %collective-permute-start.9 = (bf16[512,384]{1,0:T(8,128)(2,1)S(1)}, bf16[512,384]{1,0:T(8,128)(2,1)S(1)}, u32[]{:S(2)}, u32[]{:S(2)}) collective-permute-start(bf16[512,384]{1,0:T(8,128)(2,1)S(1)} %get-tuple-element.23), channel_id=1, source_target_pairs={{0,1},{1,0},{2,3},{3,2},{4,5},{5,4},{6,7},{7,6},{8,9},{9,8},{10,11... | collective-permute-start | bytes 1179656 | tf_op jit(solution)/shard_map/ppermute | solution.py:33
  49.5 10.3 %copy-start.4 = (bf16[64,3072]{1,0:T(8,128)(2,1)S(1)}, bf16[64,3072]{1,0:T(8,128)(2,1)}, u32[]{:S(2)}) copy-start(bf16[64,3072]{1,0:T(8,128)(2,1)} %copy-done.3) | copy-start | bytes 1179652
  49.5 10.3 %copy-start.6 = (bf16[3072,384]{1,0:T(8,128)(2,1)S(1)}, bf16[3072,384]{1,0:T(8,128)(2,1)}, u32[]{:S(2)}) copy-start(bf16[3072,384]{1,0:T(8,128)(2,1)} %own_ref.3) | copy-start | bytes 7077892
  57.1 20.8 %collective-permute-start.11 = (bf16[128,3072]{1,0:T(8,128)(2,1)S(1)}, bf16[128,3072]{1,0:T(8,128)(2,1)S(1)}, u32[]{:S(2)}, u32[]{:S(2)}) collective-permute-start(bf16[128,3072]{1,0:T(8,128)(2,1)S(1)} %copy-done), channel_id=1, source_target_pairs={{0,2},{2,4},{4,6},{6,0},{1,3},{3,5},{5,7},{7,1},{8,10},{10,12},{12... | collective-permute-start | bytes 2359304 | tf_op jit(solution)/shard_map/ppermute | solution.py:29
  57.1 20.8 %collective-permute-start.12 = (bf16[128,3072]{1,0:T(8,128)(2,1)S(1)}, bf16[128,3072]{1,0:T(8,128)(2,1)S(1)}, u32[]{:S(2)}, u32[]{:S(2)}) collective-permute-start(bf16[128,3072]{1,0:T(8,128)(2,1)S(1)} %copy-done), channel_id=1, source_target_pairs={{0,6},{2,0},{4,2},{6,4},{1,7},{3,1},{5,3},{7,5},{8,14},{10,8},{12,... | collective-permute-start | bytes 2359304 | tf_op jit(solution)/shard_map/ppermute | solution.py:29
  67.7 4.5 %collective-permute-start.10 = (bf16[512,384]{1,0:T(8,128)(2,1)S(1)}, bf16[512,384]{1,0:T(8,128)(2,1)S(1)}, u32[]{:S(2)}, u32[]{:S(2)}) collective-permute-start(bf16[512,384]{1,0:T(8,128)(2,1)S(1)} %get-tuple-element.26), channel_id=1, source_target_pairs={{0,1},{1,0},{2,3},{3,2},{4,5},{5,4},{6,7},{7,6},{8,9},{9,8},{10,11... | collective-permute-start | bytes 1179656 | tf_op jit(solution)/shard_map/ppermute | solution.py:33
  77.9 26.1 %collective-permute-start.13 = (bf16[2048,256]{1,0:T(8,128)(2,1)}, bf16[2048,256]{1,0:T(8,128)(2,1)S(1)}, u32[]{:S(2)}, u32[]{:S(2)}) collective-permute-start(bf16[2048,256]{1,0:T(8,128)(2,1)} %get-tuple-element.31.refs_0_), channel_id=1, source_target_pairs={{0,224},{32,0},{64,32},{96,64},{128,96},{160,128},{192,160},{224,1... | collective-permute-start | bytes 3145736 | tf_op jit(solution)/shard_map/ppermute | solution.py:309
  81.6 25.6 %collective-permute-start.14 = (bf16[2048,256]{1,0:T(8,128)(2,1)}, bf16[2048,256]{1,0:T(8,128)(2,1)}, u32[]{:S(2)}, u32[]{:S(2)}) collective-permute-start(bf16[2048,256]{1,0:T(8,128)(2,1)} %get-tuple-element.31.refs_0_), channel_id=1, source_target_pairs={{0,32},{32,64},{64,96},{96,128},{128,160},{160,192},{192,224},{224... | collective-permute-start | bytes 3145736 | tf_op jit(solution)/shard_map/ppermute | solution.py:308
  81.7 19.9 %collective-permute-start.19 = (bf16[128,3072]{1,0:T(8,128)(2,1)S(1)}, bf16[128,3072]{1,0:T(8,128)(2,1)}, u32[]{:S(2)}, u32[]{:S(2)}) collective-permute-start(bf16[128,3072]{1,0:T(8,128)(2,1)S(1)} %copy-done), channel_id=1, source_target_pairs={{0,24},{8,16},{16,8},{24,0},{1,25},{9,17},{17,9},{25,1},{2,26},{10... | collective-permute-start | bytes 2359304 | tf_op jit(solution)/shard_map/ppermute | solution.py:304
  84.4 25.0 %collective-permute-start.16 = (bf16[2048,256]{1,0:T(8,128)(2,1)}, bf16[2048,256]{1,0:T(8,128)(2,1)}, u32[]{:S(2)}, u32[]{:S(2)}) collective-permute-start(bf16[2048,256]{1,0:T(8,128)(2,1)} %get-tuple-element.31.refs_0_), channel_id=1, source_target_pairs={{0,16},{16,0},{1,17},{17,1},{2,18},{18,2},{3,19},{19,3},{4,20},{20... | collective-permute-start | bytes 3145736 | tf_op jit(solution)/shard_map/ppermute | solution.py:33
  86.5 24.3 %copy-start.13 = (bf16[2048,128]{1,0:T(8,128)(2,1)S(1)}, bf16[2048,128]{1,0:T(8,128)(2,1)}, u32[]{:S(2)}) copy-start(bf16[2048,128]{1,0:T(8,128)(2,1)} %copy-done.12) | copy-start | bytes 1572868
  87.0 48.0 %collective-permute-start.18 = (bf16[128,3072]{1,0:T(8,128)(2,1)S(1)}, bf16[128,3072]{1,0:T(8,128)(2,1)}, u32[]{:S(2)}, u32[]{:S(2)}) collective-permute-start(bf16[128,3072]{1,0:T(8,128)(2,1)S(1)} %copy-done), channel_id=1, source_target_pairs={{0,4},{2,6},{4,0},{6,2},{1,5},{3,7},{5,1},{7,3},{8,12},{10,14},{12... | collective-permute-start | bytes 2359304 | tf_op jit(solution)/shard_map/ppermute | solution.py:29
  101.6 33.5 %collective-permute-start.20 = (bf16[128,3072]{1,0:T(8,128)(2,1)}, bf16[128,3072]{1,0:T(8,128)(2,1)}, u32[]{:S(2)}, u32[]{:S(2)}) collective-permute-start(bf16[128,3072]{1,0:T(8,128)(2,1)} %collective-permute-done.19.refs_4_), channel_id=1, source_target_pairs={{0,2},{2,4},{4,6},{6,0},{1,3},{3,5},{5,7},{7,1},{8,10},{10,12},{12... | collective-permute-start | bytes 2359304 | tf_op jit(solution)/shard_map/ppermute | solution.py:29
  104.1 31.0 %collective-permute-start.21 = (bf16[128,3072]{1,0:T(8,128)(2,1)}, bf16[128,3072]{1,0:T(8,128)(2,1)}, u32[]{:S(2)}, u32[]{:S(2)}) collective-permute-start(bf16[128,3072]{1,0:T(8,128)(2,1)} %collective-permute-done.19.refs_4_), channel_id=1, source_target_pairs={{0,6},{2,0},{4,2},{6,4},{1,7},{3,1},{5,3},{7,5},{8,14},{10,8},{12,... | collective-permute-start | bytes 2359304 | tf_op jit(solution)/shard_map/ppermute | solution.py:29
  108.2 13.6 %collective-permute-start.15 = (bf16[1024,256]{1,0:T(8,128)(2,1)S(1)}, bf16[1024,256]{1,0:T(8,128)(2,1)S(1)}, u32[]{:S(2)}, u32[]{:S(2)}) collective-permute-start(bf16[1024,256]{1,0:T(8,128)(2,1)S(1)} %slice_select_fusion), channel_id=1, source_target_pairs={{0,16},{16,0},{1,17},{17,1},{2,18},{18,2},{3,19},{19,3},{4,20},{20... | collective-permute-start | bytes 1572872 | tf_op jit(solution)/shard_map/ppermute | solution.py:33
  110.5 13.2 %collective-permute-start.17 = (bf16[1024,256]{1,0:T(8,128)(2,1)S(1)}, bf16[1024,256]{1,0:T(8,128)(2,1)S(1)}, u32[]{:S(2)}, u32[]{:S(2)}) collective-permute-start(bf16[1024,256]{1,0:T(8,128)(2,1)S(1)} %slice.24), channel_id=1, source_target_pairs={{0,32},{32,64},{64,96},{96,128},{128,160},{160,192},{192,224},{224... | collective-permute-start | bytes 1572872 | tf_op jit(solution)/shard_map/ppermute | solution.py:317
  121.9 19.2 %collective-permute-start.22 = (bf16[128,3072]{1,0:T(8,128)(2,1)}, bf16[128,3072]{1,0:T(8,128)(2,1)}, u32[]{:S(2)}, u32[]{:S(2)}) collective-permute-start(bf16[128,3072]{1,0:T(8,128)(2,1)} %collective-permute-done.19.refs_4_), channel_id=1, source_target_pairs={{0,4},{2,6},{4,0},{6,2},{1,5},{3,7},{5,1},{7,3},{8,12},{10,14},{12... | collective-permute-start | bytes 2359304 | tf_op jit(solution)/shard_map/ppermute | solution.py:29
  129.9 21.4 %all-to-all-start = ((bf16[8,256,128]{2,1,0:T(8,128)(2,1)}), bf16[8,256,128]{2,1,0:T(8,128)(2,1)S(1)}, u32[]{:S(2)}, u32[]{:S(2)}) async-start(bf16[8,256,128]{2,1,0:T(8,128)(2,1)} %bitcast.26), calls=%async_computation | async-start | bytes 1048576 | tf_op jit(solution)/shard_map/all_to_all | solution.py:330
  155.2 2.5 %collective-permute-start.23 = (bf16[128,3072]{1,0:T(8,128)(2,1)S(1)}, bf16[128,3072]{1,0:T(8,128)(2,1)S(1)}, u32[]{:S(2)}, u32[]{:S(2)}) collective-permute-start(bf16[128,3072]{1,0:T(8,128)(2,1)S(1)} %get-tuple-element.36), channel_id=1, source_target_pairs={{0,1},{1,0},{2,3},{3,2},{4,5},{5,4},{6,7},{7,6},{8,9},{9,8},{10,11... | collective-permute-start | bytes 2359304 | tf_op jit(solution)/shard_map/ppermute | solution.py:33
  (10 other events, 29.1 us)

commit v5 on v4

--- a/solution.py
+++ b/solution.py
@@ -23,6 +23,11 @@
 WHOLE_VM = pl.BlockSpec(memory_space=VM)
 WHOLE_SM = pl.BlockSpec(memory_space=SM)
 WHOLE_ANY = pl.BlockSpec(memory_space=pl.ANY)
+WHOLE_HBM = pl.BlockSpec(memory_space=pltpu.HBM)
+
+
+def in_hbm(arrays):
+    return [pltpu.with_memory_space_constraint(a, pltpu.HBM) for a in arrays]
 
 
 def round_x(array, by):
@@ -33,27 +38,38 @@
     return lax.ppermute(array, axis, [(0, 1), (1, 0)])
 
 
+def opposite(array):
+    return lax.ppermute(array, ("yl", "yh"), [(i, 3 - i) for i in range(4)])
+
+
 def qkv_kernel(heights, own_ref, other_ref, *refs):
     pieces = refs[: len(heights)]
-    mine_ref, theirs_ref, rows_ref, sems = refs[len(heights) :]
+    mine_ref, theirs_ref, rows_ref, w_ref, row_sems, w_sems = refs[len(heights) :]
+    width, group = own_ref.shape[1], 256
     copies, start = [], 0
     for i, height in enumerate(heights):
-        copies.append((pltpu.make_async_copy(pieces[i], rows_ref.at[pl.ds(start, height)], sems.at[i]), start + height))
+        copies.append(pltpu.make_async_copy(pieces[i], rows_ref.at[pl.ds(start, height)], row_sems.at[i]))
         start += height
-    for copy, _ in copies:
+    spans = [(other_ref, 0, group), (other_ref, group, width), (own_ref, 0, 2 * group - width), (own_ref, 2 * group - width, width)]
+    loads, place = [], 0
+    for i, (ref, low, high) in enumerate(spans):
+        loads.append(pltpu.make_async_copy(ref.at[:, low:high], w_ref.at[:, place : place + high - low], w_sems.at[i]))
+        place += high - low
+    for copy in loads[:1] + copies + loads[1:]:
         copy.start()
-    part = start // 2
-    for low in range(0, start, part):
-        for copy, end in copies:
-            if low < end <= low + part:
-                copy.wait()
-        rows = rows_ref[low : low + part, :]
-        theirs_ref[low : low + part, TILE:] = jnp.dot(rows, other_ref[:, TILE:], preferred_element_type=F32).astype(BF)
-        both = jnp.concatenate([other_ref[:, :TILE], own_ref[:, :TILE]], axis=1)
-        both = jnp.dot(rows, both, preferred_element_type=F32).astype(BF)
-        theirs_ref[low : low + part, :TILE] = both[:, :TILE]
-        mine_ref[low : low + part, :TILE] = both[:, TILE:]
-        mine_ref[low : low + part, TILE:] = jnp.dot(rows, own_ref[:, TILE:], preferred_element_type=F32).astype(BF)
+    for copy in copies:
+        copy.wait()
+    for g, needed in enumerate(((0,), (1, 2), (3,))):
+        for i in needed:
+            loads[i].wait()
+        low, high = g * group, (g + 1) * group
+        done = jnp.dot(rows_ref[...], w_ref[:, low:high], preferred_element_type=F32).astype(BF)
+        if low < width:
+            stop = min(high, width)
+            theirs_ref[:, low:stop] = done[:, : stop - low]
+        if high > width:
+            first = max(low, width)
+            mine_ref[:, first - width : high - width] = done[:, first - low :]
 
 
 def qkv(own, other, pieces):
@@ -62,12 +78,17 @@
     return pl.pallas_call(
         functools.partial(qkv_kernel, heights),
         out_shape=(jax.ShapeDtypeStruct((n, width), BF),) * 2,
-        in_specs=[WHOLE_VM] * 2 + [WHOLE_ANY] * len(pieces),
+        in_specs=[WHOLE_HBM] * 2 + [WHOLE_ANY] * len(pieces),
         out_specs=(WHOLE_VM,) * 2,
-        scratch_shapes=[VM((n, depth), BF), pltpu.SemaphoreType.DMA((len(pieces),))],
+        scratch_shapes=[
+            VM((n, depth), BF),
+            VM((depth, 2 * width), BF),
+            pltpu.SemaphoreType.DMA((len(pieces),)),
+            pltpu.SemaphoreType.DMA((4,)),
+        ],
         compiler_params=pltpu.CompilerParams(vmem_limit_bytes=24 << 20),
         cost_estimate=pl.CostEstimate(flops=4 * n * depth * width, bytes_accessed=8 << 20, transcendentals=0),
-    )(own, other, *pieces)
+    )(*in_hbm((own, other)), *pieces)
 
 
 def hot_rows(want, block_ref):
@@ -98,39 +119,50 @@
     lax.fori_loop(0, want_ref.shape[0] // rows, step, 0)
 
 
-def place_far_kernel(block_ref, want_ref, first_ref, second_ref, near_ref, q_ref, kv_ref):
+def place_far_kernel(block_ref, want_ref, first_ref, second_ref, near_ref, q_ref, kv_ref, before_ref, sems):
     rows = 512
-
-    def step(i, carry):
-        start = pl.multiple_of(i * rows, rows)
-        spot = pl.ds(start, rows)
-        done = pick(want_ref[spot, :], block_ref, first_ref, second_ref) + near_ref[spot, :].astype(F32)
+    steps = want_ref.shape[0] // rows
+    copies = [
+        pltpu.make_async_copy(near_ref.at[pl.ds(i * rows, rows)], before_ref.at[pl.ds(i * rows, rows)], sems.at[i])
+        for i in range(steps)
+    ]
+    for copy in copies:
+        copy.start()
+    for i, copy in enumerate(copies):
+        spot = slice(i * rows, (i + 1) * rows)
+        done = pick(want_ref[spot, :], block_ref, first_ref, second_ref)
+        copy.wait()
+        done = done + before_ref[spot, :].astype(F32)
         q_ref[spot, :] = done[:, :TILE].astype(BF)
         kv_ref[spot, TILE:] = done[:, 2 * TILE :].astype(BF)
         for t in range(0, rows, TILE):
             keys = done[t : t + TILE, TILE : 2 * TILE]
-            kv_ref[pl.ds(pl.multiple_of(start + t, TILE), TILE), :TILE] = keys.T.astype(BF)
-        return carry
-
-    lax.fori_loop(0, want_ref.shape[0] // rows, step, 0)
-
-
-def place(blocks, want, first, second, near=None):
+            kv_ref[i * rows + t : i * rows + t + TILE, :TILE] = keys.T.astype(BF)
+
+
+def place_near(blocks, want, first, second):
     n, width = want.shape[0], first.shape[1]
-    if near is None:
-        kernel, out = place_near_kernel, jax.ShapeDtypeStruct((n, width), BF)
-    else:
-        kernel = place_far_kernel
-        out = (jax.ShapeDtypeStruct((n, TILE), BF), jax.ShapeDtypeStruct((n, width - TILE), BF))
-    operands = (want, first, second) + (() if near is None else (near,))
-    return pl.pallas_call(
-        kernel,
-        out_shape=out,
-        in_specs=[WHOLE_SM] + [WHOLE_VM] * len(operands),
-        out_specs=WHOLE_VM if near is None else (WHOLE_VM,) * 2,
+    return pl.pallas_call(
+        place_near_kernel,
+        out_shape=jax.ShapeDtypeStruct((n, width), BF),
+        in_specs=[WHOLE_SM] + [WHOLE_VM] * 3,
+        out_specs=WHOLE_VM,
         compiler_params=pltpu.CompilerParams(vmem_limit_bytes=24 << 20),
         cost_estimate=pl.CostEstimate(flops=n * n * width, bytes_accessed=4 << 20, transcendentals=0),
-    )(blocks, *operands)
+    )(blocks, want, first, second)
+
+
+def place_far(blocks, want, first, second, near):
+    n, width = want.shape[0], first.shape[1]
+    return pl.pallas_call(
+        place_far_kernel,
+        out_shape=(pltpu.HBM((n, TILE), BF), jax.ShapeDtypeStruct((n, width - TILE), BF)),
+        in_specs=[WHOLE_SM] + [WHOLE_VM] * 3 + [WHOLE_ANY],
+        out_specs=(WHOLE_VM,) * 2,
+        scratch_shapes=[VM((n, width), BF), pltpu.SemaphoreType.DMA((4,))],
+        compiler_params=pltpu.CompilerParams(vmem_limit_bytes=24 << 20),
+        cost_estimate=pl.CostEstimate(flops=n * n * width, bytes_accessed=4 << 20, transcendentals=0),
+    )(blocks, want, first, second, *in_hbm((near,)))
 
 
 def attend_kernel(sizes, together, parts, last, index_ref, count_ref, q_ref, *refs):
@@ -234,31 +266,43 @@
 
 
 def project_kernel(order_ref, att_ref, *refs):
-    weights, mine_ref, other_ref = refs[:-2], refs[-2], refs[-1]
-    chips = att_ref.shape[0]
+    weights, (mine_ref, other_ref, w_ref, sems) = refs[:-4], refs[-4:]
+    chips, width, groups = att_ref.shape[0], mine_ref.shape[1], 3
+    span = width // groups
+    loads = []
+    for g in range(groups):
+        for b, ref in enumerate(weights):
+            columns = slice(g * span, (g + 1) * span)
+            loads.append(
+                pltpu.make_async_copy(ref.at[:, columns], w_ref.at[pl.ds(b * TILE, TILE), columns], sems.at[g * chips + b])
+            )
+    for copy in loads:
+        copy.start()
     own = pl.multiple_of(order_ref[chips] * TILE, TILE)
     away = pl.multiple_of(TILE - own, TILE)
     mine = jnp.concatenate([att_ref[order_ref[b], pl.ds(own, TILE), :] for b in range(chips)], axis=1)
     other = jnp.concatenate([att_ref[order_ref[b], pl.ds(away, TILE), :] for b in range(chips)], axis=1)
     left = jnp.concatenate([mine, other], axis=0)
-    step = 256
-    for column in range(0, mine_ref.shape[1], step):
-        right = jnp.concatenate([w[:, column : column + step] for w in weights], axis=0)
-        done = jnp.dot(left, right, preferred_element_type=F32)
-        mine_ref[:, column : column + step] = done[:TILE]
-        other_ref[:, column : column + step] = done[TILE:].astype(BF)
+    for g in range(groups):
+        for copy in loads[g * chips : (g + 1) * chips]:
+            copy.wait()
+        for column in range(g * span, (g + 1) * span, 256):
+            done = jnp.dot(left, w_ref[:, column : column + 256], preferred_element_type=F32)
+            mine_ref[:, column : column + 256] = done[:TILE]
+            other_ref[:, column : column + 256] = done[TILE:].astype(BF)
 
 
 def project(order, attended, weights):
-    width = weights[0].shape[1]
+    width, chips = weights[0].shape[1], len(weights)
     return pl.pallas_call(
         project_kernel,
         out_shape=(jax.ShapeDtypeStruct((TILE, width), F32), jax.ShapeDtypeStruct((TILE, width), BF)),
-        in_specs=[WHOLE_SM] + [WHOLE_VM] * (1 + len(weights)),
+        in_specs=[WHOLE_SM, WHOLE_VM] + [WHOLE_HBM] * chips,
         out_specs=(WHOLE_VM,) * 2,
+        scratch_shapes=[VM((chips * TILE, width), BF), pltpu.SemaphoreType.DMA((3 * chips,))],
         compiler_params=pltpu.CompilerParams(vmem_limit_bytes=24 << 20),
         cost_estimate=pl.CostEstimate(flops=4 * TILE * 8 * TILE * width, bytes_accessed=10 << 20, transcendentals=0),
-    )(order, attended, *weights)
+    )(order, attended, *in_hbm(weights))
 
 
 def listed(place, chosen, slots):
@@ -293,29 +337,7 @@
     near_mine, near_theirs = qkv(w_qkv, w_other, [tokens, one, three, far_own])
     near_other = swap(near_theirs, "core")
     want = source_row[0][:, None]
-    near = place(blocks(NEAR), want, near_mine, near_other)
-    far_two, near = after((far_two, near))
-    far_mine, far_theirs = qkv(w_qkv, w_other, [low, high, f_one, f_three, far_two])
-    far_other = swap(far_theirs, "core")
-
-    w_start, _ = after((w_out, near))
-    w_one, w_three = round_x(w_start, 1), round_x(w_start, -1)
-    w_turn, _ = after((w_out, far_two))
-    w_two, w_far = round_x(w_turn, 2), lax.ppermute(w_turn, ("yl", "yh"), [(i, 3 - i) for i in range(4)])
-
-    q, kv = place(blocks(FAR), want, far_mine, far_other, near)
-    kv, _ = after((kv, (w_one, w_three)))
-    behind = lax.ppermute(kv, "z", [(i, (i + 1) % 8) for i in range(8)])
-    ahead = lax.ppermute(kv, "z", [(i, (i + 7) % 8) for i in range(8)])
-    beside = swap(kv, "yl")
-
-    wf_one, wf_three, wf_two = (round_x(w_far, by) for by in (1, -1, 2))
-
-    mid = kv.shape[0] // 2
-    cross_low = swap(jnp.where(yl == 0, ahead[:mid], behind[:mid]), "yl")
-    onward = [(2 * i, 2 * ((i + 1) % 8)) for i in range(8)] + [(2 * i + 1, 2 * ((i + 7) % 8) + 1) for i in range(8)]
-    cross_high = lax.ppermute(beside[mid:], CTX, onward)
-
+    near = place_near(blocks(NEAR), want, near_mine, near_other)
     tiles, slots = key_tiles.shape
     relative = key_tiles - ((z * 2 + yl) - 2) * tiles
     frame, inside = relative // tiles, relative % tiles
@@ -324,6 +346,30 @@
     valid = jnp.arange(slots)[None, :] < key_count[:, None]
     index, count = listed(window * tiles + inside, valid & ~crossing, slots)
     cross_index, cross_count = listed(inside, valid & crossing, tiles)
+    lists = (index, count, cross_index, cross_count)
+    far_two, near, (index, count, cross_index, cross_count) = after((far_two, near, lists))
+    far_mine, far_theirs = qkv(w_qkv, w_other, [low, high, f_one, f_three, far_two])
+    far_other = swap(far_theirs, "core")
+
+    w_start, _ = after((w_out, near))
+    w_one, w_three = round_x(w_start, 1), round_x(w_start, -1)
+    w_turn, _ = after((w_out, far_two))
+    w_two, w_far = round_x(w_turn, 2), opposite(w_turn)
+
+    q, kv = place_far(blocks(FAR), want, far_mine, far_other, near)
+    kv, _ = after((kv, (w_one, w_three)))
+    behind = lax.ppermute(kv, "z", [(i, (i + 1) % 8) for i in range(8)])
+    ahead = lax.ppermute(kv, "z", [(i, (i + 7) % 8) for i in range(8)])
+    beside = swap(kv, "yl")
+
+    wf_one, wf_three, wf_two = opposite(w_one), opposite(w_three), round_x(w_far, 2)
+
+    mid = kv.shape[0] // 2
+    (ahead_low, behind_low), _ = after(((ahead[:mid], behind[:mid]), (w_two, w_far)))
+    cross_low = swap(jnp.where(yl == 0, ahead_low, behind_low), "yl")
+    onward = [(2 * i, 2 * ((i + 1) % 8)) for i in range(8)] + [(2 * i + 1, 2 * ((i + 7) % 8) + 1) for i in range(8)]
+    cross_high = lax.ppermute(beside[mid:], CTX, onward)
+
     state = attend(index, count, q, [kv, behind, beside, ahead], (24, slots), together=4)
     attended = attend(cross_index, cross_count, q, [cross_low, cross_high], (6, tiles), state, together=4)
 

time: 159 us -> 151 us (0.950)
  waiting for transfers between devices: 69.2 us -> 49 us
  starting transfers between devices: 36.5 us -> 50.8 us
  local copies, waits for them, and re-layouts: 8.53 us -> 2.86 us
  Pallas kernels: 38.5 us -> 42.7 us
    ppermute x1, waiting for transfers between devices: 2.5 us -> 16 us  [body(): ahead = lax.ppermute(kv, 'z', [(i, (i + 7) % 8) for i in range(8)])]
    ppermute x12 -> x10, waiting for transfers between devices: 31.2 us -> 18.4 us  [round_x(): return lax.ppermute(array, 'x', [(i, (i + by) % 4) for i in range(4)])]
    all_to_all x1, waiting for transfers between devices: 10.2 us -> 0.16 us  [body(): lax.all_to_all(attended.reshape(8, 2 * TILE, TILE), CHIPS, split_axis=0,...]
    ppermute x8, starting transfers between devices: 12.8 us -> 19.5 us  [swap(): return lax.ppermute(array, axis, [(0, 1), (1, 0)])]
    unnamed x34 -> x8, local copies, waits for them, and re-layouts: 6.46 us -> 0.25 us
    ppermute x1 -> x3, waiting for transfers between devices: 13.7 us -> 8.88 us  [opposite(): return lax.ppermute(array, ('yl', 'yh'), [(i, 3 - i) for i in range(4)])]
    ppermute x1 -> x3, starting transfers between devices: 2.76 us -> 7.19 us  [opposite(): return lax.ppermute(array, ('yl', 'yh'), [(i, 3 - i) for i in range(4)])]
    pallas_call x2, Pallas kernels: 8.9 us -> 12.7 us  [qkv(): pl.pallas_call(functools.partial(qkv_kernel, heights), out_shape=(jax.Sha...]
  transfers between devices with their start and end apart: 25 -> 25, of which waited for: 12 -> 11; matrix products, arithmetic and copies ran while one was open for 4% -> 5% of each run, Pallas kernels for 22% -> 25%
where the time goes in v5:
time: 151 us
  starting transfers between devices  50.8 us (34%)
  waiting for transfers between devices  49 us (32%)
  Pallas kernels  42.7 us (28%)
  other arithmetic  5.32 us (4%)
  local copies, waits for them, and re-layouts  2.86 us (2%)
    ppermute x8, starting transfers between devices, swap(): return lax.ppermute(array, axis, [(0, 1), (1, 0)])  19.5 us
    ppermute x10, waiting for transfers between devices, round_x(): return lax.ppermute(array, 'x', [(i, (i + by) % 4) for i in range(4)])  18.4 us
    pallas_call x2, Pallas kernels, attend(): pl.pallas_call(functools.partial(attend_kernel, sizes, together, len(fram...  16.6 us
    ppermute x1, waiting for transfers between devices, body(): ahead = lax.ppermute(kv, 'z', [(i, (i + 7) % 8) for i in range(8)])  16 us
    pallas_call x2, Pallas kernels, qkv(): pl.pallas_call(functools.partial(qkv_kernel, heights), out_shape=(jax.Sha...  12.7 us
    ppermute x10, starting transfers between devices, round_x(): return lax.ppermute(array, 'x', [(i, (i + by) % 4) for i in range(4)])  12.4 us
    ppermute x3, waiting for transfers between devices, opposite(): return lax.ppermute(array, ('yl', 'yh'), [(i, 3 - i) for i in range(4)])  8.88 us
    all_to_all x1, starting transfers between devices, body(): lax.all_to_all(attended.reshape(8, 2 * TILE, TILE), CHIPS, split_axis=0,...  7.96 us
  transfers between devices with their start and end apart: 25, of which 11 were waited for; matrix products, arithmetic and copies ran while one was open for 5% of the time, Pallas kernels for 25%

profile of v5, /device:TPU:1, one launch (start us, length us, event | category | flops | bytes accessed | tf_op | source)
XLA Modules:
  0.0 150.9 jit_solution(8451981609404423719)
XLA Ops:
  0.0 3.2 %collective-permute-start.5 = (bf16[3072,384]{1,0:T(8,128)(2,1)}, bf16[3072,384]{1,0:T(8,128)(2,1)}, u32[]{:S(2)}, u32[]{:S(2)}) collective-permute-start(bf16[3072,384]{1,0:T(8,128)(2,1)} %own_ref.3), channel_id=1, source_target_pairs={{0,1},{1,0},{2,3},{3,2},{4,5},{5,4},{6,7},{7,6},{8,9},{9,8},{10,11... | collective-permute-start | bytes 7077896 | tf_op jit(solution)/shard_map/ppermute | solution.py:38
  3.2 2.7 %collective-permute-start.2 = (bf16[128,3072]{1,0:T(8,128)(2,1)}, bf16[128,3072]{1,0:T(8,128)(2,1)S(1)}, u32[]{:S(2)}, u32[]{:S(2)}) collective-permute-start(bf16[128,3072]{1,0:T(8,128)(2,1)} %refs_0_.2), channel_id=1, source_target_pairs={{0,6},{2,0},{4,2},{6,4},{1,7},{3,1},{5,3},{7,5},{8,14},{10,8},{12,... | collective-permute-start | bytes 2359304 | tf_op jit(solution)/shard_map/ppermute | solution.py:34
  5.9 1.2 collective-permute-start.6
  7.1 0.9 convert_reduce_fusion
  8.9 15.0 %collective-permute-done.refs_1_ = bf16[128,3072]{1,0:T(8,128)(2,1)S(1)} collective-permute-done((bf16[128,3072]{1,0:T(8,128)(2,1)}, bf16[128,3072]{1,0:T(8,128)(2,1)S(1)}, u32[]{:S(2)}, u32[]{:S(2)}) %collective-permute-start) | collective-permute-done | bytes 786464 | tf_op jit(solution)/shard_map/ppermute | solution.py:34
  25.5 2.7 %collective-permute-start.3 = (bf16[64,3072]{1,0:T(8,128)(2,1)}, bf16[64,3072]{1,0:T(8,128)(2,1)S(1)}, u32[]{:S(2)}, u32[]{:S(2)}) collective-permute-start(bf16[64,3072]{1,0:T(8,128)(2,1)} %slice.21), channel_id=1, source_target_pairs={{0,6},{2,0},{4,2},{6,4},{1,7},{3,1},{5,3},{7,5},{8,14},{10,8},{12,... | collective-permute-start | bytes 1179656 | tf_op jit(solution)/shard_map/ppermute | solution.py:34
  28.8 1.1 select_reduce_fusion
  30.1 2.7 %collective-permute-start.9 = (bf16[128,3072]{1,0:T(8,128)(2,1)}, bf16[128,3072]{1,0:T(8,128)(2,1)S(1)}, u32[]{:S(2)}, u32[]{:S(2)}) collective-permute-start(bf16[128,3072]{1,0:T(8,128)(2,1)} %collective-permute-done.6.refs_3_), channel_id=1, source_target_pairs={{0,6},{2,0},{4,2},{6,4},{1,7},{3,1},{5,3},{7,5},{8,14},{10,8},{12,... | collective-permute-start | bytes 2359304 | tf_op jit(solution)/shard_map/ppermute | solution.py:34
  32.8 3.3 %collective-permute-done.1.refs_0_ = bf16[64,3072]{1,0:T(8,128)(2,1)S(1)} collective-permute-done((bf16[64,3072]{1,0:T(8,128)(2,1)}, bf16[64,3072]{1,0:T(8,128)(2,1)S(1)}, u32[]{:S(2)}, u32[]{:S(2)}) %collective-permute-start.1) | collective-permute-done | bytes 393248 | tf_op jit(solution)/shard_map/ppermute | solution.py:34
  37.0 6.7 %shard_map.64 = (bf16[512,384]{1,0:T(8,128)(2,1)S(1)}, bf16[512,384]{1,0:T(8,128)(2,1)S(1)}) custom-call(bf16[3072,384]{1,0:T(8,128)(2,1)} %own_ref.3, bf16[3072,384]{1,0:T(8,128)(2,1)} %collective-permute-done.5.other_ref, bf16[128,3072]{1,0:T(8,128)(2,1)S(1)} %copy-done, bf16[128,3072]{1,0:T(8,128)(2,1)S(1)} %collective-permute-done.refs_1_, ...), custom_call_target="tpu_custom_call" | custom-call | flops 2415919104 | bytes 8388608 | tf_op jit(solution)/shard_map/pallas_call | solution.py:78
  43.8 4.0 %collective-permute-start.7 = (bf16[512,384]{1,0:T(8,128)(2,1)S(1)}, bf16[512,384]{1,0:T(8,128)(2,1)S(1)}, u32[]{:S(2)}, u32[]{:S(2)}) collective-permute-start(bf16[512,384]{1,0:T(8,128)(2,1)S(1)} %get-tuple-element.28), channel_id=1, source_target_pairs={{0,1},{1,0},{2,3},{3,2},{4,5},{5,4},{6,7},{7,6},{8,9},{9,8},{10,11... | collective-permute-start | bytes 1179656 | tf_op jit(solution)/shard_map/ppermute | solution.py:38
  49.1 3.6 %shard_map.65.near_ref = bf16[2048,384]{1,0:T(8,128)(2,1)S(1)} custom-call(f32[8]{0:T(128)S(1)} %convert_element_type.18.block_ref, s32[2048,1]{1,0:T(8,128)S(1)} %copy.9.want_ref, bf16[512,384]{1,0:T(8,128)(2,1)S(1)} %get-tuple-element.27.first_ref, bf16[512,384]{1,0:T(8,128)(2,1)S(1)} %collective-permute-done.7.second_ref), custom_call_target="tpu_custom_call" | custom-call | flops 1610612736 | bytes 4194304 | tf_op jit(solution)/shard_map/pallas_call | solution.py:145
  52.7 0.9 collective-permute-done.4.refs_4_
  53.6 3.0 %collective-permute-start.12 = (bf16[128,3072]{1,0:T(8,128)(2,1)}, bf16[128,3072]{1,0:T(8,128)(2,1)}, u32[]{:S(2)}, u32[]{:S(2)}) collective-permute-start(bf16[128,3072]{1,0:T(8,128)(2,1)} %refs_0_.3), channel_id=1, source_target_pairs={{0,6},{2,0},{4,2},{6,4},{1,7},{3,1},{5,3},{7,5},{8,14},{10,8},{12,... | collective-permute-start | bytes 2359304 | tf_op jit(solution)/shard_map/ppermute | solution.py:34
  56.6 6.0 %shard_map.66 = (bf16[512,384]{1,0:T(8,128)(2,1)S(1)}, bf16[512,384]{1,0:T(8,128)(2,1)S(1)}) custom-call(bf16[3072,384]{1,0:T(8,128)(2,1)} %own_ref.3, bf16[3072,384]{1,0:T(8,128)(2,1)} %collective-permute-done.5.other_ref, bf16[64,3072]{1,0:T(8,128)(2,1)S(1)} %collective-permute-done.1.refs_0_, bf16[64,3072]{1,0:T(8,128)(2,1)S(1)} %collective-permute-done.3.refs_1_, ...), custom_call_target="tpu_custom_call" | custom-call | flops 2415919104 | bytes 8388608 | tf_op jit(solution)/shard_map/pallas_call | solution.py:78
  62.6 4.6 %collective-permute-start.10 = (bf16[512,384]{1,0:T(8,128)(2,1)S(1)}, bf16[512,384]{1,0:T(8,128)(2,1)S(1)}, u32[]{:S(2)}, u32[]{:S(2)}) collective-permute-start(bf16[512,384]{1,0:T(8,128)(2,1)S(1)} %get-tuple-element.34), channel_id=1, source_target_pairs={{0,1},{1,0},{2,3},{3,2},{4,5},{5,4},{6,7},{7,6},{8,9},{9,8},{10,11... | collective-permute-start | bytes 1179656 | tf_op jit(solution)/shard_map/ppermute | solution.py:38
  67.4 1.3 collective-permute-done.10.second_ref
  68.6 5.4 %shard_map.67 = (bf16[2048,128]{1,0:T(8,128)(2,1)}, bf16[2048,256]{1,0:T(8,128)(2,1)}) custom-call(f32[8]{0:T(128)S(1)} %convert_element_type.21.block_ref, s32[2048,1]{1,0:T(8,128)S(1)} %copy.9.want_ref, bf16[512,384]{1,0:T(8,128)(2,1)S(1)} %get-tuple-element.33.first_ref, bf16[512,384]{1,0:T(8,128)(2,1)S(1)} %collective-permute-done.10.second_ref, ...), custom_call_target="tpu_custom_call" | custom-call | flops 1610612736 | bytes 4194304 | tf_op jit(solution)/shard_map/pallas_call | solution.py:157
  74.0 3.7 %collective-permute-start.13 = (bf16[2048,256]{1,0:T(8,128)(2,1)}, bf16[2048,256]{1,0:T(8,128)(2,1)S(1)}, u32[]{:S(2)}, u32[]{:S(2)}) collective-permute-start(bf16[2048,256]{1,0:T(8,128)(2,1)} %get-tuple-element.39.refs_0_), channel_id=1, source_target_pairs={{0,224},{32,0},{64,32},{96,64},{128,96},{160,128},{192,160},{224,1... | collective-permute-start | bytes 3145736 | tf_op jit(solution)/shard_map/ppermute | solution.py:362
  77.7 2.7 %collective-permute-start.16 = (bf16[128,3072]{1,0:T(8,128)(2,1)}, bf16[128,3072]{1,0:T(8,128)(2,1)}, u32[]{:S(2)}, u32[]{:S(2)}) collective-permute-start(bf16[128,3072]{1,0:T(8,128)(2,1)} %refs_0_.3), channel_id=1, source_target_pairs={{0,24},{8,16},{16,8},{24,0},{1,25},{9,17},{17,9},{25,1},{2,26},{10... | collective-permute-start | bytes 2359304 | tf_op jit(solution)/shard_map/ppermute | solution.py:42
  80.5 1.2 collective-permute-start.15
  81.7 16.0 %collective-permute-done.13.refs_3_ = bf16[2048,256]{1,0:T(8,128)(2,1)S(1)} collective-permute-done((bf16[2048,256]{1,0:T(8,128)(2,1)}, bf16[2048,256]{1,0:T(8,128)(2,1)S(1)}, u32[]{:S(2)}, u32[]{:S(2)}) %collective-permute-start.13) | collective-permute-done | bytes 1048608 | tf_op jit(solution)/shard_map/ppermute | solution.py:362
  97.7 4.4 %collective-permute-start.20 = (bf16[128,3072]{1,0:T(8,128)(2,1)}, bf16[128,3072]{1,0:T(8,128)(2,1)}, u32[]{:S(2)}, u32[]{:S(2)}) collective-permute-start(bf16[128,3072]{1,0:T(8,128)(2,1)} %collective-permute-done.11.refs_1_), channel_id=1, source_target_pairs={{0,24},{8,16},{16,8},{24,0},{1,25},{9,17},{17,9},{25,1},{2,26},{10... | collective-permute-start | bytes 2359304 | tf_op jit(solution)/shard_map/ppermute | solution.py:42
  103.4 10.4 %shard_map.68 = (f32[2048,128]{1,0:T(8,128)S(1)}, f32[2048,128]{1,0:T(8,128)S(1)}) custom-call(s32[16,30]{1,0:T(8,128)S(1)} %copy.14.index_ref, s32[16]{0:T(128)S(1)} %get-tuple-element.44.count_ref, bf16[2048,128]{1,0:T(8,128)(2,1)S(1)} %copy-done.2, bf16[2048,256]{1,0:T(8,128)(2,1)} %get-tuple-element.39.refs_0_, ...), custom_call_target="tpu_custom_call" | custom-call | flops 16106127360 | bytes 6291456 | tf_op jit(solution)/shard_map/pallas_call | solution.py:251
  113.8 1.1 collective-permute-done.17.refs_0_
  115.0 6.1 %shard_map.69 = bf16[2048,128]{1,0:T(8,128)(2,1)} custom-call(s32[16,16]{1,0:T(8,128)S(1)} %select_reduce_fusion.3.index_ref, s32[16]{0:T(128)S(1)} %get-tuple-element.30.count_ref, bf16[2048,128]{1,0:T(8,128)(2,1)S(1)} %copy-done.2, bf16[1024,256]{1,0:T(8,128)(2,1)S(1)} %collective-permute-done.17.refs_0_, ...), custom_call_target="tpu_custom_call" | custom-call | flops 8589934592 | bytes 6291456 | tf_op jit(solution)/shard_map/pallas_call | solution.py:251
  121.1 8.0 %all-to-all-start = ((bf16[8,256,128]{2,1,0:T(8,128)(2,1)}), bf16[8,256,128]{2,1,0:T(8,128)(2,1)S(1)}, u32[]{:S(2)}, u32[]{:S(2)}) async-start(bf16[8,256,128]{2,1,0:T(8,128)(2,1)} %bitcast.26), calls=%async_computation | async-start | bytes 1048576 | tf_op jit(solution)/shard_map/all_to_all | solution.py:376
  129.2 8.9 %collective-permute-done.21.refs_6_ = bf16[128,3072]{1,0:T(8,128)(2,1)} collective-permute-done((bf16[128,3072]{1,0:T(8,128)(2,1)}, bf16[128,3072]{1,0:T(8,128)(2,1)}, u32[]{:S(2)}, u32[]{:S(2)}) %collective-permute-start.21) | collective-permute-done | bytes 786464 | tf_op jit(solution)/shard_map/ppermute | solution.py:42
  138.2 4.4 %shard_map.70 = (f32[128,3072]{1,0:T(8,128)S(1)}, bf16[128,3072]{1,0:T(8,128)(2,1)S(1)}) custom-call(s32[9]{0:T(128)S(1)} %stack.93.order_ref, bf16[8,256,128]{2,1,0:T(8,128)(2,1)S(1)} %all-to-all-done.att_ref, bf16[128,3072]{1,0:T(8,128)(2,1)} %refs_0_.3, bf16[128,3072]{1,0:T(8,128)(2,1)} %collective-permute-done.11.refs_1_, ...), custom_call_target="tpu_custom_call" | custom-call | flops 1610612736 | bytes 10485760 | tf_op jit(solution)/shard_map/pallas_call | solution.py:297
  142.6 5.3 %collective-permute-start.23 = (bf16[128,3072]{1,0:T(8,128)(2,1)S(1)}, bf16[128,3072]{1,0:T(8,128)(2,1)S(1)}, u32[]{:S(2)}, u32[]{:S(2)}) collective-permute-start(bf16[128,3072]{1,0:T(8,128)(2,1)S(1)} %get-tuple-element.48), channel_id=1, source_target_pairs={{0,1},{1,0},{2,3},{3,2},{4,5},{5,4},{6,7},{7,6},{8,9},{9,8},{10,11... | collective-permute-start | bytes 2359304 | tf_op jit(solution)/shard_map/ppermute | solution.py:38
  147.9 1.9 %collective-permute-done.23 = bf16[128,3072]{1,0:T(8,128)(2,1)S(1)} collective-permute-done((bf16[128,3072]{1,0:T(8,128)(2,1)S(1)}, bf16[128,3072]{1,0:T(8,128)(2,1)S(1)}, u32[]{:S(2)}, u32[]{:S(2)}) %collective-permute-start.23) | collective-permute-done | bytes 786464 | tf_op jit(solution)/shard_map/ppermute | solution.py:38
  149.8 1.1 add_convert_fusion
  (61 shorter events, 7.3 us)
Async XLA Ops:
  0.0 28.3 %copy-start.3 = (s32[1,2048]{1,0:T(1,128)S(1)}, s32[1,2048]{1,0:T(1,128)}, u32[]{:S(2)}) copy-start(s32[1,2048]{1,0:T(1,128)} %param.9) | copy-start | bytes 24580
  0.0 37.0 %collective-permute-start.5 = (bf16[3072,384]{1,0:T(8,128)(2,1)}, bf16[3072,384]{1,0:T(8,128)(2,1)}, u32[]{:S(2)}, u32[]{:S(2)}) collective-permute-start(bf16[3072,384]{1,0:T(8,128)(2,1)} %own_ref.3), channel_id=1, source_target_pairs={{0,1},{1,0},{2,3},{3,2},{4,5},{5,4},{6,7},{7,6},{8,9},{9,8},{10,11... | collective-permute-start | bytes 7077896 | tf_op jit(solution)/shard_map/ppermute | solution.py:38
  3.2 20.7 %collective-permute-start = (bf16[128,3072]{1,0:T(8,128)(2,1)}, bf16[128,3072]{1,0:T(8,128)(2,1)S(1)}, u32[]{:S(2)}, u32[]{:S(2)}) collective-permute-start(bf16[128,3072]{1,0:T(8,128)(2,1)} %refs_0_.2), channel_id=1, source_target_pairs={{0,2},{2,4},{4,6},{6,0},{1,3},{3,5},{5,7},{7,1},{8,10},{10,12},{12... | collective-permute-start | bytes 2359304 | tf_op jit(solution)/shard_map/ppermute | solution.py:34
  3.2 21.5 %collective-permute-start.2 = (bf16[128,3072]{1,0:T(8,128)(2,1)}, bf16[128,3072]{1,0:T(8,128)(2,1)S(1)}, u32[]{:S(2)}, u32[]{:S(2)}) collective-permute-start(bf16[128,3072]{1,0:T(8,128)(2,1)} %refs_0_.2), channel_id=1, source_target_pairs={{0,6},{2,0},{4,2},{6,4},{1,7},{3,1},{5,3},{7,5},{8,14},{10,8},{12,... | collective-permute-start | bytes 2359304 | tf_op jit(solution)/shard_map/ppermute | solution.py:34
  5.9 24.1 %collective-permute-start.6 = (bf16[128,3072]{1,0:T(8,128)(2,1)}, bf16[128,3072]{1,0:T(8,128)(2,1)}, u32[]{:S(2)}, u32[]{:S(2)}) collective-permute-start(bf16[128,3072]{1,0:T(8,128)(2,1)} %refs_0_.2), channel_id=1, source_target_pairs={{0,8},{8,0},{1,9},{9,1},{2,10},{10,2},{3,11},{11,3},{4,12},{12,4},... | collective-permute-start | bytes 2359304 | tf_op jit(solution)/shard_map/ppermute | solution.py:38
  24.7 11.4 %collective-permute-start.1 = (bf16[64,3072]{1,0:T(8,128)(2,1)}, bf16[64,3072]{1,0:T(8,128)(2,1)S(1)}, u32[]{:S(2)}, u32[]{:S(2)}) collective-permute-start(bf16[64,3072]{1,0:T(8,128)(2,1)} %slice.20), channel_id=1, source_target_pairs={{0,2},{2,4},{4,6},{6,0},{1,3},{3,5},{5,7},{7,1},{8,10},{10,12},{12... | collective-permute-start | bytes 1179656 | tf_op jit(solution)/shard_map/ppermute | solution.py:34
  25.5 10.6 %collective-permute-start.3 = (bf16[64,3072]{1,0:T(8,128)(2,1)}, bf16[64,3072]{1,0:T(8,128)(2,1)S(1)}, u32[]{:S(2)}, u32[]{:S(2)}) collective-permute-start(bf16[64,3072]{1,0:T(8,128)(2,1)} %slice.21), channel_id=1, source_target_pairs={{0,6},{2,0},{4,2},{6,4},{1,7},{3,1},{5,3},{7,5},{8,14},{10,8},{12,... | collective-permute-start | bytes 1179656 | tf_op jit(solution)/shard_map/ppermute | solution.py:34
  30.0 7.0 %copy-start = (bf16[128,3072]{1,0:T(8,128)(2,1)S(1)}, bf16[128,3072]{1,0:T(8,128)(2,1)}, u32[]{:S(2)}) copy-start(bf16[128,3072]{1,0:T(8,128)(2,1)} %refs_0_.2) | copy-start | bytes 2359300
  30.0 26.6 %collective-permute-start.8 = (bf16[128,3072]{1,0:T(8,128)(2,1)}, bf16[128,3072]{1,0:T(8,128)(2,1)S(1)}, u32[]{:S(2)}, u32[]{:S(2)}) collective-permute-start(bf16[128,3072]{1,0:T(8,128)(2,1)} %collective-permute-done.6.refs_3_), channel_id=1, source_target_pairs={{0,2},{2,4},{4,6},{6,0},{1,3},{3,5},{5,7},{7,1},{8,10},{10,12},{12... | collective-permute-start | bytes 2359304 | tf_op jit(solution)/shard_map/ppermute | solution.py:34
  30.1 26.5 %collective-permute-start.9 = (bf16[128,3072]{1,0:T(8,128)(2,1)}, bf16[128,3072]{1,0:T(8,128)(2,1)S(1)}, u32[]{:S(2)}, u32[]{:S(2)}) collective-permute-start(bf16[128,3072]{1,0:T(8,128)(2,1)} %collective-permute-done.6.refs_3_), channel_id=1, source_target_pairs={{0,6},{2,0},{4,2},{6,4},{1,7},{3,1},{5,3},{7,5},{8,14},{10,8},{12,... | collective-permute-start | bytes 2359304 | tf_op jit(solution)/shard_map/ppermute | solution.py:34
  36.2 17.4 %collective-permute-start.4 = (bf16[128,3072]{1,0:T(8,128)(2,1)S(1)}, bf16[128,3072]{1,0:T(8,128)(2,1)S(1)}, u32[]{:S(2)}, u32[]{:S(2)}) collective-permute-start(bf16[128,3072]{1,0:T(8,128)(2,1)S(1)} %pad_maximum_fusion), channel_id=1, source_target_pairs={{0,8},{8,0},{1,9},{9,1},{2,10},{10,2},{3,11},{11,3},{4,12},{12,4},... | collective-permute-start | bytes 2359304 | tf_op jit(solution)/shard_map/ppermute | solution.py:38
  43.8 5.3 %collective-permute-start.7 = (bf16[512,384]{1,0:T(8,128)(2,1)S(1)}, bf16[512,384]{1,0:T(8,128)(2,1)S(1)}, u32[]{:S(2)}, u32[]{:S(2)}) collective-permute-start(bf16[512,384]{1,0:T(8,128)(2,1)S(1)} %get-tuple-element.28), channel_id=1, source_target_pairs={{0,1},{1,0},{2,3},{3,2},{4,5},{5,4},{6,7},{7,6},{8,9},{9,8},{10,11... | collective-permute-start | bytes 1179656 | tf_op jit(solution)/shard_map/ppermute | solution.py:38
  52.7 9.9 %copy-start.1 = (bf16[2048,384]{1,0:T(8,128)(2,1)}, bf16[2048,384]{1,0:T(8,128)(2,1)S(1)}, u32[]{:S(2)}) copy-start(bf16[2048,384]{1,0:T(8,128)(2,1)S(1)} %shard_map.65.near_ref) | copy-start | bytes 4718596
  53.6 20.4 %collective-permute-start.11 = (bf16[128,3072]{1,0:T(8,128)(2,1)}, bf16[128,3072]{1,0:T(8,128)(2,1)}, u32[]{:S(2)}, u32[]{:S(2)}) collective-permute-start(bf16[128,3072]{1,0:T(8,128)(2,1)} %refs_0_.3), channel_id=1, source_target_pairs={{0,2},{2,4},{4,6},{6,0},{1,3},{3,5},{5,7},{7,1},{8,10},{10,12},{12... | collective-permute-start | bytes 2359304 | tf_op jit(solution)/shard_map/ppermute | solution.py:34
  53.6 20.4 %collective-permute-start.12 = (bf16[128,3072]{1,0:T(8,128)(2,1)}, bf16[128,3072]{1,0:T(8,128)(2,1)}, u32[]{:S(2)}, u32[]{:S(2)}) collective-permute-start(bf16[128,3072]{1,0:T(8,128)(2,1)} %refs_0_.3), channel_id=1, source_target_pairs={{0,6},{2,0},{4,2},{6,4},{1,7},{3,1},{5,3},{7,5},{8,14},{10,8},{12,... | collective-permute-start | bytes 2359304 | tf_op jit(solution)/shard_map/ppermute | solution.py:34
  62.6 6.0 %collective-permute-start.10 = (bf16[512,384]{1,0:T(8,128)(2,1)S(1)}, bf16[512,384]{1,0:T(8,128)(2,1)S(1)}, u32[]{:S(2)}, u32[]{:S(2)}) collective-permute-start(bf16[512,384]{1,0:T(8,128)(2,1)S(1)} %get-tuple-element.34), channel_id=1, source_target_pairs={{0,1},{1,0},{2,3},{3,2},{4,5},{5,4},{6,7},{7,6},{8,9},{9,8},{10,11... | collective-permute-start | bytes 1179656 | tf_op jit(solution)/shard_map/ppermute | solution.py:38
  74.0 23.7 %collective-permute-start.13 = (bf16[2048,256]{1,0:T(8,128)(2,1)}, bf16[2048,256]{1,0:T(8,128)(2,1)S(1)}, u32[]{:S(2)}, u32[]{:S(2)}) collective-permute-start(bf16[2048,256]{1,0:T(8,128)(2,1)} %get-tuple-element.39.refs_0_), channel_id=1, source_target_pairs={{0,224},{32,0},{64,32},{96,64},{128,96},{160,128},{192,160},{224,1... | collective-permute-start | bytes 3145736 | tf_op jit(solution)/shard_map/ppermute | solution.py:362
  77.7 24.5 %collective-permute-start.14 = (bf16[2048,256]{1,0:T(8,128)(2,1)}, bf16[2048,256]{1,0:T(8,128)(2,1)S(1)}, u32[]{:S(2)}, u32[]{:S(2)}) collective-permute-start(bf16[2048,256]{1,0:T(8,128)(2,1)} %get-tuple-element.39.refs_0_), channel_id=1, source_target_pairs={{0,32},{32,64},{64,96},{96,128},{128,160},{160,192},{192,224},{224... | collective-permute-start | bytes 3145736 | tf_op jit(solution)/shard_map/ppermute | solution.py:361
  77.7 24.4 %collective-permute-start.16 = (bf16[128,3072]{1,0:T(8,128)(2,1)}, bf16[128,3072]{1,0:T(8,128)(2,1)}, u32[]{:S(2)}, u32[]{:S(2)}) collective-permute-start(bf16[128,3072]{1,0:T(8,128)(2,1)} %refs_0_.3), channel_id=1, source_target_pairs={{0,24},{8,16},{16,8},{24,0},{1,25},{9,17},{17,9},{25,1},{2,26},{10... | collective-permute-start | bytes 2359304 | tf_op jit(solution)/shard_map/ppermute | solution.py:42
  80.5 21.9 %collective-permute-start.15 = (bf16[128,3072]{1,0:T(8,128)(2,1)}, bf16[128,3072]{1,0:T(8,128)(2,1)}, u32[]{:S(2)}, u32[]{:S(2)}) collective-permute-start(bf16[128,3072]{1,0:T(8,128)(2,1)} %refs_0_.3), channel_id=1, source_target_pairs={{0,4},{2,6},{4,0},{6,2},{1,5},{3,7},{5,1},{7,3},{8,12},{10,14},{12... | collective-permute-start | bytes 2359304 | tf_op jit(solution)/shard_map/ppermute | solution.py:34
  81.7 21.4 %collective-permute-start.18 = (bf16[2048,256]{1,0:T(8,128)(2,1)}, bf16[2048,256]{1,0:T(8,128)(2,1)S(1)}, u32[]{:S(2)}, u32[]{:S(2)}) collective-permute-start(bf16[2048,256]{1,0:T(8,128)(2,1)} %get-tuple-element.39.refs_0_), channel_id=1, source_target_pairs={{0,16},{16,0},{1,17},{17,1},{2,18},{18,2},{3,19},{19,3},{4,20},{20... | collective-permute-start | bytes 3145736 | tf_op jit(solution)/shard_map/ppermute | solution.py:38
  97.7 31.5 %collective-permute-start.20 = (bf16[128,3072]{1,0:T(8,128)(2,1)}, bf16[128,3072]{1,0:T(8,128)(2,1)}, u32[]{:S(2)}, u32[]{:S(2)}) collective-permute-start(bf16[128,3072]{1,0:T(8,128)(2,1)} %collective-permute-done.11.refs_1_), channel_id=1, source_target_pairs={{0,24},{8,16},{16,8},{24,0},{1,25},{9,17},{17,9},{25,1},{2,26},{10... | collective-permute-start | bytes 2359304 | tf_op jit(solution)/shard_map/ppermute | solution.py:42
  102.1 35.9 %collective-permute-start.21 = (bf16[128,3072]{1,0:T(8,128)(2,1)}, bf16[128,3072]{1,0:T(8,128)(2,1)}, u32[]{:S(2)}, u32[]{:S(2)}) collective-permute-start(bf16[128,3072]{1,0:T(8,128)(2,1)} %collective-permute-done.12.refs_2_), channel_id=1, source_target_pairs={{0,24},{8,16},{16,8},{24,0},{1,25},{9,17},{17,9},{25,1},{2,26},{10... | collective-permute-start | bytes 2359304 | tf_op jit(solution)/shard_map/ppermute | solution.py:42
  102.2 35.8 %collective-permute-start.22 = (bf16[128,3072]{1,0:T(8,128)(2,1)}, bf16[128,3072]{1,0:T(8,128)(2,1)}, u32[]{:S(2)}, u32[]{:S(2)}) collective-permute-start(bf16[128,3072]{1,0:T(8,128)(2,1)} %collective-permute-done.16.refs_4_), channel_id=1, source_target_pairs={{0,4},{2,6},{4,0},{6,2},{1,5},{3,7},{5,1},{7,3},{8,12},{10,14},{12... | collective-permute-start | bytes 2359304 | tf_op jit(solution)/shard_map/ppermute | solution.py:34
  102.4 1.0 copy-start.2
  102.5 12.5 %collective-permute-start.17 = (bf16[1024,256]{1,0:T(8,128)(2,1)S(1)}, bf16[1024,256]{1,0:T(8,128)(2,1)S(1)}, u32[]{:S(2)}, u32[]{:S(2)}) collective-permute-start(bf16[1024,256]{1,0:T(8,128)(2,1)S(1)} %broadcast_select_fusion), channel_id=1, source_target_pairs={{0,16},{16,0},{1,17},{17,1},{2,18},{18,2},{3,19},{19,3},{4,20},{20... | collective-permute-start | bytes 1572872 | tf_op jit(solution)/shard_map/ppermute | solution.py:38
  103.1 11.9 %collective-permute-start.19 = (bf16[1024,256]{1,0:T(8,128)(2,1)S(1)}, bf16[1024,256]{1,0:T(8,128)(2,1)S(1)}, u32[]{:S(2)}, u32[]{:S(2)}) collective-permute-start(bf16[1024,256]{1,0:T(8,128)(2,1)S(1)} %slice.24), channel_id=1, source_target_pairs={{0,32},{32,64},{64,96},{96,128},{128,160},{160,192},{192,224},{224... | collective-permute-start | bytes 1572872 | tf_op jit(solution)/shard_map/ppermute | solution.py:371
  121.1 17.1 %all-to-all-start = ((bf16[8,256,128]{2,1,0:T(8,128)(2,1)}), bf16[8,256,128]{2,1,0:T(8,128)(2,1)S(1)}, u32[]{:S(2)}, u32[]{:S(2)}) async-start(bf16[8,256,128]{2,1,0:T(8,128)(2,1)} %bitcast.26), calls=%async_computation | async-start | bytes 1048576 | tf_op jit(solution)/shard_map/all_to_all | solution.py:376
  142.6 7.2 %collective-permute-start.23 = (bf16[128,3072]{1,0:T(8,128)(2,1)S(1)}, bf16[128,3072]{1,0:T(8,128)(2,1)S(1)}, u32[]{:S(2)}, u32[]{:S(2)}) collective-permute-start(bf16[128,3072]{1,0:T(8,128)(2,1)S(1)} %get-tuple-element.48), channel_id=1, source_target_pairs={{0,1},{1,0},{2,3},{3,2},{4,5},{5,4},{6,7},{7,6},{8,9},{9,8},{10,11... | collective-permute-start | bytes 2359304 | tf_op jit(solution)/shard_map/ppermute | solution.py:38

commit v6 on v5

--- a/solution.py
+++ b/solution.py
@@ -42,52 +42,53 @@
     return lax.ppermute(array, ("yl", "yh"), [(i, 3 - i) for i in range(4)])
 
 
-def qkv_kernel(heights, own_ref, other_ref, *refs):
+def qkv_kernel(heights, first, chunks, own_ref, other_ref, *refs):
     pieces = refs[: len(heights)]
-    mine_ref, theirs_ref, rows_ref, w_ref, row_sems, w_sems = refs[len(heights) :]
-    width, group = own_ref.shape[1], 256
-    copies, start = [], 0
-    for i, height in enumerate(heights):
-        copies.append(pltpu.make_async_copy(pieces[i], rows_ref.at[pl.ds(start, height)], row_sems.at[i]))
-        start += height
-    spans = [(other_ref, 0, group), (other_ref, group, width), (own_ref, 0, 2 * group - width), (own_ref, 2 * group - width, width)]
-    loads, place = [], 0
-    for i, (ref, low, high) in enumerate(spans):
-        loads.append(pltpu.make_async_copy(ref.at[:, low:high], w_ref.at[:, place : place + high - low], w_sems.at[i]))
-        place += high - low
-    for copy in loads[:1] + copies + loads[1:]:
-        copy.start()
-    for copy in copies:
-        copy.wait()
-    for g, needed in enumerate(((0,), (1, 2), (3,))):
-        for i in needed:
-            loads[i].wait()
-        low, high = g * group, (g + 1) * group
-        done = jnp.dot(rows_ref[...], w_ref[:, low:high], preferred_element_type=F32).astype(BF)
-        if low < width:
-            stop = min(high, width)
-            theirs_ref[:, low:stop] = done[:, : stop - low]
-        if high > width:
-            first = max(low, width)
-            mine_ref[:, first - width : high - width] = done[:, first - low :]
-
-
-def qkv(own, other, pieces):
-    heights = tuple(p.shape[0] for p in pieces)
-    n, depth, width = sum(heights), own.shape[0], own.shape[1]
-    return pl.pallas_call(
-        functools.partial(qkv_kernel, heights),
+    mine_ref, theirs_ref, rows_ref, w_ref, sum_ref, sems = refs[len(heights) :]
+    width = mine_ref.shape[1]
+    span = own_ref.shape[0] // chunks
+    loads = []
+    for c in range(chunks):
+        depth = pl.ds(c * span, span)
+        group, start = [], 0
+        for side, ref in enumerate((other_ref, own_ref)):
+            group.append((ref.at[depth, first : first + width], w_ref.at[depth, side * width : (side + 1) * width]))
+        for piece, height in zip(pieces, heights):
+            group.append((piece.at[:, depth], rows_ref.at[pl.ds(start, height), depth]))
+            start += height
+        loads.append([pltpu.make_async_copy(a, b, sems.at[c, i]) for i, (a, b) in enumerate(group)])
+    for group in loads:
+        for copy in group:
+            copy.start()
+    for c, group in enumerate(loads):
+        for copy in group:
+            copy.wait()
+        depth = slice(c * span, (c + 1) * span)
+        done = jnp.dot(rows_ref[:, depth], w_ref[depth, :], preferred_element_type=F32)
+        if c > 0:
+            done = done + sum_ref[...]
+        if c < chunks - 1:
+            sum_ref[...] = done
+    theirs_ref[...] = done[:, :width].astype(BF)
+    mine_ref[...] = done[:, width:].astype(BF)
+
+
+def qkv(own, other, pieces, first, last):
+    heights, chunks = tuple(p.shape[0] for p in pieces), 3
+    n, depth, width = sum(heights), own.shape[0], last - first
+    return pl.pallas_call(
+        functools.partial(qkv_kernel, heights, first, chunks),
         out_shape=(jax.ShapeDtypeStruct((n, width), BF),) * 2,
         in_specs=[WHOLE_HBM] * 2 + [WHOLE_ANY] * len(pieces),
         out_specs=(WHOLE_VM,) * 2,
         scratch_shapes=[
             VM((n, depth), BF),
             VM((depth, 2 * width), BF),
-            pltpu.SemaphoreType.DMA((len(pieces),)),
-            pltpu.SemaphoreType.DMA((4,)),
+            VM((n, 2 * width), F32),
+            pltpu.SemaphoreType.DMA((chunks, 2 + len(pieces))),
         ],
         compiler_params=pltpu.CompilerParams(vmem_limit_bytes=24 << 20),
-        cost_estimate=pl.CostEstimate(flops=4 * n * depth * width, bytes_accessed=8 << 20, transcendentals=0),
+        cost_estimate=pl.CostEstimate(flops=4 * n * width, bytes_accessed=1 << 10, transcendentals=0),
     )(*in_hbm((own, other)), *pieces)
 
 
@@ -334,7 +335,7 @@
     far_next, _ = after((far_own, (one, three)))
     f_one, f_three = round_x(far_next, 1), round_x(far_next, -1)
     far_two = swap(jnp.concatenate([low, high], axis=0), "yh")
-    near_mine, near_theirs = qkv(w_qkv, w_other, [tokens, one, three, far_own])
+    near_mine, near_theirs = qkv(w_qkv, w_other, [tokens, one, three, far_own], 0, 3 * TILE)
     near_other = swap(near_theirs, "core")
     want = source_row[0][:, None]
     near = place_near(blocks(NEAR), want, near_mine, near_other)
@@ -348,27 +349,29 @@
     cross_index, cross_count = listed(inside, valid & crossing, tiles)
     lists = (index, count, cross_index, cross_count)
     far_two, near, (index, count, cross_index, cross_count) = after((far_two, near, lists))
-    far_mine, far_theirs = qkv(w_qkv, w_other, [low, high, f_one, f_three, far_two])
+    far_mine, far_theirs = qkv(w_qkv, w_other, [low, high, f_one, f_three, far_two], 0, 3 * TILE)
     far_other = swap(far_theirs, "core")
 
-    w_start, _ = after((w_out, near))
+    w_start, _ = after((w_out, near_theirs))
     w_one, w_three = round_x(w_start, 1), round_x(w_start, -1)
     w_turn, _ = after((w_out, far_two))
     w_two, w_far = round_x(w_turn, 2), opposite(w_turn)
 
+    far_other, _ = after((far_other, (w_one, w_three)))
     q, kv = place_far(blocks(FAR), want, far_mine, far_other, near)
-    kv, _ = after((kv, (w_one, w_three)))
     behind = lax.ppermute(kv, "z", [(i, (i + 1) % 8) for i in range(8)])
     ahead = lax.ppermute(kv, "z", [(i, (i + 7) % 8) for i in range(8)])
     beside = swap(kv, "yl")
 
-    wf_one, wf_three, wf_two = opposite(w_one), opposite(w_three), round_x(w_far, 2)
-
     mid = kv.shape[0] // 2
     (ahead_low, behind_low), _ = after(((ahead[:mid], behind[:mid]), (w_two, w_far)))
-    cross_low = swap(jnp.where(yl == 0, ahead_low, behind_low), "yl")
+    cross = jnp.where(yl == 0, ahead_low, behind_low)
+    cross_low = swap(cross, "yl")
     onward = [(2 * i, 2 * ((i + 1) % 8)) for i in range(8)] + [(2 * i + 1, 2 * ((i + 7) % 8) + 1) for i in range(8)]
-    cross_high = lax.ppermute(beside[mid:], CTX, onward)
+    beside_high = beside[mid:]
+    cross_high = lax.ppermute(beside_high, CTX, onward)
+    (g_one, g_three, g_far), _ = after(((w_one, w_three, w_far), (cross, beside_high)))
+    wf_one, wf_three, wf_two = opposite(g_one), opposite(g_three), round_x(g_far, 2)
 
     state = attend(index, count, q, [kv, behind, beside, ahead], (24, slots), together=4)
     attended = attend(cross_index, cross_count, q, [cross_low, cross_high], (6, tiles), state, together=4)

time: 151 us -> 159 us (1.053)
  waiting for transfers between devices: 49 us -> 64 us
  starting transfers between devices: 50.8 us -> 43.1 us
    ppermute x1, waiting for transfers between devices: 16 us -> 0.01 us  [body(): ahead = lax.ppermute(kv, 'z', [(i, (i + 7) % 8) for i in range(8)])]
    ppermute x8, waiting for transfers between devices: 5.62 us -> 19.9 us  [swap(): return lax.ppermute(array, axis, [(0, 1), (1, 0)])]
    ppermute x10, waiting for transfers between devices: 18.4 us -> 25.8 us  [round_x(): return lax.ppermute(array, 'x', [(i, (i + by) % 4) for i in range(4)])]
    ppermute x3, waiting for transfers between devices: 8.88 us -> 15.5 us  [opposite(): return lax.ppermute(array, ('yl', 'yh'), [(i, 3 - i) for i in range(4)])]
    ppermute x10, starting transfers between devices: 12.4 us -> 8.41 us  [round_x(): return lax.ppermute(array, 'x', [(i, (i + by) % 4) for i in range(4)])]
    all_to_all x1, starting transfers between devices: 7.96 us -> 4.5 us  [body(): lax.all_to_all(attended.reshape(8, 2 * TILE, TILE), CHIPS, split_axis=0,...]
    ppermute x3, starting transfers between devices: 7.19 us -> 4.1 us  [opposite(): return lax.ppermute(array, ('yl', 'yh'), [(i, 3 - i) for i in range(4)])]
    ppermute x1, waiting for transfers between devices: 0.01 us -> 2.77 us  [body(): behind = lax.ppermute(kv, 'z', [(i, (i + 1) % 8) for i in range(8)])]
  transfers between devices with their start and end apart: 25 -> 25, of which waited for: 11 -> 12; matrix products, arithmetic and copies ran while one was open for 5% -> 4% of each run, Pallas kernels for 25% -> 20%
where the time goes in v6:
time: 159 us
  waiting for transfers between devices  64 us (40%)
  starting transfers between devices  43.1 us (27%)
  Pallas kernels  41.3 us (26%)
  other arithmetic  6.2 us (4%)
  local copies, waits for them, and re-layouts  3.99 us (3%)
    ppermute x10, waiting for transfers between devices, round_x(): return lax.ppermute(array, 'x', [(i, (i + by) % 4) for i in range(4)])  25.8 us
    ppermute x8, waiting for transfers between devices, swap(): return lax.ppermute(array, axis, [(0, 1), (1, 0)])  19.9 us
    ppermute x8, starting transfers between devices, swap(): return lax.ppermute(array, axis, [(0, 1), (1, 0)])  18.8 us
    pallas_call x2, Pallas kernels, attend(): pl.pallas_call(functools.partial(attend_kernel, sizes, together, len(fram...  16.5 us
    ppermute x3, waiting for transfers between devices, opposite(): return lax.ppermute(array, ('yl', 'yh'), [(i, 3 - i) for i in range(4)])  15.5 us
    pallas_call x2, Pallas kernels, qkv(): pl.pallas_call(functools.partial(qkv_kernel, heights, first, chunks), out...  11.3 us
    ppermute x10, starting transfers between devices, round_x(): return lax.ppermute(array, 'x', [(i, (i + by) % 4) for i in range(4)])  8.41 us
    pallas_call x1, Pallas kernels, place_far(): pl.pallas_call(place_far_kernel, out_shape=(pltpu.HBM((n, TILE), BF), jax...  5.35 us
  transfers between devices with their start and end apart: 25, of which 12 were waited for; matrix products, arithmetic and copies ran while one was open for 4% of the time, Pallas kernels for 20%

profile of v6, /device:TPU:1, one launch (start us, length us, event | category | flops | bytes accessed | tf_op | source)
XLA Modules:
  0.0 158.8 jit_solution(7451130087343251346)
XLA Ops:
  0.0 3.2 %collective-permute-start.5 = (bf16[3072,384]{1,0:T(8,128)(2,1)}, bf16[3072,384]{1,0:T(8,128)(2,1)}, u32[]{:S(2)}, u32[]{:S(2)}) collective-permute-start(bf16[3072,384]{1,0:T(8,128)(2,1)} %own_ref.3), channel_id=1, source_target_pairs={{0,1},{1,0},{2,3},{3,2},{4,5},{5,4},{6,7},{7,6},{8,9},{9,8},{10,11... | collective-permute-start | bytes 7077896 | tf_op jit(solution)/shard_map/ppermute | solution.py:38
  4.7 2.2 %collective-permute-start.6 = (bf16[128,3072]{1,0:T(8,128)(2,1)}, bf16[128,3072]{1,0:T(8,128)(2,1)S(1)}, u32[]{:S(2)}, u32[]{:S(2)}) collective-permute-start(bf16[128,3072]{1,0:T(8,128)(2,1)} %refs_0_.2), channel_id=1, source_target_pairs={{0,8},{8,0},{1,9},{9,1},{2,10},{10,2},{3,11},{11,3},{4,12},{12,4},... | collective-permute-start | bytes 2359304 | tf_op jit(solution)/shard_map/ppermute | solution.py:38
  8.7 14.0 %collective-permute-done.2.refs_2_ = bf16[128,3072]{1,0:T(8,128)(2,1)S(1)} collective-permute-done((bf16[128,3072]{1,0:T(8,128)(2,1)}, bf16[128,3072]{1,0:T(8,128)(2,1)S(1)}, u32[]{:S(2)}, u32[]{:S(2)}) %collective-permute-start.2) | collective-permute-done | bytes 786464 | tf_op jit(solution)/shard_map/ppermute | solution.py:34
  22.7 2.0 %collective-permute-start.3 = (bf16[64,3072]{1,0:T(8,128)(2,1)S(1)}, bf16[64,3072]{1,0:T(8,128)(2,1)S(1)}, u32[]{:S(2)}, u32[]{:S(2)}) collective-permute-start(bf16[64,3072]{1,0:T(8,128)(2,1)S(1)} %slice.21), channel_id=1, source_target_pairs={{0,6},{2,0},{4,2},{6,4},{1,7},{3,1},{5,3},{7,5},{8,14},{10,8},{12,... | collective-permute-start | bytes 1179656 | tf_op jit(solution)/shard_map/ppermute | solution.py:34
  25.0 2.6 %collective-permute-start.9 = (bf16[128,3072]{1,0:T(8,128)(2,1)S(1)}, bf16[128,3072]{1,0:T(8,128)(2,1)}, u32[]{:S(2)}, u32[]{:S(2)}) collective-permute-start(bf16[128,3072]{1,0:T(8,128)(2,1)S(1)} %collective-permute-done.6.refs_3_), channel_id=1, source_target_pairs={{0,6},{2,0},{4,2},{6,4},{1,7},{3,1},{5,3},{7,5},{8,14},{10,8},{12,... | collective-permute-start | bytes 2359304 | tf_op jit(solution)/shard_map/ppermute | solution.py:34
  27.6 5.0 %collective-permute-done.3.refs_1_ = bf16[64,3072]{1,0:T(8,128)(2,1)S(1)} collective-permute-done((bf16[64,3072]{1,0:T(8,128)(2,1)S(1)}, bf16[64,3072]{1,0:T(8,128)(2,1)S(1)}, u32[]{:S(2)}, u32[]{:S(2)}) %collective-permute-start.3) | collective-permute-done | bytes 393248 | tf_op jit(solution)/shard_map/ppermute | solution.py:34
  32.6 3.0 %collective-permute-done.1.refs_0_ = bf16[64,3072]{1,0:T(8,128)(2,1)S(1)} collective-permute-done((bf16[64,3072]{1,0:T(8,128)(2,1)S(1)}, bf16[64,3072]{1,0:T(8,128)(2,1)S(1)}, u32[]{:S(2)}, u32[]{:S(2)}) %collective-permute-start.1) | collective-permute-done | bytes 393248 | tf_op jit(solution)/shard_map/ppermute | solution.py:34
  36.5 2.9 %collective-permute-start.4 = (bf16[128,3072]{1,0:T(8,128)(2,1)}, bf16[128,3072]{1,0:T(8,128)(2,1)}, u32[]{:S(2)}, u32[]{:S(2)}) collective-permute-start(bf16[128,3072]{1,0:T(8,128)(2,1)} %pad_maximum_fusion), channel_id=1, source_target_pairs={{0,8},{8,0},{1,9},{9,1},{2,10},{10,2},{3,11},{11,3},{4,12},{12,4},... | collective-permute-start | bytes 2359304 | tf_op jit(solution)/shard_map/ppermute | solution.py:38
  39.4 5.7 %shard_map.64 = (bf16[512,384]{1,0:T(8,128)(2,1)S(1)}, bf16[512,384]{1,0:T(8,128)(2,1)}) custom-call(bf16[3072,384]{1,0:T(8,128)(2,1)} %own_ref.3, bf16[3072,384]{1,0:T(8,128)(2,1)} %collective-permute-done.5.other_ref, bf16[128,3072]{1,0:T(8,128)(2,1)S(1)} %copy-done, bf16[128,3072]{1,0:T(8,128)(2,1)S(1)} %collective-permute-done.refs_1_, ...), custom_call_target="tpu_custom_call" | custom-call | flops 786432 | bytes 1024 | tf_op jit(solution)/shard_map/pallas_call | solution.py:79
  45.9 3.9 %collective-permute-start.7 = (bf16[512,384]{1,0:T(8,128)(2,1)}, bf16[512,384]{1,0:T(8,128)(2,1)S(1)}, u32[]{:S(2)}, u32[]{:S(2)}) collective-permute-start(bf16[512,384]{1,0:T(8,128)(2,1)} %get-tuple-element.31), channel_id=1, source_target_pairs={{0,1},{1,0},{2,3},{3,2},{4,5},{5,4},{6,7},{7,6},{8,9},{9,8},{10,11... | collective-permute-start | bytes 1179656 | tf_op jit(solution)/shard_map/ppermute | solution.py:38
  55.2 3.6 %shard_map.65.near_ref = bf16[2048,384]{1,0:T(8,128)(2,1)S(1)} custom-call(f32[8]{0:T(128)S(1)} %convert_element_type.18.block_ref, s32[2048,1]{1,0:T(8,128)S(1)} %copy.9.want_ref, bf16[512,384]{1,0:T(8,128)(2,1)S(1)} %copy-done.2, bf16[512,384]{1,0:T(8,128)(2,1)S(1)} %collective-permute-done.7.second_ref), custom_call_target="tpu_custom_call" | custom-call | flops 1610612736 | bytes 4194304 | tf_op jit(solution)/shard_map/pallas_call | solution.py:146
  58.8 1.1 copy-done.3
  60.0 5.7 %shard_map.66 = (bf16[512,384]{1,0:T(8,128)(2,1)S(1)}, bf16[512,384]{1,0:T(8,128)(2,1)S(1)}) custom-call(bf16[3072,384]{1,0:T(8,128)(2,1)} %own_ref.3, bf16[3072,384]{1,0:T(8,128)(2,1)} %collective-permute-done.5.other_ref, bf16[64,3072]{1,0:T(8,128)(2,1)S(1)} %collective-permute-done.1.refs_0_, bf16[64,3072]{1,0:T(8,128)(2,1)S(1)} %collective-permute-done.3.refs_1_, ...), custom_call_target="tpu_custom_call" | custom-call | flops 786432 | bytes 1024 | tf_op jit(solution)/shard_map/pallas_call | solution.py:79
  66.4 1.3 collective-permute-done.10.second_ref
  67.7 2.7 %collective-permute-done.12.refs_2_ = bf16[128,3072]{1,0:T(8,128)(2,1)} collective-permute-done((bf16[128,3072]{1,0:T(8,128)(2,1)}, bf16[128,3072]{1,0:T(8,128)(2,1)}, u32[]{:S(2)}, u32[]{:S(2)}) %collective-permute-start.12) | collective-permute-done | bytes 786464 | tf_op jit(solution)/shard_map/ppermute | solution.py:34
  70.4 1.2 collective-permute-done.11.refs_1_
  71.6 5.4 %shard_map.67 = (bf16[2048,128]{1,0:T(8,128)(2,1)}, bf16[2048,256]{1,0:T(8,128)(2,1)}) custom-call(f32[8]{0:T(128)S(1)} %convert_element_type.21.block_ref, s32[2048,1]{1,0:T(8,128)S(1)} %copy.9.want_ref, bf16[512,384]{1,0:T(8,128)(2,1)S(1)} %get-tuple-element.36.first_ref, bf16[512,384]{1,0:T(8,128)(2,1)S(1)} %collective-permute-done.10.second_ref, ...), custom_call_target="tpu_custom_call" | custom-call | flops 1610612736 | bytes 4194304 | tf_op jit(solution)/shard_map/pallas_call | solution.py:158
  77.4 1.6 %collective-permute-start.14 = (bf16[2048,256]{1,0:T(8,128)(2,1)}, bf16[2048,256]{1,0:T(8,128)(2,1)S(1)}, u32[]{:S(2)}, u32[]{:S(2)}) collective-permute-start(bf16[2048,256]{1,0:T(8,128)(2,1)} %get-tuple-element.42.refs_0_), channel_id=1, source_target_pairs={{0,32},{32,64},{64,96},{96,128},{128,160},{160,192},{192,224},{224... | collective-permute-start | bytes 3145736 | tf_op jit(solution)/shard_map/ppermute | solution.py:362
  79.0 3.9 %collective-permute-start.13 = (bf16[2048,256]{1,0:T(8,128)(2,1)}, bf16[2048,256]{1,0:T(8,128)(2,1)S(1)}, u32[]{:S(2)}, u32[]{:S(2)}) collective-permute-start(bf16[2048,256]{1,0:T(8,128)(2,1)} %get-tuple-element.42.refs_0_), channel_id=1, source_target_pairs={{0,224},{32,0},{64,32},{96,64},{128,96},{160,128},{192,160},{224,1... | collective-permute-start | bytes 3145736 | tf_op jit(solution)/shard_map/ppermute | solution.py:363
  83.0 1.4 collective-permute-start.16
  84.5 16.3 %collective-permute-done.18.refs_2_ = bf16[2048,256]{1,0:T(8,128)(2,1)S(1)} collective-permute-done((bf16[2048,256]{1,0:T(8,128)(2,1)}, bf16[2048,256]{1,0:T(8,128)(2,1)S(1)}, u32[]{:S(2)}, u32[]{:S(2)}) %collective-permute-start.18) | collective-permute-done | bytes 1048608 | tf_op jit(solution)/shard_map/ppermute | solution.py:38
  100.8 1.7 %collective-permute-start.19 = (bf16[1024,256]{1,0:T(8,128)(2,1)S(1)}, bf16[1024,256]{1,0:T(8,128)(2,1)S(1)}, u32[]{:S(2)}, u32[]{:S(2)}) collective-permute-start(bf16[1024,256]{1,0:T(8,128)(2,1)S(1)} %slice.24), channel_id=1, source_target_pairs={{0,32},{32,64},{64,96},{96,128},{128,160},{160,192},{192,224},{224... | collective-permute-start | bytes 1572872 | tf_op jit(solution)/shard_map/ppermute | solution.py:372
  102.5 2.8 %collective-permute-done.14.refs_1_ = bf16[2048,256]{1,0:T(8,128)(2,1)S(1)} collective-permute-done((bf16[2048,256]{1,0:T(8,128)(2,1)}, bf16[2048,256]{1,0:T(8,128)(2,1)S(1)}, u32[]{:S(2)}, u32[]{:S(2)}) %collective-permute-start.14) | collective-permute-done | bytes 1048608 | tf_op jit(solution)/shard_map/ppermute | solution.py:362
  105.5 1.9 %collective-permute-start.17 = (bf16[1024,256]{1,0:T(8,128)(2,1)S(1)}, bf16[1024,256]{1,0:T(8,128)(2,1)S(1)}, u32[]{:S(2)}, u32[]{:S(2)}) collective-permute-start(bf16[1024,256]{1,0:T(8,128)(2,1)S(1)} %broadcast_select_fusion), channel_id=1, source_target_pairs={{0,16},{16,0},{1,17},{17,1},{2,18},{18,2},{3,19},{19,3},{4,20},{20... | collective-permute-start | bytes 1572872 | tf_op jit(solution)/shard_map/ppermute | solution.py:38
  107.3 1.7 %collective-permute-start.20 = (bf16[128,3072]{1,0:T(8,128)(2,1)}, bf16[128,3072]{1,0:T(8,128)(2,1)}, u32[]{:S(2)}, u32[]{:S(2)}) collective-permute-start(bf16[128,3072]{1,0:T(8,128)(2,1)} %collective-permute-done.11.refs_1_), channel_id=1, source_target_pairs={{0,24},{8,16},{16,8},{24,0},{1,25},{9,17},{17,9},{25,1},{2,26},{10... | collective-permute-start | bytes 2359304 | tf_op jit(solution)/shard_map/ppermute | solution.py:42
  111.1 10.4 %shard_map.68 = (f32[2048,128]{1,0:T(8,128)S(1)}, f32[2048,128]{1,0:T(8,128)S(1)}) custom-call(s32[16,30]{1,0:T(8,128)S(1)} %copy.14.index_ref, s32[16]{0:T(128)S(1)} %get-tuple-element.47.count_ref, bf16[2048,128]{1,0:T(8,128)(2,1)S(1)} %copy-done.4, bf16[2048,256]{1,0:T(8,128)(2,1)} %get-tuple-element.42.refs_0_, ...), custom_call_target="tpu_custom_call" | custom-call | flops 16106127360 | bytes 6291456 | tf_op jit(solution)/shard_map/pallas_call | solution.py:252
  121.5 6.2 %shard_map.69 = bf16[2048,128]{1,0:T(8,128)(2,1)} custom-call(s32[16,16]{1,0:T(8,128)S(1)} %select_reduce_fusion.3.index_ref, s32[16]{0:T(128)S(1)} %get-tuple-element.33.count_ref, bf16[2048,128]{1,0:T(8,128)(2,1)S(1)} %copy-done.4, bf16[1024,256]{1,0:T(8,128)(2,1)S(1)} %collective-permute-done.17.refs_0_, ...), custom_call_target="tpu_custom_call" | custom-call | flops 8589934592 | bytes 6291456 | tf_op jit(solution)/shard_map/pallas_call | solution.py:252
  127.6 4.5 %all-to-all-start = ((bf16[8,256,128]{2,1,0:T(8,128)(2,1)}), bf16[8,256,128]{2,1,0:T(8,128)(2,1)S(1)}, u32[]{:S(2)}, u32[]{:S(2)}) async-start(bf16[8,256,128]{2,1,0:T(8,128)(2,1)} %bitcast.26), calls=%async_computation | async-start | bytes 1048576 | tf_op jit(solution)/shard_map/all_to_all | solution.py:379
  132.2 15.5 %collective-permute-done.21.refs_6_ = bf16[128,3072]{1,0:T(8,128)(2,1)} collective-permute-done((bf16[128,3072]{1,0:T(8,128)(2,1)}, bf16[128,3072]{1,0:T(8,128)(2,1)}, u32[]{:S(2)}, u32[]{:S(2)}) %collective-permute-start.21) | collective-permute-done | bytes 786464 | tf_op jit(solution)/shard_map/ppermute | solution.py:42
  147.8 4.4 %shard_map.70 = (f32[128,3072]{1,0:T(8,128)S(1)}, bf16[128,3072]{1,0:T(8,128)(2,1)S(1)}) custom-call(s32[9]{0:T(128)S(1)} %stack.93.order_ref, bf16[8,256,128]{2,1,0:T(8,128)(2,1)S(1)} %all-to-all-done.att_ref, bf16[128,3072]{1,0:T(8,128)(2,1)} %refs_0_.3, bf16[128,3072]{1,0:T(8,128)(2,1)} %collective-permute-done.11.refs_1_, ...), custom_call_target="tpu_custom_call" | custom-call | flops 1610612736 | bytes 10485760 | tf_op jit(solution)/shard_map/pallas_call | solution.py:298
  152.2 3.6 %collective-permute-start.23 = (bf16[128,3072]{1,0:T(8,128)(2,1)S(1)}, bf16[128,3072]{1,0:T(8,128)(2,1)S(1)}, u32[]{:S(2)}, u32[]{:S(2)}) collective-permute-start(bf16[128,3072]{1,0:T(8,128)(2,1)S(1)} %get-tuple-element.54), channel_id=1, source_target_pairs={{0,1},{1,0},{2,3},{3,2},{4,5},{5,4},{6,7},{7,6},{8,9},{9,8},{10,11... | collective-permute-start | bytes 2359304 | tf_op jit(solution)/shard_map/ppermute | solution.py:38
  155.8 1.9 %collective-permute-done.23 = bf16[128,3072]{1,0:T(8,128)(2,1)S(1)} collective-permute-done((bf16[128,3072]{1,0:T(8,128)(2,1)S(1)}, bf16[128,3072]{1,0:T(8,128)(2,1)S(1)}, u32[]{:S(2)}, u32[]{:S(2)}) %collective-permute-start.23) | collective-permute-done | bytes 786464 | tf_op jit(solution)/shard_map/ppermute | solution.py:38
  (65 shorter events, 15.4 us)
Async XLA Ops:
  0.0 39.4 %collective-permute-start.5 = (bf16[3072,384]{1,0:T(8,128)(2,1)}, bf16[3072,384]{1,0:T(8,128)(2,1)}, u32[]{:S(2)}, u32[]{:S(2)}) collective-permute-start(bf16[3072,384]{1,0:T(8,128)(2,1)} %own_ref.3), channel_id=1, source_target_pairs={{0,1},{1,0},{2,3},{3,2},{4,5},{5,4},{6,7},{7,6},{8,9},{9,8},{10,11... | collective-permute-start | bytes 7077896 | tf_op jit(solution)/shard_map/ppermute | solution.py:38
  3.2 19.4 %collective-permute-start.2 = (bf16[128,3072]{1,0:T(8,128)(2,1)}, bf16[128,3072]{1,0:T(8,128)(2,1)S(1)}, u32[]{:S(2)}, u32[]{:S(2)}) collective-permute-start(bf16[128,3072]{1,0:T(8,128)(2,1)} %refs_0_.2), channel_id=1, source_target_pairs={{0,6},{2,0},{4,2},{6,4},{1,7},{3,1},{5,3},{7,5},{8,14},{10,8},{12,... | collective-permute-start | bytes 2359304 | tf_op jit(solution)/shard_map/ppermute | solution.py:34
  4.0 20.7 %collective-permute-start = (bf16[128,3072]{1,0:T(8,128)(2,1)}, bf16[128,3072]{1,0:T(8,128)(2,1)S(1)}, u32[]{:S(2)}, u32[]{:S(2)}) collective-permute-start(bf16[128,3072]{1,0:T(8,128)(2,1)} %refs_0_.2), channel_id=1, source_target_pairs={{0,2},{2,4},{4,6},{6,0},{1,3},{3,5},{5,7},{7,1},{8,10},{10,12},{12... | collective-permute-start | bytes 2359304 | tf_op jit(solution)/shard_map/ppermute | solution.py:34
  4.7 20.3 %collective-permute-start.6 = (bf16[128,3072]{1,0:T(8,128)(2,1)}, bf16[128,3072]{1,0:T(8,128)(2,1)S(1)}, u32[]{:S(2)}, u32[]{:S(2)}) collective-permute-start(bf16[128,3072]{1,0:T(8,128)(2,1)} %refs_0_.2), channel_id=1, source_target_pairs={{0,8},{8,0},{1,9},{9,1},{2,10},{10,2},{3,11},{11,3},{4,12},{12,4},... | collective-permute-start | bytes 2359304 | tf_op jit(solution)/shard_map/ppermute | solution.py:38
  8.7 30.8 %copy-start = (bf16[128,3072]{1,0:T(8,128)(2,1)S(1)}, bf16[128,3072]{1,0:T(8,128)(2,1)}, u32[]{:S(2)}) copy-start(bf16[128,3072]{1,0:T(8,128)(2,1)} %refs_0_.2) | copy-start | bytes 2359300
  22.7 9.9 %collective-permute-start.3 = (bf16[64,3072]{1,0:T(8,128)(2,1)S(1)}, bf16[64,3072]{1,0:T(8,128)(2,1)S(1)}, u32[]{:S(2)}, u32[]{:S(2)}) collective-permute-start(bf16[64,3072]{1,0:T(8,128)(2,1)S(1)} %slice.21), channel_id=1, source_target_pairs={{0,6},{2,0},{4,2},{6,4},{1,7},{3,1},{5,3},{7,5},{8,14},{10,8},{12,... | collective-permute-start | bytes 1179656 | tf_op jit(solution)/shard_map/ppermute | solution.py:34
  24.7 10.8 %collective-permute-start.1 = (bf16[64,3072]{1,0:T(8,128)(2,1)S(1)}, bf16[64,3072]{1,0:T(8,128)(2,1)S(1)}, u32[]{:S(2)}, u32[]{:S(2)}) collective-permute-start(bf16[64,3072]{1,0:T(8,128)(2,1)S(1)} %slice.20), channel_id=1, source_target_pairs={{0,2},{2,4},{4,6},{6,0},{1,3},{3,5},{5,7},{7,1},{8,10},{10,12},{12... | collective-permute-start | bytes 1179656 | tf_op jit(solution)/shard_map/ppermute | solution.py:34
  25.0 35.0 %collective-permute-start.9 = (bf16[128,3072]{1,0:T(8,128)(2,1)S(1)}, bf16[128,3072]{1,0:T(8,128)(2,1)}, u32[]{:S(2)}, u32[]{:S(2)}) collective-permute-start(bf16[128,3072]{1,0:T(8,128)(2,1)S(1)} %collective-permute-done.6.refs_3_), channel_id=1, source_target_pairs={{0,6},{2,0},{4,2},{6,4},{1,7},{3,1},{5,3},{7,5},{8,14},{10,8},{12,... | collective-permute-start | bytes 2359304 | tf_op jit(solution)/shard_map/ppermute | solution.py:34
  27.6 32.4 %collective-permute-start.8 = (bf16[128,3072]{1,0:T(8,128)(2,1)S(1)}, bf16[128,3072]{1,0:T(8,128)(2,1)}, u32[]{:S(2)}, u32[]{:S(2)}) collective-permute-start(bf16[128,3072]{1,0:T(8,128)(2,1)S(1)} %collective-permute-done.6.refs_3_), channel_id=1, source_target_pairs={{0,2},{2,4},{4,6},{6,0},{1,3},{3,5},{5,7},{7,1},{8,10},{10,12},{12... | collective-permute-start | bytes 2359304 | tf_op jit(solution)/shard_map/ppermute | solution.py:34
  36.5 16.2 %copy-start.5 = (s32[1,2048]{1,0:T(1,128)S(1)}, s32[1,2048]{1,0:T(1,128)}, u32[]{:S(2)}) copy-start(s32[1,2048]{1,0:T(1,128)} %param.9) | copy-start | bytes 24580
  36.5 23.5 %collective-permute-start.4 = (bf16[128,3072]{1,0:T(8,128)(2,1)}, bf16[128,3072]{1,0:T(8,128)(2,1)}, u32[]{:S(2)}, u32[]{:S(2)}) collective-permute-start(bf16[128,3072]{1,0:T(8,128)(2,1)} %pad_maximum_fusion), channel_id=1, source_target_pairs={{0,8},{8,0},{1,9},{9,1},{2,10},{10,2},{3,11},{11,3},{4,12},{12,4},... | collective-permute-start | bytes 2359304 | tf_op jit(solution)/shard_map/ppermute | solution.py:38
  45.1 0.8 copy-start.1
  45.9 5.4 %collective-permute-start.7 = (bf16[512,384]{1,0:T(8,128)(2,1)}, bf16[512,384]{1,0:T(8,128)(2,1)S(1)}, u32[]{:S(2)}, u32[]{:S(2)}) collective-permute-start(bf16[512,384]{1,0:T(8,128)(2,1)} %get-tuple-element.31), channel_id=1, source_target_pairs={{0,1},{1,0},{2,3},{3,2},{4,5},{5,4},{6,7},{7,6},{8,9},{9,8},{10,11... | collective-permute-start | bytes 1179656 | tf_op jit(solution)/shard_map/ppermute | solution.py:38
  50.9 19.5 %collective-permute-start.12 = (bf16[128,3072]{1,0:T(8,128)(2,1)}, bf16[128,3072]{1,0:T(8,128)(2,1)}, u32[]{:S(2)}, u32[]{:S(2)}) collective-permute-start(bf16[128,3072]{1,0:T(8,128)(2,1)} %refs_0_.3), channel_id=1, source_target_pairs={{0,6},{2,0},{4,2},{6,4},{1,7},{3,1},{5,3},{7,5},{8,14},{10,8},{12,... | collective-permute-start | bytes 2359304 | tf_op jit(solution)/shard_map/ppermute | solution.py:34
  51.3 20.3 %collective-permute-start.11 = (bf16[128,3072]{1,0:T(8,128)(2,1)}, bf16[128,3072]{1,0:T(8,128)(2,1)}, u32[]{:S(2)}, u32[]{:S(2)}) collective-permute-start(bf16[128,3072]{1,0:T(8,128)(2,1)} %refs_0_.3), channel_id=1, source_target_pairs={{0,2},{2,4},{4,6},{6,0},{1,3},{3,5},{5,7},{7,1},{8,10},{10,12},{12... | collective-permute-start | bytes 2359304 | tf_op jit(solution)/shard_map/ppermute | solution.py:34
  54.2 1.0 copy-start.2
  58.8 1.1 copy-start.3
  65.7 2.0 %collective-permute-start.10 = (bf16[512,384]{1,0:T(8,128)(2,1)S(1)}, bf16[512,384]{1,0:T(8,128)(2,1)S(1)}, u32[]{:S(2)}, u32[]{:S(2)}) collective-permute-start(bf16[512,384]{1,0:T(8,128)(2,1)S(1)} %get-tuple-element.37), channel_id=1, source_target_pairs={{0,1},{1,0},{2,3},{3,2},{4,5},{5,4},{6,7},{7,6},{8,9},{9,8},{10,11... | collective-permute-start | bytes 1179656 | tf_op jit(solution)/shard_map/ppermute | solution.py:38
  76.9 23.8 %collective-permute-start.18 = (bf16[2048,256]{1,0:T(8,128)(2,1)}, bf16[2048,256]{1,0:T(8,128)(2,1)S(1)}, u32[]{:S(2)}, u32[]{:S(2)}) collective-permute-start(bf16[2048,256]{1,0:T(8,128)(2,1)} %get-tuple-element.42.refs_0_), channel_id=1, source_target_pairs={{0,16},{16,0},{1,17},{17,1},{2,18},{18,2},{3,19},{19,3},{4,20},{20... | collective-permute-start | bytes 3145736 | tf_op jit(solution)/shard_map/ppermute | solution.py:38
  77.4 27.9 %collective-permute-start.14 = (bf16[2048,256]{1,0:T(8,128)(2,1)}, bf16[2048,256]{1,0:T(8,128)(2,1)S(1)}, u32[]{:S(2)}, u32[]{:S(2)}) collective-permute-start(bf16[2048,256]{1,0:T(8,128)(2,1)} %get-tuple-element.42.refs_0_), channel_id=1, source_target_pairs={{0,32},{32,64},{64,96},{96,128},{128,160},{160,192},{192,224},{224... | collective-permute-start | bytes 3145736 | tf_op jit(solution)/shard_map/ppermute | solution.py:362
  79.0 26.3 %collective-permute-start.13 = (bf16[2048,256]{1,0:T(8,128)(2,1)}, bf16[2048,256]{1,0:T(8,128)(2,1)S(1)}, u32[]{:S(2)}, u32[]{:S(2)}) collective-permute-start(bf16[2048,256]{1,0:T(8,128)(2,1)} %get-tuple-element.42.refs_0_), channel_id=1, source_target_pairs={{0,224},{32,0},{64,32},{96,64},{128,96},{160,128},{192,160},{224,1... | collective-permute-start | bytes 3145736 | tf_op jit(solution)/shard_map/ppermute | solution.py:363
  83.0 22.4 %collective-permute-start.16 = (bf16[128,3072]{1,0:T(8,128)(2,1)}, bf16[128,3072]{1,0:T(8,128)(2,1)}, u32[]{:S(2)}, u32[]{:S(2)}) collective-permute-start(bf16[128,3072]{1,0:T(8,128)(2,1)} %refs_0_.3), channel_id=1, source_target_pairs={{0,24},{8,16},{16,8},{24,0},{1,25},{9,17},{17,9},{25,1},{2,26},{10... | collective-permute-start | bytes 2359304 | tf_op jit(solution)/shard_map/ppermute | solution.py:42
  84.4 21.0 %collective-permute-start.15 = (bf16[128,3072]{1,0:T(8,128)(2,1)}, bf16[128,3072]{1,0:T(8,128)(2,1)}, u32[]{:S(2)}, u32[]{:S(2)}) collective-permute-start(bf16[128,3072]{1,0:T(8,128)(2,1)} %refs_0_.3), channel_id=1, source_target_pairs={{0,4},{2,6},{4,0},{6,2},{1,5},{3,7},{5,1},{7,3},{8,12},{10,14},{12... | collective-permute-start | bytes 2359304 | tf_op jit(solution)/shard_map/ppermute | solution.py:34
  100.8 20.7 %collective-permute-start.19 = (bf16[1024,256]{1,0:T(8,128)(2,1)S(1)}, bf16[1024,256]{1,0:T(8,128)(2,1)S(1)}, u32[]{:S(2)}, u32[]{:S(2)}) collective-permute-start(bf16[1024,256]{1,0:T(8,128)(2,1)S(1)} %slice.24), channel_id=1, source_target_pairs={{0,32},{32,64},{64,96},{96,128},{128,160},{160,192},{192,224},{224... | collective-permute-start | bytes 1572872 | tf_op jit(solution)/shard_map/ppermute | solution.py:372
  105.3 5.7 %copy-start.4 = (bf16[2048,128]{1,0:T(8,128)(2,1)S(1)}, bf16[2048,128]{1,0:T(8,128)(2,1)}, u32[]{:S(2)}) copy-start(bf16[2048,128]{1,0:T(8,128)(2,1)} %get-tuple-element.41.q_ref) | copy-start | bytes 1572868
  105.5 16.0 %collective-permute-start.17 = (bf16[1024,256]{1,0:T(8,128)(2,1)S(1)}, bf16[1024,256]{1,0:T(8,128)(2,1)S(1)}, u32[]{:S(2)}, u32[]{:S(2)}) collective-permute-start(bf16[1024,256]{1,0:T(8,128)(2,1)S(1)} %broadcast_select_fusion), channel_id=1, source_target_pairs={{0,16},{16,0},{1,17},{17,1},{2,18},{18,2},{3,19},{19,3},{4,20},{20... | collective-permute-start | bytes 1572872 | tf_op jit(solution)/shard_map/ppermute | solution.py:38
  107.3 24.9 %collective-permute-start.20 = (bf16[128,3072]{1,0:T(8,128)(2,1)}, bf16[128,3072]{1,0:T(8,128)(2,1)}, u32[]{:S(2)}, u32[]{:S(2)}) collective-permute-start(bf16[128,3072]{1,0:T(8,128)(2,1)} %collective-permute-done.11.refs_1_), channel_id=1, source_target_pairs={{0,24},{8,16},{16,8},{24,0},{1,25},{9,17},{17,9},{25,1},{2,26},{10... | collective-permute-start | bytes 2359304 | tf_op jit(solution)/shard_map/ppermute | solution.py:42
  109.0 38.7 %collective-permute-start.21 = (bf16[128,3072]{1,0:T(8,128)(2,1)}, bf16[128,3072]{1,0:T(8,128)(2,1)}, u32[]{:S(2)}, u32[]{:S(2)}) collective-permute-start(bf16[128,3072]{1,0:T(8,128)(2,1)} %collective-permute-done.12.refs_2_), channel_id=1, source_target_pairs={{0,24},{8,16},{16,8},{24,0},{1,25},{9,17},{17,9},{25,1},{2,26},{10... | collective-permute-start | bytes 2359304 | tf_op jit(solution)/shard_map/ppermute | solution.py:42
  110.0 37.8 %collective-permute-start.22 = (bf16[128,3072]{1,0:T(8,128)(2,1)}, bf16[128,3072]{1,0:T(8,128)(2,1)}, u32[]{:S(2)}, u32[]{:S(2)}) collective-permute-start(bf16[128,3072]{1,0:T(8,128)(2,1)} %collective-permute-done.16.refs_4_), channel_id=1, source_target_pairs={{0,4},{2,6},{4,0},{6,2},{1,5},{3,7},{5,1},{7,3},{8,12},{10,14},{12... | collective-permute-start | bytes 2359304 | tf_op jit(solution)/shard_map/ppermute | solution.py:34
  127.6 20.1 %all-to-all-start = ((bf16[8,256,128]{2,1,0:T(8,128)(2,1)}), bf16[8,256,128]{2,1,0:T(8,128)(2,1)S(1)}, u32[]{:S(2)}, u32[]{:S(2)}) async-start(bf16[8,256,128]{2,1,0:T(8,128)(2,1)} %bitcast.26), calls=%async_computation | async-start | bytes 1048576 | tf_op jit(solution)/shard_map/all_to_all | solution.py:379
  152.2 5.5 %collective-permute-start.23 = (bf16[128,3072]{1,0:T(8,128)(2,1)S(1)}, bf16[128,3072]{1,0:T(8,128)(2,1)S(1)}, u32[]{:S(2)}, u32[]{:S(2)}) collective-permute-start(bf16[128,3072]{1,0:T(8,128)(2,1)S(1)} %get-tuple-element.54), channel_id=1, source_target_pairs={{0,1},{1,0},{2,3},{3,2},{4,5},{5,4},{6,7},{7,6},{8,9},{9,8},{10,11... | collective-permute-start | bytes 2359304 | tf_op jit(solution)/shard_map/ppermute | solution.py:38

commit v7 on v6

--- a/solution.py
+++ b/solution.py
@@ -42,29 +42,24 @@
     return lax.ppermute(array, ("yl", "yh"), [(i, 3 - i) for i in range(4)])
 
 
-def qkv_kernel(heights, first, chunks, own_ref, other_ref, *refs):
-    pieces = refs[: len(heights)]
-    mine_ref, theirs_ref, rows_ref, w_ref, sum_ref, sems = refs[len(heights) :]
+def qkv_kernel(chunks, own_ref, other_ref, *refs):
+    pieces, (mine_ref, theirs_ref, w_ref, sum_ref, sems) = refs[:-5], refs[-5:]
     width = mine_ref.shape[1]
     span = own_ref.shape[0] // chunks
     loads = []
     for c in range(chunks):
         depth = pl.ds(c * span, span)
-        group, start = [], 0
         for side, ref in enumerate((other_ref, own_ref)):
-            group.append((ref.at[depth, first : first + width], w_ref.at[depth, side * width : (side + 1) * width]))
-        for piece, height in zip(pieces, heights):
-            group.append((piece.at[:, depth], rows_ref.at[pl.ds(start, height), depth]))
-            start += height
-        loads.append([pltpu.make_async_copy(a, b, sems.at[c, i]) for i, (a, b) in enumerate(group)])
-    for group in loads:
-        for copy in group:
-            copy.start()
-    for c, group in enumerate(loads):
-        for copy in group:
-            copy.wait()
+            target = w_ref.at[depth, side * width : (side + 1) * width]
+            loads.append(pltpu.make_async_copy(ref.at[depth, :], target, sems.at[2 * c + side]))
+    for copy in loads:
+        copy.start()
+    for c in range(chunks):
         depth = slice(c * span, (c + 1) * span)
-        done = jnp.dot(rows_ref[:, depth], w_ref[depth, :], preferred_element_type=F32)
+        rows = jnp.concatenate([piece[:, depth] for piece in pieces], axis=0)
+        loads[2 * c].wait()
+        loads[2 * c + 1].wait()
+        done = jnp.dot(rows, w_ref[depth, :], preferred_element_type=F32)
         if c > 0:
             done = done + sum_ref[...]
         if c < chunks - 1:
@@ -73,22 +68,20 @@
     mine_ref[...] = done[:, width:].astype(BF)
 
 
-def qkv(own, other, pieces, first, last):
-    heights, chunks = tuple(p.shape[0] for p in pieces), 3
-    n, depth, width = sum(heights), own.shape[0], last - first
-    return pl.pallas_call(
-        functools.partial(qkv_kernel, heights, first, chunks),
+def qkv(own, other, pieces):
+    n, depth, width, chunks = sum(p.shape[0] for p in pieces), own.shape[0], own.shape[1], 3
+    return pl.pallas_call(
+        functools.partial(qkv_kernel, chunks),
         out_shape=(jax.ShapeDtypeStruct((n, width), BF),) * 2,
-        in_specs=[WHOLE_HBM] * 2 + [WHOLE_ANY] * len(pieces),
+        in_specs=[WHOLE_HBM] * 2 + [WHOLE_VM] * len(pieces),
         out_specs=(WHOLE_VM,) * 2,
         scratch_shapes=[
-            VM((n, depth), BF),
             VM((depth, 2 * width), BF),
             VM((n, 2 * width), F32),
-            pltpu.SemaphoreType.DMA((chunks, 2 + len(pieces))),
+            pltpu.SemaphoreType.DMA((2 * chunks,)),
         ],
         compiler_params=pltpu.CompilerParams(vmem_limit_bytes=24 << 20),
-        cost_estimate=pl.CostEstimate(flops=4 * n * width, bytes_accessed=1 << 10, transcendentals=0),
+        cost_estimate=pl.CostEstimate(flops=4 * n * depth * width, bytes_accessed=8 << 20, transcendentals=0),
     )(*in_hbm((own, other)), *pieces)
 
 
@@ -103,10 +96,10 @@
     return jnp.concatenate(picks, axis=1)
 
 
-def pick(want, block_ref, first_ref, second_ref):
+def pick(want, block_ref, first_ref, second_ref, columns=slice(None)):
     hot, half = hot_rows(want, block_ref), first_ref.shape[0]
-    done = jnp.dot(hot[:, :half], first_ref[...], preferred_element_type=F32)
-    return done + jnp.dot(hot[:, half:], second_ref[...], preferred_element_type=F32)
+    done = jnp.dot(hot[:, :half], first_ref[:, columns], preferred_element_type=F32)
+    return done + jnp.dot(hot[:, half:], second_ref[:, columns], preferred_element_type=F32)
 
 
 def place_near_kernel(block_ref, want_ref, first_ref, second_ref, out_ref):
@@ -120,25 +113,27 @@
     lax.fori_loop(0, want_ref.shape[0] // rows, step, 0)
 
 
-def place_far_kernel(block_ref, want_ref, first_ref, second_ref, near_ref, q_ref, kv_ref, before_ref, sems):
-    rows = 512
+def place_far_kernel(column, turn, block_ref, want_ref, first_ref, second_ref, near_ref, out_ref, before_ref, sems):
+    rows, width = 512, out_ref.shape[1]
     steps = want_ref.shape[0] // rows
-    copies = [
-        pltpu.make_async_copy(near_ref.at[pl.ds(i * rows, rows)], before_ref.at[pl.ds(i * rows, rows)], sems.at[i])
-        for i in range(steps)
-    ]
+    columns = slice(column, column + width)
+    copies = []
+    for i in range(steps):
+        spot = pl.ds(i * rows, rows)
+        copies.append(pltpu.make_async_copy(near_ref.at[spot, columns], before_ref.at[spot], sems.at[i]))
     for copy in copies:
         copy.start()
     for i, copy in enumerate(copies):
         spot = slice(i * rows, (i + 1) * rows)
-        done = pick(want_ref[spot, :], block_ref, first_ref, second_ref)
+        done = pick(want_ref[spot, :], block_ref, first_ref, second_ref, columns)
         copy.wait()
         done = done + before_ref[spot, :].astype(F32)
-        q_ref[spot, :] = done[:, :TILE].astype(BF)
-        kv_ref[spot, TILE:] = done[:, 2 * TILE :].astype(BF)
+        if not turn:
+            out_ref[spot, :] = done.astype(BF)
+            continue
+        out_ref[spot, TILE:] = done[:, TILE:].astype(BF)
         for t in range(0, rows, TILE):
-            keys = done[t : t + TILE, TILE : 2 * TILE]
-            kv_ref[i * rows + t : i * rows + t + TILE, :TILE] = keys.T.astype(BF)
+            out_ref[i * rows + t : i * rows + t + TILE, :TILE] = done[t : t + TILE, :TILE].T.astype(BF)
 
 
 def place_near(blocks, want, first, second):
@@ -153,13 +148,13 @@
     )(blocks, want, first, second)
 
 
-def place_far(blocks, want, first, second, near):
-    n, width = want.shape[0], first.shape[1]
-    return pl.pallas_call(
-        place_far_kernel,
-        out_shape=(pltpu.HBM((n, TILE), BF), jax.ShapeDtypeStruct((n, width - TILE), BF)),
-        in_specs=[WHOLE_SM] + [WHOLE_VM] * 3 + [WHOLE_ANY],
-        out_specs=(WHOLE_VM,) * 2,
+def place_far(blocks, want, first, second, near, column, width, turn):
+    n = want.shape[0]
+    return pl.pallas_call(
+        functools.partial(place_far_kernel, column, turn),
+        out_shape=pltpu.HBM((n, width), BF),
+        in_specs=[WHOLE_SM] + [WHOLE_VM] * 3 + [WHOLE_HBM],
+        out_specs=WHOLE_VM,
         scratch_shapes=[VM((n, width), BF), pltpu.SemaphoreType.DMA((4,))],
         compiler_params=pltpu.CompilerParams(vmem_limit_bytes=24 << 20),
         cost_estimate=pl.CostEstimate(flops=n * n * width, bytes_accessed=4 << 20, transcendentals=0),
@@ -335,7 +330,7 @@
     far_next, _ = after((far_own, (one, three)))
     f_one, f_three = round_x(far_next, 1), round_x(far_next, -1)
     far_two = swap(jnp.concatenate([low, high], axis=0), "yh")
-    near_mine, near_theirs = qkv(w_qkv, w_other, [tokens, one, three, far_own], 0, 3 * TILE)
+    near_mine, near_theirs = qkv(w_qkv, w_other, [tokens, one, three, far_own])
     near_other = swap(near_theirs, "core")
     want = source_row[0][:, None]
     near = place_near(blocks(NEAR), want, near_mine, near_other)
@@ -349,29 +344,29 @@
     cross_index, cross_count = listed(inside, valid & crossing, tiles)
     lists = (index, count, cross_index, cross_count)
     far_two, near, (index, count, cross_index, cross_count) = after((far_two, near, lists))
-    far_mine, far_theirs = qkv(w_qkv, w_other, [low, high, f_one, f_three, far_two], 0, 3 * TILE)
+    far_mine, far_theirs = qkv(w_qkv, w_other, [low, high, f_one, f_three, far_two])
     far_other = swap(far_theirs, "core")
 
-    w_start, _ = after((w_out, near_theirs))
+    w_start, _ = after((w_out, near))
     w_one, w_three = round_x(w_start, 1), round_x(w_start, -1)
     w_turn, _ = after((w_out, far_two))
     w_two, w_far = round_x(w_turn, 2), opposite(w_turn)
 
-    far_other, _ = after((far_other, (w_one, w_three)))
-    q, kv = place_far(blocks(FAR), want, far_mine, far_other, near)
+    kv = place_far(blocks(FAR), want, far_mine, far_other, near, TILE, 2 * TILE, True)
+    (far_mine, far_other), _ = after(((far_mine, far_other), kv))
+    q = place_far(blocks(FAR), want, far_mine, far_other, near, 0, TILE, False)
+    kv, _ = after((kv, (w_one, w_three)))
     behind = lax.ppermute(kv, "z", [(i, (i + 1) % 8) for i in range(8)])
     ahead = lax.ppermute(kv, "z", [(i, (i + 7) % 8) for i in range(8)])
     beside = swap(kv, "yl")
 
+    wf_one, wf_three, wf_two = opposite(w_one), opposite(w_three), round_x(w_far, 2)
+
     mid = kv.shape[0] // 2
-    (ahead_low, behind_low), _ = after(((ahead[:mid], behind[:mid]), (w_two, w_far)))
-    cross = jnp.where(yl == 0, ahead_low, behind_low)
-    cross_low = swap(cross, "yl")
+    (ahead_low, behind_low), _ = after(((ahead[:mid], behind[:mid]), (w_two, w_far, q)))
+    cross_low = swap(jnp.where(yl == 0, ahead_low, behind_low), "yl")
     onward = [(2 * i, 2 * ((i + 1) % 8)) for i in range(8)] + [(2 * i + 1, 2 * ((i + 7) % 8) + 1) for i in range(8)]
-    beside_high = beside[mid:]
-    cross_high = lax.ppermute(beside_high, CTX, onward)
-    (g_one, g_three, g_far), _ = after(((w_one, w_three, w_far), (cross, beside_high)))
-    wf_one, wf_three, wf_two = opposite(g_one), opposite(g_three), round_x(g_far, 2)
+    cross_high = lax.ppermute(beside[mid:], CTX, onward)
 
     state = attend(index, count, q, [kv, behind, beside, ahead], (24, slots), together=4)
     attended = attend(cross_index, cross_count, q, [cross_low, cross_high], (6, tiles), state, together=4)

time: 159 us -> 153 us (0.962)
  waiting for transfers between devices: 64 us -> 46.5 us
  starting transfers between devices: 43.1 us -> 48.3 us
  Pallas kernels: 41.3 us -> 45.7 us
  local copies, waits for them, and re-layouts: 3.99 us -> 5.6 us
    ppermute x8, waiting for transfers between devices: 19.9 us -> 3.33 us  [swap(): return lax.ppermute(array, axis, [(0, 1), (1, 0)])]
    ppermute x1, waiting for transfers between devices: 0.01 us -> 14.3 us  [body(): ahead = lax.ppermute(kv, 'z', [(i, (i + 7) % 8) for i in range(8)])]
    ppermute x3, waiting for transfers between devices: 15.5 us -> 5.27 us  [opposite(): return lax.ppermute(array, ('yl', 'yh'), [(i, 3 - i) for i in range(4)])]
    ppermute x10, starting transfers between devices: 8.41 us -> 16.4 us  [round_x(): return lax.ppermute(array, 'x', [(i, (i + by) % 4) for i in range(4)])]
    ppermute x10, waiting for transfers between devices: 25.8 us -> 18.8 us  [round_x(): return lax.ppermute(array, 'x', [(i, (i + by) % 4) for i in range(4)])]
    pallas_call x3 -> x4, Pallas kernels: 16.7 us -> 20.7 us  [the longest x2 12 us: qkv(): pl.pallas_call(functools.partial(qkv_kernel, chunks), out_shape=(jax.Shap...]
    all_to_all x1, waiting for transfers between devices: 0.01 us -> 3.73 us  [body(): lax.all_to_all(attended.reshape(8, 2 * TILE, TILE), CHIPS, split_axis=0,...]
    ppermute x1, starting transfers between devices: 3.94 us -> 7.11 us  [body(): ahead = lax.ppermute(kv, 'z', [(i, (i + 7) % 8) for i in range(8)])]
  transfers between devices with their start and end apart: 25 -> 25, of which waited for: 12 -> 10; matrix products, arithmetic and copies ran while one was open for 4% -> 5% of each run, Pallas kernels for 20% -> 27%
where the time goes in v7:
time: 153 us; the launch traced here: 152 us
  starting transfers between devices  48.3 us (32%)
  waiting for transfers between devices  46.5 us (30%)
  Pallas kernels  45.7 us (30%)
  local copies, waits for them, and re-layouts  5.6 us (4%)
  other arithmetic  5.32 us (3%)
    ppermute x10, waiting for transfers between devices, round_x(): return lax.ppermute(array, 'x', [(i, (i + by) % 4) for i in range(4)])  18.8 us
    ppermute x8, starting transfers between devices, swap(): return lax.ppermute(array, axis, [(0, 1), (1, 0)])  18 us
    pallas_call x2, Pallas kernels, attend(): pl.pallas_call(functools.partial(attend_kernel, sizes, together, len(fram...  17 us
    ppermute x10, starting transfers between devices, round_x(): return lax.ppermute(array, 'x', [(i, (i + by) % 4) for i in range(4)])  16.4 us
    ppermute x1, waiting for transfers between devices, body(): ahead = lax.ppermute(kv, 'z', [(i, (i + 7) % 8) for i in range(8)])  14.3 us
    pallas_call x2, Pallas kernels, qkv(): pl.pallas_call(functools.partial(qkv_kernel, chunks), out_shape=(jax.Shap...  12 us
    pallas_call x2, Pallas kernels, place_far(): pl.pallas_call(functools.partial(place_far_kernel, column, turn), out_sha...  8.71 us
    ppermute x1, starting transfers between devices, body(): ahead = lax.ppermute(kv, 'z', [(i, (i + 7) % 8) for i in range(8)])  7.11 us
  transfers between devices with their start and end apart: 25, of which 10 were waited for; matrix products, arithmetic and copies ran while one was open for 5% of the time, Pallas kernels for 27%

profile of v7, /device:TPU:1, one launch (start us, length us, event | category | flops | bytes accessed | tf_op | source)
XLA Modules:
  0.0 151.7 jit_solution(114835273259935746)
XLA Ops:
  0.0 3.2 %collective-permute-start.5 = (bf16[3072,384]{1,0:T(8,128)(2,1)}, bf16[3072,384]{1,0:T(8,128)(2,1)}, u32[]{:S(2)}, u32[]{:S(2)}) collective-permute-start(bf16[3072,384]{1,0:T(8,128)(2,1)} %own_ref.3), channel_id=1, source_target_pairs={{0,1},{1,0},{2,3},{3,2},{4,5},{5,4},{6,7},{7,6},{8,9},{9,8},{10,11... | collective-permute-start | bytes 7077896 | tf_op jit(solution)/shard_map/ppermute | solution.py:38
  3.2 2.7 %collective-permute-start.2 = (bf16[128,3072]{1,0:T(8,128)(2,1)}, bf16[128,3072]{1,0:T(8,128)(2,1)S(1)}, u32[]{:S(2)}, u32[]{:S(2)}) collective-permute-start(bf16[128,3072]{1,0:T(8,128)(2,1)} %refs_0_.2), channel_id=1, source_target_pairs={{0,6},{2,0},{4,2},{6,4},{1,7},{3,1},{5,3},{7,5},{8,14},{10,8},{12,... | collective-permute-start | bytes 2359304 | tf_op jit(solution)/shard_map/ppermute | solution.py:34
  5.9 1.2 collective-permute-start.6
  8.9 15.0 %collective-permute-done.refs_1_ = bf16[128,3072]{1,0:T(8,128)(2,1)S(1)} collective-permute-done((bf16[128,3072]{1,0:T(8,128)(2,1)}, bf16[128,3072]{1,0:T(8,128)(2,1)S(1)}, u32[]{:S(2)}, u32[]{:S(2)}) %collective-permute-start) | collective-permute-done | bytes 786464 | tf_op jit(solution)/shard_map/ppermute | solution.py:34
  24.1 2.7 %collective-permute-start.3 = (bf16[64,3072]{1,0:T(8,128)(2,1)S(1)}, bf16[64,3072]{1,0:T(8,128)(2,1)S(1)}, u32[]{:S(2)}, u32[]{:S(2)}) collective-permute-start(bf16[64,3072]{1,0:T(8,128)(2,1)S(1)} %slice.21), channel_id=1, source_target_pairs={{0,6},{2,0},{4,2},{6,4},{1,7},{3,1},{5,3},{7,5},{8,14},{10,8},{12,... | collective-permute-start | bytes 1179656 | tf_op jit(solution)/shard_map/ppermute | solution.py:34
  28.8 2.7 %collective-permute-start.9 = (bf16[128,3072]{1,0:T(8,128)(2,1)}, bf16[128,3072]{1,0:T(8,128)(2,1)S(1)}, u32[]{:S(2)}, u32[]{:S(2)}) collective-permute-start(bf16[128,3072]{1,0:T(8,128)(2,1)} %collective-permute-done.6.refs_3_), channel_id=1, source_target_pairs={{0,6},{2,0},{4,2},{6,4},{1,7},{3,1},{5,3},{7,5},{8,14},{10,8},{12,... | collective-permute-start | bytes 2359304 | tf_op jit(solution)/shard_map/ppermute | solution.py:34
  31.4 3.8 %collective-permute-done.1.refs_0_ = bf16[64,3072]{1,0:T(8,128)(2,1)S(1)} collective-permute-done((bf16[64,3072]{1,0:T(8,128)(2,1)S(1)}, bf16[64,3072]{1,0:T(8,128)(2,1)S(1)}, u32[]{:S(2)}, u32[]{:S(2)}) %collective-permute-start.1) | collective-permute-done | bytes 393248 | tf_op jit(solution)/shard_map/ppermute | solution.py:34
  36.2 1.1 copy-done.5
  37.3 6.6 %shard_map.64 = (bf16[512,384]{1,0:T(8,128)(2,1)S(1)}, bf16[512,384]{1,0:T(8,128)(2,1)S(1)}) custom-call(bf16[3072,384]{1,0:T(8,128)(2,1)} %own_ref.3, bf16[3072,384]{1,0:T(8,128)(2,1)} %collective-permute-done.5.other_ref, bf16[128,3072]{1,0:T(8,128)(2,1)S(1)} %copy-done.5, bf16[128,3072]{1,0:T(8,128)(2,1)S(1)} %collective-permute-done.refs_1_, ...), custom_call_target="tpu_custom_call" | custom-call | flops 2415919104 | bytes 8388608 | tf_op jit(solution)/shard_map/pallas_call | solution.py:73
  43.9 3.5 %collective-permute-start.7 = (bf16[512,384]{1,0:T(8,128)(2,1)S(1)}, bf16[512,384]{1,0:T(8,128)(2,1)S(1)}, u32[]{:S(2)}, u32[]{:S(2)}) collective-permute-start(bf16[512,384]{1,0:T(8,128)(2,1)S(1)} %get-tuple-element.28), channel_id=1, source_target_pairs={{0,1},{1,0},{2,3},{3,2},{4,5},{5,4},{6,7},{7,6},{8,9},{9,8},{10,11... | collective-permute-start | bytes 1179656 | tf_op jit(solution)/shard_map/ppermute | solution.py:38
  48.7 3.6 %shard_map.65.near_ref = bf16[2048,384]{1,0:T(8,128)(2,1)S(1)} custom-call(f32[8]{0:T(128)S(1)} %convert_element_type.19.block_ref, s32[2048,1]{1,0:T(8,128)S(1)} %copy.10.want_ref, bf16[512,384]{1,0:T(8,128)(2,1)S(1)} %get-tuple-element.27.first_ref, bf16[512,384]{1,0:T(8,128)(2,1)S(1)} %collective-permute-done.7.second_ref), custom_call_target="tpu_custom_call" | custom-call | flops 1610612736 | bytes 4194304 | tf_op jit(solution)/shard_map/pallas_call | solution.py:141
  52.3 1.1 copy-done
  53.9 2.7 %collective-permute-start.12 = (bf16[128,3072]{1,0:T(8,128)(2,1)}, bf16[128,3072]{1,0:T(8,128)(2,1)}, u32[]{:S(2)}, u32[]{:S(2)}) collective-permute-start(bf16[128,3072]{1,0:T(8,128)(2,1)} %refs_0_.3), channel_id=1, source_target_pairs={{0,6},{2,0},{4,2},{6,4},{1,7},{3,1},{5,3},{7,5},{8,14},{10,8},{12,... | collective-permute-start | bytes 2359304 | tf_op jit(solution)/shard_map/ppermute | solution.py:34
  56.6 5.4 %shard_map.66 = (bf16[512,384]{1,0:T(8,128)(2,1)S(1)}, bf16[512,384]{1,0:T(8,128)(2,1)S(1)}) custom-call(bf16[3072,384]{1,0:T(8,128)(2,1)} %own_ref.3, bf16[3072,384]{1,0:T(8,128)(2,1)} %collective-permute-done.5.other_ref, bf16[64,3072]{1,0:T(8,128)(2,1)S(1)} %collective-permute-done.1.refs_0_, bf16[64,3072]{1,0:T(8,128)(2,1)S(1)} %collective-permute-done.3.refs_1_, ...), custom_call_target="tpu_custom_call" | custom-call | flops 2415919104 | bytes 8388608 | tf_op jit(solution)/shard_map/pallas_call | solution.py:73
  62.0 3.6 %collective-permute-start.10 = (bf16[512,384]{1,0:T(8,128)(2,1)S(1)}, bf16[512,384]{1,0:T(8,128)(2,1)S(1)}, u32[]{:S(2)}, u32[]{:S(2)}) collective-permute-start(bf16[512,384]{1,0:T(8,128)(2,1)S(1)} %get-tuple-element.34), channel_id=1, source_target_pairs={{0,1},{1,0},{2,3},{3,2},{4,5},{5,4},{6,7},{7,6},{8,9},{9,8},{10,11... | collective-permute-start | bytes 1179656 | tf_op jit(solution)/shard_map/ppermute | solution.py:38
  65.7 1.3 collective-permute-done.10.second_ref
  67.0 4.9 %shard_map.67.refs_0_ = bf16[2048,256]{1,0:T(8,128)(2,1)} custom-call(f32[8]{0:T(128)S(1)} %convert_element_type.22.block_ref, s32[2048,1]{1,0:T(8,128)S(1)} %copy.10.want_ref, bf16[512,384]{1,0:T(8,128)(2,1)S(1)} %get-tuple-element.36.first_ref, bf16[512,384]{1,0:T(8,128)(2,1)S(1)} %collective-permute-done.10.second_ref, bf16[2048,384]{1,0:T(8,128)(2,1)} %copy-done), custom_call_target="tpu_custom_call" | custom-call | flops 1073741824 | bytes 4194304 | tf_op jit(solution)/shard_map/pallas_call | solution.py:153
  71.9 7.1 %collective-permute-start.13 = (bf16[2048,256]{1,0:T(8,128)(2,1)}, bf16[2048,256]{1,0:T(8,128)(2,1)S(1)}, u32[]{:S(2)}, u32[]{:S(2)}) collective-permute-start(bf16[2048,256]{1,0:T(8,128)(2,1)} %shard_map.67.refs_0_), channel_id=1, source_target_pairs={{0,224},{32,0},{64,32},{96,64},{128,96},{160,128},{192,160},{224,1... | collective-permute-start | bytes 3145736 | tf_op jit(solution)/shard_map/ppermute | solution.py:360
  79.0 2.6 %collective-permute-start.15 = (bf16[128,3072]{1,0:T(8,128)(2,1)}, bf16[128,3072]{1,0:T(8,128)(2,1)}, u32[]{:S(2)}, u32[]{:S(2)}) collective-permute-start(bf16[128,3072]{1,0:T(8,128)(2,1)} %refs_0_.3), channel_id=1, source_target_pairs={{0,4},{2,6},{4,0},{6,2},{1,5},{3,7},{5,1},{7,3},{8,12},{10,14},{12... | collective-permute-start | bytes 2359304 | tf_op jit(solution)/shard_map/ppermute | solution.py:34
  81.6 3.8 %shard_map.68.q_ref = bf16[2048,128]{1,0:T(8,128)(2,1)} custom-call(f32[8]{0:T(128)S(1)} %convert_element_type.22.block_ref, s32[2048,1]{1,0:T(8,128)S(1)} %copy.10.want_ref, bf16[512,384]{1,0:T(8,128)(2,1)S(1)} %get-tuple-element.36.first_ref, bf16[512,384]{1,0:T(8,128)(2,1)S(1)} %collective-permute-done.10.second_ref, bf16[2048,384]{1,0:T(8,128)(2,1)} %copy-done), custom_call_target="tpu_custom_call" | custom-call | flops 536870912 | bytes 4194304 | tf_op jit(solution)/shard_map/pallas_call | solution.py:153
  85.5 14.3 %collective-permute-done.13.refs_3_ = bf16[2048,256]{1,0:T(8,128)(2,1)S(1)} collective-permute-done((bf16[2048,256]{1,0:T(8,128)(2,1)}, bf16[2048,256]{1,0:T(8,128)(2,1)S(1)}, u32[]{:S(2)}, u32[]{:S(2)}) %collective-permute-start.13) | collective-permute-done | bytes 1048608 | tf_op jit(solution)/shard_map/ppermute | solution.py:360
  99.8 2.8 %collective-permute-start.21 = (bf16[128,3072]{1,0:T(8,128)(2,1)}, bf16[128,3072]{1,0:T(8,128)(2,1)}, u32[]{:S(2)}, u32[]{:S(2)}) collective-permute-start(bf16[128,3072]{1,0:T(8,128)(2,1)} %collective-permute-done.12.refs_2_), channel_id=1, source_target_pairs={{0,24},{8,16},{16,8},{24,0},{1,25},{9,17},{17,9},{25,1},{2,26},{10... | collective-permute-start | bytes 2359304 | tf_op jit(solution)/shard_map/ppermute | solution.py:42
  102.9 2.5 %collective-permute-start.22 = (bf16[128,3072]{1,0:T(8,128)(2,1)}, bf16[128,3072]{1,0:T(8,128)(2,1)}, u32[]{:S(2)}, u32[]{:S(2)}) collective-permute-start(bf16[128,3072]{1,0:T(8,128)(2,1)} %collective-permute-done.16.refs_4_), channel_id=1, source_target_pairs={{0,4},{2,6},{4,0},{6,2},{1,5},{3,7},{5,1},{7,3},{8,12},{10,14},{12... | collective-permute-start | bytes 2359304 | tf_op jit(solution)/shard_map/ppermute | solution.py:34
  106.7 1.2 slice.24
  108.0 10.8 %shard_map.69 = (f32[2048,128]{1,0:T(8,128)S(1)}, f32[2048,128]{1,0:T(8,128)S(1)}) custom-call(s32[16,30]{1,0:T(8,128)S(1)} %copy.16.index_ref, s32[16]{0:T(128)S(1)} %get-tuple-element.44.count_ref, bf16[2048,128]{1,0:T(8,128)(2,1)S(1)} %copy-done.2, bf16[2048,256]{1,0:T(8,128)(2,1)S(1)} %copy-done.1, bf16[2048,256]{1,0:T(8,128)(2,1)} %collective-permute-done.14.refs_1_, ...), custom_call_target="tpu_custom_call" | custom-call | flops 16106127360 | bytes 6291456 | tf_op jit(solution)/shard_map/pallas_call | solution.py:247
  119.5 6.2 %shard_map.70 = bf16[2048,128]{1,0:T(8,128)(2,1)} custom-call(s32[16,16]{1,0:T(8,128)S(1)} %select_reduce_fusion.3.index_ref, s32[16]{0:T(128)S(1)} %get-tuple-element.30.count_ref, bf16[2048,128]{1,0:T(8,128)(2,1)S(1)} %copy-done.2, bf16[1024,256]{1,0:T(8,128)(2,1)S(1)} %collective-permute-done.17.refs_0_, ...), custom_call_target="tpu_custom_call" | custom-call | flops 8589934592 | bytes 6291456 | tf_op jit(solution)/shard_map/pallas_call | solution.py:247
  125.7 4.0 %all-to-all-start = ((bf16[8,256,128]{2,1,0:T(8,128)(2,1)}), bf16[8,256,128]{2,1,0:T(8,128)(2,1)S(1)}, u32[]{:S(2)}, u32[]{:S(2)}) async-start(bf16[8,256,128]{2,1,0:T(8,128)(2,1)} %bitcast.26), calls=%async_computation | async-start | bytes 1048576 | tf_op jit(solution)/shard_map/all_to_all | solution.py:374
  129.7 5.3 %collective-permute-done.21.refs_6_ = bf16[128,3072]{1,0:T(8,128)(2,1)} collective-permute-done((bf16[128,3072]{1,0:T(8,128)(2,1)}, bf16[128,3072]{1,0:T(8,128)(2,1)}, u32[]{:S(2)}, u32[]{:S(2)}) %collective-permute-start.21) | collective-permute-done | bytes 786464 | tf_op jit(solution)/shard_map/ppermute | solution.py:42
  135.0 3.7 %all-to-all-done.att_ref = bf16[8,256,128]{2,1,0:T(8,128)(2,1)S(1)} async-done(((bf16[8,256,128]{2,1,0:T(8,128)(2,1)}), bf16[8,256,128]{2,1,0:T(8,128)(2,1)S(1)}, u32[]{:S(2)}, u32[]{:S(2)}) %all-to-all-start) | async-done | bytes 524320 | tf_op jit(solution)/shard_map/all_to_all | solution.py:374
  138.8 4.4 %shard_map.71 = (f32[128,3072]{1,0:T(8,128)S(1)}, bf16[128,3072]{1,0:T(8,128)(2,1)S(1)}) custom-call(s32[9]{0:T(128)S(1)} %stack.102.order_ref, bf16[8,256,128]{2,1,0:T(8,128)(2,1)S(1)} %all-to-all-done.att_ref, bf16[128,3072]{1,0:T(8,128)(2,1)} %refs_0_.3, bf16[128,3072]{1,0:T(8,128)(2,1)} %collective-permute-done.11.refs_1_, ...), custom_call_target="tpu_custom_call" | custom-call | flops 1610612736 | bytes 10485760 | tf_op jit(solution)/shard_map/pallas_call | solution.py:293
  143.2 5.5 %collective-permute-start.23 = (bf16[128,3072]{1,0:T(8,128)(2,1)S(1)}, bf16[128,3072]{1,0:T(8,128)(2,1)S(1)}, u32[]{:S(2)}, u32[]{:S(2)}) collective-permute-start(bf16[128,3072]{1,0:T(8,128)(2,1)S(1)} %get-tuple-element.48), channel_id=1, source_target_pairs={{0,1},{1,0},{2,3},{3,2},{4,5},{5,4},{6,7},{7,6},{8,9},{9,8},{10,11... | collective-permute-start | bytes 2359304 | tf_op jit(solution)/shard_map/ppermute | solution.py:38
  148.7 1.9 %collective-permute-done.23 = bf16[128,3072]{1,0:T(8,128)(2,1)S(1)} collective-permute-done((bf16[128,3072]{1,0:T(8,128)(2,1)S(1)}, bf16[128,3072]{1,0:T(8,128)(2,1)S(1)}, u32[]{:S(2)}, u32[]{:S(2)}) %collective-permute-start.23) | collective-permute-done | bytes 786464 | tf_op jit(solution)/shard_map/ppermute | solution.py:38
  (70 shorter events, 10.3 us)
Async XLA Ops:
  0.0 26.9 %copy-start.7 = (s32[1,2048]{1,0:T(1,128)S(1)}, s32[1,2048]{1,0:T(1,128)}, u32[]{:S(2)}) copy-start(s32[1,2048]{1,0:T(1,128)} %param.9) | copy-start | bytes 24580
  0.0 36.2 %collective-permute-start.5 = (bf16[3072,384]{1,0:T(8,128)(2,1)}, bf16[3072,384]{1,0:T(8,128)(2,1)}, u32[]{:S(2)}, u32[]{:S(2)}) collective-permute-start(bf16[3072,384]{1,0:T(8,128)(2,1)} %own_ref.3), channel_id=1, source_target_pairs={{0,1},{1,0},{2,3},{3,2},{4,5},{5,4},{6,7},{7,6},{8,9},{9,8},{10,11... | collective-permute-start | bytes 7077896 | tf_op jit(solution)/shard_map/ppermute | solution.py:38
  3.2 20.7 %collective-permute-start = (bf16[128,3072]{1,0:T(8,128)(2,1)}, bf16[128,3072]{1,0:T(8,128)(2,1)S(1)}, u32[]{:S(2)}, u32[]{:S(2)}) collective-permute-start(bf16[128,3072]{1,0:T(8,128)(2,1)} %refs_0_.2), channel_id=1, source_target_pairs={{0,2},{2,4},{4,6},{6,0},{1,3},{3,5},{5,7},{7,1},{8,10},{10,12},{12... | collective-permute-start | bytes 2359304 | tf_op jit(solution)/shard_map/ppermute | solution.py:34
  3.2 20.8 %collective-permute-start.2 = (bf16[128,3072]{1,0:T(8,128)(2,1)}, bf16[128,3072]{1,0:T(8,128)(2,1)S(1)}, u32[]{:S(2)}, u32[]{:S(2)}) collective-permute-start(bf16[128,3072]{1,0:T(8,128)(2,1)} %refs_0_.2), channel_id=1, source_target_pairs={{0,6},{2,0},{4,2},{6,4},{1,7},{3,1},{5,3},{7,5},{8,14},{10,8},{12,... | collective-permute-start | bytes 2359304 | tf_op jit(solution)/shard_map/ppermute | solution.py:34
  5.9 22.8 %collective-permute-start.6 = (bf16[128,3072]{1,0:T(8,128)(2,1)}, bf16[128,3072]{1,0:T(8,128)(2,1)}, u32[]{:S(2)}, u32[]{:S(2)}) collective-permute-start(bf16[128,3072]{1,0:T(8,128)(2,1)} %refs_0_.2), channel_id=1, source_target_pairs={{0,8},{8,0},{1,9},{9,1},{2,10},{10,2},{3,11},{11,3},{4,12},{12,4},... | collective-permute-start | bytes 2359304 | tf_op jit(solution)/shard_map/ppermute | solution.py:38
  24.0 11.3 %collective-permute-start.1 = (bf16[64,3072]{1,0:T(8,128)(2,1)S(1)}, bf16[64,3072]{1,0:T(8,128)(2,1)S(1)}, u32[]{:S(2)}, u32[]{:S(2)}) collective-permute-start(bf16[64,3072]{1,0:T(8,128)(2,1)S(1)} %slice.20), channel_id=1, source_target_pairs={{0,2},{2,4},{4,6},{6,0},{1,3},{3,5},{5,7},{7,1},{8,10},{10,12},{12... | collective-permute-start | bytes 1179656 | tf_op jit(solution)/shard_map/ppermute | solution.py:34
  24.1 2.9 %copy-start.3 = (bf16[128,3072]{1,0:T(8,128)(2,1)}, bf16[128,3072]{1,0:T(8,128)(2,1)S(1)}, u32[]{:S(2)}) copy-start(bf16[128,3072]{1,0:T(8,128)(2,1)S(1)} %collective-permute-done.2.refs_2_) | copy-start | bytes 2359300
  24.1 11.1 %collective-permute-start.3 = (bf16[64,3072]{1,0:T(8,128)(2,1)S(1)}, bf16[64,3072]{1,0:T(8,128)(2,1)S(1)}, u32[]{:S(2)}, u32[]{:S(2)}) collective-permute-start(bf16[64,3072]{1,0:T(8,128)(2,1)S(1)} %slice.21), channel_id=1, source_target_pairs={{0,6},{2,0},{4,2},{6,4},{1,7},{3,1},{5,3},{7,5},{8,14},{10,8},{12,... | collective-permute-start | bytes 1179656 | tf_op jit(solution)/shard_map/ppermute | solution.py:34
  28.7 7.5 %copy-start.4 = (bf16[128,3072]{1,0:T(8,128)(2,1)S(1)}, bf16[128,3072]{1,0:T(8,128)(2,1)}, u32[]{:S(2)}) copy-start(bf16[128,3072]{1,0:T(8,128)(2,1)} %copy-done.3) | copy-start | bytes 2359300
  28.7 27.9 %collective-permute-start.8 = (bf16[128,3072]{1,0:T(8,128)(2,1)}, bf16[128,3072]{1,0:T(8,128)(2,1)S(1)}, u32[]{:S(2)}, u32[]{:S(2)}) collective-permute-start(bf16[128,3072]{1,0:T(8,128)(2,1)} %collective-permute-done.6.refs_3_), channel_id=1, source_target_pairs={{0,2},{2,4},{4,6},{6,0},{1,3},{3,5},{5,7},{7,1},{8,10},{10,12},{12... | collective-permute-start | bytes 2359304 | tf_op jit(solution)/shard_map/ppermute | solution.py:34
  28.8 27.8 %collective-permute-start.9 = (bf16[128,3072]{1,0:T(8,128)(2,1)}, bf16[128,3072]{1,0:T(8,128)(2,1)S(1)}, u32[]{:S(2)}, u32[]{:S(2)}) collective-permute-start(bf16[128,3072]{1,0:T(8,128)(2,1)} %collective-permute-done.6.refs_3_), channel_id=1, source_target_pairs={{0,6},{2,0},{4,2},{6,4},{1,7},{3,1},{5,3},{7,5},{8,14},{10,8},{12,... | collective-permute-start | bytes 2359304 | tf_op jit(solution)/shard_map/ppermute | solution.py:34
  35.3 18.2 %collective-permute-start.4 = (bf16[128,3072]{1,0:T(8,128)(2,1)S(1)}, bf16[128,3072]{1,0:T(8,128)(2,1)S(1)}, u32[]{:S(2)}, u32[]{:S(2)}) collective-permute-start(bf16[128,3072]{1,0:T(8,128)(2,1)S(1)} %pad_maximum_fusion), channel_id=1, source_target_pairs={{0,8},{8,0},{1,9},{9,1},{2,10},{10,2},{3,11},{11,3},{4,12},{12,4},... | collective-permute-start | bytes 2359304 | tf_op jit(solution)/shard_map/ppermute | solution.py:38
  43.9 4.9 %collective-permute-start.7 = (bf16[512,384]{1,0:T(8,128)(2,1)S(1)}, bf16[512,384]{1,0:T(8,128)(2,1)S(1)}, u32[]{:S(2)}, u32[]{:S(2)}) collective-permute-start(bf16[512,384]{1,0:T(8,128)(2,1)S(1)} %get-tuple-element.28), channel_id=1, source_target_pairs={{0,1},{1,0},{2,3},{3,2},{4,5},{5,4},{6,7},{7,6},{8,9},{9,8},{10,11... | collective-permute-start | bytes 1179656 | tf_op jit(solution)/shard_map/ppermute | solution.py:38
  52.3 1.1 copy-start
  53.5 18.4 %collective-permute-start.11 = (bf16[128,3072]{1,0:T(8,128)(2,1)}, bf16[128,3072]{1,0:T(8,128)(2,1)}, u32[]{:S(2)}, u32[]{:S(2)}) collective-permute-start(bf16[128,3072]{1,0:T(8,128)(2,1)} %refs_0_.3), channel_id=1, source_target_pairs={{0,2},{2,4},{4,6},{6,0},{1,3},{3,5},{5,7},{7,1},{8,10},{10,12},{12... | collective-permute-start | bytes 2359304 | tf_op jit(solution)/shard_map/ppermute | solution.py:34
  53.9 18.0 %collective-permute-start.12 = (bf16[128,3072]{1,0:T(8,128)(2,1)}, bf16[128,3072]{1,0:T(8,128)(2,1)}, u32[]{:S(2)}, u32[]{:S(2)}) collective-permute-start(bf16[128,3072]{1,0:T(8,128)(2,1)} %refs_0_.3), channel_id=1, source_target_pairs={{0,6},{2,0},{4,2},{6,4},{1,7},{3,1},{5,3},{7,5},{8,14},{10,8},{12,... | collective-permute-start | bytes 2359304 | tf_op jit(solution)/shard_map/ppermute | solution.py:34
  62.0 4.9 %collective-permute-start.10 = (bf16[512,384]{1,0:T(8,128)(2,1)S(1)}, bf16[512,384]{1,0:T(8,128)(2,1)S(1)}, u32[]{:S(2)}, u32[]{:S(2)}) collective-permute-start(bf16[512,384]{1,0:T(8,128)(2,1)S(1)} %get-tuple-element.34), channel_id=1, source_target_pairs={{0,1},{1,0},{2,3},{3,2},{4,5},{5,4},{6,7},{7,6},{8,9},{9,8},{10,11... | collective-permute-start | bytes 1179656 | tf_op jit(solution)/shard_map/ppermute | solution.py:38
  71.9 27.9 %collective-permute-start.13 = (bf16[2048,256]{1,0:T(8,128)(2,1)}, bf16[2048,256]{1,0:T(8,128)(2,1)S(1)}, u32[]{:S(2)}, u32[]{:S(2)}) collective-permute-start(bf16[2048,256]{1,0:T(8,128)(2,1)} %shard_map.67.refs_0_), channel_id=1, source_target_pairs={{0,224},{32,0},{64,32},{96,64},{128,96},{160,128},{192,160},{224,1... | collective-permute-start | bytes 3145736 | tf_op jit(solution)/shard_map/ppermute | solution.py:360
  79.0 23.9 %collective-permute-start.14 = (bf16[2048,256]{1,0:T(8,128)(2,1)}, bf16[2048,256]{1,0:T(8,128)(2,1)}, u32[]{:S(2)}, u32[]{:S(2)}) collective-permute-start(bf16[2048,256]{1,0:T(8,128)(2,1)} %shard_map.67.refs_0_), channel_id=1, source_target_pairs={{0,32},{32,64},{64,96},{96,128},{128,160},{160,192},{192,224},{224... | collective-permute-start | bytes 3145736 | tf_op jit(solution)/shard_map/ppermute | solution.py:359
  79.0 20.8 %collective-permute-start.16 = (bf16[128,3072]{1,0:T(8,128)(2,1)}, bf16[128,3072]{1,0:T(8,128)(2,1)}, u32[]{:S(2)}, u32[]{:S(2)}) collective-permute-start(bf16[128,3072]{1,0:T(8,128)(2,1)} %refs_0_.3), channel_id=1, source_target_pairs={{0,24},{8,16},{16,8},{24,0},{1,25},{9,17},{17,9},{25,1},{2,26},{10... | collective-permute-start | bytes 2359304 | tf_op jit(solution)/shard_map/ppermute | solution.py:42
  79.0 27.5 %collective-permute-start.15 = (bf16[128,3072]{1,0:T(8,128)(2,1)}, bf16[128,3072]{1,0:T(8,128)(2,1)}, u32[]{:S(2)}, u32[]{:S(2)}) collective-permute-start(bf16[128,3072]{1,0:T(8,128)(2,1)} %refs_0_.3), channel_id=1, source_target_pairs={{0,4},{2,6},{4,0},{6,2},{1,5},{3,7},{5,1},{7,3},{8,12},{10,14},{12... | collective-permute-start | bytes 2359304 | tf_op jit(solution)/shard_map/ppermute | solution.py:34
  81.6 25.1 %collective-permute-start.18 = (bf16[2048,256]{1,0:T(8,128)(2,1)}, bf16[2048,256]{1,0:T(8,128)(2,1)}, u32[]{:S(2)}, u32[]{:S(2)}) collective-permute-start(bf16[2048,256]{1,0:T(8,128)(2,1)} %shard_map.67.refs_0_), channel_id=1, source_target_pairs={{0,16},{16,0},{1,17},{17,1},{2,18},{18,2},{3,19},{19,3},{4,20},{20... | collective-permute-start | bytes 3145736 | tf_op jit(solution)/shard_map/ppermute | solution.py:38
  99.8 29.9 %collective-permute-start.20 = (bf16[128,3072]{1,0:T(8,128)(2,1)}, bf16[128,3072]{1,0:T(8,128)(2,1)S(1)}, u32[]{:S(2)}, u32[]{:S(2)}) collective-permute-start(bf16[128,3072]{1,0:T(8,128)(2,1)} %collective-permute-done.11.refs_1_), channel_id=1, source_target_pairs={{0,24},{8,16},{16,8},{24,0},{1,25},{9,17},{17,9},{25,1},{2,26},{10... | collective-permute-start | bytes 2359304 | tf_op jit(solution)/shard_map/ppermute | solution.py:42
  99.8 35.2 %collective-permute-start.21 = (bf16[128,3072]{1,0:T(8,128)(2,1)}, bf16[128,3072]{1,0:T(8,128)(2,1)}, u32[]{:S(2)}, u32[]{:S(2)}) collective-permute-start(bf16[128,3072]{1,0:T(8,128)(2,1)} %collective-permute-done.12.refs_2_), channel_id=1, source_target_pairs={{0,24},{8,16},{16,8},{24,0},{1,25},{9,17},{17,9},{25,1},{2,26},{10... | collective-permute-start | bytes 2359304 | tf_op jit(solution)/shard_map/ppermute | solution.py:42
  102.9 32.1 %collective-permute-start.22 = (bf16[128,3072]{1,0:T(8,128)(2,1)}, bf16[128,3072]{1,0:T(8,128)(2,1)}, u32[]{:S(2)}, u32[]{:S(2)}) collective-permute-start(bf16[128,3072]{1,0:T(8,128)(2,1)} %collective-permute-done.16.refs_4_), channel_id=1, source_target_pairs={{0,4},{2,6},{4,0},{6,2},{1,5},{3,7},{5,1},{7,3},{8,12},{10,14},{12... | collective-permute-start | bytes 2359304 | tf_op jit(solution)/shard_map/ppermute | solution.py:34
  106.5 1.5 copy-start.1
  106.5 1.5 copy-start.2
  106.6 12.2 %collective-permute-start.17 = (bf16[1024,256]{1,0:T(8,128)(2,1)S(1)}, bf16[1024,256]{1,0:T(8,128)(2,1)S(1)}, u32[]{:S(2)}, u32[]{:S(2)}) collective-permute-start(bf16[1024,256]{1,0:T(8,128)(2,1)S(1)} %broadcast_select_fusion), channel_id=1, source_target_pairs={{0,16},{16,0},{1,17},{17,1},{2,18},{18,2},{3,19},{19,3},{4,20},{20... | collective-permute-start | bytes 1572872 | tf_op jit(solution)/shard_map/ppermute | solution.py:38
  107.9 11.6 %collective-permute-start.19 = (bf16[1024,256]{1,0:T(8,128)(2,1)S(1)}, bf16[1024,256]{1,0:T(8,128)(2,1)S(1)}, u32[]{:S(2)}, u32[]{:S(2)}) collective-permute-start(bf16[1024,256]{1,0:T(8,128)(2,1)S(1)} %slice.24), channel_id=1, source_target_pairs={{0,32},{32,64},{64,96},{96,128},{128,160},{160,192},{192,224},{224... | collective-permute-start | bytes 1572872 | tf_op jit(solution)/shard_map/ppermute | solution.py:369
  125.7 13.1 %all-to-all-start = ((bf16[8,256,128]{2,1,0:T(8,128)(2,1)}), bf16[8,256,128]{2,1,0:T(8,128)(2,1)S(1)}, u32[]{:S(2)}, u32[]{:S(2)}) async-start(bf16[8,256,128]{2,1,0:T(8,128)(2,1)} %bitcast.26), calls=%async_computation | async-start | bytes 1048576 | tf_op jit(solution)/shard_map/all_to_all | solution.py:374
  129.7 9.0 %copy-start.6 = (bf16[128,3072]{1,0:T(8,128)(2,1)}, bf16[128,3072]{1,0:T(8,128)(2,1)S(1)}, u32[]{:S(2)}) copy-start(bf16[128,3072]{1,0:T(8,128)(2,1)S(1)} %collective-permute-done.20.refs_5_) | copy-start | bytes 2359300
  143.2 7.4 %collective-permute-start.23 = (bf16[128,3072]{1,0:T(8,128)(2,1)S(1)}, bf16[128,3072]{1,0:T(8,128)(2,1)S(1)}, u32[]{:S(2)}, u32[]{:S(2)}) collective-permute-start(bf16[128,3072]{1,0:T(8,128)(2,1)S(1)} %get-tuple-element.48), channel_id=1, source_target_pairs={{0,1},{1,0},{2,3},{3,2},{4,5},{5,4},{6,7},{7,6},{8,9},{9,8},{10,11... | collective-permute-start | bytes 2359304 | tf_op jit(solution)/shard_map/ppermute | solution.py:38
  (1 other events, 1.1 us)

commit v8 on v7

--- a/solution.py
+++ b/solution.py
@@ -113,27 +113,25 @@
     lax.fori_loop(0, want_ref.shape[0] // rows, step, 0)
 
 
-def place_far_kernel(column, turn, block_ref, want_ref, first_ref, second_ref, near_ref, out_ref, before_ref, sems):
-    rows, width = 512, out_ref.shape[1]
+def place_far_kernel(block_ref, want_ref, first_ref, second_ref, near_ref, q_ref, kv_ref, before_ref, sems):
+    rows = 512
     steps = want_ref.shape[0] // rows
-    columns = slice(column, column + width)
-    copies = []
-    for i in range(steps):
-        spot = pl.ds(i * rows, rows)
-        copies.append(pltpu.make_async_copy(near_ref.at[spot, columns], before_ref.at[spot], sems.at[i]))
+    copies = [
+        pltpu.make_async_copy(near_ref.at[pl.ds(i * rows, rows)], before_ref.at[pl.ds(i * rows, rows)], sems.at[i])
+        for i in range(steps)
+    ]
     for copy in copies:
         copy.start()
     for i, copy in enumerate(copies):
         spot = slice(i * rows, (i + 1) * rows)
-        done = pick(want_ref[spot, :], block_ref, first_ref, second_ref, columns)
+        done = pick(want_ref[spot, :], block_ref, first_ref, second_ref)
         copy.wait()
         done = done + before_ref[spot, :].astype(F32)
-        if not turn:
-            out_ref[spot, :] = done.astype(BF)
-            continue
-        out_ref[spot, TILE:] = done[:, TILE:].astype(BF)
+        q_ref[spot, :] = done[:, :TILE].astype(BF)
+        kv_ref[spot, TILE:] = done[:, 2 * TILE :].astype(BF)
         for t in range(0, rows, TILE):
-            out_ref[i * rows + t : i * rows + t + TILE, :TILE] = done[t : t + TILE, :TILE].T.astype(BF)
+            keys = done[t : t + TILE, TILE : 2 * TILE]
+            kv_ref[i * rows + t : i * rows + t + TILE, :TILE] = keys.T.astype(BF)
 
 
 def place_near(blocks, want, first, second):
@@ -148,13 +146,13 @@
     )(blocks, want, first, second)
 
 
-def place_far(blocks, want, first, second, near, column, width, turn):
-    n = want.shape[0]
-    return pl.pallas_call(
-        functools.partial(place_far_kernel, column, turn),
-        out_shape=pltpu.HBM((n, width), BF),
-        in_specs=[WHOLE_SM] + [WHOLE_VM] * 3 + [WHOLE_HBM],
-        out_specs=WHOLE_VM,
+def place_far(blocks, want, first, second, near):
+    n, width = want.shape[0], first.shape[1]
+    return pl.pallas_call(
+        place_far_kernel,
+        out_shape=(pltpu.HBM((n, TILE), BF), jax.ShapeDtypeStruct((n, width - TILE), BF)),
+        in_specs=[WHOLE_SM] + [WHOLE_VM] * 3 + [WHOLE_ANY],
+        out_specs=(WHOLE_VM,) * 2,
         scratch_shapes=[VM((n, width), BF), pltpu.SemaphoreType.DMA((4,))],
         compiler_params=pltpu.CompilerParams(vmem_limit_bytes=24 << 20),
         cost_estimate=pl.CostEstimate(flops=n * n * width, bytes_accessed=4 << 20, transcendentals=0),
@@ -265,13 +263,14 @@
     weights, (mine_ref, other_ref, w_ref, sems) = refs[:-4], refs[-4:]
     chips, width, groups = att_ref.shape[0], mine_ref.shape[1], 3
     span = width // groups
+    pieces = len(weights)
     loads = []
     for g in range(groups):
+        columns, start = slice(g * span, (g + 1) * span), 0
         for b, ref in enumerate(weights):
-            columns = slice(g * span, (g + 1) * span)
-            loads.append(
-                pltpu.make_async_copy(ref.at[:, columns], w_ref.at[pl.ds(b * TILE, TILE), columns], sems.at[g * chips + b])
-            )
+            target = w_ref.at[pl.ds(start, ref.shape[0]), columns]
+            loads.append(pltpu.make_async_copy(ref.at[:, columns], target, sems.at[g * pieces + b]))
+            start += ref.shape[0]
     for copy in loads:
         copy.start()
     own = pl.multiple_of(order_ref[chips] * TILE, TILE)
@@ -280,7 +279,7 @@
     other = jnp.concatenate([att_ref[order_ref[b], pl.ds(away, TILE), :] for b in range(chips)], axis=1)
     left = jnp.concatenate([mine, other], axis=0)
     for g in range(groups):
-        for copy in loads[g * chips : (g + 1) * chips]:
+        for copy in loads[g * pieces : (g + 1) * pieces]:
             copy.wait()
         for column in range(g * span, (g + 1) * span, 256):
             done = jnp.dot(left, w_ref[:, column : column + 256], preferred_element_type=F32)
@@ -289,13 +288,13 @@
 
 
 def project(order, attended, weights):
-    width, chips = weights[0].shape[1], len(weights)
+    width, rows = weights[0].shape[1], sum(w.shape[0] for w in weights)
     return pl.pallas_call(
         project_kernel,
         out_shape=(jax.ShapeDtypeStruct((TILE, width), F32), jax.ShapeDtypeStruct((TILE, width), BF)),
-        in_specs=[WHOLE_SM, WHOLE_VM] + [WHOLE_HBM] * chips,
+        in_specs=[WHOLE_SM, WHOLE_VM] + [WHOLE_HBM] * len(weights),
         out_specs=(WHOLE_VM,) * 2,
-        scratch_shapes=[VM((chips * TILE, width), BF), pltpu.SemaphoreType.DMA((3 * chips,))],
+        scratch_shapes=[VM((rows, width), BF), pltpu.SemaphoreType.DMA((3 * len(weights),))],
         compiler_params=pltpu.CompilerParams(vmem_limit_bytes=24 << 20),
         cost_estimate=pl.CostEstimate(flops=4 * TILE * 8 * TILE * width, bytes_accessed=10 << 20, transcendentals=0),
     )(order, attended, *in_hbm(weights))
@@ -349,31 +348,31 @@
 
     w_start, _ = after((w_out, near))
     w_one, w_three = round_x(w_start, 1), round_x(w_start, -1)
+    w_far = opposite(w_start)
     w_turn, _ = after((w_out, far_two))
-    w_two, w_far = round_x(w_turn, 2), opposite(w_turn)
-
-    kv = place_far(blocks(FAR), want, far_mine, far_other, near, TILE, 2 * TILE, True)
-    (far_mine, far_other), _ = after(((far_mine, far_other), kv))
-    q = place_far(blocks(FAR), want, far_mine, far_other, near, 0, TILE, False)
-    kv, _ = after((kv, (w_one, w_three)))
+    w_two = round_x(w_turn, 2)
+
+    q, kv = place_far(blocks(FAR), want, far_mine, far_other, near)
+    kv, _ = after((kv, (w_one, w_three, w_far)))
     behind = lax.ppermute(kv, "z", [(i, (i + 1) % 8) for i in range(8)])
     ahead = lax.ppermute(kv, "z", [(i, (i + 7) % 8) for i in range(8)])
     beside = swap(kv, "yl")
 
-    wf_one, wf_three, wf_two = opposite(w_one), opposite(w_three), round_x(w_far, 2)
+    wf_pair = opposite(jnp.concatenate([w_one, w_three], axis=0))
 
     mid = kv.shape[0] // 2
-    (ahead_low, behind_low), _ = after(((ahead[:mid], behind[:mid]), (w_two, w_far, q)))
-    cross_low = swap(jnp.where(yl == 0, ahead_low, behind_low), "yl")
+    cross_low = swap(jnp.where(yl == 0, ahead[:mid], behind[:mid]), "yl")
     onward = [(2 * i, 2 * ((i + 1) % 8)) for i in range(8)] + [(2 * i + 1, 2 * ((i + 7) % 8) + 1) for i in range(8)]
     cross_high = lax.ppermute(beside[mid:], CTX, onward)
 
     state = attend(index, count, q, [kv, behind, beside, ahead], (24, slots), together=4)
+    w_last, _ = after((w_far, state))
+    wf_two = round_x(w_last, 2)
     attended = attend(cross_index, cross_count, q, [cross_low, cross_high], (6, tiles), state, together=4)
 
     pieces = lax.all_to_all(attended.reshape(8, 2 * TILE, TILE), CHIPS, split_axis=0, concat_axis=0, tiled=True)
     order = jnp.stack(chips(((0, 0), (0, 1), (0, 3), (0, 2), (1, 0), (1, 1), (1, 3), (1, 2))) + [core]).astype(jnp.int32)
-    weights = [w_out, w_one, w_three, w_two, w_far, wf_one, wf_three, wf_two]
+    weights = [w_out, w_one, w_three, w_two, w_far, wf_pair, wf_two]
     mine, other = project(order, pieces, weights)
     return (mine + swap(other, "core").astype(F32)).astype(BF)
 

time: 153 us -> 151 us (0.987)
  waiting for transfers between devices: 46.5 us -> 54.3 us
  starting transfers between devices: 48.3 us -> 42.4 us
  Pallas kernels: 45.7 us -> 42 us
  local copies, waits for them, and re-layouts: 5.6 us -> 2.56 us
  other arithmetic: 5.32 us -> 7.93 us
    ppermute x1, waiting for transfers between devices: 14.3 us -> 0.01 us  [body(): ahead = lax.ppermute(kv, 'z', [(i, (i + 7) % 8) for i in range(8)])]
    ppermute x8, waiting for transfers between devices: 3.33 us -> 17 us  [swap(): return lax.ppermute(array, axis, [(0, 1), (1, 0)])]
    ppermute x10, starting transfers between devices: 16.4 us -> 7.58 us  [round_x(): return lax.ppermute(array, 'x', [(i, (i + by) % 4) for i in range(4)])]
    ppermute x10, waiting for transfers between devices: 18.8 us -> 27.1 us  [round_x(): return lax.ppermute(array, 'x', [(i, (i + by) % 4) for i in range(4)])]
    ppermute x3 -> x2, waiting for transfers between devices: 5.27 us -> 0.01 us  [opposite(): return lax.ppermute(array, ('yl', 'yh'), [(i, 3 - i) for i in range(4)])]
    all_to_all x1, waiting for transfers between devices: 3.73 us -> 7.37 us  [body(): lax.all_to_all(attended.reshape(8, 2 * TILE, TILE), CHIPS, split_axis=0,...]
    ppermute x8, starting transfers between devices: 18 us -> 21.4 us  [swap(): return lax.ppermute(array, axis, [(0, 1), (1, 0)])]
    pallas_call x2 -> x1, Pallas kernels: 8.71 us -> 5.35 us  [place_far(): pl.pallas_call(place_far_kernel, out_shape=(pltpu.HBM((n, TILE), BF), jax...]
  transfers between devices with their start and end apart: 25 -> 24, of which waited for: 10 -> 10; matrix products, arithmetic and copies ran while one was open for 5% -> 6% of each run, Pallas kernels for 27% -> 25%
where the time goes in v8:
time: 151 us; the launch traced here: 149 us
  waiting for transfers between devices  54.3 us (36%)
  starting transfers between devices  42.4 us (28%)
  Pallas kernels  42 us (28%)
  other arithmetic  7.93 us (5%)
  local copies, waits for them, and re-layouts  2.56 us (2%)
    ppermute x10, waiting for transfers between devices, round_x(): return lax.ppermute(array, 'x', [(i, (i + by) % 4) for i in range(4)])  27.1 us
    ppermute x8, starting transfers between devices, swap(): return lax.ppermute(array, axis, [(0, 1), (1, 0)])  21.4 us
    ppermute x8, waiting for transfers between devices, swap(): return lax.ppermute(array, axis, [(0, 1), (1, 0)])  17 us
    pallas_call x2, Pallas kernels, attend(): pl.pallas_call(functools.partial(attend_kernel, sizes, together, len(fram...  16.6 us
    pallas_call x2, Pallas kernels, qkv(): pl.pallas_call(functools.partial(qkv_kernel, chunks), out_shape=(jax.Shap...  12 us
    ppermute x10, starting transfers between devices, round_x(): return lax.ppermute(array, 'x', [(i, (i + by) % 4) for i in range(4)])  7.58 us
    all_to_all x1, waiting for transfers between devices, body(): lax.all_to_all(attended.reshape(8, 2 * TILE, TILE), CHIPS, split_axis=0,...  7.37 us
    pallas_call x1, Pallas kernels, place_far(): pl.pallas_call(place_far_kernel, out_shape=(pltpu.HBM((n, TILE), BF), jax...  5.35 us
  transfers between devices with their start and end apart: 24, of which 10 were waited for; matrix products, arithmetic and copies ran while one was open for 6% of the time, Pallas kernels for 25%

profile of v8, /device:TPU:1, one launch (start us, length us, event | category | flops | bytes accessed | tf_op | source)
XLA Modules:
  0.0 149.4 jit_solution(15133455107108055889)
XLA Ops:
  0.0 3.2 %collective-permute-start.5 = (bf16[3072,384]{1,0:T(8,128)(2,1)}, bf16[3072,384]{1,0:T(8,128)(2,1)}, u32[]{:S(2)}, u32[]{:S(2)}) collective-permute-start(bf16[3072,384]{1,0:T(8,128)(2,1)} %own_ref.3), channel_id=1, source_target_pairs={{0,1},{1,0},{2,3},{3,2},{4,5},{5,4},{6,7},{7,6},{8,9},{9,8},{10,11... | collective-permute-start | bytes 7077896 | tf_op jit(solution)/shard_map/ppermute | solution.py:38
  4.7 2.2 %collective-permute-start.6 = (bf16[128,3072]{1,0:T(8,128)(2,1)}, bf16[128,3072]{1,0:T(8,128)(2,1)}, u32[]{:S(2)}, u32[]{:S(2)}) collective-permute-start(bf16[128,3072]{1,0:T(8,128)(2,1)} %refs_0_.2), channel_id=1, source_target_pairs={{0,8},{8,0},{1,9},{9,1},{2,10},{10,2},{3,11},{11,3},{4,12},{12,4},... | collective-permute-start | bytes 2359304 | tf_op jit(solution)/shard_map/ppermute | solution.py:38
  8.7 14.0 %collective-permute-done.2.refs_2_ = bf16[128,3072]{1,0:T(8,128)(2,1)S(1)} collective-permute-done((bf16[128,3072]{1,0:T(8,128)(2,1)}, bf16[128,3072]{1,0:T(8,128)(2,1)S(1)}, u32[]{:S(2)}, u32[]{:S(2)}) %collective-permute-start.2) | collective-permute-done | bytes 786464 | tf_op jit(solution)/shard_map/ppermute | solution.py:34
  23.5 1.9 %collective-permute-start.3 = (bf16[64,3072]{1,0:T(8,128)(2,1)}, bf16[64,3072]{1,0:T(8,128)(2,1)S(1)}, u32[]{:S(2)}, u32[]{:S(2)}) collective-permute-start(bf16[64,3072]{1,0:T(8,128)(2,1)} %slice.21), channel_id=1, source_target_pairs={{0,6},{2,0},{4,2},{6,4},{1,7},{3,1},{5,3},{7,5},{8,14},{10,8},{12,... | collective-permute-start | bytes 1179656 | tf_op jit(solution)/shard_map/ppermute | solution.py:34
  28.1 2.7 %collective-permute-start.9 = (bf16[128,3072]{1,0:T(8,128)(2,1)}, bf16[128,3072]{1,0:T(8,128)(2,1)S(1)}, u32[]{:S(2)}, u32[]{:S(2)}) collective-permute-start(bf16[128,3072]{1,0:T(8,128)(2,1)} %collective-permute-done.6.refs_3_), channel_id=1, source_target_pairs={{0,6},{2,0},{4,2},{6,4},{1,7},{3,1},{5,3},{7,5},{8,14},{10,8},{12,... | collective-permute-start | bytes 2359304 | tf_op jit(solution)/shard_map/ppermute | solution.py:34
  30.8 2.9 %collective-permute-done.3.refs_1_ = bf16[64,3072]{1,0:T(8,128)(2,1)S(1)} collective-permute-done((bf16[64,3072]{1,0:T(8,128)(2,1)}, bf16[64,3072]{1,0:T(8,128)(2,1)S(1)}, u32[]{:S(2)}, u32[]{:S(2)}) %collective-permute-start.3) | collective-permute-done | bytes 393248 | tf_op jit(solution)/shard_map/ppermute | solution.py:34
  33.7 3.4 %collective-permute-done.1.refs_0_ = bf16[64,3072]{1,0:T(8,128)(2,1)S(1)} collective-permute-done((bf16[64,3072]{1,0:T(8,128)(2,1)}, bf16[64,3072]{1,0:T(8,128)(2,1)S(1)}, u32[]{:S(2)}, u32[]{:S(2)}) %collective-permute-start.1) | collective-permute-done | bytes 393248 | tf_op jit(solution)/shard_map/ppermute | solution.py:34
  37.2 2.8 %collective-permute-start.4 = (bf16[128,3072]{1,0:T(8,128)(2,1)S(1)}, bf16[128,3072]{1,0:T(8,128)(2,1)S(1)}, u32[]{:S(2)}, u32[]{:S(2)}) collective-permute-start(bf16[128,3072]{1,0:T(8,128)(2,1)S(1)} %pad_maximum_fusion.1), channel_id=1, source_target_pairs={{0,8},{8,0},{1,9},{9,1},{2,10},{10,2},{3,11},{11,3},{4,12},{12,4},... | collective-permute-start | bytes 2359304 | tf_op jit(solution)/shard_map/ppermute | solution.py:38
  40.0 6.6 %shard_map.64 = (bf16[512,384]{1,0:T(8,128)(2,1)S(1)}, bf16[512,384]{1,0:T(8,128)(2,1)S(1)}) custom-call(bf16[3072,384]{1,0:T(8,128)(2,1)} %own_ref.3, bf16[3072,384]{1,0:T(8,128)(2,1)} %collective-permute-done.5.other_ref, bf16[128,3072]{1,0:T(8,128)(2,1)S(1)} %copy-done, bf16[128,3072]{1,0:T(8,128)(2,1)S(1)} %collective-permute-done.refs_1_, ...), custom_call_target="tpu_custom_call" | custom-call | flops 2415919104 | bytes 8388608 | tf_op jit(solution)/shard_map/pallas_call | solution.py:73
  46.6 4.1 %collective-permute-start.7 = (bf16[512,384]{1,0:T(8,128)(2,1)S(1)}, bf16[512,384]{1,0:T(8,128)(2,1)S(1)}, u32[]{:S(2)}, u32[]{:S(2)}) collective-permute-start(bf16[512,384]{1,0:T(8,128)(2,1)S(1)} %get-tuple-element.27), channel_id=1, source_target_pairs={{0,1},{1,0},{2,3},{3,2},{4,5},{5,4},{6,7},{7,6},{8,9},{9,8},{10,11... | collective-permute-start | bytes 1179656 | tf_op jit(solution)/shard_map/ppermute | solution.py:38
  52.0 3.6 %shard_map.65.near_ref = bf16[2048,384]{1,0:T(8,128)(2,1)S(1)} custom-call(f32[8]{0:T(128)S(1)} %convert_element_type.18.block_ref, s32[2048,1]{1,0:T(8,128)S(1)} %copy.9.want_ref, bf16[512,384]{1,0:T(8,128)(2,1)S(1)} %get-tuple-element.26.first_ref, bf16[512,384]{1,0:T(8,128)(2,1)S(1)} %collective-permute-done.7.second_ref), custom_call_target="tpu_custom_call" | custom-call | flops 1610612736 | bytes 4194304 | tf_op jit(solution)/shard_map/pallas_call | solution.py:139
  55.7 1.3 collective-permute-start.13
  57.1 1.5 collective-permute-start.11
  58.5 5.4 %shard_map.66 = (bf16[512,384]{1,0:T(8,128)(2,1)S(1)}, bf16[512,384]{1,0:T(8,128)(2,1)S(1)}) custom-call(bf16[3072,384]{1,0:T(8,128)(2,1)} %own_ref.3, bf16[3072,384]{1,0:T(8,128)(2,1)} %collective-permute-done.5.other_ref, bf16[64,3072]{1,0:T(8,128)(2,1)S(1)} %collective-permute-done.1.refs_0_, bf16[64,3072]{1,0:T(8,128)(2,1)S(1)} %collective-permute-done.3.refs_1_, ...), custom_call_target="tpu_custom_call" | custom-call | flops 2415919104 | bytes 8388608 | tf_op jit(solution)/shard_map/pallas_call | solution.py:73
  64.0 5.4 %collective-permute-start.10 = (bf16[512,384]{1,0:T(8,128)(2,1)S(1)}, bf16[512,384]{1,0:T(8,128)(2,1)S(1)}, u32[]{:S(2)}, u32[]{:S(2)}) collective-permute-start(bf16[512,384]{1,0:T(8,128)(2,1)S(1)} %get-tuple-element.33), channel_id=1, source_target_pairs={{0,1},{1,0},{2,3},{3,2},{4,5},{5,4},{6,7},{7,6},{8,9},{9,8},{10,11... | collective-permute-start | bytes 1179656 | tf_op jit(solution)/shard_map/ppermute | solution.py:38
  69.4 1.3 collective-permute-done.10.second_ref
  70.7 5.4 %shard_map.67 = (bf16[2048,128]{1,0:T(8,128)(2,1)}, bf16[2048,256]{1,0:T(8,128)(2,1)}) custom-call(f32[8]{0:T(128)S(1)} %convert_element_type.21.block_ref, s32[2048,1]{1,0:T(8,128)S(1)} %copy.9.want_ref, bf16[512,384]{1,0:T(8,128)(2,1)S(1)} %get-tuple-element.32.first_ref, bf16[512,384]{1,0:T(8,128)(2,1)S(1)} %collective-permute-done.10.second_ref, ...), custom_call_target="tpu_custom_call" | custom-call | flops 1610612736 | bytes 4194304 | tf_op jit(solution)/shard_map/pallas_call | solution.py:151
  76.2 1.7 %collective-permute-start.15 = (bf16[2048,256]{1,0:T(8,128)(2,1)}, bf16[2048,256]{1,0:T(8,128)(2,1)S(1)}, u32[]{:S(2)}, u32[]{:S(2)}) collective-permute-start(bf16[2048,256]{1,0:T(8,128)(2,1)} %get-tuple-element.38.refs_0_), channel_id=1, source_target_pairs={{0,32},{32,64},{64,96},{96,128},{128,160},{160,192},{192,224},{224... | collective-permute-start | bytes 3145736 | tf_op jit(solution)/shard_map/ppermute | solution.py:357
  77.9 4.0 %collective-permute-start.14 = (bf16[2048,256]{1,0:T(8,128)(2,1)}, bf16[2048,256]{1,0:T(8,128)(2,1)S(1)}, u32[]{:S(2)}, u32[]{:S(2)}) collective-permute-start(bf16[2048,256]{1,0:T(8,128)(2,1)} %get-tuple-element.38.refs_0_), channel_id=1, source_target_pairs={{0,224},{32,0},{64,32},{96,64},{128,96},{160,128},{192,160},{224,1... | collective-permute-start | bytes 3145736 | tf_op jit(solution)/shard_map/ppermute | solution.py:358
  82.0 2.6 %pad_maximum_fusion = bf16[256,3072]{1,0:T(8,128)(2,1)} fusion(bf16[128,3072]{1,0:T(8,128)(2,1)} %collective-permute-done.12.refs_2_, bf16[128,3072]{1,0:T(8,128)(2,1)} %collective-permute-done.11.refs_1_), kind=kLoop, calls=%fused_computation | loop fusion | flops 3145728 | bytes 3145728 | tf_op jit(solution)/shard_map/concatenate | solution.py:361
  85.1 13.7 %collective-permute-done.17.refs_2_ = bf16[2048,256]{1,0:T(8,128)(2,1)S(1)} collective-permute-done((bf16[2048,256]{1,0:T(8,128)(2,1)}, bf16[2048,256]{1,0:T(8,128)(2,1)S(1)}, u32[]{:S(2)}, u32[]{:S(2)}) %collective-permute-start.17) | collective-permute-done | bytes 1048608 | tf_op jit(solution)/shard_map/ppermute | solution.py:38
  98.8 1.7 %collective-permute-start.18 = (bf16[1024,256]{1,0:T(8,128)(2,1)S(1)}, bf16[1024,256]{1,0:T(8,128)(2,1)S(1)}, u32[]{:S(2)}, u32[]{:S(2)}) collective-permute-start(bf16[1024,256]{1,0:T(8,128)(2,1)S(1)} %slice.24), channel_id=1, source_target_pairs={{0,32},{32,64},{64,96},{96,128},{128,160},{160,192},{192,224},{224... | collective-permute-start | bytes 1572872 | tf_op jit(solution)/shard_map/ppermute | solution.py:366
  100.5 2.8 %collective-permute-done.15.refs_1_ = bf16[2048,256]{1,0:T(8,128)(2,1)S(1)} collective-permute-done((bf16[2048,256]{1,0:T(8,128)(2,1)}, bf16[2048,256]{1,0:T(8,128)(2,1)S(1)}, u32[]{:S(2)}, u32[]{:S(2)}) %collective-permute-start.15) | collective-permute-done | bytes 1048608 | tf_op jit(solution)/shard_map/ppermute | solution.py:357
  103.3 1.7 %collective-permute-start.16 = (bf16[1024,256]{1,0:T(8,128)(2,1)S(1)}, bf16[1024,256]{1,0:T(8,128)(2,1)S(1)}, u32[]{:S(2)}, u32[]{:S(2)}) collective-permute-start(bf16[1024,256]{1,0:T(8,128)(2,1)S(1)} %slice_select_fusion), channel_id=1, source_target_pairs={{0,16},{16,0},{1,17},{17,1},{2,18},{18,2},{3,19},{19,3},{4,20},{20... | collective-permute-start | bytes 1572872 | tf_op jit(solution)/shard_map/ppermute | solution.py:38
  105.1 10.4 %shard_map.68 = (f32[2048,128]{1,0:T(8,128)S(1)}, f32[2048,128]{1,0:T(8,128)S(1)}) custom-call(s32[16,30]{1,0:T(8,128)S(1)} %copy.14.index_ref, s32[16]{0:T(128)S(1)} %get-tuple-element.40.count_ref, bf16[2048,128]{1,0:T(8,128)(2,1)S(1)} %copy-done.2, bf16[2048,256]{1,0:T(8,128)(2,1)} %get-tuple-element.38.refs_0_, ...), custom_call_target="tpu_custom_call" | custom-call | flops 16106127360 | bytes 6291456 | tf_op jit(solution)/shard_map/pallas_call | solution.py:245
  115.6 6.2 %shard_map.69 = bf16[2048,128]{1,0:T(8,128)(2,1)} custom-call(s32[16,16]{1,0:T(8,128)S(1)} %select_reduce_fusion.3.index_ref, s32[16]{0:T(128)S(1)} %get-tuple-element.29.count_ref, bf16[2048,128]{1,0:T(8,128)(2,1)S(1)} %copy-done.2, bf16[1024,256]{1,0:T(8,128)(2,1)S(1)} %collective-permute-done.16.refs_0_, ...), custom_call_target="tpu_custom_call" | custom-call | flops 8589934592 | bytes 6291456 | tf_op jit(solution)/shard_map/pallas_call | solution.py:245
  121.8 4.2 %all-to-all-start = ((bf16[8,256,128]{2,1,0:T(8,128)(2,1)}), bf16[8,256,128]{2,1,0:T(8,128)(2,1)S(1)}, u32[]{:S(2)}, u32[]{:S(2)}) async-start(bf16[8,256,128]{2,1,0:T(8,128)(2,1)} %bitcast.26), calls=%async_computation | async-start | bytes 1048576 | tf_op jit(solution)/shard_map/all_to_all | solution.py:373
  126.1 6.7 %collective-permute-done.21.refs_6_ = bf16[128,3072]{1,0:T(8,128)(2,1)S(1)} collective-permute-done((bf16[128,3072]{1,0:T(8,128)(2,1)}, bf16[128,3072]{1,0:T(8,128)(2,1)S(1)}, u32[]{:S(2)}, u32[]{:S(2)}) %collective-permute-start.21) | collective-permute-done | bytes 786464 | tf_op jit(solution)/shard_map/ppermute | solution.py:34
  132.8 7.4 %all-to-all-done.att_ref = bf16[8,256,128]{2,1,0:T(8,128)(2,1)S(1)} async-done(((bf16[8,256,128]{2,1,0:T(8,128)(2,1)}), bf16[8,256,128]{2,1,0:T(8,128)(2,1)S(1)}, u32[]{:S(2)}, u32[]{:S(2)}) %all-to-all-start) | async-done | bytes 524320 | tf_op jit(solution)/shard_map/all_to_all | solution.py:373
  140.2 4.4 %shard_map.70 = (f32[128,3072]{1,0:T(8,128)S(1)}, bf16[128,3072]{1,0:T(8,128)(2,1)S(1)}) custom-call(s32[9]{0:T(128)S(1)} %stack.93.order_ref, bf16[8,256,128]{2,1,0:T(8,128)(2,1)S(1)} %all-to-all-done.att_ref, bf16[128,3072]{1,0:T(8,128)(2,1)} %refs_0_.3, bf16[128,3072]{1,0:T(8,128)(2,1)} %collective-permute-done.11.refs_1_, ...), custom_call_target="tpu_custom_call" | custom-call | flops 1610612736 | bytes 10485760 | tf_op jit(solution)/shard_map/pallas_call | solution.py:292
  144.6 1.8 %collective-permute-start.22 = (bf16[128,3072]{1,0:T(8,128)(2,1)S(1)}, bf16[128,3072]{1,0:T(8,128)(2,1)S(1)}, u32[]{:S(2)}, u32[]{:S(2)}) collective-permute-start(bf16[128,3072]{1,0:T(8,128)(2,1)S(1)} %get-tuple-element.46), channel_id=1, source_target_pairs={{0,1},{1,0},{2,3},{3,2},{4,5},{5,4},{6,7},{7,6},{8,9},{9,8},{10,11... | collective-permute-start | bytes 2359304 | tf_op jit(solution)/shard_map/ppermute | solution.py:38
  146.4 1.9 %collective-permute-done.22 = bf16[128,3072]{1,0:T(8,128)(2,1)S(1)} collective-permute-done((bf16[128,3072]{1,0:T(8,128)(2,1)S(1)}, bf16[128,3072]{1,0:T(8,128)(2,1)S(1)}, u32[]{:S(2)}, u32[]{:S(2)}) %collective-permute-start.22) | collective-permute-done | bytes 786464 | tf_op jit(solution)/shard_map/ppermute | solution.py:38
  (60 shorter events, 10.2 us)
Async XLA Ops:
  0.0 27.7 %copy-start.4 = (s32[1,2048]{1,0:T(1,128)S(1)}, s32[1,2048]{1,0:T(1,128)}, u32[]{:S(2)}) copy-start(s32[1,2048]{1,0:T(1,128)} %param.9) | copy-start | bytes 24580
  0.0 40.0 %collective-permute-start.5 = (bf16[3072,384]{1,0:T(8,128)(2,1)}, bf16[3072,384]{1,0:T(8,128)(2,1)}, u32[]{:S(2)}, u32[]{:S(2)}) collective-permute-start(bf16[3072,384]{1,0:T(8,128)(2,1)} %own_ref.3), channel_id=1, source_target_pairs={{0,1},{1,0},{2,3},{3,2},{4,5},{5,4},{6,7},{7,6},{8,9},{9,8},{10,11... | collective-permute-start | bytes 7077896 | tf_op jit(solution)/shard_map/ppermute | solution.py:38
  3.2 19.5 %collective-permute-start.2 = (bf16[128,3072]{1,0:T(8,128)(2,1)}, bf16[128,3072]{1,0:T(8,128)(2,1)S(1)}, u32[]{:S(2)}, u32[]{:S(2)}) collective-permute-start(bf16[128,3072]{1,0:T(8,128)(2,1)} %refs_0_.2), channel_id=1, source_target_pairs={{0,6},{2,0},{4,2},{6,4},{1,7},{3,1},{5,3},{7,5},{8,14},{10,8},{12,... | collective-permute-start | bytes 2359304 | tf_op jit(solution)/shard_map/ppermute | solution.py:34
  4.0 21.4 %collective-permute-start = (bf16[128,3072]{1,0:T(8,128)(2,1)}, bf16[128,3072]{1,0:T(8,128)(2,1)S(1)}, u32[]{:S(2)}, u32[]{:S(2)}) collective-permute-start(bf16[128,3072]{1,0:T(8,128)(2,1)} %refs_0_.2), channel_id=1, source_target_pairs={{0,2},{2,4},{4,6},{6,0},{1,3},{3,5},{5,7},{7,1},{8,10},{10,12},{12... | collective-permute-start | bytes 2359304 | tf_op jit(solution)/shard_map/ppermute | solution.py:34
  4.7 23.4 %collective-permute-start.6 = (bf16[128,3072]{1,0:T(8,128)(2,1)}, bf16[128,3072]{1,0:T(8,128)(2,1)}, u32[]{:S(2)}, u32[]{:S(2)}) collective-permute-start(bf16[128,3072]{1,0:T(8,128)(2,1)} %refs_0_.2), channel_id=1, source_target_pairs={{0,8},{8,0},{1,9},{9,1},{2,10},{10,2},{3,11},{11,3},{4,12},{12,4},... | collective-permute-start | bytes 2359304 | tf_op jit(solution)/shard_map/ppermute | solution.py:38
  23.5 10.2 %collective-permute-start.3 = (bf16[64,3072]{1,0:T(8,128)(2,1)}, bf16[64,3072]{1,0:T(8,128)(2,1)S(1)}, u32[]{:S(2)}, u32[]{:S(2)}) collective-permute-start(bf16[64,3072]{1,0:T(8,128)(2,1)} %slice.21), channel_id=1, source_target_pairs={{0,6},{2,0},{4,2},{6,4},{1,7},{3,1},{5,3},{7,5},{8,14},{10,8},{12,... | collective-permute-start | bytes 1179656 | tf_op jit(solution)/shard_map/ppermute | solution.py:34
  26.2 11.0 %collective-permute-start.1 = (bf16[64,3072]{1,0:T(8,128)(2,1)}, bf16[64,3072]{1,0:T(8,128)(2,1)S(1)}, u32[]{:S(2)}, u32[]{:S(2)}) collective-permute-start(bf16[64,3072]{1,0:T(8,128)(2,1)} %slice.20), channel_id=1, source_target_pairs={{0,2},{2,4},{4,6},{6,0},{1,3},{3,5},{5,7},{7,1},{8,10},{10,12},{12... | collective-permute-start | bytes 1179656 | tf_op jit(solution)/shard_map/ppermute | solution.py:34
  28.1 12.0 %copy-start = (bf16[128,3072]{1,0:T(8,128)(2,1)S(1)}, bf16[128,3072]{1,0:T(8,128)(2,1)}, u32[]{:S(2)}) copy-start(bf16[128,3072]{1,0:T(8,128)(2,1)} %refs_0_.2) | copy-start | bytes 2359300
  28.1 30.4 %collective-permute-start.9 = (bf16[128,3072]{1,0:T(8,128)(2,1)}, bf16[128,3072]{1,0:T(8,128)(2,1)S(1)}, u32[]{:S(2)}, u32[]{:S(2)}) collective-permute-start(bf16[128,3072]{1,0:T(8,128)(2,1)} %collective-permute-done.6.refs_3_), channel_id=1, source_target_pairs={{0,6},{2,0},{4,2},{6,4},{1,7},{3,1},{5,3},{7,5},{8,14},{10,8},{12,... | collective-permute-start | bytes 2359304 | tf_op jit(solution)/shard_map/ppermute | solution.py:34
  30.8 27.7 %collective-permute-start.8 = (bf16[128,3072]{1,0:T(8,128)(2,1)}, bf16[128,3072]{1,0:T(8,128)(2,1)S(1)}, u32[]{:S(2)}, u32[]{:S(2)}) collective-permute-start(bf16[128,3072]{1,0:T(8,128)(2,1)} %collective-permute-done.6.refs_3_), channel_id=1, source_target_pairs={{0,2},{2,4},{4,6},{6,0},{1,3},{3,5},{5,7},{7,1},{8,10},{10,12},{12... | collective-permute-start | bytes 2359304 | tf_op jit(solution)/shard_map/ppermute | solution.py:34
  37.2 18.5 %collective-permute-start.4 = (bf16[128,3072]{1,0:T(8,128)(2,1)S(1)}, bf16[128,3072]{1,0:T(8,128)(2,1)S(1)}, u32[]{:S(2)}, u32[]{:S(2)}) collective-permute-start(bf16[128,3072]{1,0:T(8,128)(2,1)S(1)} %pad_maximum_fusion.1), channel_id=1, source_target_pairs={{0,8},{8,0},{1,9},{9,1},{2,10},{10,2},{3,11},{11,3},{4,12},{12,4},... | collective-permute-start | bytes 2359304 | tf_op jit(solution)/shard_map/ppermute | solution.py:38
  46.6 5.5 %collective-permute-start.7 = (bf16[512,384]{1,0:T(8,128)(2,1)S(1)}, bf16[512,384]{1,0:T(8,128)(2,1)S(1)}, u32[]{:S(2)}, u32[]{:S(2)}) collective-permute-start(bf16[512,384]{1,0:T(8,128)(2,1)S(1)} %get-tuple-element.27), channel_id=1, source_target_pairs={{0,1},{1,0},{2,3},{3,2},{4,5},{5,4},{6,7},{7,6},{8,9},{9,8},{10,11... | collective-permute-start | bytes 1179656 | tf_op jit(solution)/shard_map/ppermute | solution.py:38
  55.7 8.3 %copy-start.1 = (bf16[2048,384]{1,0:T(8,128)(2,1)}, bf16[2048,384]{1,0:T(8,128)(2,1)S(1)}, u32[]{:S(2)}) copy-start(bf16[2048,384]{1,0:T(8,128)(2,1)S(1)} %shard_map.65.near_ref) | copy-start | bytes 4718596
  55.7 20.3 %collective-permute-start.13 = (bf16[128,3072]{1,0:T(8,128)(2,1)}, bf16[128,3072]{1,0:T(8,128)(2,1)}, u32[]{:S(2)}, u32[]{:S(2)}) collective-permute-start(bf16[128,3072]{1,0:T(8,128)(2,1)} %refs_0_.3), channel_id=1, source_target_pairs={{0,24},{8,16},{16,8},{24,0},{1,25},{9,17},{17,9},{25,1},{2,26},{10... | collective-permute-start | bytes 2359304 | tf_op jit(solution)/shard_map/ppermute | solution.py:42
  57.1 19.0 %collective-permute-start.12 = (bf16[128,3072]{1,0:T(8,128)(2,1)}, bf16[128,3072]{1,0:T(8,128)(2,1)}, u32[]{:S(2)}, u32[]{:S(2)}) collective-permute-start(bf16[128,3072]{1,0:T(8,128)(2,1)} %refs_0_.3), channel_id=1, source_target_pairs={{0,6},{2,0},{4,2},{6,4},{1,7},{3,1},{5,3},{7,5},{8,14},{10,8},{12,... | collective-permute-start | bytes 2359304 | tf_op jit(solution)/shard_map/ppermute | solution.py:34
  57.1 19.0 %collective-permute-start.11 = (bf16[128,3072]{1,0:T(8,128)(2,1)}, bf16[128,3072]{1,0:T(8,128)(2,1)}, u32[]{:S(2)}, u32[]{:S(2)}) collective-permute-start(bf16[128,3072]{1,0:T(8,128)(2,1)} %refs_0_.3), channel_id=1, source_target_pairs={{0,2},{2,4},{4,6},{6,0},{1,3},{3,5},{5,7},{7,1},{8,10},{10,12},{12... | collective-permute-start | bytes 2359304 | tf_op jit(solution)/shard_map/ppermute | solution.py:34
  64.0 6.7 %collective-permute-start.10 = (bf16[512,384]{1,0:T(8,128)(2,1)S(1)}, bf16[512,384]{1,0:T(8,128)(2,1)S(1)}, u32[]{:S(2)}, u32[]{:S(2)}) collective-permute-start(bf16[512,384]{1,0:T(8,128)(2,1)S(1)} %get-tuple-element.33), channel_id=1, source_target_pairs={{0,1},{1,0},{2,3},{3,2},{4,5},{5,4},{6,7},{7,6},{8,9},{9,8},{10,11... | collective-permute-start | bytes 1179656 | tf_op jit(solution)/shard_map/ppermute | solution.py:38
  76.1 22.7 %collective-permute-start.17 = (bf16[2048,256]{1,0:T(8,128)(2,1)}, bf16[2048,256]{1,0:T(8,128)(2,1)S(1)}, u32[]{:S(2)}, u32[]{:S(2)}) collective-permute-start(bf16[2048,256]{1,0:T(8,128)(2,1)} %get-tuple-element.38.refs_0_), channel_id=1, source_target_pairs={{0,16},{16,0},{1,17},{17,1},{2,18},{18,2},{3,19},{19,3},{4,20},{20... | collective-permute-start | bytes 3145736 | tf_op jit(solution)/shard_map/ppermute | solution.py:38
  76.2 27.1 %collective-permute-start.15 = (bf16[2048,256]{1,0:T(8,128)(2,1)}, bf16[2048,256]{1,0:T(8,128)(2,1)S(1)}, u32[]{:S(2)}, u32[]{:S(2)}) collective-permute-start(bf16[2048,256]{1,0:T(8,128)(2,1)} %get-tuple-element.38.refs_0_), channel_id=1, source_target_pairs={{0,32},{32,64},{64,96},{96,128},{128,160},{160,192},{192,224},{224... | collective-permute-start | bytes 3145736 | tf_op jit(solution)/shard_map/ppermute | solution.py:357
  77.9 25.4 %collective-permute-start.14 = (bf16[2048,256]{1,0:T(8,128)(2,1)}, bf16[2048,256]{1,0:T(8,128)(2,1)S(1)}, u32[]{:S(2)}, u32[]{:S(2)}) collective-permute-start(bf16[2048,256]{1,0:T(8,128)(2,1)} %get-tuple-element.38.refs_0_), channel_id=1, source_target_pairs={{0,224},{32,0},{64,32},{96,64},{128,96},{160,128},{192,160},{224,1... | collective-permute-start | bytes 3145736 | tf_op jit(solution)/shard_map/ppermute | solution.py:358
  82.0 44.1 %collective-permute-start.19 = (bf16[128,3072]{1,0:T(8,128)(2,1)}, bf16[128,3072]{1,0:T(8,128)(2,1)}, u32[]{:S(2)}, u32[]{:S(2)}) collective-permute-start(bf16[128,3072]{1,0:T(8,128)(2,1)} %refs_0_.3), channel_id=1, source_target_pairs={{0,4},{2,6},{4,0},{6,2},{1,5},{3,7},{5,1},{7,3},{8,12},{10,14},{12... | collective-permute-start | bytes 2359304 | tf_op jit(solution)/shard_map/ppermute | solution.py:34
  84.6 20.5 %copy-start.2 = (bf16[2048,128]{1,0:T(8,128)(2,1)S(1)}, bf16[2048,128]{1,0:T(8,128)(2,1)}, u32[]{:S(2)}) copy-start(bf16[2048,128]{1,0:T(8,128)(2,1)} %get-tuple-element.35.q_ref) | copy-start | bytes 1572868
  84.6 41.5 %collective-permute-start.20 = (bf16[256,3072]{1,0:T(8,128)(2,1)}, bf16[256,3072]{1,0:T(8,128)(2,1)}, u32[]{:S(2)}, u32[]{:S(2)}) collective-permute-start(bf16[256,3072]{1,0:T(8,128)(2,1)} %pad_maximum_fusion), channel_id=1, source_target_pairs={{0,24},{8,16},{16,8},{24,0},{1,25},{9,17},{17,9},{25,1},{2,26},{10... | collective-permute-start | bytes 4718600 | tf_op jit(solution)/shard_map/ppermute | solution.py:42
  98.8 16.8 %collective-permute-start.18 = (bf16[1024,256]{1,0:T(8,128)(2,1)S(1)}, bf16[1024,256]{1,0:T(8,128)(2,1)S(1)}, u32[]{:S(2)}, u32[]{:S(2)}) collective-permute-start(bf16[1024,256]{1,0:T(8,128)(2,1)S(1)} %slice.24), channel_id=1, source_target_pairs={{0,32},{32,64},{64,96},{96,128},{128,160},{160,192},{192,224},{224... | collective-permute-start | bytes 1572872 | tf_op jit(solution)/shard_map/ppermute | solution.py:366
  103.3 12.3 %collective-permute-start.16 = (bf16[1024,256]{1,0:T(8,128)(2,1)S(1)}, bf16[1024,256]{1,0:T(8,128)(2,1)S(1)}, u32[]{:S(2)}, u32[]{:S(2)}) collective-permute-start(bf16[1024,256]{1,0:T(8,128)(2,1)S(1)} %slice_select_fusion), channel_id=1, source_target_pairs={{0,16},{16,0},{1,17},{17,1},{2,18},{18,2},{3,19},{19,3},{4,20},{20... | collective-permute-start | bytes 1572872 | tf_op jit(solution)/shard_map/ppermute | solution.py:38
  115.5 17.3 %collective-permute-start.21 = (bf16[128,3072]{1,0:T(8,128)(2,1)}, bf16[128,3072]{1,0:T(8,128)(2,1)S(1)}, u32[]{:S(2)}, u32[]{:S(2)}) collective-permute-start(bf16[128,3072]{1,0:T(8,128)(2,1)} %collective-permute-done.13.refs_4_), channel_id=1, source_target_pairs={{0,4},{2,6},{4,0},{6,2},{1,5},{3,7},{5,1},{7,3},{8,12},{10,14},{12... | collective-permute-start | bytes 2359304 | tf_op jit(solution)/shard_map/ppermute | solution.py:34
  121.8 18.4 %all-to-all-start = ((bf16[8,256,128]{2,1,0:T(8,128)(2,1)}), bf16[8,256,128]{2,1,0:T(8,128)(2,1)S(1)}, u32[]{:S(2)}, u32[]{:S(2)}) async-start(bf16[8,256,128]{2,1,0:T(8,128)(2,1)} %bitcast.26), calls=%async_computation | async-start | bytes 1048576 | tf_op jit(solution)/shard_map/all_to_all | solution.py:373
  132.8 7.4 %copy-start.3 = (bf16[128,3072]{1,0:T(8,128)(2,1)}, bf16[128,3072]{1,0:T(8,128)(2,1)S(1)}, u32[]{:S(2)}) copy-start(bf16[128,3072]{1,0:T(8,128)(2,1)S(1)} %collective-permute-done.21.refs_6_) | copy-start | bytes 2359300
  144.6 3.8 %collective-permute-start.22 = (bf16[128,3072]{1,0:T(8,128)(2,1)S(1)}, bf16[128,3072]{1,0:T(8,128)(2,1)S(1)}, u32[]{:S(2)}, u32[]{:S(2)}) collective-permute-start(bf16[128,3072]{1,0:T(8,128)(2,1)S(1)} %get-tuple-element.46), channel_id=1, source_target_pairs={{0,1},{1,0},{2,3},{3,2},{4,5},{5,4},{6,7},{7,6},{8,9},{9,8},{10,11... | collective-permute-start | bytes 2359304 | tf_op jit(solution)/shard_map/ppermute | solution.py:38

commit v9 on v8

--- a/solution.py
+++ b/solution.py
@@ -259,18 +259,15 @@
     )(index, count, q, *frames, *(old or ()))
 
 
-def project_kernel(order_ref, att_ref, *refs):
+def project_kernel(early, order_ref, att_ref, *refs):
     weights, (mine_ref, other_ref, w_ref, sems) = refs[:-4], refs[-4:]
     chips, width, groups = att_ref.shape[0], mine_ref.shape[1], 3
     span = width // groups
-    pieces = len(weights)
     loads = []
     for g in range(groups):
-        columns, start = slice(g * span, (g + 1) * span), 0
-        for b, ref in enumerate(weights):
-            target = w_ref.at[pl.ds(start, ref.shape[0]), columns]
-            loads.append(pltpu.make_async_copy(ref.at[:, columns], target, sems.at[g * pieces + b]))
-            start += ref.shape[0]
+        columns = slice(g * span, (g + 1) * span)
+        for i, b in enumerate(early):
+            loads.append(pltpu.make_async_copy(weights[b].at[:, columns], w_ref.at[i, :, columns], sems.at[g * len(early) + i]))
     for copy in loads:
         copy.start()
     own = pl.multiple_of(order_ref[chips] * TILE, TILE)
@@ -278,26 +275,31 @@
     mine = jnp.concatenate([att_ref[order_ref[b], pl.ds(own, TILE), :] for b in range(chips)], axis=1)
     other = jnp.concatenate([att_ref[order_ref[b], pl.ds(away, TILE), :] for b in range(chips)], axis=1)
     left = jnp.concatenate([mine, other], axis=0)
+    step = 256
     for g in range(groups):
-        for copy in loads[g * pieces : (g + 1) * pieces]:
+        for copy in loads[g * len(early) : (g + 1) * len(early)]:
             copy.wait()
-        for column in range(g * span, (g + 1) * span, 256):
-            done = jnp.dot(left, w_ref[:, column : column + 256], preferred_element_type=F32)
-            mine_ref[:, column : column + 256] = done[:TILE]
-            other_ref[:, column : column + 256] = done[TILE:].astype(BF)
-
-
-def project(order, attended, weights):
-    width, rows = weights[0].shape[1], sum(w.shape[0] for w in weights)
-    return pl.pallas_call(
-        project_kernel,
+        for column in range(g * span, (g + 1) * span, step):
+            columns = slice(column, column + step)
+            right = [w_ref[early.index(b), :, columns] if b in early else w[:, columns] for b, w in enumerate(weights)]
+            done = jnp.dot(left, jnp.concatenate(right, axis=0), preferred_element_type=F32)
+            mine_ref[:, columns] = done[:TILE]
+            other_ref[:, columns] = done[TILE:].astype(BF)
+
+
+def project(order, attended, weights, early):
+    width = weights[0].shape[1]
+    spaces = [pltpu.HBM if b in early else pltpu.VMEM for b in range(len(weights))]
+    weights = [pltpu.with_memory_space_constraint(w, space) for w, space in zip(weights, spaces)]
+    return pl.pallas_call(
+        functools.partial(project_kernel, early),
         out_shape=(jax.ShapeDtypeStruct((TILE, width), F32), jax.ShapeDtypeStruct((TILE, width), BF)),
-        in_specs=[WHOLE_SM, WHOLE_VM] + [WHOLE_HBM] * len(weights),
+        in_specs=[WHOLE_SM, WHOLE_VM] + [WHOLE_HBM if b in early else WHOLE_VM for b in range(len(weights))],
         out_specs=(WHOLE_VM,) * 2,
-        scratch_shapes=[VM((rows, width), BF), pltpu.SemaphoreType.DMA((3 * len(weights),))],
+        scratch_shapes=[VM((len(early), TILE, width), BF), pltpu.SemaphoreType.DMA((3 * len(early),))],
         compiler_params=pltpu.CompilerParams(vmem_limit_bytes=24 << 20),
         cost_estimate=pl.CostEstimate(flops=4 * TILE * 8 * TILE * width, bytes_accessed=10 << 20, transcendentals=0),
-    )(order, attended, *in_hbm(weights))
+    )(order, attended, *weights)
 
 
 def listed(place, chosen, slots):
@@ -373,7 +375,7 @@
     pieces = lax.all_to_all(attended.reshape(8, 2 * TILE, TILE), CHIPS, split_axis=0, concat_axis=0, tiled=True)
     order = jnp.stack(chips(((0, 0), (0, 1), (0, 3), (0, 2), (1, 0), (1, 1), (1, 3), (1, 2))) + [core]).astype(jnp.int32)
     weights = [w_out, w_one, w_three, w_two, w_far, wf_pair, wf_two]
-    mine, other = project(order, pieces, weights)
+    mine, other = project(order, pieces, weights, (0, 1, 2, 4))
     return (mine + swap(other, "core").astype(F32)).astype(BF)
 
 

time: 151 us -> 153 us (1.013)
  transfers between devices with their start and end apart: 24 -> 24, of which waited for: 10 -> 10; matrix products, arithmetic and copies ran while one was open for 6% -> 8% of each run, Pallas kernels for 25% -> 25%
where the time goes in v9:
time: 153 us
  waiting for transfers between devices  53.2 us (35%)
  starting transfers between devices  43.4 us (28%)
  Pallas kernels  43.1 us (28%)
  other arithmetic  9.13 us (6%)
  local copies, waits for them, and re-layouts  3.58 us (2%)
    ppermute x10, waiting for transfers between devices, round_x(): return lax.ppermute(array, 'x', [(i, (i + by) % 4) for i in range(4)])  27.2 us
    ppermute x8, starting transfers between devices, swap(): return lax.ppermute(array, axis, [(0, 1), (1, 0)])  22.4 us
    pallas_call x2, Pallas kernels, attend(): pl.pallas_call(functools.partial(attend_kernel, sizes, together, len(fram...  17.6 us
    ppermute x8, waiting for transfers between devices, swap(): return lax.ppermute(array, axis, [(0, 1), (1, 0)])  17.1 us
    pallas_call x2, Pallas kernels, qkv(): pl.pallas_call(functools.partial(qkv_kernel, chunks), out_shape=(jax.Shap...  12 us
    ppermute x10, starting transfers between devices, round_x(): return lax.ppermute(array, 'x', [(i, (i + by) % 4) for i in range(4)])  7.59 us
    all_to_all x1, waiting for transfers between devices, body(): lax.all_to_all(attended.reshape(8, 2 * TILE, TILE), CHIPS, split_axis=0,...  7.1 us
    pallas_call x1, Pallas kernels, place_far(): pl.pallas_call(place_far_kernel, out_shape=(pltpu.HBM((n, TILE), BF), jax...  5.34 us
  transfers between devices with their start and end apart: 24, of which 10 were waited for; matrix products, arithmetic and copies ran while one was open for 8% of the time, Pallas kernels for 25%

profile of v9, /device:TPU:1, one launch (start us, length us, event | category | flops | bytes accessed | tf_op | source)
XLA Modules:
  0.0 152.6 jit_solution(5565738267678665071)
XLA Ops:
  0.0 3.2 %collective-permute-start.5 = (bf16[3072,384]{1,0:T(8,128)(2,1)}, bf16[3072,384]{1,0:T(8,128)(2,1)}, u32[]{:S(2)}, u32[]{:S(2)}) collective-permute-start(bf16[3072,384]{1,0:T(8,128)(2,1)} %own_ref.3), channel_id=1, source_target_pairs={{0,1},{1,0},{2,3},{3,2},{4,5},{5,4},{6,7},{7,6},{8,9},{9,8},{10,11... | collective-permute-start | bytes 7077896 | tf_op jit(solution)/shard_map/ppermute | solution.py:38
  4.7 2.2 %collective-permute-start.6 = (bf16[128,3072]{1,0:T(8,128)(2,1)}, bf16[128,3072]{1,0:T(8,128)(2,1)}, u32[]{:S(2)}, u32[]{:S(2)}) collective-permute-start(bf16[128,3072]{1,0:T(8,128)(2,1)} %refs_0_.2), channel_id=1, source_target_pairs={{0,8},{8,0},{1,9},{9,1},{2,10},{10,2},{3,11},{11,3},{4,12},{12,4},... | collective-permute-start | bytes 2359304 | tf_op jit(solution)/shard_map/ppermute | solution.py:38
  8.7 14.0 %collective-permute-done.2.refs_2_ = bf16[128,3072]{1,0:T(8,128)(2,1)S(1)} collective-permute-done((bf16[128,3072]{1,0:T(8,128)(2,1)}, bf16[128,3072]{1,0:T(8,128)(2,1)S(1)}, u32[]{:S(2)}, u32[]{:S(2)}) %collective-permute-start.2) | collective-permute-done | bytes 786464 | tf_op jit(solution)/shard_map/ppermute | solution.py:34
  23.5 1.9 %collective-permute-start.3 = (bf16[64,3072]{1,0:T(8,128)(2,1)}, bf16[64,3072]{1,0:T(8,128)(2,1)S(1)}, u32[]{:S(2)}, u32[]{:S(2)}) collective-permute-start(bf16[64,3072]{1,0:T(8,128)(2,1)} %slice.21), channel_id=1, source_target_pairs={{0,6},{2,0},{4,2},{6,4},{1,7},{3,1},{5,3},{7,5},{8,14},{10,8},{12,... | collective-permute-start | bytes 1179656 | tf_op jit(solution)/shard_map/ppermute | solution.py:34
  28.1 2.7 %collective-permute-start.9 = (bf16[128,3072]{1,0:T(8,128)(2,1)}, bf16[128,3072]{1,0:T(8,128)(2,1)S(1)}, u32[]{:S(2)}, u32[]{:S(2)}) collective-permute-start(bf16[128,3072]{1,0:T(8,128)(2,1)} %collective-permute-done.6.refs_3_), channel_id=1, source_target_pairs={{0,6},{2,0},{4,2},{6,4},{1,7},{3,1},{5,3},{7,5},{8,14},{10,8},{12,... | collective-permute-start | bytes 2359304 | tf_op jit(solution)/shard_map/ppermute | solution.py:34
  30.8 2.9 %collective-permute-done.3.refs_1_ = bf16[64,3072]{1,0:T(8,128)(2,1)S(1)} collective-permute-done((bf16[64,3072]{1,0:T(8,128)(2,1)}, bf16[64,3072]{1,0:T(8,128)(2,1)S(1)}, u32[]{:S(2)}, u32[]{:S(2)}) %collective-permute-start.3) | collective-permute-done | bytes 393248 | tf_op jit(solution)/shard_map/ppermute | solution.py:34
  33.7 3.4 %collective-permute-done.1.refs_0_ = bf16[64,3072]{1,0:T(8,128)(2,1)S(1)} collective-permute-done((bf16[64,3072]{1,0:T(8,128)(2,1)}, bf16[64,3072]{1,0:T(8,128)(2,1)S(1)}, u32[]{:S(2)}, u32[]{:S(2)}) %collective-permute-start.1) | collective-permute-done | bytes 393248 | tf_op jit(solution)/shard_map/ppermute | solution.py:34
  37.2 2.8 %collective-permute-start.4 = (bf16[128,3072]{1,0:T(8,128)(2,1)S(1)}, bf16[128,3072]{1,0:T(8,128)(2,1)S(1)}, u32[]{:S(2)}, u32[]{:S(2)}) collective-permute-start(bf16[128,3072]{1,0:T(8,128)(2,1)S(1)} %pad_maximum_fusion.1), channel_id=1, source_target_pairs={{0,8},{8,0},{1,9},{9,1},{2,10},{10,2},{3,11},{11,3},{4,12},{12,4},... | collective-permute-start | bytes 2359304 | tf_op jit(solution)/shard_map/ppermute | solution.py:38
  40.0 6.6 %shard_map.64 = (bf16[512,384]{1,0:T(8,128)(2,1)S(1)}, bf16[512,384]{1,0:T(8,128)(2,1)S(1)}) custom-call(bf16[3072,384]{1,0:T(8,128)(2,1)} %own_ref.3, bf16[3072,384]{1,0:T(8,128)(2,1)} %collective-permute-done.5.other_ref, bf16[128,3072]{1,0:T(8,128)(2,1)S(1)} %copy-done, bf16[128,3072]{1,0:T(8,128)(2,1)S(1)} %collective-permute-done.refs_1_, ...), custom_call_target="tpu_custom_call" | custom-call | flops 2415919104 | bytes 8388608 | tf_op jit(solution)/shard_map/pallas_call | solution.py:73
  46.6 4.1 %collective-permute-start.7 = (bf16[512,384]{1,0:T(8,128)(2,1)S(1)}, bf16[512,384]{1,0:T(8,128)(2,1)S(1)}, u32[]{:S(2)}, u32[]{:S(2)}) collective-permute-start(bf16[512,384]{1,0:T(8,128)(2,1)S(1)} %get-tuple-element.27), channel_id=1, source_target_pairs={{0,1},{1,0},{2,3},{3,2},{4,5},{5,4},{6,7},{7,6},{8,9},{9,8},{10,11... | collective-permute-start | bytes 1179656 | tf_op jit(solution)/shard_map/ppermute | solution.py:38
  52.0 3.6 %shard_map.65.near_ref = bf16[2048,384]{1,0:T(8,128)(2,1)S(1)} custom-call(f32[8]{0:T(128)S(1)} %convert_element_type.18.block_ref, s32[2048,1]{1,0:T(8,128)S(1)} %copy.9.want_ref, bf16[512,384]{1,0:T(8,128)(2,1)S(1)} %get-tuple-element.26.first_ref, bf16[512,384]{1,0:T(8,128)(2,1)S(1)} %collective-permute-done.7.second_ref), custom_call_target="tpu_custom_call" | custom-call | flops 1610612736 | bytes 4194304 | tf_op jit(solution)/shard_map/pallas_call | solution.py:139
  55.7 1.4 collective-permute-start.13
  57.0 1.5 collective-permute-start.11
  58.5 5.4 %shard_map.66 = (bf16[512,384]{1,0:T(8,128)(2,1)S(1)}, bf16[512,384]{1,0:T(8,128)(2,1)S(1)}) custom-call(bf16[3072,384]{1,0:T(8,128)(2,1)} %own_ref.3, bf16[3072,384]{1,0:T(8,128)(2,1)} %collective-permute-done.5.other_ref, bf16[64,3072]{1,0:T(8,128)(2,1)S(1)} %collective-permute-done.1.refs_0_, bf16[64,3072]{1,0:T(8,128)(2,1)S(1)} %collective-permute-done.3.refs_1_, ...), custom_call_target="tpu_custom_call" | custom-call | flops 2415919104 | bytes 8388608 | tf_op jit(solution)/shard_map/pallas_call | solution.py:73
  64.0 5.4 %collective-permute-start.10 = (bf16[512,384]{1,0:T(8,128)(2,1)S(1)}, bf16[512,384]{1,0:T(8,128)(2,1)S(1)}, u32[]{:S(2)}, u32[]{:S(2)}) collective-permute-start(bf16[512,384]{1,0:T(8,128)(2,1)S(1)} %get-tuple-element.33), channel_id=1, source_target_pairs={{0,1},{1,0},{2,3},{3,2},{4,5},{5,4},{6,7},{7,6},{8,9},{9,8},{10,11... | collective-permute-start | bytes 1179656 | tf_op jit(solution)/shard_map/ppermute | solution.py:38
  69.4 1.3 collective-permute-done.10.second_ref
  70.7 5.3 %shard_map.67 = (bf16[2048,128]{1,0:T(8,128)(2,1)}, bf16[2048,256]{1,0:T(8,128)(2,1)}) custom-call(f32[8]{0:T(128)S(1)} %convert_element_type.21.block_ref, s32[2048,1]{1,0:T(8,128)S(1)} %copy.9.want_ref, bf16[512,384]{1,0:T(8,128)(2,1)S(1)} %get-tuple-element.32.first_ref, bf16[512,384]{1,0:T(8,128)(2,1)S(1)} %collective-permute-done.10.second_ref, ...), custom_call_target="tpu_custom_call" | custom-call | flops 1610612736 | bytes 4194304 | tf_op jit(solution)/shard_map/pallas_call | solution.py:151
  76.2 1.7 %collective-permute-start.15 = (bf16[2048,256]{1,0:T(8,128)(2,1)}, bf16[2048,256]{1,0:T(8,128)(2,1)}, u32[]{:S(2)}, u32[]{:S(2)}) collective-permute-start(bf16[2048,256]{1,0:T(8,128)(2,1)} %get-tuple-element.38.refs_0_), channel_id=1, source_target_pairs={{0,32},{32,64},{64,96},{96,128},{128,160},{160,192},{192,224},{224... | collective-permute-start | bytes 3145736 | tf_op jit(solution)/shard_map/ppermute | solution.py:359
  77.9 4.1 %collective-permute-start.14 = (bf16[2048,256]{1,0:T(8,128)(2,1)}, bf16[2048,256]{1,0:T(8,128)(2,1)}, u32[]{:S(2)}, u32[]{:S(2)}) collective-permute-start(bf16[2048,256]{1,0:T(8,128)(2,1)} %get-tuple-element.38.refs_0_), channel_id=1, source_target_pairs={{0,224},{32,0},{64,32},{96,64},{128,96},{160,128},{192,160},{224,1... | collective-permute-start | bytes 3145736 | tf_op jit(solution)/shard_map/ppermute | solution.py:360
  82.0 2.6 %pad_maximum_fusion = bf16[256,3072]{1,0:T(8,128)(2,1)} fusion(bf16[128,3072]{1,0:T(8,128)(2,1)} %collective-permute-done.12.refs_2_, bf16[128,3072]{1,0:T(8,128)(2,1)} %collective-permute-done.11.refs_1_), kind=kLoop, calls=%fused_computation | loop fusion | flops 3145728 | bytes 3145728 | tf_op jit(solution)/shard_map/concatenate | solution.py:363
  85.0 13.8 %collective-permute-done.17.refs_2_ = bf16[2048,256]{1,0:T(8,128)(2,1)} collective-permute-done((bf16[2048,256]{1,0:T(8,128)(2,1)}, bf16[2048,256]{1,0:T(8,128)(2,1)}, u32[]{:S(2)}, u32[]{:S(2)}) %collective-permute-start.17) | collective-permute-done | bytes 1048608 | tf_op jit(solution)/shard_map/ppermute | solution.py:38
  99.8 1.7 %collective-permute-start.18 = (bf16[1024,256]{1,0:T(8,128)(2,1)S(1)}, bf16[1024,256]{1,0:T(8,128)(2,1)S(1)}, u32[]{:S(2)}, u32[]{:S(2)}) collective-permute-start(bf16[1024,256]{1,0:T(8,128)(2,1)S(1)} %slice.24), channel_id=1, source_target_pairs={{0,32},{32,64},{64,96},{96,128},{128,160},{160,192},{192,224},{224... | collective-permute-start | bytes 1572872 | tf_op jit(solution)/shard_map/ppermute | solution.py:368
  101.5 1.8 %collective-permute-done.15.refs_1_ = bf16[2048,256]{1,0:T(8,128)(2,1)} collective-permute-done((bf16[2048,256]{1,0:T(8,128)(2,1)}, bf16[2048,256]{1,0:T(8,128)(2,1)}, u32[]{:S(2)}, u32[]{:S(2)}) %collective-permute-start.15) | collective-permute-done | bytes 1048608 | tf_op jit(solution)/shard_map/ppermute | solution.py:359
  104.5 2.8 %collective-permute-start.16 = (bf16[1024,256]{1,0:T(8,128)(2,1)S(1)}, bf16[1024,256]{1,0:T(8,128)(2,1)S(1)}, u32[]{:S(2)}, u32[]{:S(2)}) collective-permute-start(bf16[1024,256]{1,0:T(8,128)(2,1)S(1)} %slice_select_fusion), channel_id=1, source_target_pairs={{0,16},{16,0},{1,17},{17,1},{2,18},{18,2},{3,19},{19,3},{4,20},{20... | collective-permute-start | bytes 1572872 | tf_op jit(solution)/shard_map/ppermute | solution.py:38
  107.3 11.4 %shard_map.68 = (f32[2048,128]{1,0:T(8,128)S(1)}, f32[2048,128]{1,0:T(8,128)S(1)}) custom-call(s32[16,30]{1,0:T(8,128)S(1)} %copy.14.index_ref, s32[16]{0:T(128)S(1)} %get-tuple-element.40.count_ref, bf16[2048,128]{1,0:T(8,128)(2,1)S(1)} %copy-done.2, bf16[2048,256]{1,0:T(8,128)(2,1)} %get-tuple-element.38.refs_0_, ...), custom_call_target="tpu_custom_call" | custom-call | flops 16106127360 | bytes 6291456 | tf_op jit(solution)/shard_map/pallas_call | solution.py:245
  118.8 6.2 %shard_map.69 = bf16[2048,128]{1,0:T(8,128)(2,1)} custom-call(s32[16,16]{1,0:T(8,128)S(1)} %select_reduce_fusion.3.index_ref, s32[16]{0:T(128)S(1)} %get-tuple-element.29.count_ref, bf16[2048,128]{1,0:T(8,128)(2,1)S(1)} %copy-done.2, bf16[1024,256]{1,0:T(8,128)(2,1)S(1)} %collective-permute-done.16.refs_0_, ...), custom_call_target="tpu_custom_call" | custom-call | flops 8589934592 | bytes 6291456 | tf_op jit(solution)/shard_map/pallas_call | solution.py:245
  125.0 4.2 %all-to-all-start = ((bf16[8,256,128]{2,1,0:T(8,128)(2,1)}), bf16[8,256,128]{2,1,0:T(8,128)(2,1)S(1)}, u32[]{:S(2)}, u32[]{:S(2)}) async-start(bf16[8,256,128]{2,1,0:T(8,128)(2,1)} %bitcast.26), calls=%async_computation | async-start | bytes 1048576 | tf_op jit(solution)/shard_map/all_to_all | solution.py:375
  129.4 6.8 %collective-permute-done.21.refs_6_ = bf16[128,3072]{1,0:T(8,128)(2,1)} collective-permute-done((bf16[128,3072]{1,0:T(8,128)(2,1)}, bf16[128,3072]{1,0:T(8,128)(2,1)}, u32[]{:S(2)}, u32[]{:S(2)}) %collective-permute-start.21) | collective-permute-done | bytes 786464 | tf_op jit(solution)/shard_map/ppermute | solution.py:34
  136.1 7.1 %all-to-all-done.att_ref = bf16[8,256,128]{2,1,0:T(8,128)(2,1)S(1)} async-done(((bf16[8,256,128]{2,1,0:T(8,128)(2,1)}), bf16[8,256,128]{2,1,0:T(8,128)(2,1)S(1)}, u32[]{:S(2)}, u32[]{:S(2)}) %all-to-all-start) | async-done | bytes 524320 | tf_op jit(solution)/shard_map/all_to_all | solution.py:375
  143.2 4.6 %shard_map.70 = (f32[128,3072]{1,0:T(8,128)S(1)}, bf16[128,3072]{1,0:T(8,128)(2,1)S(1)}) custom-call(s32[9]{0:T(128)S(1)} %stack.93.order_ref, bf16[8,256,128]{2,1,0:T(8,128)(2,1)S(1)} %all-to-all-done.att_ref, bf16[128,3072]{1,0:T(8,128)(2,1)} %refs_0_.3, bf16[128,3072]{1,0:T(8,128)(2,1)} %collective-permute-done.11.refs_1_, ...), custom_call_target="tpu_custom_call" | custom-call | flops 1610612736 | bytes 10485760 | tf_op jit(solution)/shard_map/pallas_call | solution.py:294
  147.8 1.8 %collective-permute-start.22 = (bf16[128,3072]{1,0:T(8,128)(2,1)S(1)}, bf16[128,3072]{1,0:T(8,128)(2,1)S(1)}, u32[]{:S(2)}, u32[]{:S(2)}) collective-permute-start(bf16[128,3072]{1,0:T(8,128)(2,1)S(1)} %get-tuple-element.46), channel_id=1, source_target_pairs={{0,1},{1,0},{2,3},{3,2},{4,5},{5,4},{6,7},{7,6},{8,9},{9,8},{10,11... | collective-permute-start | bytes 2359304 | tf_op jit(solution)/shard_map/ppermute | solution.py:38
  149.7 1.9 %collective-permute-done.22 = bf16[128,3072]{1,0:T(8,128)(2,1)S(1)} collective-permute-done((bf16[128,3072]{1,0:T(8,128)(2,1)S(1)}, bf16[128,3072]{1,0:T(8,128)(2,1)S(1)}, u32[]{:S(2)}, u32[]{:S(2)}) %collective-permute-start.22) | collective-permute-done | bytes 786464 | tf_op jit(solution)/shard_map/ppermute | solution.py:38
  (58 shorter events, 12.3 us)
Async XLA Ops:
  0.0 27.7 %copy-start.3 = (s32[1,2048]{1,0:T(1,128)S(1)}, s32[1,2048]{1,0:T(1,128)}, u32[]{:S(2)}) copy-start(s32[1,2048]{1,0:T(1,128)} %param.9) | copy-start | bytes 24580
  0.0 40.0 %collective-permute-start.5 = (bf16[3072,384]{1,0:T(8,128)(2,1)}, bf16[3072,384]{1,0:T(8,128)(2,1)}, u32[]{:S(2)}, u32[]{:S(2)}) collective-permute-start(bf16[3072,384]{1,0:T(8,128)(2,1)} %own_ref.3), channel_id=1, source_target_pairs={{0,1},{1,0},{2,3},{3,2},{4,5},{5,4},{6,7},{7,6},{8,9},{9,8},{10,11... | collective-permute-start | bytes 7077896 | tf_op jit(solution)/shard_map/ppermute | solution.py:38
  3.2 19.5 %collective-permute-start.2 = (bf16[128,3072]{1,0:T(8,128)(2,1)}, bf16[128,3072]{1,0:T(8,128)(2,1)S(1)}, u32[]{:S(2)}, u32[]{:S(2)}) collective-permute-start(bf16[128,3072]{1,0:T(8,128)(2,1)} %refs_0_.2), channel_id=1, source_target_pairs={{0,6},{2,0},{4,2},{6,4},{1,7},{3,1},{5,3},{7,5},{8,14},{10,8},{12,... | collective-permute-start | bytes 2359304 | tf_op jit(solution)/shard_map/ppermute | solution.py:34
  4.0 21.4 %collective-permute-start = (bf16[128,3072]{1,0:T(8,128)(2,1)}, bf16[128,3072]{1,0:T(8,128)(2,1)S(1)}, u32[]{:S(2)}, u32[]{:S(2)}) collective-permute-start(bf16[128,3072]{1,0:T(8,128)(2,1)} %refs_0_.2), channel_id=1, source_target_pairs={{0,2},{2,4},{4,6},{6,0},{1,3},{3,5},{5,7},{7,1},{8,10},{10,12},{12... | collective-permute-start | bytes 2359304 | tf_op jit(solution)/shard_map/ppermute | solution.py:34
  4.7 23.4 %collective-permute-start.6 = (bf16[128,3072]{1,0:T(8,128)(2,1)}, bf16[128,3072]{1,0:T(8,128)(2,1)}, u32[]{:S(2)}, u32[]{:S(2)}) collective-permute-start(bf16[128,3072]{1,0:T(8,128)(2,1)} %refs_0_.2), channel_id=1, source_target_pairs={{0,8},{8,0},{1,9},{9,1},{2,10},{10,2},{3,11},{11,3},{4,12},{12,4},... | collective-permute-start | bytes 2359304 | tf_op jit(solution)/shard_map/ppermute | solution.py:38
  23.5 10.2 %collective-permute-start.3 = (bf16[64,3072]{1,0:T(8,128)(2,1)}, bf16[64,3072]{1,0:T(8,128)(2,1)S(1)}, u32[]{:S(2)}, u32[]{:S(2)}) collective-permute-start(bf16[64,3072]{1,0:T(8,128)(2,1)} %slice.21), channel_id=1, source_target_pairs={{0,6},{2,0},{4,2},{6,4},{1,7},{3,1},{5,3},{7,5},{8,14},{10,8},{12,... | collective-permute-start | bytes 1179656 | tf_op jit(solution)/shard_map/ppermute | solution.py:34
  26.2 11.0 %collective-permute-start.1 = (bf16[64,3072]{1,0:T(8,128)(2,1)}, bf16[64,3072]{1,0:T(8,128)(2,1)S(1)}, u32[]{:S(2)}, u32[]{:S(2)}) collective-permute-start(bf16[64,3072]{1,0:T(8,128)(2,1)} %slice.20), channel_id=1, source_target_pairs={{0,2},{2,4},{4,6},{6,0},{1,3},{3,5},{5,7},{7,1},{8,10},{10,12},{12... | collective-permute-start | bytes 1179656 | tf_op jit(solution)/shard_map/ppermute | solution.py:34
  28.0 12.0 %copy-start = (bf16[128,3072]{1,0:T(8,128)(2,1)S(1)}, bf16[128,3072]{1,0:T(8,128)(2,1)}, u32[]{:S(2)}) copy-start(bf16[128,3072]{1,0:T(8,128)(2,1)} %refs_0_.2) | copy-start | bytes 2359300
  28.1 30.4 %collective-permute-start.9 = (bf16[128,3072]{1,0:T(8,128)(2,1)}, bf16[128,3072]{1,0:T(8,128)(2,1)S(1)}, u32[]{:S(2)}, u32[]{:S(2)}) collective-permute-start(bf16[128,3072]{1,0:T(8,128)(2,1)} %collective-permute-done.6.refs_3_), channel_id=1, source_target_pairs={{0,6},{2,0},{4,2},{6,4},{1,7},{3,1},{5,3},{7,5},{8,14},{10,8},{12,... | collective-permute-start | bytes 2359304 | tf_op jit(solution)/shard_map/ppermute | solution.py:34
  30.8 27.7 %collective-permute-start.8 = (bf16[128,3072]{1,0:T(8,128)(2,1)}, bf16[128,3072]{1,0:T(8,128)(2,1)S(1)}, u32[]{:S(2)}, u32[]{:S(2)}) collective-permute-start(bf16[128,3072]{1,0:T(8,128)(2,1)} %collective-permute-done.6.refs_3_), channel_id=1, source_target_pairs={{0,2},{2,4},{4,6},{6,0},{1,3},{3,5},{5,7},{7,1},{8,10},{10,12},{12... | collective-permute-start | bytes 2359304 | tf_op jit(solution)/shard_map/ppermute | solution.py:34
  37.2 18.5 %collective-permute-start.4 = (bf16[128,3072]{1,0:T(8,128)(2,1)S(1)}, bf16[128,3072]{1,0:T(8,128)(2,1)S(1)}, u32[]{:S(2)}, u32[]{:S(2)}) collective-permute-start(bf16[128,3072]{1,0:T(8,128)(2,1)S(1)} %pad_maximum_fusion.1), channel_id=1, source_target_pairs={{0,8},{8,0},{1,9},{9,1},{2,10},{10,2},{3,11},{11,3},{4,12},{12,4},... | collective-permute-start | bytes 2359304 | tf_op jit(solution)/shard_map/ppermute | solution.py:38
  46.6 5.5 %collective-permute-start.7 = (bf16[512,384]{1,0:T(8,128)(2,1)S(1)}, bf16[512,384]{1,0:T(8,128)(2,1)S(1)}, u32[]{:S(2)}, u32[]{:S(2)}) collective-permute-start(bf16[512,384]{1,0:T(8,128)(2,1)S(1)} %get-tuple-element.27), channel_id=1, source_target_pairs={{0,1},{1,0},{2,3},{3,2},{4,5},{5,4},{6,7},{7,6},{8,9},{9,8},{10,11... | collective-permute-start | bytes 1179656 | tf_op jit(solution)/shard_map/ppermute | solution.py:38
  55.7 8.3 %copy-start.1 = (bf16[2048,384]{1,0:T(8,128)(2,1)}, bf16[2048,384]{1,0:T(8,128)(2,1)S(1)}, u32[]{:S(2)}) copy-start(bf16[2048,384]{1,0:T(8,128)(2,1)S(1)} %shard_map.65.near_ref) | copy-start | bytes 4718596
  55.7 20.4 %collective-permute-start.13 = (bf16[128,3072]{1,0:T(8,128)(2,1)}, bf16[128,3072]{1,0:T(8,128)(2,1)}, u32[]{:S(2)}, u32[]{:S(2)}) collective-permute-start(bf16[128,3072]{1,0:T(8,128)(2,1)} %refs_0_.3), channel_id=1, source_target_pairs={{0,24},{8,16},{16,8},{24,0},{1,25},{9,17},{17,9},{25,1},{2,26},{10... | collective-permute-start | bytes 2359304 | tf_op jit(solution)/shard_map/ppermute | solution.py:42
  57.0 19.0 %collective-permute-start.12 = (bf16[128,3072]{1,0:T(8,128)(2,1)}, bf16[128,3072]{1,0:T(8,128)(2,1)}, u32[]{:S(2)}, u32[]{:S(2)}) collective-permute-start(bf16[128,3072]{1,0:T(8,128)(2,1)} %refs_0_.3), channel_id=1, source_target_pairs={{0,6},{2,0},{4,2},{6,4},{1,7},{3,1},{5,3},{7,5},{8,14},{10,8},{12,... | collective-permute-start | bytes 2359304 | tf_op jit(solution)/shard_map/ppermute | solution.py:34
  57.0 19.0 %collective-permute-start.11 = (bf16[128,3072]{1,0:T(8,128)(2,1)}, bf16[128,3072]{1,0:T(8,128)(2,1)}, u32[]{:S(2)}, u32[]{:S(2)}) collective-permute-start(bf16[128,3072]{1,0:T(8,128)(2,1)} %refs_0_.3), channel_id=1, source_target_pairs={{0,2},{2,4},{4,6},{6,0},{1,3},{3,5},{5,7},{7,1},{8,10},{10,12},{12... | collective-permute-start | bytes 2359304 | tf_op jit(solution)/shard_map/ppermute | solution.py:34
  64.0 6.7 %collective-permute-start.10 = (bf16[512,384]{1,0:T(8,128)(2,1)S(1)}, bf16[512,384]{1,0:T(8,128)(2,1)S(1)}, u32[]{:S(2)}, u32[]{:S(2)}) collective-permute-start(bf16[512,384]{1,0:T(8,128)(2,1)S(1)} %get-tuple-element.33), channel_id=1, source_target_pairs={{0,1},{1,0},{2,3},{3,2},{4,5},{5,4},{6,7},{7,6},{8,9},{9,8},{10,11... | collective-permute-start | bytes 1179656 | tf_op jit(solution)/shard_map/ppermute | solution.py:38
  76.1 22.7 %collective-permute-start.17 = (bf16[2048,256]{1,0:T(8,128)(2,1)}, bf16[2048,256]{1,0:T(8,128)(2,1)}, u32[]{:S(2)}, u32[]{:S(2)}) collective-permute-start(bf16[2048,256]{1,0:T(8,128)(2,1)} %get-tuple-element.38.refs_0_), channel_id=1, source_target_pairs={{0,16},{16,0},{1,17},{17,1},{2,18},{18,2},{3,19},{19,3},{4,20},{20... | collective-permute-start | bytes 3145736 | tf_op jit(solution)/shard_map/ppermute | solution.py:38
  76.2 27.1 %collective-permute-start.15 = (bf16[2048,256]{1,0:T(8,128)(2,1)}, bf16[2048,256]{1,0:T(8,128)(2,1)}, u32[]{:S(2)}, u32[]{:S(2)}) collective-permute-start(bf16[2048,256]{1,0:T(8,128)(2,1)} %get-tuple-element.38.refs_0_), channel_id=1, source_target_pairs={{0,32},{32,64},{64,96},{96,128},{128,160},{160,192},{192,224},{224... | collective-permute-start | bytes 3145736 | tf_op jit(solution)/shard_map/ppermute | solution.py:359
  77.9 25.4 %collective-permute-start.14 = (bf16[2048,256]{1,0:T(8,128)(2,1)}, bf16[2048,256]{1,0:T(8,128)(2,1)}, u32[]{:S(2)}, u32[]{:S(2)}) collective-permute-start(bf16[2048,256]{1,0:T(8,128)(2,1)} %get-tuple-element.38.refs_0_), channel_id=1, source_target_pairs={{0,224},{32,0},{64,32},{96,64},{128,96},{160,128},{192,160},{224,1... | collective-permute-start | bytes 3145736 | tf_op jit(solution)/shard_map/ppermute | solution.py:360
  82.0 47.4 %collective-permute-start.19 = (bf16[128,3072]{1,0:T(8,128)(2,1)}, bf16[128,3072]{1,0:T(8,128)(2,1)S(1)}, u32[]{:S(2)}, u32[]{:S(2)}) collective-permute-start(bf16[128,3072]{1,0:T(8,128)(2,1)} %refs_0_.3), channel_id=1, source_target_pairs={{0,4},{2,6},{4,0},{6,2},{1,5},{3,7},{5,1},{7,3},{8,12},{10,14},{12... | collective-permute-start | bytes 2359304 | tf_op jit(solution)/shard_map/ppermute | solution.py:34
  84.6 22.7 %copy-start.2 = (bf16[2048,128]{1,0:T(8,128)(2,1)S(1)}, bf16[2048,128]{1,0:T(8,128)(2,1)}, u32[]{:S(2)}) copy-start(bf16[2048,128]{1,0:T(8,128)(2,1)} %get-tuple-element.35.q_ref) | copy-start | bytes 1572868
  84.6 44.7 %collective-permute-start.20 = (bf16[256,3072]{1,0:T(8,128)(2,1)}, bf16[256,3072]{1,0:T(8,128)(2,1)S(1)}, u32[]{:S(2)}, u32[]{:S(2)}) collective-permute-start(bf16[256,3072]{1,0:T(8,128)(2,1)} %pad_maximum_fusion), channel_id=1, source_target_pairs={{0,24},{8,16},{16,8},{24,0},{1,25},{9,17},{17,9},{25,1},{2,26},{10... | collective-permute-start | bytes 4718600 | tf_op jit(solution)/shard_map/ppermute | solution.py:42
  99.8 19.0 %collective-permute-start.18 = (bf16[1024,256]{1,0:T(8,128)(2,1)S(1)}, bf16[1024,256]{1,0:T(8,128)(2,1)S(1)}, u32[]{:S(2)}, u32[]{:S(2)}) collective-permute-start(bf16[1024,256]{1,0:T(8,128)(2,1)S(1)} %slice.24), channel_id=1, source_target_pairs={{0,32},{32,64},{64,96},{96,128},{128,160},{160,192},{192,224},{224... | collective-permute-start | bytes 1572872 | tf_op jit(solution)/shard_map/ppermute | solution.py:368
  104.5 14.3 %collective-permute-start.16 = (bf16[1024,256]{1,0:T(8,128)(2,1)S(1)}, bf16[1024,256]{1,0:T(8,128)(2,1)S(1)}, u32[]{:S(2)}, u32[]{:S(2)}) collective-permute-start(bf16[1024,256]{1,0:T(8,128)(2,1)S(1)} %slice_select_fusion), channel_id=1, source_target_pairs={{0,16},{16,0},{1,17},{17,1},{2,18},{18,2},{3,19},{19,3},{4,20},{20... | collective-permute-start | bytes 1572872 | tf_op jit(solution)/shard_map/ppermute | solution.py:38
  118.7 17.4 %collective-permute-start.21 = (bf16[128,3072]{1,0:T(8,128)(2,1)}, bf16[128,3072]{1,0:T(8,128)(2,1)}, u32[]{:S(2)}, u32[]{:S(2)}) collective-permute-start(bf16[128,3072]{1,0:T(8,128)(2,1)} %collective-permute-done.13.refs_4_), channel_id=1, source_target_pairs={{0,4},{2,6},{4,0},{6,2},{1,5},{3,7},{5,1},{7,3},{8,12},{10,14},{12... | collective-permute-start | bytes 2359304 | tf_op jit(solution)/shard_map/ppermute | solution.py:34
  125.0 18.2 %all-to-all-start = ((bf16[8,256,128]{2,1,0:T(8,128)(2,1)}), bf16[8,256,128]{2,1,0:T(8,128)(2,1)S(1)}, u32[]{:S(2)}, u32[]{:S(2)}) async-start(bf16[8,256,128]{2,1,0:T(8,128)(2,1)} %bitcast.26), calls=%async_computation | async-start | bytes 1048576 | tf_op jit(solution)/shard_map/all_to_all | solution.py:375
  147.8 3.8 %collective-permute-start.22 = (bf16[128,3072]{1,0:T(8,128)(2,1)S(1)}, bf16[128,3072]{1,0:T(8,128)(2,1)S(1)}, u32[]{:S(2)}, u32[]{:S(2)}) collective-permute-start(bf16[128,3072]{1,0:T(8,128)(2,1)S(1)} %get-tuple-element.46), channel_id=1, source_target_pairs={{0,1},{1,0},{2,3},{3,2},{4,5},{5,4},{6,7},{7,6},{8,9},{9,8},{10,11... | collective-permute-start | bytes 2359304 | tf_op jit(solution)/shard_map/ppermute | solution.py:38
